TPU v7x, 32 devices: a whole 2x2x4 slice. The times are simulated.
32 devices in a mesh: sensor: 8 (over z, y), step: 4 (over x, core).
Axes of the slice: x: 2, y: 2, z: 4, core: 2. Of those that a mesh axis runs over, the one named last changes fastest.
Arguments:
- inputs: bfloat16 [12, 512, 512], P('step', 'sensor'), may hold values from -6 to 6
- cotangent: bfloat16 [12, 512, 512], P('step', 'sensor'), may hold values from -6 to 6
- w_query: bfloat16 [512, 512], replicated, may hold values from -0.25 to 0.25
- w_key: bfloat16 [512, 512], replicated, may hold values from -0.25 to 0.25
- w_value: bfloat16 [512, 512], replicated, may hold values from -0.25 to 0.25
- w_up: bfloat16 [512, 256], replicated, may hold values from -0.25 to 0.25
- w_down: bfloat16 [256, 512], replicated, may hold values from -0.375 to 0.375
- feature_proj: float32 [8, 64, 64], replicated, may hold values from -5 to 5
- live_count: int32 [8], P('sensor'), may hold values from 32 to 64, as said below
Outputs:
- grad_inputs: bfloat16 [12, 512, 512], P('step', 'sensor')
- grad_query: float32 [512, 512], P('sensor', 'step')
- grad_key: float32 [512, 512], P('sensor', 'step')
- grad_value: float32 [512, 512], P('sensor', 'step')
Inputs may be any that keep to these rules, and one draw needn't show every extreme that they name: `live_count`: some group has all 64 sensors live; every group has at least half of them live.
All inputs are finite; a program needn't handle non-finite values.
Results may differ from a plain program's by a relative error of at most 0.012.
Values sent between devices are 32-bit elements; how exact they have to be, the bound alone decides.
No kernel may reach another device: no remote copies, remote signals or barrier semaphores. Data moves between devices by JAX's collectives and lax.ppermute only.
A program may use at most 64 MiB of HBM per device.

v0:
```python
import math

import jax
import jax.numpy as jnp
from jax import lax
from jax.sharding import PartitionSpec as P

HIGH = lax.Precision.HIGHEST


def feature_map(scaled, feature_proj):
    projected = jnp.einsum("...he,her->...hr", scaled, feature_proj, precision=HIGH)
    return jnp.exp(
        projected - 0.5 * jnp.sum(scaled * scaled, -1, keepdims=True)
    ) * feature_proj.shape[2] ** (-0.5)


def feature_back(incoming, feat, scaled, feature_proj):
    weighted = incoming * feat
    return jnp.einsum(
        "...hr,her->...he", weighted, feature_proj, precision=HIGH
    ) - scaled * jnp.sum(weighted, -1, keepdims=True)


def shards(inputs, cotangent, w_query, w_key, w_value, w_up, w_down, feature_proj, live_count):
    steps_here, sensors_here, width = inputs.shape
    heads, head_dim, feats = feature_proj.shape
    factor = head_dim ** (-0.25)
    valid = (jnp.arange(sensors_here, dtype=jnp.int32) < live_count[0]).astype(jnp.float32)
    flat_in = inputs.reshape(steps_here * sensors_here, width)

    def project(weight):
        return jnp.dot(flat_in, weight, preferred_element_type=jnp.float32).reshape(
            steps_here, sensors_here, heads, head_dim
        )

    scaled_query = project(w_query) * factor
    scaled_key = project(w_key) * factor
    values = project(w_value)
    feat_query = feature_map(scaled_query, feature_proj)
    feat_key = feature_map(scaled_key, feature_proj)
    masked_key = feat_key * valid[None, :, None, None]
    local_summary = jnp.einsum("tnhr,tnhe->thre", masked_key, values, precision=HIGH)
    local_normal = jnp.sum(masked_key, 1)
    summed = [
        lax.psum((local_summary[moment], local_normal[moment]), "sensor")
        for moment in range(steps_here)
    ]
    summary = jnp.stack([entry[0] for entry in summed])
    normal_sum = jnp.stack([entry[1] for entry in summed])
    numer = jnp.einsum("tnhr,thre->tnhe", feat_query, summary, precision=HIGH)
    denom = jnp.einsum("tnhr,thr->tnh", feat_query, normal_sum, precision=HIGH)
    attended = numer / denom[..., None]
    flat_att = attended.reshape(steps_here * sensors_here, width)
    rms_val = jnp.sqrt(jnp.mean(flat_att * flat_att, -1, keepdims=True) + 1e-06)
    normed = flat_att / rms_val
    pre_act = jnp.dot(normed.astype(jnp.bfloat16), w_up, preferred_element_type=jnp.float32)
    masked_cot = (cotangent * valid.astype(jnp.bfloat16)[None, :, None]).reshape(
        steps_here * sensors_here, width
    )
    grad_hidden = jnp.dot(masked_cot, w_down.T, preferred_element_type=jnp.float32)
    _, gelu_back = jax.vjp(jax.nn.gelu, pre_act)
    grad_pre = gelu_back(grad_hidden)[0].astype(jnp.bfloat16)
    grad_normed = jnp.dot(grad_pre, w_up.T, preferred_element_type=jnp.float32)
    grad_att = (grad_normed - normed * jnp.mean(grad_normed * normed, -1, keepdims=True)) / rms_val
    grad_att = grad_att.reshape(steps_here, sensors_here, heads, head_dim)
    grad_num = grad_att / denom[..., None]
    grad_den = -jnp.sum(grad_att * attended, -1) / denom
    grad_fq = (
        jnp.einsum("tnhe,thre->tnhr", grad_num, summary, precision=HIGH)
        + grad_den[..., None] * normal_sum[:, None]
    )
    local_gsum = jnp.einsum("tnhr,tnhe->thre", feat_query, grad_num, precision=HIGH)
    local_gnorm = jnp.einsum("tnhr,tnh->thr", feat_query, grad_den, precision=HIGH)
    gathered = [
        lax.psum((local_gsum[moment], local_gnorm[moment]), "sensor")
        for moment in range(steps_here)
    ]
    grad_summary = jnp.stack([entry[0] for entry in gathered])
    grad_normal = jnp.stack([entry[1] for entry in gathered])
    grad_fk = (
        jnp.einsum("tnhe,thre->tnhr", values, grad_summary, precision=HIGH) + grad_normal[:, None]
    ) * valid[None, :, None, None]
    grad_val = jnp.einsum("tnhr,thre->tnhe", masked_key, grad_summary, precision=HIGH)
    grad_q = feature_back(grad_fq, feat_query, scaled_query, feature_proj) * factor
    grad_k = feature_back(grad_fk, feat_key, scaled_key, feature_proj) * factor
    flat_rows = steps_here * sensors_here
    grad_q = grad_q.reshape(flat_rows, width).astype(jnp.bfloat16)
    grad_k = grad_k.reshape(flat_rows, width).astype(jnp.bfloat16)
    grad_val = grad_val.reshape(flat_rows, width).astype(jnp.bfloat16)
    grad_in = jnp.dot(grad_q, w_query.T, preferred_element_type=jnp.float32)
    grad_in = grad_in + jnp.dot(grad_k, w_key.T, preferred_element_type=jnp.float32)
    grad_in = grad_in + jnp.dot(grad_val, w_value.T, preferred_element_type=jnp.float32)
    grad_inputs = grad_in.astype(jnp.bfloat16).reshape(steps_here, sensors_here, width)
    weight_q = jnp.einsum("nd,nk->dk", flat_in, grad_q, preferred_element_type=jnp.float32)
    weight_k = jnp.einsum("nd,nk->dk", flat_in, grad_k, preferred_element_type=jnp.float32)
    weight_v = jnp.einsum("nd,nk->dk", flat_in, grad_val, preferred_element_type=jnp.float32)
    partial_sums = (
        lax.psum_scatter(weight_q, "sensor", scatter_dimension=0, tiled=True),
        lax.psum_scatter(weight_k, "sensor", scatter_dimension=0, tiled=True),
        lax.psum_scatter(weight_v, "sensor", scatter_dimension=0, tiled=True),
    )
    reduced = (
        lax.psum_scatter(partial_sums[0], "step", scatter_dimension=1, tiled=True),
        lax.psum_scatter(partial_sums[1], "step", scatter_dimension=1, tiled=True),
        lax.psum_scatter(partial_sums[2], "step", scatter_dimension=1, tiled=True),
    )
    total_rows = steps_here * lax.axis_size("step") * sensors_here * lax.axis_size("sensor")
    norm_scale = 1.0 / math.sqrt(total_rows)
    return (grad_inputs, reduced[0] * norm_scale, reduced[1] * norm_scale, reduced[2] * norm_scale)


def solution(mesh):
    placed = (
        P("step", "sensor", None),
        P("step", "sensor", None),
        P(),
        P(),
        P(),
        P(),
        P(),
        P(),
        P("sensor"),
    )
    return jax.shard_map(
        shards,
        mesh=mesh,
        in_specs=placed,
        out_specs=(
            P("step", "sensor", None),
            P("sensor", "step"),
            P("sensor", "step"),
            P("sensor", "step"),
        ),
        check_vma=False,
    )
```

profile of v0, /device:TPU:0, one launch (start us, length us, event | category | flops | bytes accessed | tf_op | source)
XLA Modules:
  0.0 468.4 jit_solution(15220190872507572797)
XLA Ops:
  7.9 1.3 copy.101
  9.5 0.7 copy-done.1
  10.6 1.3 multiply_reduce_fusion.3
  11.9 2.4 fusion.76
  14.4 1.4 fusion.28
  15.8 0.9 fusion.78
  16.8 1.0 copy-done.6
  18.0 1.4 multiply_reduce_fusion.2
  19.4 0.8 copy-done.13
  20.5 1.5 fusion.4
  22.7 0.7 copy-done.22
  23.3 39.0 %all-reduce.1 = (f32[1,8,64]{2,0,1:T(1,128)S(1)}, f32[1,8,64]{2,0,1:T(1,128)S(1)}, f32[1,8,64]{2,0,1:T(1,128)S(1)}) all-reduce(f32[1,8,64]{2,0,1:T(1,128)} %get-tuple-element.50, f32[1,8,64]{2,0,1:T(1,128)} %get-tuple-element.51, f32[1,8,64]{2,0,1:T(1,128)S(1)} %copy-done.22), channel_id=1, replica_groups=mesh['sensor'=8,'step'=4] {'sensor'}, use_global_device_ids=true, to_apply=%region_8.0 | all-reduce | flops 1536 | bytes 12288 | tf_op jit(solution)/shard_map/psum | solution.py:46
  63.0 1.3 fusion.34
  64.3 30.5 %all-reduce.9.cloned.1.call-done = (f32[1,8,64,64]{3,2,1,0:T(8,128)}, f32[1,8,64,64]{3,2,1,0:T(8,128)}, f32[1,8,64,64]{3,2,1,0:T(8,128)}) async-done(((f32[1,8,64,64]{3,2,1,0:T(8,128)}, f32[1,8,64,64]{3,2,1,0:T(8,128)}, f32[1,8,64,64]{3,2,1,0:T(8,128)}), (f32[1,8,64,64]{3,2,1,0:T(8,128)}, f32[1,8,64,64]{3,2,1,0:T(8,128)}, f32[1,8,64,64]{3,2,1,0:T(8,128)})) %all-reduce.9.cloned.1.call-update) | async-done | bytes 393232 | tf_op jit(solution)/shard_map/psum | solution.py:46
  94.8 1.0 constant_dynamic-update-slice_fusion.2
  95.9 0.9 copy-done.14
  96.8 2.3 multiply_reduce_fusion.1
  99.1 0.6 sqrt.12
  99.8 2.3 copy.113
  102.1 2.1 reshape.91
  104.2 3.1 multiply_reduce_fusion.4
  107.4 0.7 copy-done.24
  108.0 2.0 subtract_divide_fusion
  110.0 2.1 reshape.92
  112.1 2.3 copy.114
  114.4 1.6 multiply_reduce_fusion
  116.6 1.4 fusion.30
  118.1 2.6 fusion.83
  120.6 1.0 fusion.77
  121.7 4.0 fusion.16
  125.6 2.0 copy.123
  127.6 1.3 convert_element_type.57
  128.9 1.3 convolution_bitcast_fusion.2
  130.2 2.5 copy.166
  133.1 62.8 %all-reduce.7.cloned.1.call-done = (f32[1,8,64,64]{3,2,1,0:T(8,128)}, f32[1,8,64,64]{3,2,1,0:T(8,128)}, f32[1,8,64,64]{3,2,1,0:T(8,128)}) async-done(((f32[1,8,64,64]{3,2,1,0:T(8,128)}, f32[1,8,64,64]{3,2,1,0:T(8,128)}, f32[1,8,64,64]{3,2,1,0:T(8,128)}), (f32[1,8,64,64]{3,2,1,0:T(8,128)}, f32[1,8,64,64]{3,2,1,0:T(8,128)}, f32[1,8,64,64]{3,2,1,0:T(8,128)})) %all-reduce.7.cloned.1.call-update) | async-done | bytes 393232 | tf_op jit(solution)/shard_map/psum | solution.py:76
  195.9 1.0 constant_dynamic-update-slice_fusion.5
  197.0 0.9 copy-done.16
  197.9 0.9 copy-done.2
  198.8 2.2 fusion.17
  201.0 1.2 copy.133
  202.5 1.3 convolution_bitcast_fusion
  203.8 2.6 copy.170
  207.1 0.8 fusion.32
  207.9 35.1 %all-reduce = (f32[1,8,64]{2,0,1:T(1,128)S(1)}, f32[1,8,64]{2,0,1:T(1,128)S(1)}, f32[1,8,64]{2,0,1:T(1,128)S(1)}) all-reduce(f32[1,8,64]{2,0,1:T(1,128)S(1)} %get-tuple-element.47, f32[1,8,64]{2,0,1:T(1,128)S(1)} %get-tuple-element.48, f32[1,8,64]{2,0,1:T(1,128)S(1)} %get-tuple-element.46), channel_id=1, replica_groups=mesh['sensor'=8,'step'=4] {'sensor'}, use_global_device_ids=true, to_apply=%region_18.0 | all-reduce | flops 1536 | bytes 12288 | tf_op jit(solution)/shard_map/psum | solution.py:76
  243.0 2.7 fusion.84
  245.8 1.9 fusion.15
  248.5 1.3 copy.168
  249.9 11.7 %reduce-scatter.19.cloned.1.call-done = f32[64,512]{1,0:T(8,128)} async-done(((f32[512,512]{1,0:T(8,128)}), f32[64,512]{1,0:T(8,128)}) %reduce-scatter.19.cloned.1.call-update) | async-done | bytes 131088
  261.6 1.7 copy.167
  263.4 0.9 copy-done.10
  264.6 63.0 %reduce-scatter.23.cloned.1.call-done = f32[64,512]{1,0:T(8,128)} async-done(((f32[512,512]{1,0:T(8,128)}), f32[64,512]{1,0:T(8,128)}) %reduce-scatter.23.cloned.1.call-update) | async-done | bytes 131088
  327.6 1.7 copy.171
  330.4 1.0 fusion.18
  331.4 61.9 %reduce-scatter.21.cloned.1.call-done = f32[64,512]{1,0:T(8,128)} async-done(((f32[512,512]{1,0:T(8,128)}), f32[64,512]{1,0:T(8,128)}) %reduce-scatter.21.cloned.1.call-update) | async-done | bytes 131088
  393.3 1.8 copy.169
  395.1 19.8 %reduce-scatter.13.cloned.1.call-done = f32[64,128]{0,1:T(8,128)} async-done(((f32[64,512]{0,1:T(8,128)}), f32[64,128]{0,1:T(8,128)}) %reduce-scatter.13.cloned.1.call-update) | async-done | bytes 32784 | tf_op jit(solution)/shard_map/reduce_scatter | solution.py:104
  414.8 0.8 broadcast_multiply_fusion.6
  415.7 0.7 copy.134
  416.4 21.0 %reduce-scatter.17.cloned.1.call-done = f32[64,128]{0,1:T(8,128)} async-done(((f32[64,512]{0,1:T(8,128)}), f32[64,128]{0,1:T(8,128)}) %reduce-scatter.17.cloned.1.call-update) | async-done | bytes 32784 | tf_op jit(solution)/shard_map/reduce_scatter | solution.py:106
  437.3 0.8 broadcast_multiply_fusion.4
  438.2 0.7 copy.136
  438.9 21.2 %reduce-scatter.15.cloned.1.call-done = f32[64,128]{0,1:T(8,128)} async-done(((f32[64,512]{0,1:T(8,128)}), f32[64,128]{0,1:T(8,128)}) %reduce-scatter.15.cloned.1.call-update) | async-done | bytes 32784 | tf_op jit(solution)/shard_map/reduce_scatter | solution.py:105
  460.0 0.8 broadcast_multiply_fusion.5
  460.9 0.7 copy.135
  (90 shorter events, 6.9 us)
Async XLA Ops:
  7.2 4.8 %copy-start = (f32[8,64,64]{2,1,0:T(8,128)S(1)}, f32[8,64,64]{2,1,0:T(8,128)}, u32[]{:S(2)}) copy-start(f32[8,64,64]{2,1,0:T(8,128)} %param.16) | copy-start | bytes 393220
  7.2 87.6 %all-reduce.9.cloned.1.call-start = ((), (), s32[]{:S(2)}) async-start(), calls=%async_computation.13 | async-start | bytes 1572864 | tf_op jit(solution)/shard_map/psum | solution.py:46
  7.9 1.3 copy-start.7
  9.3 0.9 copy-start.1
  16.7 1.0 copy-start.6
  16.7 179.2 %all-reduce.7.cloned.1.call-start = ((), (), s32[]{:S(2)}) async-start(), calls=%async_computation.12 | async-start | bytes 1572864 | tf_op jit(solution)/shard_map/psum | solution.py:76
  18.0 1.4 copy-start.18
  19.3 0.9 copy-start.13
  22.7 0.7 copy-start.22
  94.8 1.0 copy-start.15
  95.8 0.9 copy-start.14
  96.8 2.3 copy-start.11
  102.1 2.1 copy-start.23
  107.3 0.7 copy-start.24
  116.0 0.6 copy-start.19
  116.6 1.5 copy-start.12
  116.6 1.5 copy-start.21
  121.6 140.0 %reduce-scatter.19.cloned.1.call-start = ((), (), s32[]{:S(2)}) async-start(), calls=%async_computation.9 | async-start | bytes 1179648
  128.9 1.3 copy-start.9
  132.8 194.8 %reduce-scatter.23.cloned.1.call-start = ((), (), s32[]{:S(2)}) async-start(), calls=%async_computation.11 | async-start | bytes 1179648
  195.9 1.0 copy-start.17
  196.9 0.9 copy-start.16
  197.9 0.9 copy-start.2
  206.4 0.7 copy-start.20
  206.4 36.7 %copy-start.3 = (f32[3,8,64,64]{3,2,1,0:T(8,128)S(1)}, f32[3,8,64,64]{3,2,1,0:T(8,128)}, u32[]{:S(2)}) copy-start(f32[3,8,64,64]{3,2,1,0:T(8,128)} %copy-done.2) | copy-start | bytes 1179652
  206.4 186.9 %reduce-scatter.21.cloned.1.call-start = ((), (), s32[]{:S(2)}) async-start(), calls=%async_computation.10 | async-start | bytes 1179648
  243.0 2.7 copy-start.4
  249.9 165.0 %reduce-scatter.13.cloned.1.call-start = ((), (), s32[]{:S(2)}) async-start(), calls=%async_computation.6 | async-start | bytes 327680 | tf_op jit(solution)/shard_map/reduce_scatter | solution.py:104
  263.3 0.9 copy-start.10
  263.4 174.0 %reduce-scatter.17.cloned.1.call-start = ((), (), s32[]{:S(2)}) async-start(), calls=%async_computation.8 | async-start | bytes 327680 | tf_op jit(solution)/shard_map/reduce_scatter | solution.py:106
  264.6 64.8 %copy-start.5 = (bf16[512,512]{1,0:T(8,128)(2,1)S(1)}, bf16[512,512]{1,0:T(8,128)(2,1)}, u32[]{:S(2)}) copy-start(bf16[512,512]{1,0:T(8,128)(2,1)} %param.12) | copy-start | bytes 1572868
  329.3 1.0 copy-start.8
  329.4 130.7 %reduce-scatter.15.cloned.1.call-start = ((), (), s32[]{:S(2)}) async-start(), calls=%async_computation.7 | async-start | bytes 327680 | tf_op jit(solution)/shard_map/reduce_scatter | solution.py:105
Sparse Core Ops, SparseCore 0:
  16.9 77.9 all-reduce.8
  121.7 74.1 all-reduce.6
  199.3 62.2 reduce-scatter.18
  265.2 62.3 reduce-scatter.22
  330.8 62.3 reduce-scatter.20
  395.7 19.0 reduce-scatter.12
  417.3 20.0 reduce-scatter.16
  439.9 20.0 reduce-scatter.14
where the time goes:
time: 470 us; the launch traced here: 468 us
  waiting for transfers between devices  292 us (62%)
  blocking collectives  74.1 us (16%)
  local copies, waits for them, and re-layouts  44.1 us (9%)
  matrix products  35.6 us (8%)
  between operations  15.2 us (3%)
  other arithmetic  6.9 us (1%)
    unnamed x11, waiting for transfers between devices  137 us
    psum x1, waiting for transfers between devices, shards(): lax.psum((local_gsum[moment], local_gnorm[moment]), 'sensor')  62.8 us
    psum x1, blocking collectives, shards(): lax.psum((local_summary[moment], local_normal[moment]), 'sensor')  39 us
    psum x1, blocking collectives, shards(): lax.psum((local_gsum[moment], local_gnorm[moment]), 'sensor')  35.1 us
    psum x1, waiting for transfers between devices, shards(): lax.psum((local_summary[moment], local_normal[moment]), 'sensor')  30.5 us
    unnamed x66, local copies, waits for them, and re-layouts  26.9 us
    reduce_scatter x1, waiting for transfers between devices, shards(): lax.psum_scatter(partial_sums[1], 'step', scatter_dimension=1, tiled=True)  21.2 us
    reduce_scatter x1, waiting for transfers between devices, shards(): lax.psum_scatter(partial_sums[2], 'step', scatter_dimension=1, tiled=True)  21 us
  transfers between devices with their start and end apart: 8, of which 8 were waited for; matrix products, arithmetic and copies ran while one was open for 9% of the time, Pallas kernels for 0%

commit v1 on v0

v1 whole, which is shorter than its diff:
```python
import functools
import math

import jax
import jax.numpy as jnp
from jax import lax
from jax.experimental import pallas as pl
from jax.experimental.pallas import tpu as pltpu
from jax.sharding import PartitionSpec as P

F32 = jnp.float32
BF16 = jnp.bfloat16
NN = (((1,), (0,)), ((), ()))
NT = (((1,), (1,)), ((), ()))
TN = (((0,), (0,)), ((), ()))
VMEM = pl.BlockSpec(memory_space=pltpu.VMEM)
SMEM = pl.BlockSpec(memory_space=pltpu.SMEM)
LANES = 128
WIDE = 256


def dot(a, b, dims=NN):
    return lax.dot_general(a, b, dims, preferred_element_type=F32)


def split(x):
    high = x.astype(BF16)
    return high, (x - high.astype(F32)).astype(BF16)


def dot3(a, b, dims=NN):
    return dot(a[0], b[0], dims) + (dot(a[0], b[1], dims) + dot(a[1], b[0], dims))


def head_mask(size):
    rows = lax.broadcasted_iota(jnp.int32, (WIDE, WIDE), 0) // size
    cols = lax.broadcasted_iota(jnp.int32, (WIDE, WIDE), 1) // size
    return rows == cols


def spread(x, mask):
    return jnp.where(mask, jnp.concatenate([x] * (WIDE // x.shape[0]), 0), 0.0)


def gather_diagonal(x, size):
    head = lax.broadcasted_iota(jnp.int32, (size, WIDE), 1) // size
    out = x[:size]
    for g in range(1, WIDE // size):
        out = jnp.where(head == g, x[g * size : (g + 1) * size], out)
    return out


def head_sums(x, ones):
    high, low = split(x)
    return dot(high, ones) + dot(low, ones)


def halves(x):
    return [x[:, h : h + WIDE] for h in range(0, x.shape[1], WIDE)]


def projection(proj_ref):
    heads = proj_ref.shape[0]
    per = WIDE // proj_ref.shape[1]
    return [
        jnp.concatenate([proj_ref[g + h] for h in range(per)], -1) for g in range(0, heads, per)
    ]


def feature_map(scaled, proj, mask, ones, size):
    out = []
    for u, p in zip(halves(scaled), proj):
        projected = dot3(split(u), split(spread(p, mask)))
        out.append(jnp.exp(projected - 0.5 * head_sums(u * u, ones)) * size ** (-0.5))
    return jnp.concatenate(out, -1)


def feature_back(weighted, scaled, proj, mask, ones):
    out = []
    for w, u, p in zip(halves(weighted), halves(scaled), proj):
        high, low = split(w)
        back = dot3((high, low), split(spread(p, mask)), NT)
        out.append(back - u * (dot(high, ones) + dot(low, ones)))
    return jnp.concatenate(out, -1)


def store_summary(out_ref, step, matrices, sums):
    chunks = out_ref.shape[0]
    groups = sums.shape[1] // LANES
    per_half = WIDE // LANES
    for group in range(groups):
        part = matrices[group // per_half][:, (group % per_half) * LANES :][:, :LANES]
        row = (step * groups + group) * 8
        for chunk in range(chunks):
            out_ref[chunk, row : row + 8, :] = part[chunk * 8 : chunk * 8 + 8]
        slot = step * groups + group
        base = out_ref.shape[1] - 8
        out_ref[slot // 8, base + slot % 8 : base + slot % 8 + 1, :] = sums[
            :, group * LANES : (group + 1) * LANES
        ]


def load_summary(in_ref, step, groups):
    chunks = in_ref.shape[0]
    columns, sums = [], []
    for group in range(groups):
        slot = step * groups + group
        row = slot * 8
        columns.append(
            jnp.concatenate([in_ref[c, row : row + 8, :] for c in range(chunks)], 0)
        )
        base = in_ref.shape[1] - 8
        sums.append(in_ref[slot // 8, base + slot % 8 : base + slot % 8 + 1, :])
    whole = jnp.concatenate(columns, -1)
    return halves(whole), jnp.concatenate(sums, -1)


def outer_sums(a, b, size):
    out = []
    for x, y in zip(halves(a), halves(b)):
        xh, xl = split(x)
        yh, yl = split(y)
        whole = dot(
            jnp.concatenate([xh, xh, xl], 0), jnp.concatenate([yh, yl, yh], 0), TN
        )
        out.append(gather_diagonal(whole, size))
    return out


def key_kernel(steps, factor, live_ref, x_ref, wk_ref, wv_ref, proj_ref, u_ref, v_ref, f_ref, s_ref, x32_ref):
    size = proj_ref.shape[1]
    x = x_ref[...]
    x32_ref[...] = x.astype(F32)
    rows = x.shape[0] // steps
    mask = head_mask(size)
    ones = jnp.where(mask, 1.0, 0.0).astype(BF16)
    scaled = dot(x, wk_ref[...]) * factor
    values = dot(x, wv_ref[...])
    u_ref[...] = scaled
    v_ref[...] = values
    feat = feature_map(scaled, projection(proj_ref), mask, ones, proj_ref.shape[2])
    place = lax.broadcasted_iota(jnp.int32, feat.shape, 0) % rows
    feat = jnp.where(place < live_ref[0], feat, 0.0)
    f_ref[...] = feat
    base = s_ref.shape[1] - 8
    for chunk in range(s_ref.shape[0]):
        s_ref[chunk, base:, :] = jnp.zeros((8, LANES), F32)
    for step in range(steps):
        part = slice(step * rows, (step + 1) * rows)
        store_summary(
            s_ref,
            step,
            outer_sums(feat[part], values[part], size),
            jnp.sum(feat[part], 0, keepdims=True),
        )


def query_kernel(steps, factor, live_ref, x_ref, cot_ref, wq_ref, wd_ref, proj_ref, u_ref, f_ref, gh_ref):
    size = proj_ref.shape[1]
    mask = head_mask(size)
    ones = jnp.where(mask, 1.0, 0.0).astype(BF16)
    scaled = dot(x_ref[...], wq_ref[...]) * factor
    u_ref[...] = scaled
    f_ref[...] = feature_map(scaled, projection(proj_ref), mask, ones, proj_ref.shape[2])
    rows = x_ref.shape[0] // steps
    hidden = dot(cot_ref[...], wd_ref[...], NT)
    place = lax.broadcasted_iota(jnp.int32, hidden.shape, 0) % rows
    gh_ref[...] = jnp.where(place < live_ref[0], hidden, 0.0)


def sum_kernel(in_ref, out_ref):
    total = in_ref[0]
    for chunk in range(1, in_ref.shape[0]):
        total = total + in_ref[chunk]
    for chunk in range(out_ref.shape[0]):
        out_ref[chunk] = total


def middle_kernel(steps, size, s_ref, f_ref, gh_ref, wu_ref, num_ref, den_ref, g_ref):
    mask = head_mask(size)
    ones = jnp.where(mask, 1.0, 0.0).astype(BF16)
    feat = f_ref[...]
    width = feat.shape[1]
    rows = feat.shape[0] // steps
    groups = width // LANES
    numer, weighted = [], []
    for step in range(steps):
        matrices, sums = load_summary(s_ref, step, groups)
        part = feat[step * rows : (step + 1) * rows]
        numer.append(
            jnp.concatenate(
                [dot3(split(f), split(spread(m, mask))) for f, m in zip(halves(part), matrices)],
                -1,
            )
        )
        weighted.append(part * sums)
    numer = jnp.concatenate(numer, 0)
    weighted = jnp.concatenate(weighted, 0)
    denom = jnp.concatenate([head_sums(w, ones) for w in halves(weighted)], -1)
    inverse = 1.0 / denom
    attended = numer * inverse
    scale = lax.rsqrt(jnp.mean(attended * attended, -1, keepdims=True) + 1e-06)
    normed = attended * scale
    wu = wu_ref[...]
    pre = dot(normed.astype(BF16), wu)
    c = math.sqrt(2.0 / math.pi)
    square = pre * pre
    t = jnp.tanh(c * pre * (1.0 + 0.044715 * square))
    slope = 0.5 * (1.0 + t) + 0.5 * pre * (1.0 - t * t) * (c * (1.0 + 3 * 0.044715 * square))
    grad_pre = (gh_ref[...] * slope).astype(BF16)
    grad_normed = dot(grad_pre, wu, NT)
    grad_att = (grad_normed - normed * jnp.mean(grad_normed * normed, -1, keepdims=True)) * scale
    grad_num = grad_att * inverse
    along = grad_att * attended
    grad_den = -jnp.concatenate([head_sums(a, ones) for a in halves(along)], -1) * inverse
    num_ref[...] = grad_num
    den_ref[...] = grad_den
    base = g_ref.shape[1] - 8
    for chunk in range(g_ref.shape[0]):
        g_ref[chunk, base:, :] = jnp.zeros((8, LANES), F32)
    for step in range(steps):
        part = slice(step * rows, (step + 1) * rows)
        store_summary(
            g_ref,
            step,
            outer_sums(feat[part], grad_num[part], size),
            jnp.sum(feat[part] * grad_den[part], 0, keepdims=True),
        )


def send_columns(grads, send_refs, own_ref, me, size):
    count = len(send_refs) + 1
    for shift, ref in enumerate([own_ref] + list(send_refs)):
        target = lax.rem(me + shift, count)
        for place, g in enumerate(grads):
            ref[:, place * size : (place + 1) * size] = g[:, pl.ds(pl.multiple_of(target * size, size), size)]


def query_back_kernel(steps, factor, axis, cols, s_ref, num_ref, den_ref, f_ref, u_ref, proj_ref, g_ref, own_ref, *rest):
    send_refs, scratch = rest[:-1], rest[-1]
    size = proj_ref.shape[1]
    mask = head_mask(size)
    ones = jnp.where(mask, 1.0, 0.0).astype(BF16)
    feat = f_ref[...]
    rows = feat.shape[0] // steps
    groups = feat.shape[1] // LANES
    out = []
    for step in range(steps):
        matrices, sums = load_summary(s_ref, step, groups)
        part = slice(step * rows, (step + 1) * rows)
        back = jnp.concatenate(
            [
                dot3(split(n), split(spread(m, mask)), NT)
                for n, m in zip(halves(num_ref[part, :]), matrices)
            ],
            -1,
        )
        out.append(back + den_ref[part, :] * sums)
    weighted = jnp.concatenate(out, 0) * feat
    grad = (feature_back(weighted, u_ref[...], projection(proj_ref), mask, ones) * factor).astype(BF16)
    g_ref[...] = grad
    scratch[...] = grad.astype(F32)
    send_columns([scratch], send_refs, own_ref, lax.axis_index(axis), cols)


def key_back_kernel(steps, factor, axis, cols, g_ref, v_ref, f_ref, u_ref, proj_ref, gk_ref, gv_ref, own_ref, *rest):
    send_refs, scratch_k, scratch_v = rest[:-2], rest[-2], rest[-1]
    size = proj_ref.shape[1]
    mask = head_mask(size)
    ones = jnp.where(mask, 1.0, 0.0).astype(BF16)
    feat = f_ref[...]
    rows = feat.shape[0] // steps
    groups = feat.shape[1] // LANES
    back, grad_v = [], []
    for step in range(steps):
        matrices, sums = load_summary(g_ref, step, groups)
        spreads = [split(spread(m, mask)) for m in matrices]
        part = slice(step * rows, (step + 1) * rows)
        back.append(
            jnp.concatenate(
                [dot3(split(v), m, NT) for v, m in zip(halves(v_ref[part, :]), spreads)], -1
            )
            + sums
        )
        grad_v.append(
            jnp.concatenate([dot3(split(f), m) for f, m in zip(halves(feat[part]), spreads)], -1)
        )
    weighted = jnp.concatenate(back, 0) * feat
    grad_k = (feature_back(weighted, u_ref[...], projection(proj_ref), mask, ones) * factor).astype(BF16)
    grad_v = jnp.concatenate(grad_v, 0).astype(BF16)
    gk_ref[...] = grad_k
    gv_ref[...] = grad_v
    scratch_k[...] = grad_k.astype(F32)
    scratch_v[...] = grad_v.astype(F32)
    send_columns([scratch_k, scratch_v], send_refs, own_ref, lax.axis_index(axis), cols)


def rows_kernel(gq_ref, gk_ref, gv_ref, wq_ref, wk_ref, wv_ref, out_ref):
    total = dot(gq_ref[...], wq_ref[...], NT)
    total = total + dot(gk_ref[...], wk_ref[...], NT)
    out_ref[...] = (total + dot(gv_ref[...], wv_ref[...], NT)).astype(BF16)


def outer_kernel(count, *refs):
    xs, gq, gkv, out_ref = refs[:count], refs[count : 2 * count], refs[2 * count : 3 * count], refs[-1]
    x = jnp.concatenate([r[...].astype(BF16) for r in xs], 0)
    q = jnp.concatenate([r[...].astype(BF16) for r in gq], 0)
    kv = jnp.concatenate([r[...].astype(BF16) for r in gkv], 0)
    total = dot(x, jnp.concatenate([q, kv], -1), TN)
    chunks, rows = out_ref.shape[:2]
    for chunk in range(chunks):
        out_ref[chunk] = total[chunk * rows : (chunk + 1) * rows]


def final_kernel(scale, in_ref, *outs):
    total = in_ref[0]
    for chunk in range(1, in_ref.shape[0]):
        total = total + in_ref[chunk]
    cols = outs[0].shape[1]
    for place, ref in enumerate(outs):
        ref[...] = total[:, place * cols : (place + 1) * cols] * scale


def call(kernel, name, outs, args, flops=0, smem=0, scratch=()):
    size = lambda a: math.prod(a.shape) * a.dtype.itemsize
    return pl.pallas_call(
        kernel,
        name=name,
        out_shape=outs,
        in_specs=[SMEM] * smem + [VMEM] * (len(args) - smem),
        out_specs=jax.tree.map(lambda _: VMEM, outs),
        scratch_shapes=list(scratch),
        cost_estimate=pl.CostEstimate(
            flops=flops,
            bytes_accessed=sum(size(a) for a in list(args) + list(jax.tree.leaves(outs))),
            transcendentals=0,
        ),
        compiler_params=pltpu.CompilerParams(vmem_limit_bytes=40 * 1024 * 1024),
    )(*args)


def shape(dims, kind=F32):
    return jax.ShapeDtypeStruct(dims, kind)


def reduce_summary(chunks):
    n = lax.axis_size("sensor")
    if n != chunks.shape[0]:
        return lax.psum(chunks, "sensor")
    parts = lax.all_to_all(chunks, "sensor", 0, 0, tiled=True)
    total = call(sum_kernel, "sum_chunks", shape(chunks.shape), (parts,))
    return lax.all_to_all(total, "sensor", 0, 0, tiled=True)


def shift_all(arrays, count):
    return [
        lax.ppermute(a, "step", [(i, (i + shift) % count) for i in range(count)])
        for shift, a in enumerate(arrays, 1)
    ]


def shards(inputs, cotangent, w_query, w_key, w_value, w_up, w_down, feature_proj, live_count):
    steps, sensors, width = inputs.shape
    heads, size, feats = feature_proj.shape
    hidden = w_up.shape[1]
    factor = size ** (-0.25)
    rows = steps * sensors
    count = lax.axis_size("step")
    devices = lax.axis_size("sensor")
    cols = width // count
    x = inputs.reshape(rows, width)
    cot = cotangent.reshape(rows, width)
    whole = shape((rows, width))
    half = shape((rows, width), BF16)
    packed = shape((feats // 8, (steps * width // LANES) * 8 + 8, LANES))
    product = 2 * rows * width * width

    key, value, feat_key, local, x32 = call(
        functools.partial(key_kernel, steps, factor),
        "keys",
        (whole, whole, whole, packed, whole),
        (live_count, x, w_key, w_value, feature_proj),
        flops=3 * product,
        smem=1,
    )
    summary = reduce_summary(local)
    query, feat_query, grad_hidden = call(
        functools.partial(query_kernel, steps, factor),
        "queries",
        (whole, whole, shape((rows, hidden))),
        (live_count, x, cot, w_query, w_down, feature_proj),
        flops=3 * product,
        smem=1,
    )
    xs = [x] + shift_all([x32] * (count - 1), count)
    grad_num, grad_den, local_grad = call(
        functools.partial(middle_kernel, steps, size),
        "middle",
        (whole, whole, packed),
        (summary, feat_query, grad_hidden, w_up),
        flops=4 * product,
    )
    grad_summary = reduce_summary(local_grad)
    grad_q, own_q, *send_q = call(
        functools.partial(query_back_kernel, steps, factor, "step", cols),
        "query_back",
        (half,) + (shape((rows, cols)),) * count,
        (summary, grad_num, grad_den, feat_query, query, feature_proj),
        flops=3 * product,
        scratch=[pltpu.VMEM((rows, width), F32)],
    )
    got_q = [own_q] + shift_all(send_q, count)
    grad_k, grad_v, own_kv, *send_kv = call(
        functools.partial(key_back_kernel, steps, factor, "step", cols),
        "key_back",
        (half, half) + (shape((rows, 2 * cols)),) * count,
        (grad_summary, value, feat_key, key, feature_proj),
        flops=4 * product,
        scratch=[pltpu.VMEM((rows, width), F32)] * 2,
    )
    got_kv = [own_kv] + shift_all(send_kv, count)
    grad_in = call(
        rows_kernel,
        "input_rows",
        half,
        (grad_q, grad_k, grad_v, w_query, w_key, w_value),
        flops=3 * product,
    )
    partial = call(
        functools.partial(outer_kernel, count),
        "weight_partials",
        shape((devices, width // devices, 3 * cols)),
        (*xs, *got_q, *got_kv),
        flops=3 * product,
    )
    parts = lax.all_to_all(partial, "sensor", 0, 0, tiled=True)
    scale = 1.0 / math.sqrt(rows * count * devices)
    out = shape((width // devices, cols))
    grads = call(functools.partial(final_kernel, scale), "weight_sums", (out, out, out), (parts,))
    return (grad_in.reshape(inputs.shape), *grads)


def solution(mesh):
    return jax.shard_map(
        shards,
        mesh=mesh,
        in_specs=(P("step", "sensor", None),) * 2 + (P(),) * 6 + (P("sensor"),),
        out_specs=(P("step", "sensor", None),) + (P("sensor", "step"),) * 3,
        check_vma=False,
    )
```

time: 470 us -> 128 us (0.27)
  waiting for transfers between devices: 292 us -> 41.5 us
  blocking collectives: 74.1 us -> 35.6 us
  matrix products: 35.6 us -> 0 us
  local copies, waits for them, and re-layouts: 44.1 us -> 14.8 us
  starting transfers between devices: 0.55 us -> 20.6 us
  between operations: 15.2 us -> 1.51 us
  Pallas kernels: 0 us -> 13.4 us
  other arithmetic: 6.9 us -> 0 us
    unnamed x11 -> x0, waiting for transfers between devices: 137 us -> none
    psum x2 -> x0, waiting for transfers between devices: 93.4 us -> none  [the longest x1 62.8 us: shards(): lax.psum((local_gsum[moment], local_gnorm[moment]), 'sensor')]
    psum x2 -> x0, blocking collectives: 74.1 us -> none  [the longest x1 39 us: shards(): lax.psum((local_summary[moment], local_normal[moment]), 'sensor')]
    reduce_scatter x3 -> x0, waiting for transfers between devices: 61.9 us -> none  [the longest x1 21.2 us: shards(): lax.psum_scatter(partial_sums[1], 'step', scatter_dimension=1, tiled=True)]
    dot_general x23 -> x0, matrix products: 35.6 us -> none  [the longest x2 5.84 us: feature_back(): jnp.einsum('...hr,her->...he', weighted, feature_proj, precision=HIGH)]
    all_to_all x0 -> x2, blocking collectives: none -> 35.6 us  [reduce_summary(): parts = lax.all_to_all(chunks, 'sensor', 0, 0, tiled=True)]
    all_to_all x0 -> x3, waiting for transfers between devices: none -> 31.2 us  [the longest x1 19.7 us: shards(): parts = lax.all_to_all(partial, 'sensor', 0, 0, tiled=True)]
    pallas_call x0 -> x10, Pallas kernels: none -> 13.4 us  [call(): pl.pallas_call(kernel, name=name, out_shape=outs, in_specs=[SMEM] * smem...]
  transfers between devices with their start and end apart: 8 -> 12, of which waited for: 8 -> 6; matrix products, arithmetic and copies ran while one was open for 9% -> 0% of each run, Pallas kernels for 0% -> 5%
where the time goes in v1:
time: 128 us; the launch traced here: 127 us
  waiting for transfers between devices  41.5 us (32%)
  blocking collectives  35.6 us (28%)
  starting transfers between devices  20.6 us (16%)
  local copies, waits for them, and re-layouts  14.8 us (12%)
  Pallas kernels  13.4 us (10%)
  between operations  1.51 us (1%)
    all_to_all x2, blocking collectives, reduce_summary(): parts = lax.all_to_all(chunks, 'sensor', 0, 0, tiled=True)  35.6 us
    all_to_all x1, waiting for transfers between devices, shards(): parts = lax.all_to_all(partial, 'sensor', 0, 0, tiled=True)  19.7 us
    unnamed x68, local copies, waits for them, and re-layouts  14.8 us
    pallas_call x10, Pallas kernels, call(): pl.pallas_call(kernel, name=name, out_shape=outs, in_specs=[SMEM] * smem...  13.4 us
    all_to_all x2, waiting for transfers between devices, reduce_summary(): return lax.all_to_all(total, 'sensor', 0, 0, tiled=True)  11.5 us
    ppermute x9, waiting for transfers between devices, shift_all(): lax.ppermute(a, 'step', [(i, (i + shift) % count) for i in range(count)])  10.2 us
    ppermute x9, starting transfers between devices, shift_all(): lax.ppermute(a, 'step', [(i, (i + shift) % count) for i in range(count)])  7.51 us
    all_to_all x2, starting transfers between devices, reduce_summary(): return lax.all_to_all(total, 'sensor', 0, 0, tiled=True)  7.06 us
  transfers between devices with their start and end apart: 12, of which 6 were waited for; matrix products, arithmetic and copies ran while one was open for 0% of the time, Pallas kernels for 5%

profile of v1, /device:TPU:0, one launch (start us, length us, event | category | flops | bytes accessed | tf_op | source)
XLA Modules:
  0.0 127.4 jit_solution(6558014383115583228)
XLA Ops:
  1.3 0.0 copy-start
  1.3 0.9 copy-done
  2.2 1.0 copy-done.2
  3.3 1.0 copy-done.4
  4.3 0.9 copy-done.7
  5.2 1.1 keys.1
  6.4 19.7 %all_to_all.25.in_ref = f32[8,104,128]{2,1,0:T(8,128)S(1)} all-to-all(f32[8,104,128]{2,1,0:T(8,128)S(1)} %get-tuple-element.29), channel_id=1, replica_groups=mesh['sensor'=8,'step'=4] {'sensor'}, dimensions={0} | all-to-all | bytes 851968 | tf_op jit(solution)/shard_map/all_to_all | solution.py:350
  26.1 0.0 copy-done.9
  26.1 0.0 copy-done.11
  26.1 0.0 copy-start.28
  26.1 0.8 sum_chunks.2
  27.0 3.6 %all-to-all-start.1 = ((f32[8,104,128]{2,1,0:T(8,128)}), f32[8,104,128]{2,1,0:T(8,128)S(1)}, u32[]{:S(2)}, u32[]{:S(2)}) async-start(f32[8,104,128]{2,1,0:T(8,128)} %sum_chunks.2), calls=%async_computation.1 | async-start | bytes 851968 | tf_op jit(solution)/shard_map/all_to_all | solution.py:352
  30.6 0.0 copy-done.8
  30.6 0.0 copy-done.21
  30.6 0.0 copy-done.28
  30.6 0.0 copy-done.1
  30.6 0.0 copy-start.29
  30.6 0.7 queries.1
  31.3 0.0 copy-start.13
  31.3 0.7 copy-done.13
  32.1 10.6 %all-to-all-done.1.s_ref = f32[8,104,128]{2,1,0:T(8,128)S(1)} async-done(((f32[8,104,128]{2,1,0:T(8,128)}), f32[8,104,128]{2,1,0:T(8,128)S(1)}, u32[]{:S(2)}, u32[]{:S(2)}) %all-to-all-start.1) | async-done | bytes 426016 | tf_op jit(solution)/shard_map/all_to_all | solution.py:352
  42.6 0.0 copy-done.29
  42.6 1.8 %middle.1 = (f32[192,512]{1,0:T(8,128)S(1)}, f32[192,512]{1,0:T(8,128)S(1)}, f32[8,104,128]{2,1,0:T(8,128)S(1)}) custom-call(f32[8,104,128]{2,1,0:T(8,128)S(1)} %all-to-all-done.1.s_ref, f32[192,512]{1,0:T(8,128)S(1)} %get-tuple-element.30.f_ref, f32[192,256]{1,0:T(8,128)S(1)} %get-tuple-element.31.gh_ref, bf16[512,256]{1,0:T(8,128)(2,1)S(1)} %copy-done.29), custom_call_target="tpu_custom_call" | custom-call | flops 402653184 | bytes 2490368 | tf_op jit(solution)/shard_map/middle/pallas_call | solution.py:326
  44.5 0.7 copy-done.17
  45.2 15.8 %all_to_all.26.in_ref = f32[8,104,128]{2,1,0:T(8,128)S(1)} all-to-all(f32[8,104,128]{2,1,0:T(8,128)S(1)} %get-tuple-element.36), channel_id=1, replica_groups=mesh['sensor'=8,'step'=4] {'sensor'}, dimensions={0} | all-to-all | bytes 851968 | tf_op jit(solution)/shard_map/all_to_all | solution.py:350
  61.0 0.8 sum_chunks.3
  61.8 3.5 %all-to-all-start.3 = ((f32[8,104,128]{2,1,0:T(8,128)}), f32[8,104,128]{2,1,0:T(8,128)S(1)}, u32[]{:S(2)}, u32[]{:S(2)}) async-start(f32[8,104,128]{2,1,0:T(8,128)} %sum_chunks.3), calls=%async_computation.3 | async-start | bytes 851968 | tf_op jit(solution)/shard_map/all_to_all | solution.py:352
  65.3 0.1 collective-permute-start
  65.4 1.6 %collective-permute-start.1 = (f32[192,512]{1,0:T(8,128)}, f32[192,512]{1,0:T(8,128)S(1)}, u32[]{:S(2)}, u32[]{:S(2)}) collective-permute-start(f32[192,512]{1,0:T(8,128)} %get-tuple-element.42), channel_id=1, source_target_pairs={{0,2},{1,3},{2,0},{3,1},{4,6},{5,7},{6,4},{7,5},{8,10},{9,11},{10,... | collective-permute-start | bytes 1179656 | tf_op jit(solution)/shard_map/ppermute | solution.py:357
  66.9 1.4 %collective-permute-start.2 = (f32[192,512]{1,0:T(8,128)}, f32[192,512]{1,0:T(8,128)S(1)}, u32[]{:S(2)}, u32[]{:S(2)}) collective-permute-start(f32[192,512]{1,0:T(8,128)} %get-tuple-element.42), channel_id=1, source_target_pairs={{0,3},{1,0},{2,1},{3,2},{4,7},{5,4},{6,5},{7,6},{8,11},{9,8},{10,9... | collective-permute-start | bytes 1179656 | tf_op jit(solution)/shard_map/ppermute | solution.py:357
  68.3 1.0 copy-done.14
  69.3 1.0 copy-done.16
  70.3 1.0 copy-done.18
  71.3 1.0 copy-done.20
  72.3 2.0 %query_back.1 = (bf16[192,512]{1,0:T(8,128)(2,1)S(1)}, f32[192,128]{1,0:T(8,128)S(1)}, f32[192,128]{1,0:T(8,128)}, f32[192,128]{1,0:T(8,128)S(1)}, f32[192,128]{1,0:T(8,128)S(1)}) custom-call(f32[8,104,128]{2,1,0:T(8,128)S(1)} %all-to-all-done.1.s_ref, f32[192,512]{1,0:T(8,128)S(1)} %copy-done.18, f32[192,512]{1,0:T(8,128)S(1)} %copy-done.20, ...), custom_call_target="tpu_custom_call" | custom-call | flops 301989888 | bytes 2719744 | tf_op jit(solution)/shard_map/query_back/pallas_call | solution.py:326
  74.3 0.7 copy-done.22
  75.0 0.6 copy-done.30
  75.6 0.6 copy-done.32
  76.3 0.0 collective-permute-start.3
  76.3 0.9 all-to-all-done.3.g_ref
  77.2 1.0 copy-done.10
  78.2 1.0 copy-done.12
  79.2 1.8 %key_back.1 = (bf16[192,512]{1,0:T(8,128)(2,1)S(1)}, bf16[192,512]{1,0:T(8,128)(2,1)S(1)}, f32[192,256]{1,0:T(8,128)S(1)}, f32[192,256]{1,0:T(8,128)S(1)}, f32[1...) custom-call(f32[8,104,128]{2,1,0:T(8,128)S(1)} %all-to-all-done.3.g_ref, f32[192,512]{1,0:T(8,128)S(1)} %copy-done.10, ...), custom_call_target="tpu_custom_call" | custom-call | flops 402653184 | bytes 2916352 | tf_op jit(solution)/shard_map/key_back/pallas_call | solution.py:326
  81.0 0.7 copy-done.24
  81.6 0.7 copy-done.26
  82.3 0.0 collective-permute-start.6
  82.3 0.0 collective-permute-done.refs_1_
  82.3 1.5 %collective-permute-start.7 = (f32[192,256]{1,0:T(8,128)S(1)}, f32[192,256]{1,0:T(8,128)S(1)}, u32[]{:S(2)}, u32[]{:S(2)}) collective-permute-start(f32[192,256]{1,0:T(8,128)S(1)} %get-tuple-element.49), channel_id=1, source_target_pairs={{0,2},{1,3},{2,0},{3,1},{4,6},{5,7},{6,4},{7,5},{8,10},{9,11},{10,... | collective-permute-start | bytes 589832 | tf_op jit(solution)/shard_map/ppermute | solution.py:357
  83.9 0.0 collective-permute-done.1.refs_2_
  83.9 1.9 %collective-permute-start.8 = (f32[192,256]{1,0:T(8,128)S(1)}, f32[192,256]{1,0:T(8,128)S(1)}, u32[]{:S(2)}, u32[]{:S(2)}) collective-permute-start(f32[192,256]{1,0:T(8,128)S(1)} %get-tuple-element.50), channel_id=1, source_target_pairs={{0,3},{1,0},{2,1},{3,2},{4,7},{5,4},{6,5},{7,6},{8,11},{9,8},{10,9... | collective-permute-start | bytes 589832 | tf_op jit(solution)/shard_map/ppermute | solution.py:357
  85.7 0.0 collective-permute-done.2.refs_3_
  85.7 0.5 collective-permute-start.4
  86.3 0.8 collective-permute-done.3.refs_5_
  87.0 0.6 collective-permute-start.5
  87.6 9.0 %collective-permute-done.4.refs_6_ = f32[192,128]{1,0:T(8,128)S(1)} collective-permute-done((f32[192,128]{1,0:T(8,128)S(1)}, f32[192,128]{1,0:T(8,128)S(1)}, u32[]{:S(2)}, u32[]{:S(2)}) %collective-permute-start.4) | collective-permute-done | bytes 98336 | tf_op jit(solution)/shard_map/ppermute | solution.py:357
  96.5 0.5 collective-permute-done.5.refs_7_
  97.1 0.0 collective-permute-done.6.refs_9_
  97.1 0.0 collective-permute-done.7.refs_10_
  97.1 0.0 collective-permute-done.8.refs_11_
  97.1 2.4 %weight_partials.1 = f32[8,64,384]{2,1,0:T(8,128)} custom-call(bf16[192,512]{1,0:T(8,128)(2,1)S(1)} %bitcast.5, f32[192,512]{1,0:T(8,128)S(1)} %collective-permute-done.refs_1_, f32[192,512]{1,0:T(8,128)S(1)} %collective-permute-done.1.refs_2_, f32[192,512]{1,0:T(8,128)S(1)} %collective-permute-done.2.refs_3_, f32[192,128]{1,0:T(8,128)S(1)} %get-tuple-element.43.refs_4_, ...), custom_call_target="tpu_custom_call" | custom-call | flops 301989888 | bytes 3342336 | tf_op jit(solution)/shard_map/weight_partials/pallas_call | solution.py:326
  99.5 6.0 %all-to-all-start.4 = ((f32[8,64,384]{2,1,0:T(8,128)}), f32[8,64,384]{2,1,0:T(8,128)S(1)}, u32[]{:S(2)}, u32[]{:S(2)}) async-start(f32[8,64,384]{2,1,0:T(8,128)} %weight_partials.1), calls=%async_computation.4 | async-start | bytes 1572864 | tf_op jit(solution)/shard_map/all_to_all | solution.py:436
  105.6 1.3 %input_rows.1 = bf16[192,512]{1,0:T(8,128)(2,1)} custom-call(bf16[192,512]{1,0:T(8,128)(2,1)S(1)} %copy-done.23, bf16[192,512]{1,0:T(8,128)(2,1)S(1)} %copy-done.25, bf16[192,512]{1,0:T(8,128)(2,1)S(1)} %copy-done.27, bf16[512,512]{1,0:T(8,128)(2,1)S(1)} %copy-done.6, bf16[512,512]{1,0:T(8,128)(2,1)S(1)} %copy-done.3, bf16[512,512]{1,0:T(8,128)(2,1)S(1)} %copy-done.5), custom_call_target="tpu_custom_call" | custom-call | flops 301989888 | bytes 2359296 | tf_op jit(solution)/shard_map/input_rows/pallas_call | solution.py:326
  106.9 19.7 %all-to-all-done.4.in_ref = f32[8,64,384]{2,1,0:T(8,128)S(1)} async-done(((f32[8,64,384]{2,1,0:T(8,128)}), f32[8,64,384]{2,1,0:T(8,128)S(1)}, u32[]{:S(2)}, u32[]{:S(2)}) %all-to-all-start.4) | async-done | bytes 786464 | tf_op jit(solution)/shard_map/all_to_all | solution.py:436
  126.7 0.7 weight_sums.1
  (40 shorter events, 0.1 us)
Async XLA Ops:
  1.3 1.0 copy-start
  2.2 1.0 copy-start.2
  3.3 1.0 copy-start.4
  4.3 0.9 copy-start.7
  6.4 19.7 %copy-start.9 = (f32[192,512]{1,0:T(8,128)}, f32[192,512]{1,0:T(8,128)S(1)}, u32[]{:S(2)}) copy-start(f32[192,512]{1,0:T(8,128)S(1)} %get-tuple-element.37.v_ref) | copy-start | bytes 1179652
  6.4 19.7 %copy-start.11 = (f32[192,512]{1,0:T(8,128)}, f32[192,512]{1,0:T(8,128)S(1)}, u32[]{:S(2)}) copy-start(f32[192,512]{1,0:T(8,128)S(1)} %get-tuple-element.38.f_ref) | copy-start | bytes 1179652
  26.1 4.4 %copy-start.8 = (bf16[3,64,512]{2,1,0:T(8,128)(2,1)S(1)}, bf16[3,64,512]{2,1,0:T(8,128)(2,1)}, u32[]{:S(2)}) copy-start(bf16[3,64,512]{2,1,0:T(8,128)(2,1)} %param.9) | copy-start | bytes 589828
  26.1 4.4 %copy-start.21 = (bf16[256,512]{1,0:T(8,128)(2,1)S(1)}, bf16[256,512]{1,0:T(8,128)(2,1)}, u32[]{:S(2)}) copy-start(bf16[256,512]{1,0:T(8,128)(2,1)} %wd_ref.1) | copy-start | bytes 786436
  26.1 4.4 %copy-start.28 = (bf16[3,64,512]{2,1,0:T(8,128)(2,1)S(1)}, bf16[3,64,512]{2,1,0:T(8,128)(2,1)}, u32[]{:S(2)}) copy-start(bf16[3,64,512]{2,1,0:T(8,128)(2,1)} %param.10) | copy-start | bytes 589828
  26.9 3.6 %copy-start.1 = (f32[8,64,64]{2,1,0:T(8,128)S(1)}, f32[8,64,64]{2,1,0:T(8,128)}, u32[]{:S(2)}) copy-start(f32[8,64,64]{2,1,0:T(8,128)} %proj_ref.7) | copy-start | bytes 393220
  26.9 3.6 %copy-start.6 = (bf16[512,512]{1,0:T(8,128)(2,1)S(1)}, bf16[512,512]{1,0:T(8,128)(2,1)}, u32[]{:S(2)}) copy-start(bf16[512,512]{1,0:T(8,128)(2,1)} %wq_ref.3) | copy-start | bytes 1572868
  27.0 15.7 %all-to-all-start.1 = ((f32[8,104,128]{2,1,0:T(8,128)}), f32[8,104,128]{2,1,0:T(8,128)S(1)}, u32[]{:S(2)}, u32[]{:S(2)}) async-start(f32[8,104,128]{2,1,0:T(8,128)} %sum_chunks.2), calls=%async_computation.1 | async-start | bytes 851968 | tf_op jit(solution)/shard_map/all_to_all | solution.py:352
  30.6 12.0 %copy-start.29 = (bf16[512,256]{1,0:T(8,128)(2,1)S(1)}, bf16[512,256]{1,0:T(8,128)(2,1)}, u32[]{:S(2)}) copy-start(bf16[512,256]{1,0:T(8,128)(2,1)} %wu_ref.1) | copy-start | bytes 786436
  31.3 0.8 copy-start.13
  32.1 12.4 %copy-start.15 = (f32[192,512]{1,0:T(8,128)}, f32[192,512]{1,0:T(8,128)S(1)}, u32[]{:S(2)}) copy-start(f32[192,512]{1,0:T(8,128)S(1)} %get-tuple-element.30.f_ref) | copy-start | bytes 1179652
  44.5 0.7 copy-start.17
  45.2 15.8 %copy-start.19 = (f32[192,512]{1,0:T(8,128)}, f32[192,512]{1,0:T(8,128)S(1)}, u32[]{:S(2)}) copy-start(f32[192,512]{1,0:T(8,128)S(1)} %get-tuple-element.33.den_ref) | copy-start | bytes 1179652
  61.8 15.4 %all-to-all-start.3 = ((f32[8,104,128]{2,1,0:T(8,128)}), f32[8,104,128]{2,1,0:T(8,128)S(1)}, u32[]{:S(2)}, u32[]{:S(2)}) async-start(f32[8,104,128]{2,1,0:T(8,128)} %sum_chunks.3), calls=%async_computation.3 | async-start | bytes 851968 | tf_op jit(solution)/shard_map/all_to_all | solution.py:352
  65.3 17.0 %collective-permute-start = (f32[192,512]{1,0:T(8,128)}, f32[192,512]{1,0:T(8,128)S(1)}, u32[]{:S(2)}, u32[]{:S(2)}) collective-permute-start(f32[192,512]{1,0:T(8,128)} %get-tuple-element.42), channel_id=1, source_target_pairs={{0,1},{1,2},{2,3},{3,0},{4,5},{5,6},{6,7},{7,4},{8,9},{9,10},{10,1... | collective-permute-start | bytes 1179656 | tf_op jit(solution)/shard_map/ppermute | solution.py:357
  65.4 18.5 %collective-permute-start.1 = (f32[192,512]{1,0:T(8,128)}, f32[192,512]{1,0:T(8,128)S(1)}, u32[]{:S(2)}, u32[]{:S(2)}) collective-permute-start(f32[192,512]{1,0:T(8,128)} %get-tuple-element.42), channel_id=1, source_target_pairs={{0,2},{1,3},{2,0},{3,1},{4,6},{5,7},{6,4},{7,5},{8,10},{9,11},{10,... | collective-permute-start | bytes 1179656 | tf_op jit(solution)/shard_map/ppermute | solution.py:357
  66.9 18.8 %collective-permute-start.2 = (f32[192,512]{1,0:T(8,128)}, f32[192,512]{1,0:T(8,128)S(1)}, u32[]{:S(2)}, u32[]{:S(2)}) collective-permute-start(f32[192,512]{1,0:T(8,128)} %get-tuple-element.42), channel_id=1, source_target_pairs={{0,3},{1,0},{2,1},{3,2},{4,7},{5,4},{6,5},{7,6},{8,11},{9,8},{10,9... | collective-permute-start | bytes 1179656 | tf_op jit(solution)/shard_map/ppermute | solution.py:357
  68.3 1.0 copy-start.14
  69.3 1.0 copy-start.16
  70.3 1.0 copy-start.18
  71.3 1.0 copy-start.20
  74.3 0.7 copy-start.22
  75.0 0.6 copy-start.30
  75.6 0.6 copy-start.32
  76.3 10.8 %collective-permute-start.3 = (f32[192,128]{1,0:T(8,128)}, f32[192,128]{1,0:T(8,128)}, u32[]{:S(2)}, u32[]{:S(2)}) collective-permute-start(f32[192,128]{1,0:T(8,128)} %get-tuple-element.44), channel_id=1, source_target_pairs={{0,1},{1,2},{2,3},{3,0},{4,5},{5,6},{6,7},{7,4},{8,9},{9,10},{10,1... | collective-permute-start | bytes 294920 | tf_op jit(solution)/shard_map/ppermute | solution.py:357
  77.2 1.0 copy-start.10
  78.2 1.0 copy-start.12
  79.2 6.5 %copy-start.33 = (f32[192,128]{1,0:T(8,128)S(1)}, f32[192,128]{1,0:T(8,128)}, u32[]{:S(2)}) copy-start(f32[192,128]{1,0:T(8,128)} %copy-done.32) | copy-start | bytes 294916
  79.2 7.8 %copy-start.31 = (f32[192,128]{1,0:T(8,128)S(1)}, f32[192,128]{1,0:T(8,128)}, u32[]{:S(2)}) copy-start(f32[192,128]{1,0:T(8,128)} %copy-done.30) | copy-start | bytes 294916
  81.0 0.7 copy-start.24
  81.6 0.7 copy-start.26
  82.3 14.7 %collective-permute-start.6 = (f32[192,256]{1,0:T(8,128)S(1)}, f32[192,256]{1,0:T(8,128)S(1)}, u32[]{:S(2)}, u32[]{:S(2)}) collective-permute-start(f32[192,256]{1,0:T(8,128)S(1)} %get-tuple-element.48), channel_id=1, source_target_pairs={{0,1},{1,2},{2,3},{3,0},{4,5},{5,6},{6,7},{7,4},{8,9},{9,10},{10,1... | collective-permute-start | bytes 589832 | tf_op jit(solution)/shard_map/ppermute | solution.py:357
  82.3 14.7 %collective-permute-start.7 = (f32[192,256]{1,0:T(8,128)S(1)}, f32[192,256]{1,0:T(8,128)S(1)}, u32[]{:S(2)}, u32[]{:S(2)}) collective-permute-start(f32[192,256]{1,0:T(8,128)S(1)} %get-tuple-element.49), channel_id=1, source_target_pairs={{0,2},{1,3},{2,0},{3,1},{4,6},{5,7},{6,4},{7,5},{8,10},{9,11},{10,... | collective-permute-start | bytes 589832 | tf_op jit(solution)/shard_map/ppermute | solution.py:357
  83.9 13.2 %collective-permute-start.8 = (f32[192,256]{1,0:T(8,128)S(1)}, f32[192,256]{1,0:T(8,128)S(1)}, u32[]{:S(2)}, u32[]{:S(2)}) collective-permute-start(f32[192,256]{1,0:T(8,128)S(1)} %get-tuple-element.50), channel_id=1, source_target_pairs={{0,3},{1,0},{2,1},{3,2},{4,7},{5,4},{6,5},{7,6},{8,11},{9,8},{10,9... | collective-permute-start | bytes 589832 | tf_op jit(solution)/shard_map/ppermute | solution.py:357
  85.7 10.8 %collective-permute-start.4 = (f32[192,128]{1,0:T(8,128)S(1)}, f32[192,128]{1,0:T(8,128)S(1)}, u32[]{:S(2)}, u32[]{:S(2)}) collective-permute-start(f32[192,128]{1,0:T(8,128)S(1)} %copy-done.33), channel_id=1, source_target_pairs={{0,2},{1,3},{2,0},{3,1},{4,6},{5,7},{6,4},{7,5},{8,10},{9,11},{10,... | collective-permute-start | bytes 294920 | tf_op jit(solution)/shard_map/ppermute | solution.py:357
  87.0 10.0 %collective-permute-start.5 = (f32[192,128]{1,0:T(8,128)S(1)}, f32[192,128]{1,0:T(8,128)S(1)}, u32[]{:S(2)}, u32[]{:S(2)}) collective-permute-start(f32[192,128]{1,0:T(8,128)S(1)} %copy-done.31), channel_id=1, source_target_pairs={{0,3},{1,0},{2,1},{3,2},{4,7},{5,4},{6,5},{7,6},{8,11},{9,8},{10,9... | collective-permute-start | bytes 294920 | tf_op jit(solution)/shard_map/ppermute | solution.py:357
  97.1 8.5 %copy-start.27 = (bf16[192,512]{1,0:T(8,128)(2,1)S(1)}, bf16[192,512]{1,0:T(8,128)(2,1)}, u32[]{:S(2)}) copy-start(bf16[192,512]{1,0:T(8,128)(2,1)} %copy-done.26) | copy-start | bytes 589828
  99.5 6.0 %copy-start.3 = (bf16[512,512]{1,0:T(8,128)(2,1)S(1)}, bf16[512,512]{1,0:T(8,128)(2,1)}, u32[]{:S(2)}) copy-start(bf16[512,512]{1,0:T(8,128)(2,1)} %wk_ref.3) | copy-start | bytes 1572868
  99.5 6.1 %copy-start.5 = (bf16[512,512]{1,0:T(8,128)(2,1)S(1)}, bf16[512,512]{1,0:T(8,128)(2,1)}, u32[]{:S(2)}) copy-start(bf16[512,512]{1,0:T(8,128)(2,1)} %wv_ref.3) | copy-start | bytes 1572868
  99.5 6.1 %copy-start.23 = (bf16[192,512]{1,0:T(8,128)(2,1)S(1)}, bf16[192,512]{1,0:T(8,128)(2,1)}, u32[]{:S(2)}) copy-start(bf16[192,512]{1,0:T(8,128)(2,1)} %copy-done.22) | copy-start | bytes 589828
  99.5 6.1 %copy-start.25 = (bf16[192,512]{1,0:T(8,128)(2,1)S(1)}, bf16[192,512]{1,0:T(8,128)(2,1)}, u32[]{:S(2)}) copy-start(bf16[192,512]{1,0:T(8,128)(2,1)} %copy-done.24) | copy-start | bytes 589828
  99.5 27.2 %all-to-all-start.4 = ((f32[8,64,384]{2,1,0:T(8,128)}), f32[8,64,384]{2,1,0:T(8,128)S(1)}, u32[]{:S(2)}, u32[]{:S(2)}) async-start(f32[8,64,384]{2,1,0:T(8,128)} %weight_partials.1), calls=%async_computation.4 | async-start | bytes 1572864 | tf_op jit(solution)/shard_map/all_to_all | solution.py:436

commit v2 on v1

--- a/solution.py
+++ b/solution.py
@@ -84,35 +84,49 @@
     return jnp.concatenate(out, -1)
 
 
-def store_summary(out_ref, step, matrices, sums):
-    chunks = out_ref.shape[0]
+def store_summary(out_ref, step, steps, matrices, sums):
+    quarters = out_ref.shape[0]
+    high = matrices[0].shape[0] // quarters
     groups = sums.shape[1] // LANES
     per_half = WIDE // LANES
     for group in range(groups):
         part = matrices[group // per_half][:, (group % per_half) * LANES :][:, :LANES]
-        row = (step * groups + group) * 8
-        for chunk in range(chunks):
-            out_ref[chunk, row : row + 8, :] = part[chunk * 8 : chunk * 8 + 8]
+        row = (step * groups + group) * high
+        for quarter in range(quarters):
+            out_ref[quarter, row : row + high, :] = part[quarter * high : (quarter + 1) * high]
         slot = step * groups + group
-        base = out_ref.shape[1] - 8
-        out_ref[slot // 8, base + slot % 8 : base + slot % 8 + 1, :] = sums[
-            :, group * LANES : (group + 1) * LANES
-        ]
-
-
-def load_summary(in_ref, step, groups):
-    chunks = in_ref.shape[0]
+        place = steps * groups * high + slot // quarters
+        out_ref[slot % quarters, place : place + 1, :] = sums[:, group * LANES : (group + 1) * LANES]
+
+
+def clear_tail(out_ref):
+    tail = out_ref.shape[1] - 8
+    for quarter in range(out_ref.shape[0]):
+        out_ref[quarter, tail:, :] = jnp.zeros((8, LANES), F32)
+
+
+def load_summary(in_ref, step, steps, groups, high):
+    quarters = in_ref.shape[0]
     columns, sums = [], []
     for group in range(groups):
         slot = step * groups + group
-        row = slot * 8
+        row = slot * high
         columns.append(
-            jnp.concatenate([in_ref[c, row : row + 8, :] for c in range(chunks)], 0)
-        )
-        base = in_ref.shape[1] - 8
-        sums.append(in_ref[slot // 8, base + slot % 8 : base + slot % 8 + 1, :])
-    whole = jnp.concatenate(columns, -1)
-    return halves(whole), jnp.concatenate(sums, -1)
+            jnp.concatenate([in_ref[q, row : row + high, :] for q in range(quarters)], 0)
+        )
+        place = steps * groups * high + slot // quarters
+        sums.append(in_ref[slot % quarters, place : place + 1, :])
+    return halves(jnp.concatenate(columns, -1)), jnp.concatenate(sums, -1)
+
+
+def deal(scratch, refs, me):
+    for partner, ref in enumerate(refs):
+        ref[...] = scratch[(me ^ partner) % len(refs)]
+
+
+def collect(scratch, refs, me):
+    for partner, ref in enumerate(refs):
+        scratch[(me ^ partner) % len(refs)] = ref[...]
 
 
 def outer_sums(a, b, size):
@@ -127,7 +141,8 @@
     return out
 
 
-def key_kernel(steps, factor, live_ref, x_ref, wk_ref, wv_ref, proj_ref, u_ref, v_ref, f_ref, s_ref, x32_ref):
+def key_kernel(steps, factor, live_ref, x_ref, wk_ref, wv_ref, proj_ref, u_ref, v_ref, f_ref, x32_ref, *rest):
+    out_refs, s_ref = rest[:-1], rest[-1]
     size = proj_ref.shape[1]
     x = x_ref[...]
     x32_ref[...] = x.astype(F32)
@@ -142,17 +157,17 @@
     place = lax.broadcasted_iota(jnp.int32, feat.shape, 0) % rows
     feat = jnp.where(place < live_ref[0], feat, 0.0)
     f_ref[...] = feat
-    base = s_ref.shape[1] - 8
-    for chunk in range(s_ref.shape[0]):
-        s_ref[chunk, base:, :] = jnp.zeros((8, LANES), F32)
+    clear_tail(s_ref)
     for step in range(steps):
         part = slice(step * rows, (step + 1) * rows)
         store_summary(
             s_ref,
             step,
+            steps,
             outer_sums(feat[part], values[part], size),
             jnp.sum(feat[part], 0, keepdims=True),
         )
+    deal(s_ref, out_refs, lax.axis_index("sensor"))
 
 
 def query_kernel(steps, factor, live_ref, x_ref, cot_ref, wq_ref, wd_ref, proj_ref, u_ref, f_ref, gh_ref):
@@ -168,15 +183,11 @@
     gh_ref[...] = jnp.where(place < live_ref[0], hidden, 0.0)
 
 
-def sum_kernel(in_ref, out_ref):
-    total = in_ref[0]
-    for chunk in range(1, in_ref.shape[0]):
-        total = total + in_ref[chunk]
-    for chunk in range(out_ref.shape[0]):
-        out_ref[chunk] = total
-
-
-def middle_kernel(steps, size, s_ref, f_ref, gh_ref, wu_ref, num_ref, den_ref, g_ref):
+def middle_kernel(steps, size, *refs):
+    in_refs, (f_ref, gh_ref, wu_ref, num_ref, den_ref) = refs[:4], refs[4:9]
+    out_refs, s_ref, g_ref = refs[9:13], refs[13], refs[14]
+    me = lax.axis_index("sensor")
+    collect(s_ref, in_refs, me)
     mask = head_mask(size)
     ones = jnp.where(mask, 1.0, 0.0).astype(BF16)
     feat = f_ref[...]
@@ -185,7 +196,7 @@
     groups = width // LANES
     numer, weighted = [], []
     for step in range(steps):
-        matrices, sums = load_summary(s_ref, step, groups)
+        matrices, sums = load_summary(s_ref, step, steps, groups, size // 4)
         part = feat[step * rows : (step + 1) * rows]
         numer.append(
             jnp.concatenate(
@@ -215,17 +226,17 @@
     grad_den = -jnp.concatenate([head_sums(a, ones) for a in halves(along)], -1) * inverse
     num_ref[...] = grad_num
     den_ref[...] = grad_den
-    base = g_ref.shape[1] - 8
-    for chunk in range(g_ref.shape[0]):
-        g_ref[chunk, base:, :] = jnp.zeros((8, LANES), F32)
+    clear_tail(g_ref)
     for step in range(steps):
         part = slice(step * rows, (step + 1) * rows)
         store_summary(
             g_ref,
             step,
+            steps,
             outer_sums(feat[part], grad_num[part], size),
             jnp.sum(feat[part] * grad_den[part], 0, keepdims=True),
         )
+    deal(g_ref, out_refs, me)
 
 
 def send_columns(grads, send_refs, own_ref, me, size):
@@ -236,8 +247,9 @@
             ref[:, place * size : (place + 1) * size] = g[:, pl.ds(pl.multiple_of(target * size, size), size)]
 
 
-def query_back_kernel(steps, factor, axis, cols, s_ref, num_ref, den_ref, f_ref, u_ref, proj_ref, g_ref, own_ref, *rest):
-    send_refs, scratch = rest[:-1], rest[-1]
+def query_back_kernel(steps, factor, axis, cols, s0, s1, s2, s3, num_ref, den_ref, f_ref, u_ref, proj_ref, g_ref, own_ref, *rest):
+    send_refs, scratch, s_ref = rest[:-2], rest[-2], rest[-1]
+    collect(s_ref, (s0, s1, s2, s3), lax.axis_index("sensor"))
     size = proj_ref.shape[1]
     mask = head_mask(size)
     ones = jnp.where(mask, 1.0, 0.0).astype(BF16)
@@ -246,7 +258,7 @@
     groups = feat.shape[1] // LANES
     out = []
     for step in range(steps):
-        matrices, sums = load_summary(s_ref, step, groups)
+        matrices, sums = load_summary(s_ref, step, steps, groups, size // 4)
         part = slice(step * rows, (step + 1) * rows)
         back = jnp.concatenate(
             [
@@ -263,8 +275,9 @@
     send_columns([scratch], send_refs, own_ref, lax.axis_index(axis), cols)
 
 
-def key_back_kernel(steps, factor, axis, cols, g_ref, v_ref, f_ref, u_ref, proj_ref, gk_ref, gv_ref, own_ref, *rest):
-    send_refs, scratch_k, scratch_v = rest[:-2], rest[-2], rest[-1]
+def key_back_kernel(steps, factor, axis, cols, g0, g1, g2, g3, v_ref, f_ref, u_ref, proj_ref, gk_ref, gv_ref, own_ref, *rest):
+    send_refs, scratch_k, scratch_v, g_ref = rest[:-3], rest[-3], rest[-2], rest[-1]
+    collect(g_ref, (g0, g1, g2, g3), lax.axis_index("sensor"))
     size = proj_ref.shape[1]
     mask = head_mask(size)
     ones = jnp.where(mask, 1.0, 0.0).astype(BF16)
@@ -273,7 +286,7 @@
     groups = feat.shape[1] // LANES
     back, grad_v = [], []
     for step in range(steps):
-        matrices, sums = load_summary(g_ref, step, groups)
+        matrices, sums = load_summary(g_ref, step, steps, groups, size // 4)
         spreads = [split(spread(m, mask)) for m in matrices]
         part = slice(step * rows, (step + 1) * rows)
         back.append(
@@ -307,9 +320,22 @@
     q = jnp.concatenate([r[...].astype(BF16) for r in gq], 0)
     kv = jnp.concatenate([r[...].astype(BF16) for r in gkv], 0)
     total = dot(x, jnp.concatenate([q, kv], -1), TN)
-    chunks, rows = out_ref.shape[:2]
-    for chunk in range(chunks):
-        out_ref[chunk] = total[chunk * rows : (chunk + 1) * rows]
+    chunks, rows = out_ref.shape[0], out_ref.shape[-2]
+    for chunk in range(total.shape[0] // rows):
+        part = total[chunk * rows : (chunk + 1) * rows]
+        if len(out_ref.shape) == 4:
+            out_ref[chunk % chunks, chunk // chunks] = part
+        else:
+            out_ref[chunk] = part
+
+
+def halve_kernel(in_ref, own_ref, away_ref):
+    mine = lax.axis_index("sensor") // in_ref.shape[0]
+    for ref, block in ((own_ref, mine), (away_ref, 1 - mine)):
+        total = in_ref[0, block]
+        for part in range(1, in_ref.shape[0]):
+            total = total + in_ref[part, block]
+        ref[...] = total
 
 
 def final_kernel(scale, in_ref, *outs):
@@ -335,7 +361,7 @@
             bytes_accessed=sum(size(a) for a in list(args) + list(jax.tree.leaves(outs))),
             transcendentals=0,
         ),
-        compiler_params=pltpu.CompilerParams(vmem_limit_bytes=40 * 1024 * 1024),
+        compiler_params=pltpu.CompilerParams(vmem_limit_bytes=16 * 1024 * 1024),
     )(*args)
 
 
@@ -343,13 +369,21 @@
     return jax.ShapeDtypeStruct(dims, kind)
 
 
-def reduce_summary(chunks):
-    n = lax.axis_size("sensor")
-    if n != chunks.shape[0]:
-        return lax.psum(chunks, "sensor")
-    parts = lax.all_to_all(chunks, "sensor", 0, 0, tiled=True)
-    total = call(sum_kernel, "sum_chunks", shape(chunks.shape), (parts,))
-    return lax.all_to_all(total, "sensor", 0, 0, tiled=True)
+def trade(parts, axis):
+    count = lax.axis_size(axis)
+    return [parts[0]] + [
+        lax.ppermute(a, axis, [(i, i ^ d) for i in range(count)]) for d, a in enumerate(parts) if d
+    ]
+
+
+def reduce_summary(parts):
+    count = lax.axis_size("sensor")
+    total = sum(trade(parts, "sensor"))
+    bit = len(parts)
+    while bit < count:
+        total = total + lax.ppermute(total, "sensor", [(i, i ^ bit) for i in range(count)])
+        bit *= 2
+    return trade([total] * len(parts), "sensor")
 
 
 def shift_all(arrays, count):
@@ -372,16 +406,19 @@
     cot = cotangent.reshape(rows, width)
     whole = shape((rows, width))
     half = shape((rows, width), BF16)
-    packed = shape((feats // 8, (steps * width // LANES) * 8 + 8, LANES))
+    quarter = (steps * (width // LANES) * (size // 4) + 8, LANES)
+    packed = (shape(quarter),) * 4
+    held = pltpu.VMEM((4, *quarter), F32)
     product = 2 * rows * width * width
 
-    key, value, feat_key, local, x32 = call(
+    key, value, feat_key, x32, *local = call(
         functools.partial(key_kernel, steps, factor),
         "keys",
-        (whole, whole, whole, packed, whole),
+        (whole,) * 4 + packed,
         (live_count, x, w_key, w_value, feature_proj),
         flops=3 * product,
         smem=1,
+        scratch=[held],
     )
     summary = reduce_summary(local)
     query, feat_query, grad_hidden = call(
@@ -393,30 +430,31 @@
         smem=1,
     )
     xs = [x] + shift_all([x32] * (count - 1), count)
-    grad_num, grad_den, local_grad = call(
+    grad_num, grad_den, *local_grad = call(
         functools.partial(middle_kernel, steps, size),
         "middle",
-        (whole, whole, packed),
-        (summary, feat_query, grad_hidden, w_up),
+        (whole, whole) + packed,
+        (*summary, feat_query, grad_hidden, w_up),
         flops=4 * product,
+        scratch=[held] * 2,
     )
     grad_summary = reduce_summary(local_grad)
     grad_q, own_q, *send_q = call(
         functools.partial(query_back_kernel, steps, factor, "step", cols),
         "query_back",
         (half,) + (shape((rows, cols)),) * count,
-        (summary, grad_num, grad_den, feat_query, query, feature_proj),
+        (*summary, grad_num, grad_den, feat_query, query, feature_proj),
         flops=3 * product,
-        scratch=[pltpu.VMEM((rows, width), F32)],
+        scratch=[pltpu.VMEM((rows, width), F32), held],
     )
     got_q = [own_q] + shift_all(send_q, count)
     grad_k, grad_v, own_kv, *send_kv = call(
         functools.partial(key_back_kernel, steps, factor, "step", cols),
         "key_back",
         (half, half) + (shape((rows, 2 * cols)),) * count,
-        (grad_summary, value, feat_key, key, feature_proj),
+        (*grad_summary, value, feat_key, key, feature_proj),
         flops=4 * product,
-        scratch=[pltpu.VMEM((rows, width), F32)] * 2,
+        scratch=[pltpu.VMEM((rows, width), F32)] * 2 + [held],
     )
     got_kv = [own_kv] + shift_all(send_kv, count)
     grad_in = call(
@@ -426,14 +464,22 @@
         (grad_q, grad_k, grad_v, w_query, w_key, w_value),
         flops=3 * product,
     )
+    tile = (width // devices, 3 * cols)
     partial = call(
         functools.partial(outer_kernel, count),
         "weight_partials",
-        shape((devices, width // devices, 3 * cols)),
+        shape((4, 2, *tile) if devices == 8 else (devices, *tile)),
         (*xs, *got_q, *got_kv),
         flops=3 * product,
     )
-    parts = lax.all_to_all(partial, "sensor", 0, 0, tiled=True)
+    if devices == 8:
+        quads = [[0, 1, 2, 3], [4, 5, 6, 7]]
+        far = [(i, i ^ 4) for i in range(devices)]
+        parts = lax.all_to_all(partial, "sensor", 0, 0, tiled=True, axis_index_groups=quads)
+        total, away = call(halve_kernel, "quarter_sums", (shape(tile), shape(tile)), (parts,))
+        parts = jnp.stack([total, lax.ppermute(away, "sensor", far)])
+    else:
+        parts = lax.all_to_all(partial, "sensor", 0, 0, tiled=True)
     scale = 1.0 / math.sqrt(rows * count * devices)
     out = shape((width // devices, cols))
     grads = call(functools.partial(final_kernel, scale), "weight_sums", (out, out, out), (parts,))

time: 128 us -> 97.9 us (0.76)
  blocking collectives: 35.6 us -> 14.9 us
  local copies, waits for them, and re-layouts: 14.8 us -> 3.99 us
  starting transfers between devices: 20.6 us -> 28.6 us
  Pallas kernels: 13.4 us -> 9.55 us
  waiting for transfers between devices: 41.5 us -> 39 us
    all_to_all x3 -> x0, waiting for transfers between devices: 31.2 us -> none  [the longest x1 19.7 us: shards(): parts = lax.all_to_all(partial, 'sensor', 0, 0, tiled=True)]
    ppermute x0 -> x15, waiting for transfers between devices: none -> 28.9 us  [the longest x12 17.4 us: trade(): lax.ppermute(a, axis, [(i, i ^ d) for i in range(count)])]
    ppermute x0 -> x15, starting transfers between devices: none -> 23.5 us  [the longest x12 14.2 us: trade(): lax.ppermute(a, axis, [(i, i ^ d) for i in range(count)])]
    all_to_all x2 -> x1, blocking collectives: 35.6 us -> 14.9 us  [shards(): lax.all_to_all(partial, 'sensor', 0, 0, tiled=True, axis_index_groups=quads)]
    all_to_all x3 -> x0, starting transfers between devices: 13.1 us -> none  [the longest x2 7.06 us: reduce_summary(): return lax.all_to_all(total, 'sensor', 0, 0, tiled=True)]
    unnamed x68 -> x24, local copies, waits for them, and re-layouts: 14.8 us -> 3.99 us
    pallas_call x10 -> x9, Pallas kernels: 13.4 us -> 9.55 us  [call(): pl.pallas_call(kernel, name=name, out_shape=outs, in_specs=[SMEM] * smem...]
    ppermute x9, starting transfers between devices: 7.51 us -> 5.11 us  [shift_all(): lax.ppermute(a, 'step', [(i, (i + shift) % count) for i in range(count)])]
  transfers between devices with their start and end apart: 12 -> 24, of which waited for: 6 -> 14; matrix products, arithmetic and copies ran while one was open for 0% -> 0% of each run, Pallas kernels for 5% -> 5%
where the time goes in v2:
time: 97.9 us; the launch traced here: 97.6 us
  waiting for transfers between devices  39 us (40%)
  starting transfers between devices  28.6 us (29%)
  blocking collectives  14.9 us (15%)
  Pallas kernels  9.55 us (10%)
  local copies, waits for them, and re-layouts  3.99 us (4%)
  between operations  1.46 us (1%)
    ppermute x12, waiting for transfers between devices, trade(): lax.ppermute(a, axis, [(i, i ^ d) for i in range(count)])  17.4 us
    all_to_all x1, blocking collectives, shards(): lax.all_to_all(partial, 'sensor', 0, 0, tiled=True, axis_index_groups=quads)  14.9 us
    ppermute x12, starting transfers between devices, trade(): lax.ppermute(a, axis, [(i, i ^ d) for i in range(count)])  14.2 us
    ppermute x9, waiting for transfers between devices, shift_all(): lax.ppermute(a, 'step', [(i, (i + shift) % count) for i in range(count)])  10 us
    pallas_call x9, Pallas kernels, call(): pl.pallas_call(kernel, name=name, out_shape=outs, in_specs=[SMEM] * smem...  9.55 us
    ppermute x2, waiting for transfers between devices, reduce_summary(): lax.ppermute(total, 'sensor', [(i, i ^ bit) for i in range(count)])  8.53 us
    ppermute x2, starting transfers between devices, reduce_summary(): lax.ppermute(total, 'sensor', [(i, i ^ bit) for i in range(count)])  5.38 us
    ppermute x9, starting transfers between devices, shift_all(): lax.ppermute(a, 'step', [(i, (i + shift) % count) for i in range(count)])  5.11 us
  transfers between devices with their start and end apart: 24, of which 14 were waited for; matrix products, arithmetic and copies ran while one was open for 0% of the time, Pallas kernels for 5%

profile of v2, /device:TPU:0, one launch (start us, length us, event | category | flops | bytes accessed | tf_op | source)
XLA Modules:
  0.0 97.6 jit_solution(6998451776284182073)
XLA Ops:
  1.3 0.0 copy-start
  1.3 0.9 copy-done
  2.2 1.0 %copy-done.2 = bf16[512,512]{1,0:T(8,128)(2,1)S(1)} copy-done((bf16[512,512]{1,0:T(8,128)(2,1)S(1)}, bf16[512,512]{1,0:T(8,128)(2,1)}, u32[]{:S(2)}) %copy-start.2) | copy-done | bytes 524312
  3.3 1.0 %copy-done.4 = bf16[512,512]{1,0:T(8,128)(2,1)S(1)} copy-done((bf16[512,512]{1,0:T(8,128)(2,1)S(1)}, bf16[512,512]{1,0:T(8,128)(2,1)}, u32[]{:S(2)}) %copy-start.4) | copy-done | bytes 524312
  4.3 0.9 copy-done.7
  5.2 1.1 %keys.1 = (f32[192,512]{1,0:T(8,128)S(1)}, f32[192,512]{1,0:T(8,128)S(1)}, f32[192,512]{1,0:T(8,128)S(1)}, f32[192,512]{1,0:T(8,128)S(1)}, f32[200,128]{1,0:T(8,...) custom-call(s32[1]{0:T(128)S(6)} %copy.13.live_ref, ...), custom_call_target="tpu_custom_call" | custom-call | flops 301989888 | bytes 3358724 | tf_op jit(solution)/shard_map/keys/pallas_call | solution.py:352
  6.4 0.0 copy-start.6
  6.4 4.0 %collective-permute-start.2 = (f32[200,128]{1,0:T(8,128)S(1)}, f32[200,128]{1,0:T(8,128)S(1)}, u32[]{:S(2)}, u32[]{:S(2)}) collective-permute-start(f32[200,128]{1,0:T(8,128)S(1)} %get-tuple-element.40), channel_id=1, source_target_pairs={{0,12},{4,8},{8,4},{12,0},{16,28},{20,24},{24,20},{28,16},{1,13},{... | collective-permute-start | bytes 307208 | tf_op jit(solution)/shard_map/ppermute | solution.py:375
  10.4 0.4 collective-permute-start.1
  10.9 0.2 collective-permute-start
  11.1 3.0 %collective-permute-done.2 = f32[200,128]{1,0:T(8,128)S(1)} collective-permute-done((f32[200,128]{1,0:T(8,128)S(1)}, f32[200,128]{1,0:T(8,128)S(1)}, u32[]{:S(2)}, u32[]{:S(2)}) %collective-permute-start.2) | collective-permute-done | bytes 102432 | tf_op jit(solution)/shard_map/ppermute | solution.py:375
  14.1 1.6 %collective-permute-done.1 = f32[200,128]{1,0:T(8,128)S(1)} collective-permute-done((f32[200,128]{1,0:T(8,128)S(1)}, f32[200,128]{1,0:T(8,128)S(1)}, u32[]{:S(2)}, u32[]{:S(2)}) %collective-permute-start.1) | collective-permute-done | bytes 102432 | tf_op jit(solution)/shard_map/ppermute | solution.py:375
  15.7 0.0 collective-permute-done
  15.8 0.0 copy-start.1
  15.8 2.7 %collective-permute-start.3 = (f32[200,128]{1,0:T(8,128)S(1)}, f32[200,128]{1,0:T(8,128)S(1)}, u32[]{:S(2)}, u32[]{:S(2)}) collective-permute-start(f32[200,128]{1,0:T(8,128)S(1)} %add_add_fusion.1), channel_id=1, source_target_pairs={{0,16},{4,20},{8,24},{12,28},{16,0},{20,4},{24,8},{28,12},{1,17},{... | collective-permute-start | bytes 307208 | tf_op jit(solution)/shard_map/ppermute | solution.py:384
  18.5 4.5 %collective-permute-done.3 = f32[200,128]{1,0:T(8,128)S(1)} collective-permute-done((f32[200,128]{1,0:T(8,128)S(1)}, f32[200,128]{1,0:T(8,128)S(1)}, u32[]{:S(2)}, u32[]{:S(2)}) %collective-permute-start.3) | collective-permute-done | bytes 102432 | tf_op jit(solution)/shard_map/ppermute | solution.py:384
  23.0 2.0 %collective-permute-start.4 = (f32[200,128]{1,0:T(8,128)S(1)}, f32[200,128]{1,0:T(8,128)S(1)}, u32[]{:S(2)}, u32[]{:S(2)}) collective-permute-start(f32[200,128]{1,0:T(8,128)S(1)} %add.27.refs_0_.s0), channel_id=1, source_target_pairs={{0,4},{4,0},{8,12},{12,8},{16,20},{20,16},{24,28},{28,24},{1,5},{5... | collective-permute-start | bytes 307208 | tf_op jit(solution)/shard_map/ppermute | solution.py:375
  25.0 0.4 collective-permute-start.5
  25.4 1.1 %collective-permute-start.6 = (f32[200,128]{1,0:T(8,128)S(1)}, f32[200,128]{1,0:T(8,128)S(1)}, u32[]{:S(2)}, u32[]{:S(2)}) collective-permute-start(f32[200,128]{1,0:T(8,128)S(1)} %add.27.refs_0_.s0), channel_id=1, source_target_pairs={{0,12},{4,8},{8,4},{12,0},{16,28},{20,24},{24,20},{28,16},{1,13},{... | collective-permute-start | bytes 307208 | tf_op jit(solution)/shard_map/ppermute | solution.py:375
  26.6 0.0 copy-start.11
  26.6 0.7 queries.1
  27.3 1.0 %collective-permute-done.4.refs_1_.s1 = f32[200,128]{1,0:T(8,128)S(1)} collective-permute-done((f32[200,128]{1,0:T(8,128)S(1)}, f32[200,128]{1,0:T(8,128)S(1)}, u32[]{:S(2)}, u32[]{:S(2)}) %collective-permute-start.4) | collective-permute-done | bytes 102432 | tf_op jit(solution)/shard_map/ppermute | solution.py:375
  28.3 1.6 %collective-permute-done.5.refs_2_.s2 = f32[200,128]{1,0:T(8,128)S(1)} collective-permute-done((f32[200,128]{1,0:T(8,128)S(1)}, f32[200,128]{1,0:T(8,128)S(1)}, u32[]{:S(2)}, u32[]{:S(2)}) %collective-permute-start.5) | collective-permute-done | bytes 102432 | tf_op jit(solution)/shard_map/ppermute | solution.py:375
  29.9 1.4 %collective-permute-done.6.refs_3_.s3 = f32[200,128]{1,0:T(8,128)S(1)} collective-permute-done((f32[200,128]{1,0:T(8,128)S(1)}, f32[200,128]{1,0:T(8,128)S(1)}, u32[]{:S(2)}, u32[]{:S(2)}) %collective-permute-start.6) | collective-permute-done | bytes 102432 | tf_op jit(solution)/shard_map/ppermute | solution.py:375
  31.4 1.9 %middle.1 = (f32[192,512]{1,0:T(8,128)S(1)}, f32[192,512]{1,0:T(8,128)S(1)}, f32[200,128]{1,0:T(8,128)S(1)}, f32[200,128]{1,0:T(8,128)S(1)}, f32[200,128]{1,0:T(8,128)S(1)}, /*index=5*/f32[200,128]{1,0:T(8,128)S(1)}) custom-call(f32[200,128]{1,0:T(8,128)S(1)} %add.27.refs_0_.s0, f32[200,128]{1,0:T(8,128)S(1)} %collective-permute-done.4.refs_1_.s1, ...), custom_call_target="tpu_custom_call" | custom-call | flops 402653184 | bytes 2457600 | tf_op jit(solution)/shard_map/middle/pallas_call | solution.py:352
  33.3 1.5 %collective-permute-start.9 = (f32[200,128]{1,0:T(8,128)S(1)}, f32[200,128]{1,0:T(8,128)S(1)}, u32[]{:S(2)}, u32[]{:S(2)}) collective-permute-start(f32[200,128]{1,0:T(8,128)S(1)} %get-tuple-element.50), channel_id=1, source_target_pairs={{0,12},{4,8},{8,4},{12,0},{16,28},{20,24},{24,20},{28,16},{1,13},{... | collective-permute-start | bytes 307208 | tf_op jit(solution)/shard_map/ppermute | solution.py:375
  34.8 1.1 %collective-permute-start.8 = (f32[200,128]{1,0:T(8,128)S(1)}, f32[200,128]{1,0:T(8,128)S(1)}, u32[]{:S(2)}, u32[]{:S(2)}) collective-permute-start(f32[200,128]{1,0:T(8,128)S(1)} %get-tuple-element.49), channel_id=1, source_target_pairs={{0,8},{4,12},{8,0},{12,4},{16,24},{20,28},{24,16},{28,20},{1,9},{5... | collective-permute-start | bytes 307208 | tf_op jit(solution)/shard_map/ppermute | solution.py:375
  35.9 0.9 collective-permute-start.7
  36.8 0.0 collective-permute-start.14
  36.8 1.5 %collective-permute-start.15 = (f32[192,512]{1,0:T(8,128)S(1)}, f32[192,512]{1,0:T(8,128)S(1)}, u32[]{:S(2)}, u32[]{:S(2)}) collective-permute-start(f32[192,512]{1,0:T(8,128)S(1)} %get-tuple-element.56), channel_id=1, source_target_pairs={{0,2},{1,3},{2,0},{3,1},{4,6},{5,7},{6,4},{7,5},{8,10},{9,11},{10,... | collective-permute-start | bytes 1179656 | tf_op jit(solution)/shard_map/ppermute | solution.py:391
  38.3 0.9 collective-permute-done.9
  39.2 0.5 collective-permute-done.8
  39.7 0.9 collective-permute-done.7
  40.6 2.7 %collective-permute-start.10 = (f32[200,128]{1,0:T(8,128)S(1)}, f32[200,128]{1,0:T(8,128)S(1)}, u32[]{:S(2)}, u32[]{:S(2)}) collective-permute-start(f32[200,128]{1,0:T(8,128)S(1)} %add_add_fusion), channel_id=1, source_target_pairs={{0,16},{4,20},{8,24},{12,28},{16,0},{20,4},{24,8},{28,12},{1,17},{... | collective-permute-start | bytes 307208 | tf_op jit(solution)/shard_map/ppermute | solution.py:384
  43.3 0.0 collective-permute-start.16
  43.3 4.0 %collective-permute-done.10 = f32[200,128]{1,0:T(8,128)S(1)} collective-permute-done((f32[200,128]{1,0:T(8,128)S(1)}, f32[200,128]{1,0:T(8,128)S(1)}, u32[]{:S(2)}, u32[]{:S(2)}) %collective-permute-start.10) | collective-permute-done | bytes 102432 | tf_op jit(solution)/shard_map/ppermute | solution.py:384
  47.3 1.1 %collective-permute-start.11 = (f32[200,128]{1,0:T(8,128)S(1)}, f32[200,128]{1,0:T(8,128)S(1)}, u32[]{:S(2)}, u32[]{:S(2)}) collective-permute-start(f32[200,128]{1,0:T(8,128)S(1)} %add.31.g0), channel_id=1, source_target_pairs={{0,4},{4,0},{8,12},{12,8},{16,20},{20,16},{24,28},{28,24},{1,5},{5... | collective-permute-start | bytes 307208 | tf_op jit(solution)/shard_map/ppermute | solution.py:375
  48.4 0.5 collective-permute-start.12
  48.9 3.2 %collective-permute-done.11.g1 = f32[200,128]{1,0:T(8,128)S(1)} collective-permute-done((f32[200,128]{1,0:T(8,128)S(1)}, f32[200,128]{1,0:T(8,128)S(1)}, u32[]{:S(2)}, u32[]{:S(2)}) %collective-permute-start.11) | collective-permute-done | bytes 102432 | tf_op jit(solution)/shard_map/ppermute | solution.py:375
  52.1 0.9 collective-permute-start.13
  53.0 1.4 %query_back.1 = (bf16[192,512]{1,0:T(8,128)(2,1)S(1)}, f32[192,128]{1,0:T(8,128)S(1)}, f32[192,128]{1,0:T(8,128)S(1)}, f32[192,128]{1,0:T(8,128)S(1)}, f32[192,128]{1,0:T(8,128)S(1)}) custom-call(f32[200,128]{1,0:T(8,128)S(1)} %add.27.refs_0_.s0, f32[200,128]{1,0:T(8,128)S(1)} %collective-permute-done.4.refs_1_.s1, ...), custom_call_target="tpu_custom_call" | custom-call | flops 301989888 | bytes 2703360 | tf_op jit(solution)/shard_map/query_back/pallas_call | solution.py:352
  54.3 0.0 collective-permute-done.12.g2
  54.4 0.1 collective-permute-start.17
  54.4 3.2 %collective-permute-done.13.g3 = f32[200,128]{1,0:T(8,128)S(1)} collective-permute-done((f32[200,128]{1,0:T(8,128)S(1)}, f32[200,128]{1,0:T(8,128)S(1)}, u32[]{:S(2)}, u32[]{:S(2)}) %collective-permute-start.13) | collective-permute-done | bytes 102432 | tf_op jit(solution)/shard_map/ppermute | solution.py:375
  57.6 1.8 %key_back.1 = (bf16[192,512]{1,0:T(8,128)(2,1)S(1)}, bf16[192,512]{1,0:T(8,128)(2,1)S(1)}, f32[192,256]{1,0:T(8,128)S(1)}, f32[192,256]{1,0:T(8,128)S(1)}, f32[1...) custom-call(f32[200,128]{1,0:T(8,128)S(1)} %add.31.g0, f32[200,128]{1,0:T(8,128)S(1)} %collective-permute-done.11.g1, ...), custom_call_target="tpu_custom_call" | custom-call | flops 402653184 | bytes 2899968 | tf_op jit(solution)/shard_map/key_back/pallas_call | solution.py:352
  59.4 0.1 collective-permute-start.20
  59.5 0.0 collective-permute-done.14.refs_1_
  59.5 0.5 collective-permute-start.21
  60.1 0.0 collective-permute-done.15.refs_2_
  60.1 1.4 %collective-permute-start.22 = (f32[192,256]{1,0:T(8,128)S(1)}, f32[192,256]{1,0:T(8,128)S(1)}, u32[]{:S(2)}, u32[]{:S(2)}) collective-permute-start(f32[192,256]{1,0:T(8,128)S(1)} %get-tuple-element.64), channel_id=1, source_target_pairs={{0,3},{1,0},{2,1},{3,2},{4,7},{5,4},{6,5},{7,6},{8,11},{9,8},{10,9... | collective-permute-start | bytes 589832 | tf_op jit(solution)/shard_map/ppermute | solution.py:391
  61.4 0.0 collective-permute-done.16.refs_3_
  61.4 1.6 %collective-permute-start.18 = (f32[192,128]{1,0:T(8,128)S(1)}, f32[192,128]{1,0:T(8,128)S(1)}, u32[]{:S(2)}, u32[]{:S(2)}) collective-permute-start(f32[192,128]{1,0:T(8,128)S(1)} %get-tuple-element.59), channel_id=1, source_target_pairs={{0,2},{1,3},{2,0},{3,1},{4,6},{5,7},{6,4},{7,5},{8,10},{9,11},{10,... | collective-permute-start | bytes 294920 | tf_op jit(solution)/shard_map/ppermute | solution.py:391
  63.0 10.0 %collective-permute-done.18.refs_6_ = f32[192,128]{1,0:T(8,128)S(1)} collective-permute-done((f32[192,128]{1,0:T(8,128)S(1)}, f32[192,128]{1,0:T(8,128)S(1)}, u32[]{:S(2)}, u32[]{:S(2)}) %collective-permute-start.18) | collective-permute-done | bytes 98336 | tf_op jit(solution)/shard_map/ppermute | solution.py:391
  73.0 0.0 collective-permute-done.19.refs_7_
  73.0 0.0 collective-permute-done.20.refs_9_
  73.0 0.0 collective-permute-done.21.refs_10_
  73.0 0.0 collective-permute-done.22.refs_11_
  73.1 0.6 weight_partials.1
  73.7 0.0 copy-start.5
  73.7 14.9 %all_to_all.5.in_ref = f32[4,2,64,384]{3,2,1,0:T(8,128)S(1)} all-to-all(f32[4,2,64,384]{3,2,1,0:T(8,128)S(1)} %weight_partials.1), channel_id=1, replica_groups={{0,4,8,12},{16,20,24,28},{1,5,9,13},{17,21,25,29},{2,6,10,14},{18,22,26..., dimensions={0} | all-to-all | bytes 1572864 | tf_op jit(solution)/shard_map/all_to_all | solution.py:478
  88.7 3.9 %collective-permute-start.23 = (f32[64,384]{1,0:T(8,128)S(1)}, f32[64,384]{1,0:T(8,128)S(1)}, u32[]{:S(2)}, u32[]{:S(2)}) collective-permute-start(f32[64,384]{1,0:T(8,128)S(1)} %get-tuple-element.66), channel_id=1, source_target_pairs={{0,16},{4,20},{8,24},{12,28},{16,0},{20,4},{24,8},{28,12},{1,17},{... | collective-permute-start | bytes 294920 | tf_op jit(solution)/shard_map/ppermute | solution.py:480
  92.5 1.3 %input_rows.1 = bf16[192,512]{1,0:T(8,128)(2,1)} custom-call(bf16[192,512]{1,0:T(8,128)(2,1)S(1)} %get-tuple-element.46.gq_ref, bf16[192,512]{1,0:T(8,128)(2,1)S(1)} %get-tuple-element.54.gk_ref, bf16[192,512]{1,0:T(8,128)(2,1)S(1)} %get-tuple-element.55.gv_ref, bf16[512,512]{1,0:T(8,128)(2,1)S(1)} %copy-done.6, bf16[512,512]{1,0:T(8,128)(2,1)S(1)} %copy-done.3, ...), custom_call_target="tpu_custom_call" | custom-call | flops 301989888 | bytes 2359296 | tf_op jit(solution)/shard_map/input_rows/pallas_call | solution.py:352
  93.9 3.0 %collective-permute-done.23 = f32[64,384]{1,0:T(8,128)S(1)} collective-permute-done((f32[64,384]{1,0:T(8,128)S(1)}, f32[64,384]{1,0:T(8,128)S(1)}, u32[]{:S(2)}, u32[]{:S(2)}) %collective-permute-start.23) | collective-permute-done | bytes 98336 | tf_op jit(solution)/shard_map/ppermute | solution.py:480
  96.9 0.7 weight_sums.1
  (23 shorter events, 0.2 us)
Async XLA Ops:
  1.3 1.0 copy-start
  2.2 1.0 %copy-start.2 = (bf16[512,512]{1,0:T(8,128)(2,1)S(1)}, bf16[512,512]{1,0:T(8,128)(2,1)}, u32[]{:S(2)}) copy-start(bf16[512,512]{1,0:T(8,128)(2,1)} %wk_ref.3) | copy-start | bytes 1572868
  3.3 1.0 %copy-start.4 = (bf16[512,512]{1,0:T(8,128)(2,1)S(1)}, bf16[512,512]{1,0:T(8,128)(2,1)}, u32[]{:S(2)}) copy-start(bf16[512,512]{1,0:T(8,128)(2,1)} %wv_ref.3) | copy-start | bytes 1572868
  4.3 0.9 copy-start.7
  5.2 21.3 %copy-start.9 = (bf16[256,512]{1,0:T(8,128)(2,1)S(1)}, bf16[256,512]{1,0:T(8,128)(2,1)}, u32[]{:S(2)}) copy-start(bf16[256,512]{1,0:T(8,128)(2,1)} %wd_ref.1) | copy-start | bytes 786436
  5.2 21.3 %copy-start.10 = (bf16[3,64,512]{2,1,0:T(8,128)(2,1)S(1)}, bf16[3,64,512]{2,1,0:T(8,128)(2,1)}, u32[]{:S(2)}) copy-start(bf16[3,64,512]{2,1,0:T(8,128)(2,1)} %param.10) | copy-start | bytes 589828
  6.4 20.2 %copy-start.6 = (bf16[512,512]{1,0:T(8,128)(2,1)S(1)}, bf16[512,512]{1,0:T(8,128)(2,1)}, u32[]{:S(2)}) copy-start(bf16[512,512]{1,0:T(8,128)(2,1)} %wq_ref.3) | copy-start | bytes 1572868
  6.4 7.7 %collective-permute-start.2 = (f32[200,128]{1,0:T(8,128)S(1)}, f32[200,128]{1,0:T(8,128)S(1)}, u32[]{:S(2)}, u32[]{:S(2)}) collective-permute-start(f32[200,128]{1,0:T(8,128)S(1)} %get-tuple-element.40), channel_id=1, source_target_pairs={{0,12},{4,8},{8,4},{12,0},{16,28},{20,24},{24,20},{28,16},{1,13},{... | collective-permute-start | bytes 307208 | tf_op jit(solution)/shard_map/ppermute | solution.py:375
  10.4 5.3 %collective-permute-start.1 = (f32[200,128]{1,0:T(8,128)S(1)}, f32[200,128]{1,0:T(8,128)S(1)}, u32[]{:S(2)}, u32[]{:S(2)}) collective-permute-start(f32[200,128]{1,0:T(8,128)S(1)} %get-tuple-element.39), channel_id=1, source_target_pairs={{0,8},{4,12},{8,0},{12,4},{16,24},{20,28},{24,16},{28,20},{1,9},{5... | collective-permute-start | bytes 307208 | tf_op jit(solution)/shard_map/ppermute | solution.py:375
  10.9 4.8 %collective-permute-start = (f32[200,128]{1,0:T(8,128)S(1)}, f32[200,128]{1,0:T(8,128)S(1)}, u32[]{:S(2)}, u32[]{:S(2)}) collective-permute-start(f32[200,128]{1,0:T(8,128)S(1)} %get-tuple-element.38), channel_id=1, source_target_pairs={{0,4},{4,0},{8,12},{12,8},{16,20},{20,16},{24,28},{28,24},{1,5},{5... | collective-permute-start | bytes 307208 | tf_op jit(solution)/shard_map/ppermute | solution.py:375
  15.8 10.8 %copy-start.1 = (f32[8,64,64]{2,1,0:T(8,128)S(1)}, f32[8,64,64]{2,1,0:T(8,128)}, u32[]{:S(2)}) copy-start(f32[8,64,64]{2,1,0:T(8,128)} %proj_ref.7) | copy-start | bytes 393220
  15.8 7.2 %collective-permute-start.3 = (f32[200,128]{1,0:T(8,128)S(1)}, f32[200,128]{1,0:T(8,128)S(1)}, u32[]{:S(2)}, u32[]{:S(2)}) collective-permute-start(f32[200,128]{1,0:T(8,128)S(1)} %add_add_fusion.1), channel_id=1, source_target_pairs={{0,16},{4,20},{8,24},{12,28},{16,0},{20,4},{24,8},{28,12},{1,17},{... | collective-permute-start | bytes 307208 | tf_op jit(solution)/shard_map/ppermute | solution.py:384
  23.0 5.3 %collective-permute-start.4 = (f32[200,128]{1,0:T(8,128)S(1)}, f32[200,128]{1,0:T(8,128)S(1)}, u32[]{:S(2)}, u32[]{:S(2)}) collective-permute-start(f32[200,128]{1,0:T(8,128)S(1)} %add.27.refs_0_.s0), channel_id=1, source_target_pairs={{0,4},{4,0},{8,12},{12,8},{16,20},{20,16},{24,28},{28,24},{1,5},{5... | collective-permute-start | bytes 307208 | tf_op jit(solution)/shard_map/ppermute | solution.py:375
  25.0 4.9 %collective-permute-start.5 = (f32[200,128]{1,0:T(8,128)S(1)}, f32[200,128]{1,0:T(8,128)S(1)}, u32[]{:S(2)}, u32[]{:S(2)}) collective-permute-start(f32[200,128]{1,0:T(8,128)S(1)} %add.27.refs_0_.s0), channel_id=1, source_target_pairs={{0,8},{4,12},{8,0},{12,4},{16,24},{20,28},{24,16},{28,20},{1,9},{5... | collective-permute-start | bytes 307208 | tf_op jit(solution)/shard_map/ppermute | solution.py:375
  25.4 5.9 %collective-permute-start.6 = (f32[200,128]{1,0:T(8,128)S(1)}, f32[200,128]{1,0:T(8,128)S(1)}, u32[]{:S(2)}, u32[]{:S(2)}) collective-permute-start(f32[200,128]{1,0:T(8,128)S(1)} %add.27.refs_0_.s0), channel_id=1, source_target_pairs={{0,12},{4,8},{8,4},{12,0},{16,28},{20,24},{24,20},{28,16},{1,13},{... | collective-permute-start | bytes 307208 | tf_op jit(solution)/shard_map/ppermute | solution.py:375
  26.6 4.8 %copy-start.11 = (bf16[512,256]{1,0:T(8,128)(2,1)S(1)}, bf16[512,256]{1,0:T(8,128)(2,1)}, u32[]{:S(2)}) copy-start(bf16[512,256]{1,0:T(8,128)(2,1)} %refs_6_.1) | copy-start | bytes 786436
  33.3 5.9 %collective-permute-start.9 = (f32[200,128]{1,0:T(8,128)S(1)}, f32[200,128]{1,0:T(8,128)S(1)}, u32[]{:S(2)}, u32[]{:S(2)}) collective-permute-start(f32[200,128]{1,0:T(8,128)S(1)} %get-tuple-element.50), channel_id=1, source_target_pairs={{0,12},{4,8},{8,4},{12,0},{16,28},{20,24},{24,20},{28,16},{1,13},{... | collective-permute-start | bytes 307208 | tf_op jit(solution)/shard_map/ppermute | solution.py:375
  34.8 4.9 %collective-permute-start.8 = (f32[200,128]{1,0:T(8,128)S(1)}, f32[200,128]{1,0:T(8,128)S(1)}, u32[]{:S(2)}, u32[]{:S(2)}) collective-permute-start(f32[200,128]{1,0:T(8,128)S(1)} %get-tuple-element.49), channel_id=1, source_target_pairs={{0,8},{4,12},{8,0},{12,4},{16,24},{20,28},{24,16},{28,20},{1,9},{5... | collective-permute-start | bytes 307208 | tf_op jit(solution)/shard_map/ppermute | solution.py:375
  35.9 4.7 %collective-permute-start.7 = (f32[200,128]{1,0:T(8,128)S(1)}, f32[200,128]{1,0:T(8,128)S(1)}, u32[]{:S(2)}, u32[]{:S(2)}) collective-permute-start(f32[200,128]{1,0:T(8,128)S(1)} %get-tuple-element.48), channel_id=1, source_target_pairs={{0,4},{4,0},{8,12},{12,8},{16,20},{20,16},{24,28},{28,24},{1,5},{5... | collective-permute-start | bytes 307208 | tf_op jit(solution)/shard_map/ppermute | solution.py:375
  36.8 22.7 %collective-permute-start.14 = (f32[192,512]{1,0:T(8,128)S(1)}, f32[192,512]{1,0:T(8,128)S(1)}, u32[]{:S(2)}, u32[]{:S(2)}) collective-permute-start(f32[192,512]{1,0:T(8,128)S(1)} %get-tuple-element.56), channel_id=1, source_target_pairs={{0,1},{1,2},{2,3},{3,0},{4,5},{5,6},{6,7},{7,4},{8,9},{9,10},{10,1... | collective-permute-start | bytes 1179656 | tf_op jit(solution)/shard_map/ppermute | solution.py:391
  36.8 23.2 %collective-permute-start.15 = (f32[192,512]{1,0:T(8,128)S(1)}, f32[192,512]{1,0:T(8,128)S(1)}, u32[]{:S(2)}, u32[]{:S(2)}) collective-permute-start(f32[192,512]{1,0:T(8,128)S(1)} %get-tuple-element.56), channel_id=1, source_target_pairs={{0,2},{1,3},{2,0},{3,1},{4,6},{5,7},{6,4},{7,5},{8,10},{9,11},{10,... | collective-permute-start | bytes 1179656 | tf_op jit(solution)/shard_map/ppermute | solution.py:391
  40.6 6.7 %collective-permute-start.10 = (f32[200,128]{1,0:T(8,128)S(1)}, f32[200,128]{1,0:T(8,128)S(1)}, u32[]{:S(2)}, u32[]{:S(2)}) collective-permute-start(f32[200,128]{1,0:T(8,128)S(1)} %add_add_fusion), channel_id=1, source_target_pairs={{0,16},{4,20},{8,24},{12,28},{16,0},{20,4},{24,8},{28,12},{1,17},{... | collective-permute-start | bytes 307208 | tf_op jit(solution)/shard_map/ppermute | solution.py:384
  43.3 18.2 %collective-permute-start.16 = (f32[192,512]{1,0:T(8,128)S(1)}, f32[192,512]{1,0:T(8,128)S(1)}, u32[]{:S(2)}, u32[]{:S(2)}) collective-permute-start(f32[192,512]{1,0:T(8,128)S(1)} %get-tuple-element.56), channel_id=1, source_target_pairs={{0,3},{1,0},{2,1},{3,2},{4,7},{5,4},{6,5},{7,6},{8,11},{9,8},{10,9... | collective-permute-start | bytes 1179656 | tf_op jit(solution)/shard_map/ppermute | solution.py:391
  47.3 4.7 %collective-permute-start.11 = (f32[200,128]{1,0:T(8,128)S(1)}, f32[200,128]{1,0:T(8,128)S(1)}, u32[]{:S(2)}, u32[]{:S(2)}) collective-permute-start(f32[200,128]{1,0:T(8,128)S(1)} %add.31.g0), channel_id=1, source_target_pairs={{0,4},{4,0},{8,12},{12,8},{16,20},{20,16},{24,28},{28,24},{1,5},{5... | collective-permute-start | bytes 307208 | tf_op jit(solution)/shard_map/ppermute | solution.py:375
  48.4 6.0 %collective-permute-start.12 = (f32[200,128]{1,0:T(8,128)S(1)}, f32[200,128]{1,0:T(8,128)S(1)}, u32[]{:S(2)}, u32[]{:S(2)}) collective-permute-start(f32[200,128]{1,0:T(8,128)S(1)} %add.31.g0), channel_id=1, source_target_pairs={{0,8},{4,12},{8,0},{12,4},{16,24},{20,28},{24,16},{28,20},{1,9},{5... | collective-permute-start | bytes 307208 | tf_op jit(solution)/shard_map/ppermute | solution.py:375
  52.1 5.6 %collective-permute-start.13 = (f32[200,128]{1,0:T(8,128)S(1)}, f32[200,128]{1,0:T(8,128)S(1)}, u32[]{:S(2)}, u32[]{:S(2)}) collective-permute-start(f32[200,128]{1,0:T(8,128)S(1)} %add.31.g0), channel_id=1, source_target_pairs={{0,12},{4,8},{8,4},{12,0},{16,28},{20,24},{24,20},{28,16},{1,13},{... | collective-permute-start | bytes 307208 | tf_op jit(solution)/shard_map/ppermute | solution.py:375
  54.4 8.6 %collective-permute-start.17 = (f32[192,128]{1,0:T(8,128)S(1)}, f32[192,128]{1,0:T(8,128)S(1)}, u32[]{:S(2)}, u32[]{:S(2)}) collective-permute-start(f32[192,128]{1,0:T(8,128)S(1)} %get-tuple-element.58), channel_id=1, source_target_pairs={{0,1},{1,2},{2,3},{3,0},{4,5},{5,6},{6,7},{7,4},{8,9},{9,10},{10,1... | collective-permute-start | bytes 294920 | tf_op jit(solution)/shard_map/ppermute | solution.py:391
  57.6 15.4 %copy-start.8 = (bf16[3,64,512]{2,1,0:T(8,128)(2,1)S(1)}, bf16[3,64,512]{2,1,0:T(8,128)(2,1)}, u32[]{:S(2)}) copy-start(bf16[3,64,512]{2,1,0:T(8,128)(2,1)} %param.9) | copy-start | bytes 589828
  59.4 13.6 %collective-permute-start.20 = (f32[192,256]{1,0:T(8,128)S(1)}, f32[192,256]{1,0:T(8,128)S(1)}, u32[]{:S(2)}, u32[]{:S(2)}) collective-permute-start(f32[192,256]{1,0:T(8,128)S(1)} %get-tuple-element.62), channel_id=1, source_target_pairs={{0,1},{1,2},{2,3},{3,0},{4,5},{5,6},{6,7},{7,4},{8,9},{9,10},{10,1... | collective-permute-start | bytes 589832 | tf_op jit(solution)/shard_map/ppermute | solution.py:391
  59.5 13.5 %collective-permute-start.21 = (f32[192,256]{1,0:T(8,128)S(1)}, f32[192,256]{1,0:T(8,128)S(1)}, u32[]{:S(2)}, u32[]{:S(2)}) collective-permute-start(f32[192,256]{1,0:T(8,128)S(1)} %get-tuple-element.63), channel_id=1, source_target_pairs={{0,2},{1,3},{2,0},{3,1},{4,6},{5,7},{6,4},{7,5},{8,10},{9,11},{10,... | collective-permute-start | bytes 589832 | tf_op jit(solution)/shard_map/ppermute | solution.py:391
  60.1 13.0 %collective-permute-start.22 = (f32[192,256]{1,0:T(8,128)S(1)}, f32[192,256]{1,0:T(8,128)S(1)}, u32[]{:S(2)}, u32[]{:S(2)}) collective-permute-start(f32[192,256]{1,0:T(8,128)S(1)} %get-tuple-element.64), channel_id=1, source_target_pairs={{0,3},{1,0},{2,1},{3,2},{4,7},{5,4},{6,5},{7,6},{8,11},{9,8},{10,9... | collective-permute-start | bytes 589832 | tf_op jit(solution)/shard_map/ppermute | solution.py:391
  61.4 11.6 %collective-permute-start.18 = (f32[192,128]{1,0:T(8,128)S(1)}, f32[192,128]{1,0:T(8,128)S(1)}, u32[]{:S(2)}, u32[]{:S(2)}) collective-permute-start(f32[192,128]{1,0:T(8,128)S(1)} %get-tuple-element.59), channel_id=1, source_target_pairs={{0,2},{1,3},{2,0},{3,1},{4,6},{5,7},{6,4},{7,5},{8,10},{9,11},{10,... | collective-permute-start | bytes 294920 | tf_op jit(solution)/shard_map/ppermute | solution.py:391
  63.0 10.0 %collective-permute-start.19 = (f32[192,128]{1,0:T(8,128)S(1)}, f32[192,128]{1,0:T(8,128)S(1)}, u32[]{:S(2)}, u32[]{:S(2)}) collective-permute-start(f32[192,128]{1,0:T(8,128)S(1)} %get-tuple-element.60), channel_id=1, source_target_pairs={{0,3},{1,0},{2,1},{3,2},{4,7},{5,4},{6,5},{7,6},{8,11},{9,8},{10,9... | collective-permute-start | bytes 294920 | tf_op jit(solution)/shard_map/ppermute | solution.py:391
  73.7 18.9 %copy-start.5 = (bf16[512,512]{1,0:T(8,128)(2,1)S(1)}, bf16[512,512]{1,0:T(8,128)(2,1)}, u32[]{:S(2)}) copy-start(bf16[512,512]{1,0:T(8,128)(2,1)} %wv_ref.3) | copy-start | bytes 1572868
  88.6 3.9 %copy-start.3 = (bf16[512,512]{1,0:T(8,128)(2,1)S(1)}, bf16[512,512]{1,0:T(8,128)(2,1)}, u32[]{:S(2)}) copy-start(bf16[512,512]{1,0:T(8,128)(2,1)} %wk_ref.3) | copy-start | bytes 1572868
  88.7 8.2 %collective-permute-start.23 = (f32[64,384]{1,0:T(8,128)S(1)}, f32[64,384]{1,0:T(8,128)S(1)}, u32[]{:S(2)}, u32[]{:S(2)}) collective-permute-start(f32[64,384]{1,0:T(8,128)S(1)} %get-tuple-element.66), channel_id=1, source_target_pairs={{0,16},{4,20},{8,24},{12,28},{16,0},{20,4},{24,8},{28,12},{1,17},{... | collective-permute-start | bytes 294920 | tf_op jit(solution)/shard_map/ppermute | solution.py:480

commit v3 on v0

v3 whole, which is shorter than its diff:
```python
import functools
import math

import jax
import jax.numpy as jnp
from jax import lax
from jax.experimental import pallas as pl
from jax.experimental.pallas import tpu as pltpu
from jax.sharding import PartitionSpec as P

F32 = jnp.float32
BF16 = jnp.bfloat16
NN = (((1,), (0,)), ((), ()))
NT = (((1,), (1,)), ((), ()))
TN = (((0,), (0,)), ((), ()))
VMEM = pl.BlockSpec(memory_space=pltpu.VMEM)
SMEM = pl.BlockSpec(memory_space=pltpu.SMEM)
LANES = 128
WIDE = 256


def dot(a, b, dims=NN):
    return lax.dot_general(a, b, dims, preferred_element_type=F32)


def split(x):
    high = x.astype(BF16)
    return high, (x - high.astype(F32)).astype(BF16)


def dot3(a, b, dims=NN):
    return dot(a[0], b[0], dims) + (dot(a[0], b[1], dims) + dot(a[1], b[0], dims))


def head_mask(size, width):
    rows = lax.broadcasted_iota(jnp.int32, (width, width), 0) // size
    cols = lax.broadcasted_iota(jnp.int32, (width, width), 1) // size
    return rows == cols


def head_ones(mask):
    return jnp.where(mask, 1.0, 0.0).astype(BF16)


def spread(x, mask):
    return jnp.where(mask, jnp.concatenate([x] * (x.shape[1] // x.shape[0]), 0), 0.0)


def gather_diagonal(x, size):
    head = lax.broadcasted_iota(jnp.int32, (size, x.shape[1]), 1) // size
    out = x[:size]
    for g in range(1, x.shape[1] // size):
        out = jnp.where(head == g, x[g * size : (g + 1) * size], out)
    return out


def head_sums(x, ones):
    high, low = split(x)
    return dot(high, ones) + dot(low, ones)


def pieces(x, width=WIDE):
    return [x[:, h : h + width] for h in range(0, x.shape[1], width)]


def projection(proj_ref, heads=None, width=WIDE):
    heads = range(proj_ref.shape[0]) if heads is None else heads
    blocks = [proj_ref[h] for h in heads]
    per = width // proj_ref.shape[2]
    return [jnp.concatenate(blocks[g : g + per], -1) for g in range(0, len(blocks), per)]


def feature_map(scaled, proj, mask, ones, feats):
    out = []
    for u, p in zip(pieces(scaled, mask.shape[0]), proj):
        projected = dot3(split(u), split(spread(p, mask)))
        out.append(jnp.exp(projected - 0.5 * head_sums(u * u, ones)) * feats ** (-0.5))
    return jnp.concatenate(out, -1)


def feature_back(weighted, scaled, proj, mask, ones):
    out = []
    width = mask.shape[0]
    for w, u, p in zip(pieces(weighted, width), pieces(scaled, width), proj):
        high, low = split(w)
        back = dot3((high, low), split(spread(p, mask)), NT)
        out.append(back - u * (dot(high, ones) + dot(low, ones)))
    return jnp.concatenate(out, -1)


def store_summary(out_ref, matrices, sums):
    size = matrices[0].shape[0]
    base = size * len(matrices)
    out_ref[base:, :] = jnp.zeros((out_ref.shape[0] - base, LANES), F32)
    for step, (matrix, row) in enumerate(zip(matrices, sums)):
        out_ref[step * size : (step + 1) * size, :] = matrix
        out_ref[base + step : base + step + 1, :] = row


def load_summary(refs, steps, size):
    total = refs[0][...]
    for ref in refs[1:]:
        total = total + ref[...]
    base = steps * size
    return [
        (total[step * size : (step + 1) * size], total[base + step : base + step + 1])
        for step in range(steps)
    ]


def outer_sums(a, b, size):
    ah, al = split(a)
    bh, bl = split(b)
    whole = dot(ah, bh, TN) + (dot(ah, bl, TN) + dot(al, bh, TN))
    return gather_diagonal(whole, size)


def summaries(a, b, weighted, steps, size):
    high = a.shape[0] // steps
    parts = [slice(step * high, (step + 1) * high) for step in range(steps)]
    matrices = [outer_sums(a[p], b[p], size) for p in parts]
    return matrices, [jnp.sum(weighted[p], 0, keepdims=True) for p in parts]


def columns(group):
    return pl.ds(pl.multiple_of(group * LANES, LANES), LANES)


def send_columns(sources, refs, me):
    for partner, ref in enumerate(refs):
        own = columns((me ^ partner) % len(refs))
        for place, source in enumerate(sources):
            rows = source.shape[0]
            ref[:rows, place * LANES : (place + 1) * LANES] = source[:, own]


def place_rows(target, refs, steps, column=0):
    rows = target.shape[0] // (steps * len(refs))
    lanes = slice(column * LANES, column * LANES + target.shape[1])
    for partner, ref in enumerate(refs):
        for step in range(steps):
            start = (step * len(refs) + partner) * rows
            target[start : start + rows, :] = ref[step * rows : (step + 1) * rows, lanes].astype(
                target.dtype
            )


def take_rows(values, partner, count, steps):
    rows = values.shape[0] // (steps * count)
    starts = [(step * count + partner) * rows for step in range(steps)]
    return jnp.concatenate([values[s : s + rows] for s in starts], 0)


def widen_kernel(live_ref, x_any, top_ref, low_ref, x_ref, sem):
    copy = pltpu.make_async_copy(x_any, x_ref, sem)
    copy.start()
    half = x_ref.shape[0] // 2
    for ref in (top_ref, low_ref):
        tail = ref.shape[0] - half
        ref[half:, :] = jnp.full((tail, ref.shape[1]), live_ref[0]).astype(F32)
    copy.wait()
    top_ref[:half, :] = x_ref[:half].astype(F32)
    low_ref[:half, :] = x_ref[half:].astype(F32)


def own_columns(count):
    return columns(lax.axis_index("sensor") % count)


def pick_kernel(count, *refs):
    w_refs, proj_ref = refs[:3], refs[3]
    out_refs, p_ref, h_ref, sems = refs[4:7], refs[7], refs[8], refs[9]
    per = h_ref.shape[0]
    start = (lax.axis_index("sensor") % count) * per
    copies = [
        pltpu.make_async_copy(ref.at[:, own_columns(count)], out, sems.at[place])
        for place, (ref, out) in enumerate(zip(w_refs, out_refs))
    ]
    copies.append(pltpu.make_async_copy(proj_ref.at[pl.ds(start, per)], h_ref, sems.at[3]))
    for copy in copies:
        copy.start()
    for copy in copies:
        copy.wait()
    p_ref[...] = jnp.concatenate([h_ref[h] for h in range(per)], -1)


def key_kernel(steps, factor, count, *refs):
    tops, lows = refs[:count], refs[count : 2 * count]
    wk_ref, wv_ref, proj_ref, x_ref, u_ref, v_ref, f_ref, s_ref = refs[2 * count :]
    size = proj_ref.shape[0]
    mask = head_mask(size, LANES)
    rows = x_ref.shape[0] // (steps * count)
    half = steps * rows // 2
    piece = math.gcd(half, rows)
    for partner in range(count):
        for ref, base in ((tops[partner], 0), (lows[partner], half)):
            for row in range(0, half, piece):
                step, inner = divmod(base + row, rows)
                start = (step * count + partner) * rows + inner
                x_ref[start : start + piece, :] = ref[row : row + piece, :].astype(BF16)
    x = x_ref[...]
    scaled = dot(x, wk_ref[...]) * factor
    values = dot(x, wv_ref[...])
    u_ref[...] = scaled
    v_ref[...] = values
    feat = feature_map(scaled, [proj_ref[...]], mask, head_ones(mask), size)
    place = lax.broadcasted_iota(jnp.int32, (rows, LANES), 0).astype(F32)
    keep = jnp.concatenate([place < ref[half : half + 1, :LANES] for ref in tops] * steps, 0)
    feat = jnp.where(keep, feat, 0.0)
    f_ref[...] = feat
    store_summary(s_ref, *summaries(feat, values, feat, steps, size))


def query_kernel(steps, factor, count, live_ref, x_ref, cot_ref, wq_ref, wd_ref, proj_ref, u_ref, f_ref, gh_ref):
    size = proj_ref.shape[0]
    mask = head_mask(size, LANES)
    scaled = dot(x_ref[...], wq_ref[...]) * factor
    u_ref[...] = scaled
    f_ref[...] = feature_map(
        scaled, [proj_ref[...]], mask, head_ones(mask), size
    )
    hidden = dot(cot_ref[...], wd_ref[...], NT)
    place = lax.broadcasted_iota(jnp.int32, hidden.shape, 0) % (hidden.shape[0] // steps)
    gh_ref[...] = jnp.where(place < live_ref[0], hidden, 0.0)


def attend_kernel(steps, size, parts, *refs):
    s_refs, (f_ref, att_ref, inv_ref), out_refs = refs[:parts], refs[parts : parts + 3], refs[parts + 3 :]
    mask = head_mask(size, LANES)
    feat = f_ref[...]
    high = feat.shape[0] // steps
    numer, weighted = [], []
    for step, (matrix, row) in enumerate(load_summary(s_refs, steps, size)):
        part = feat[step * high : (step + 1) * high]
        numer.append(dot3(split(part), split(spread(matrix, mask))))
        weighted.append(part * row)
    inverse = 1.0 / head_sums(jnp.concatenate(weighted, 0), head_ones(mask))
    attended = jnp.concatenate(numer, 0) * inverse
    att_ref[...] = attended
    inv_ref[...] = inverse
    for partner, ref in enumerate(out_refs):
        ref[...] = take_rows(attended, partner, len(out_refs), steps)


def forward_kernel(count, *refs):
    in_refs, (gh_ref, wu_ref) = refs[:count], refs[count : count + 2]
    out_refs, scratch = refs[count + 2 : -1], refs[-1]
    me = lax.axis_index("sensor") % count
    for partner, ref in enumerate(in_refs):
        scratch[:, columns((me ^ partner) % count)] = ref[...]
    attended = scratch[...]
    scale = lax.rsqrt(jnp.mean(attended * attended, -1, keepdims=True) + 1e-06)
    normed = attended * scale
    wu = wu_ref[...]
    pre = dot(normed.astype(BF16), wu)
    c = math.sqrt(2.0 / math.pi)
    square = pre * pre
    t = jnp.tanh(c * pre * (1.0 + 0.044715 * square))
    slope = 0.5 * (1.0 + t) + 0.5 * pre * (1.0 - t * t) * (c * (1.0 + 3 * 0.044715 * square))
    grad_pre = (gh_ref[...] * slope).astype(BF16)
    grad_normed = dot(grad_pre, wu, NT)
    scratch[...] = (
        grad_normed - normed * jnp.mean(grad_normed * normed, -1, keepdims=True)
    ) * scale
    send_columns([scratch], out_refs, me)


def grad_summary_kernel(steps, size, count, *refs):
    in_refs, (att_ref, inv_ref, f_ref) = refs[:count], refs[count : count + 3]
    num_ref, den_ref, g_ref, scratch = refs[count + 3 :]
    place_rows(scratch, in_refs, steps)
    mask = head_mask(size, LANES)
    grad_att = scratch[...]
    inverse = inv_ref[...]
    feat = f_ref[...]
    grad_num = grad_att * inverse
    grad_den = -head_sums(grad_att * att_ref[...], head_ones(mask)) * inverse
    num_ref[...] = grad_num
    den_ref[...] = grad_den
    store_summary(g_ref, *summaries(feat, grad_num, feat * grad_den, steps, size))


def query_back_kernel(steps, factor, count, parts, *refs):
    s_refs, (num_ref, den_ref, f_ref, u_ref, proj_ref, g_ref) = refs[:parts], refs[parts : parts + 6]
    size = proj_ref.shape[0]
    mask = head_mask(size, LANES)
    high = f_ref.shape[0] // steps
    out = []
    for step, (matrix, row) in enumerate(load_summary(s_refs, steps, size)):
        part = slice(step * high, (step + 1) * high)
        back = dot3(split(num_ref[part, :]), split(spread(matrix, mask)), NT)
        out.append(back + den_ref[part, :] * row)
    weighted = jnp.concatenate(out, 0) * f_ref[...]
    grad = feature_back(
        weighted, u_ref[...], [proj_ref[...]], mask, head_ones(mask)
    )
    grad = (grad * factor).astype(BF16)
    g_ref[...] = grad
    for partner, ref in enumerate(refs[parts + 6 :]):
        ref[...] = take_rows(grad, partner, count, steps).astype(F32)


def key_back_kernel(steps, factor, count, parts, devices, *refs):
    g_refs, (u_ref, v_ref, f_ref, proj_ref, gq_ref) = refs[:parts], refs[parts : parts + 5]
    x_all, rest = refs[parts + 5], refs[parts + 6 :]
    back_refs, out_refs, p_ref = rest[:count], rest[count:-1], rest[-1]
    size = proj_ref.shape[0]
    mask = head_mask(size, LANES)
    high = f_ref.shape[0] // steps
    back, grad_v = [], []
    for step, (matrix, row) in enumerate(load_summary(g_refs, steps, size)):
        part = slice(step * high, (step + 1) * high)
        matrix = split(spread(matrix, mask))
        back.append(dot3(split(v_ref[part, :]), matrix, NT) + row)
        grad_v.append(dot3(split(f_ref[part, :]), matrix))
    weighted = jnp.concatenate(back, 0) * f_ref[...]
    grad_k = feature_back(
        weighted, u_ref[...], [proj_ref[...]], mask, head_ones(mask)
    )
    grad = jnp.concatenate([grad_k * factor, jnp.concatenate(grad_v, 0)], -1).astype(BF16)
    for partner, ref in enumerate(back_refs):
        ref[...] = take_rows(grad, partner, count, steps).astype(F32)
    grad = jnp.concatenate([gq_ref[...], grad], -1)
    total = dot(x_all[...], grad, TN)
    block = total.shape[0] // devices
    for place in range(devices):
        p_ref[place % count, place // count] = total[place * block : (place + 1) * block]
    me = lax.axis_index("step")
    for partner, ref in enumerate(out_refs):
        ref[...] = p_ref[(me ^ partner) % count]


def quarter_kernel(count, *refs):
    in_refs, out_refs = refs[:count], refs[count:]
    mine = lax.axis_index("sensor") // count
    for place, ref in enumerate(out_refs):
        block = (mine ^ place) % len(out_refs)
        total = in_refs[0][block]
        for part in in_refs[1:]:
            total = total + part[block]
        ref[...] = total


def rows_kernel(count, *refs):
    q_refs, kv_refs = refs[:count], refs[count : 2 * count]
    wq_ref, wk_ref, wv_ref, out_ref, q_ref, k_ref, v_ref = refs[2 * count :]
    me = lax.axis_index("sensor") % count
    for partner, (q, kv) in enumerate(zip(q_refs, kv_refs)):
        own = columns((me ^ partner) % count)
        q_ref[:, own] = q[...].astype(BF16)
        k_ref[:, own] = kv[:, :LANES].astype(BF16)
        v_ref[:, own] = kv[:, LANES:].astype(BF16)
    total = dot(q_ref[...], wq_ref[...], NT)
    total = total + dot(k_ref[...], wk_ref[...], NT)
    out_ref[...] = (total + dot(v_ref[...], wv_ref[...], NT)).astype(BF16)


def final_kernel(scale, parts, *refs):
    in_refs, outs = refs[:parts], refs[parts:]
    total = in_refs[0][...]
    for ref in in_refs[1:]:
        total = total + ref[...]
    cols = outs[0].shape[1]
    for place, ref in enumerate(outs):
        ref[...] = total[:, place * cols : (place + 1) * cols] * scale


def call(kernel, name, outs, args, flops=0, smem=0, hbm=0, scratch=(), limit=20):
    size = lambda a: math.prod(a.shape) * a.dtype.itemsize
    rest = len(args) - smem - hbm
    return pl.pallas_call(
        kernel,
        name=name,
        out_shape=outs,
        in_specs=[SMEM] * smem + [pl.BlockSpec(memory_space=pl.ANY)] * hbm + [VMEM] * rest,
        out_specs=jax.tree.map(lambda _: VMEM, outs),
        scratch_shapes=list(scratch),
        cost_estimate=pl.CostEstimate(
            flops=flops,
            bytes_accessed=sum(size(a) for a in list(args) + list(jax.tree.leaves(outs))),
            transcendentals=0,
        ),
        compiler_params=pltpu.CompilerParams(vmem_limit_bytes=limit * 1024 * 1024),
    )(*args)


def shape(dims, kind=F32):
    return jax.ShapeDtypeStruct(dims, kind)


def swap(a, axis, bit):
    return lax.ppermute(a, axis, [(i, i ^ bit) for i in range(lax.axis_size(axis))])


def trade(parts, axis):
    return [parts[0]] + [swap(a, axis, d) for d, a in enumerate(parts) if d]


def gather_halves(top, low, axis):
    near_low, next_top = swap(low, axis, 2), swap(top, axis, 1)
    near_top, next_low = swap(top, axis, 2), swap(low, axis, 1)
    across_top, across_low = swap(next_top, axis, 2), swap(near_low, axis, 1)
    return (top, next_top, near_top, across_top), (low, next_low, near_low, across_low)


def far_sum(a, count):
    bit = count
    while bit * 2 < lax.axis_size("sensor"):
        a = a + swap(a, "sensor", bit)
        bit *= 2
    return a, swap(a, "sensor", bit)


def after(a, *others):
    return lax.optimization_barrier((a, others))[0]


def shards(inputs, cotangent, w_query, w_key, w_value, w_up, w_down, feature_proj, live_count):
    steps, sensors, width = inputs.shape
    heads, size, feats = feature_proj.shape
    hidden = w_up.shape[1]
    factor = size ** (-0.25)
    rows = steps * sensors
    devices = lax.axis_size("sensor")
    count = width // LANES
    quads = devices // count
    x = inputs.reshape(rows, width)
    cot = cotangent.reshape(rows, width)
    narrow = shape((rows, LANES))
    tall = shape((rows * count, LANES))
    packed = shape((steps * size + 8, LANES))
    product = 2 * rows * width * width
    kinds = lambda *arrays: [pltpu.VMEM(a.shape, a.dtype) for a in arrays]
    wide = pltpu.VMEM((rows, width), F32)

    top, low = call(
        widen_kernel,
        "widen",
        (shape((rows // 2 + 8, width)),) * 2,
        (live_count, x),
        smem=1,
        hbm=1,
        limit=60,
        scratch=kinds(x) + [pltpu.SemaphoreType.DMA],
    )
    tops, lows = gather_halves(top, low, "sensor")
    narrow_w = shape((width, LANES), BF16)
    own_query, own_key, own_value, proj = call(
        functools.partial(pick_kernel, count),
        "pick_columns",
        (narrow_w,) * 3 + (shape((size, LANES)),),
        (w_query, w_key, w_value, feature_proj),
        hbm=4,
        scratch=[pltpu.VMEM((LANES // feats, size, feats), F32), pltpu.SemaphoreType.DMA((4,))],
    )
    x_all, key, value, feat_key, summary = call(
        functools.partial(key_kernel, steps, factor, count),
        "keys",
        (shape((rows * count, width), BF16),) + (tall,) * 3 + (packed,),
        (*tops, *lows, own_key, own_value, proj),
        flops=3 * product,
    )
    query, feat_query, grad_hidden = call(
        functools.partial(query_kernel, steps, factor, count),
        "queries",
        (tall, tall, shape((rows, hidden))),
        (live_count, x_all, cot, own_query, w_down, proj),
        flops=2 * product,
        smem=1,
    )
    summary = far_sum(summary, count)
    attended, inverse, *local_att = call(
        functools.partial(attend_kernel, steps, size, len(summary)),
        "attend",
        (tall, tall) + (narrow,) * count,
        (*summary, feat_query),
        flops=product,
    )
    local_grad = call(
        functools.partial(forward_kernel, count),
        "feed_forward",
        (narrow,) * count,
        (*trade(local_att, "sensor"), grad_hidden, w_up),
        flops=product,
        scratch=[wide],
    )
    grad_num, grad_den, grad_summary = call(
        functools.partial(grad_summary_kernel, steps, size, count),
        "grad_summary",
        (tall, tall, packed),
        (*trade(local_grad, "sensor"), attended, inverse, feat_query),
        flops=product,
        scratch=kinds(tall),
    )
    grad_summary = far_sum(grad_summary, count)
    grad_q, *local_gq = call(
        functools.partial(query_back_kernel, steps, factor, count, len(summary)),
        "query_back",
        (shape(tall.shape, BF16),) + (narrow,) * count,
        (*summary, grad_num, grad_den, feat_query, query, proj),
        flops=product,
    )
    quad_gq = trade(local_gq, "sensor")
    tile = (width // devices, 3 * LANES)
    back = call(
        functools.partial(key_back_kernel, steps, factor, count, len(grad_summary), devices),
        "key_back",
        (shape((rows, 2 * LANES)),) * count + (shape((quads, *tile)),) * count,
        (*grad_summary, key, value, feat_key, proj, after(grad_q, *quad_gq), x_all),
        flops=4 * product,
        scratch=[pltpu.VMEM((count, quads, *tile), F32)],
    )
    partial = trade(back[count:], "step")

    def turn(a, bit):
        pairs = []
        for k in range(quads):
            for q in range(count):
                for j in range(count):
                    target = (k ^ bit) * count + j
                    pairs.append(((k * count + q) * count + j, target * count + q))
        return lax.ppermute(a, ("sensor", "step"), pairs)

    if quads == 2:
        kept, away = call(
            functools.partial(quarter_kernel, count), "quarter_sums", (shape(tile),) * 2, partial
        )
        parts = (turn(kept, 0), turn(away, 1))
    else:
        groups = [[q + count * k for k in range(quads)] for q in range(count)]
        blocks = lax.all_to_all(sum(partial), "sensor", 0, 0, tiled=True, axis_index_groups=groups)
        parts = (turn(blocks.sum(0), 0),)
    grad_in = call(
        functools.partial(rows_kernel, count),
        "input_rows",
        shape((rows, width), BF16),
        (*quad_gq, *trade(back[:count], "sensor"), w_query, w_key, w_value),
        flops=3 * product,
        scratch=[pltpu.VMEM((rows, width), BF16)] * 3,
    )
    scale = 1.0 / math.sqrt(rows * lax.axis_size("step") * devices)
    out = shape((width // devices, LANES))
    grads = call(
        functools.partial(final_kernel, scale, len(parts)), "weight_sums", (out,) * 3, parts
    )
    return (grad_in.reshape(inputs.shape), *grads)


def solution(mesh):
    return jax.shard_map(
        shards,
        mesh=mesh,
        in_specs=(P("step", "sensor", None),) * 2 + (P(),) * 6 + (P("sensor"),),
        out_specs=(P("step", "sensor", None),) + (P("sensor", "step"),) * 3,
        check_vma=False,
    )
```

time: 470 us -> 83.9 us (0.18)
  the two profiles are of different devices: /device:TPU:0 before, /device:TPU:1 now
where the time goes in v3:
time: 83.9 us; the launch traced here: 83.6 us
  starting transfers between devices  37.9 us (45%)
  waiting for transfers between devices  30.1 us (36%)
  Pallas kernels  10 us (12%)
  local copies, waits for them, and re-layouts  4.11 us (5%)
  between operations  1.46 us (2%)
    ppermute x23, starting transfers between devices, swap(): lax.ppermute(a, axis, [(i, i ^ bit) for i in range(lax.axis_size(axis))])  34.7 us
    ppermute x23, waiting for transfers between devices, swap(): lax.ppermute(a, axis, [(i, i ^ bit) for i in range(lax.axis_size(axis))])  24.3 us
    pallas_call x12, Pallas kernels, call(): pl.pallas_call(kernel, name=name, out_shape=outs, in_specs=[SMEM] * smem...  10 us
    ppermute x2, waiting for transfers between devices, turn(): return lax.ppermute(a, ('sensor', 'step'), pairs)  5.79 us
    unnamed x24, local copies, waits for them, and re-layouts  4.11 us
    ppermute x2, starting transfers between devices, turn(): return lax.ppermute(a, ('sensor', 'step'), pairs)  3.17 us
  transfers between devices with their start and end apart: 25, of which 16 were waited for; matrix products, arithmetic and copies ran while one was open for 0% of the time, Pallas kernels for 4%

profile of v3, /device:TPU:1, one launch (start us, length us, event | category | flops | bytes accessed | tf_op | source)
XLA Modules:
  0.0 83.6 jit_solution(4185967427184624006)
XLA Ops:
  1.3 1.7 %widen.1 = (f32[104,512]{1,0:T(8,128)}, f32[104,512]{1,0:T(8,128)}) custom-call(s32[1]{0:T(128)S(6)} %copy.13.live_ref, bf16[192,512]{1,0:T(8,128)(2,1)} %bitcast.5), custom_call_target="tpu_custom_call" | custom-call | bytes 622596 | tf_op jit(solution)/shard_map/widen/pallas_call | solution.py:371
  3.0 2.1 %collective-permute-start = (f32[104,512]{1,0:T(8,128)}, f32[104,512]{1,0:T(8,128)S(1)}, u32[]{:S(2)}, u32[]{:S(2)}) collective-permute-start(f32[104,512]{1,0:T(8,128)} %get-tuple-element.50.refs_0_), channel_id=1, source_target_pairs={{0,4},{4,0},{8,12},{12,8},{16,20},{20,16},{24,28},{28,24},{1,5},{5... | collective-permute-start | bytes 638984 | tf_op jit(solution)/shard_map/ppermute | solution.py:392
  5.1 1.3 %collective-permute-start.4 = (f32[104,512]{1,0:T(8,128)}, f32[104,512]{1,0:T(8,128)S(1)}, u32[]{:S(2)}, u32[]{:S(2)}) collective-permute-start(f32[104,512]{1,0:T(8,128)} %get-tuple-element.51.refs_4_), channel_id=1, source_target_pairs={{0,8},{4,12},{8,0},{12,4},{16,24},{20,28},{24,16},{28,20},{1,9},{5... | collective-permute-start | bytes 638984 | tf_op jit(solution)/shard_map/ppermute | solution.py:392
  6.4 0.2 collective-permute-start.1
  6.6 0.1 collective-permute-start.3
  6.7 3.6 %collective-permute-done.refs_1_ = f32[104,512]{1,0:T(8,128)S(1)} collective-permute-done((f32[104,512]{1,0:T(8,128)}, f32[104,512]{1,0:T(8,128)S(1)}, u32[]{:S(2)}, u32[]{:S(2)}) %collective-permute-start) | collective-permute-done | bytes 213024 | tf_op jit(solution)/shard_map/ppermute | solution.py:392
  10.3 1.2 %collective-permute-start.2 = (f32[104,512]{1,0:T(8,128)S(1)}, f32[104,512]{1,0:T(8,128)S(1)}, u32[]{:S(2)}, u32[]{:S(2)}) collective-permute-start(f32[104,512]{1,0:T(8,128)S(1)} %collective-permute-done.refs_1_), channel_id=1, source_target_pairs={{0,8},{4,12},{8,0},{12,4},{16,24},{20,28},{24,16},{28,20},{1,9},{5... | collective-permute-start | bytes 638984 | tf_op jit(solution)/shard_map/ppermute | solution.py:392
  11.5 0.0 collective-permute-done.4.refs_6_
  11.5 1.2 %collective-permute-start.5 = (f32[104,512]{1,0:T(8,128)S(1)}, f32[104,512]{1,0:T(8,128)S(1)}, u32[]{:S(2)}, u32[]{:S(2)}) collective-permute-start(f32[104,512]{1,0:T(8,128)S(1)} %collective-permute-done.4.refs_6_), channel_id=1, source_target_pairs={{0,4},{4,0},{8,12},{12,8},{16,20},{20,16},{24,28},{28,24},{1,5},{5... | collective-permute-start | bytes 638984 | tf_op jit(solution)/shard_map/ppermute | solution.py:392
  12.7 1.0 %copy-done = bf16[512,512]{1,0:T(8,128)(2,1)S(1)} copy-done((bf16[512,512]{1,0:T(8,128)(2,1)S(1)}, bf16[512,512]{1,0:T(8,128)(2,1)}, u32[]{:S(2)}) %copy-start) | copy-done | bytes 524312
  13.8 1.0 %copy-done.2 = bf16[512,512]{1,0:T(8,128)(2,1)S(1)} copy-done((bf16[512,512]{1,0:T(8,128)(2,1)S(1)}, bf16[512,512]{1,0:T(8,128)(2,1)}, u32[]{:S(2)}) %copy-start.2) | copy-done | bytes 524312
  14.8 1.0 %copy-done.4 = bf16[512,512]{1,0:T(8,128)(2,1)S(1)} copy-done((bf16[512,512]{1,0:T(8,128)(2,1)S(1)}, bf16[512,512]{1,0:T(8,128)(2,1)}, u32[]{:S(2)}) %copy-start.4) | copy-done | bytes 524312
  15.9 0.9 %copy-done.6 = f32[8,64,64]{2,1,0:T(8,128)S(1)} copy-done((f32[8,64,64]{2,1,0:T(8,128)S(1)}, f32[8,64,64]{2,1,0:T(8,128)}, u32[]{:S(2)}) %copy-start.6) | copy-done | bytes 131096
  16.8 0.3 pick_columns.1
  17.1 0.0 collective-permute-done.1.refs_2_
  17.1 0.0 collective-permute-done.3.refs_5_
  17.1 3.1 %collective-permute-done.2.refs_3_ = f32[104,512]{1,0:T(8,128)S(1)} collective-permute-done((f32[104,512]{1,0:T(8,128)S(1)}, f32[104,512]{1,0:T(8,128)S(1)}, u32[]{:S(2)}, u32[]{:S(2)}) %collective-permute-start.2) | collective-permute-done | bytes 213024 | tf_op jit(solution)/shard_map/ppermute | solution.py:392
  20.3 0.0 collective-permute-done.5.refs_7_
  20.3 0.0 copy-start.7
  20.3 0.0 copy-start.11
  20.3 1.2 %keys.1 = (bf16[768,512]{1,0:T(8,128)(2,1)S(1)}, f32[768,128]{1,0:T(8,128)S(1)}, f32[768,128]{1,0:T(8,128)S(1)}, f32[768,128]{1,0:T(8,128)S(1)}, f32[200,128]{1,0:T(8,128)S(1)}) custom-call(f32[104,512]{1,0:T(8,128)S(1)} %copy-done.9, f32[104,512]{1,0:T(8,128)S(1)} %collective-permute-done.refs_1_, f32[104,512]{1,0:T(8,128)S(1)} %collective-permute-done.1.refs_2_, ...), custom_call_target="tpu_custom_call" | custom-call | flops 301989888 | bytes 4067328 | tf_op jit(solution)/shard_map/keys/pallas_call | solution.py:371
  21.5 2.4 %collective-permute-start.6 = (f32[200,128]{1,0:T(8,128)S(1)}, f32[200,128]{1,0:T(8,128)S(1)}, u32[]{:S(2)}, u32[]{:S(2)}) collective-permute-start(f32[200,128]{1,0:T(8,128)S(1)} %get-tuple-element.55.refs_0_), channel_id=1, source_target_pairs={{0,16},{4,20},{8,24},{12,28},{16,0},{20,4},{24,8},{28,12},{1,17},{... | collective-permute-start | bytes 307208 | tf_op jit(solution)/shard_map/ppermute | solution.py:392
  23.9 1.1 %queries.1 = (f32[768,128]{1,0:T(8,128)S(1)}, f32[768,128]{1,0:T(8,128)S(1)}, f32[192,256]{1,0:T(8,128)S(1)}) custom-call(s32[1]{0:T(128)S(6)} %copy.13.live_ref, bf16[768,512]{1,0:T(8,128)(2,1)S(1)} %get-tuple-element.56.x_ref.refs_7_, bf16[192,512]{1,0:T(8,128)(2,1)S(1)} %bitcast.3, bf16[512,128]{1,0:T(8,128)(2,1)S(1)} %get-tuple-element.57.wq_ref, ...), custom_call_target="tpu_custom_call" | custom-call | flops 201326592 | bytes 2392068 | tf_op jit(solution)/shard_map/queries/pallas_call | solution.py:371
  25.0 1.0 %collective-permute-done.6.refs_1_ = f32[200,128]{1,0:T(8,128)S(1)} collective-permute-done((f32[200,128]{1,0:T(8,128)S(1)}, f32[200,128]{1,0:T(8,128)S(1)}, u32[]{:S(2)}, u32[]{:S(2)}) %collective-permute-start.6) | collective-permute-done | bytes 102432 | tf_op jit(solution)/shard_map/ppermute | solution.py:392
  26.0 0.5 attend.1
  26.5 1.9 %collective-permute-start.7 = (f32[192,128]{1,0:T(8,128)S(1)}, f32[192,128]{1,0:T(8,128)S(1)}, u32[]{:S(2)}, u32[]{:S(2)}) collective-permute-start(f32[192,128]{1,0:T(8,128)S(1)} %get-tuple-element.60), channel_id=1, source_target_pairs={{0,4},{4,0},{8,12},{12,8},{16,20},{20,16},{24,28},{28,24},{1,5},{5... | collective-permute-start | bytes 294920 | tf_op jit(solution)/shard_map/ppermute | solution.py:392
  28.4 0.2 collective-permute-start.8
  28.6 1.1 %collective-permute-start.9 = (f32[192,128]{1,0:T(8,128)S(1)}, f32[192,128]{1,0:T(8,128)S(1)}, u32[]{:S(2)}, u32[]{:S(2)}) collective-permute-start(f32[192,128]{1,0:T(8,128)S(1)} %get-tuple-element.62), channel_id=1, source_target_pairs={{0,12},{4,8},{8,4},{12,0},{16,28},{20,24},{24,20},{28,16},{1,13},{... | collective-permute-start | bytes 294920 | tf_op jit(solution)/shard_map/ppermute | solution.py:392
  29.6 0.7 collective-permute-done.7.refs_1_
  30.4 1.5 %collective-permute-done.8.refs_2_ = f32[192,128]{1,0:T(8,128)S(1)} collective-permute-done((f32[192,128]{1,0:T(8,128)S(1)}, f32[192,128]{1,0:T(8,128)S(1)}, u32[]{:S(2)}, u32[]{:S(2)}) %collective-permute-start.8) | collective-permute-done | bytes 98336 | tf_op jit(solution)/shard_map/ppermute | solution.py:392
  31.8 1.2 %collective-permute-done.9.refs_3_ = f32[192,128]{1,0:T(8,128)S(1)} collective-permute-done((f32[192,128]{1,0:T(8,128)S(1)}, f32[192,128]{1,0:T(8,128)S(1)}, u32[]{:S(2)}, u32[]{:S(2)}) %collective-permute-start.9) | collective-permute-done | bytes 98336 | tf_op jit(solution)/shard_map/ppermute | solution.py:392
  33.0 0.7 feed_forward.1
  33.7 1.3 %collective-permute-start.10 = (f32[192,128]{1,0:T(8,128)S(1)}, f32[192,128]{1,0:T(8,128)S(1)}, u32[]{:S(2)}, u32[]{:S(2)}) collective-permute-start(f32[192,128]{1,0:T(8,128)S(1)} %get-tuple-element.65), channel_id=1, source_target_pairs={{0,4},{4,0},{8,12},{12,8},{16,20},{20,16},{24,28},{28,24},{1,5},{5... | collective-permute-start | bytes 294920 | tf_op jit(solution)/shard_map/ppermute | solution.py:392
  35.0 0.1 collective-permute-start.11
  35.1 1.3 %collective-permute-start.12 = (f32[192,128]{1,0:T(8,128)S(1)}, f32[192,128]{1,0:T(8,128)S(1)}, u32[]{:S(2)}, u32[]{:S(2)}) collective-permute-start(f32[192,128]{1,0:T(8,128)S(1)} %get-tuple-element.67), channel_id=1, source_target_pairs={{0,12},{4,8},{8,4},{12,0},{16,28},{20,24},{24,20},{28,16},{1,13},{... | collective-permute-start | bytes 294920 | tf_op jit(solution)/shard_map/ppermute | solution.py:392
  36.4 1.3 %collective-permute-done.10.refs_1_ = f32[192,128]{1,0:T(8,128)S(1)} collective-permute-done((f32[192,128]{1,0:T(8,128)S(1)}, f32[192,128]{1,0:T(8,128)S(1)}, u32[]{:S(2)}, u32[]{:S(2)}) %collective-permute-start.10) | collective-permute-done | bytes 98336 | tf_op jit(solution)/shard_map/ppermute | solution.py:392
  37.7 0.8 collective-permute-done.11.refs_2_
  38.5 1.0 %collective-permute-done.12.refs_3_ = f32[192,128]{1,0:T(8,128)S(1)} collective-permute-done((f32[192,128]{1,0:T(8,128)S(1)}, f32[192,128]{1,0:T(8,128)S(1)}, u32[]{:S(2)}, u32[]{:S(2)}) %collective-permute-start.12) | collective-permute-done | bytes 98336 | tf_op jit(solution)/shard_map/ppermute | solution.py:392
  39.5 0.5 grad_summary.1
  40.0 2.9 %collective-permute-start.16 = (f32[200,128]{1,0:T(8,128)S(1)}, f32[200,128]{1,0:T(8,128)S(1)}, u32[]{:S(2)}, u32[]{:S(2)}) collective-permute-start(f32[200,128]{1,0:T(8,128)S(1)} %get-tuple-element.77.refs_0_), channel_id=1, source_target_pairs={{0,16},{4,20},{8,24},{12,28},{16,0},{20,4},{24,8},{28,12},{1,17},{... | collective-permute-start | bytes 307208 | tf_op jit(solution)/shard_map/ppermute | solution.py:392
  42.9 0.7 query_back.1
  43.6 1.3 %collective-permute-start.13 = (f32[192,128]{1,0:T(8,128)S(1)}, f32[192,128]{1,0:T(8,128)S(1)}, u32[]{:S(2)}, u32[]{:S(2)}) collective-permute-start(f32[192,128]{1,0:T(8,128)S(1)} %get-tuple-element.74), channel_id=1, source_target_pairs={{0,4},{4,0},{8,12},{12,8},{16,20},{20,16},{24,28},{28,24},{1,5},{5... | collective-permute-start | bytes 294920 | tf_op jit(solution)/shard_map/ppermute | solution.py:392
  44.9 0.3 collective-permute-start.14
  45.3 1.1 %collective-permute-start.15 = (f32[192,128]{1,0:T(8,128)S(1)}, f32[192,128]{1,0:T(8,128)S(1)}, u32[]{:S(2)}, u32[]{:S(2)}) collective-permute-start(f32[192,128]{1,0:T(8,128)S(1)} %get-tuple-element.76), channel_id=1, source_target_pairs={{0,12},{4,8},{8,4},{12,0},{16,28},{20,24},{24,20},{28,16},{1,13},{... | collective-permute-start | bytes 294920 | tf_op jit(solution)/shard_map/ppermute | solution.py:392
  46.3 0.8 collective-permute-done.13.refs_1_
  47.1 1.3 %collective-permute-done.14.refs_2_ = f32[192,128]{1,0:T(8,128)S(1)} collective-permute-done((f32[192,128]{1,0:T(8,128)S(1)}, f32[192,128]{1,0:T(8,128)S(1)}, u32[]{:S(2)}, u32[]{:S(2)}) %collective-permute-start.14) | collective-permute-done | bytes 98336 | tf_op jit(solution)/shard_map/ppermute | solution.py:392
  48.4 1.2 %collective-permute-done.15.refs_3_ = f32[192,128]{1,0:T(8,128)S(1)} collective-permute-done((f32[192,128]{1,0:T(8,128)S(1)}, f32[192,128]{1,0:T(8,128)S(1)}, u32[]{:S(2)}, u32[]{:S(2)}) %collective-permute-start.15) | collective-permute-done | bytes 98336 | tf_op jit(solution)/shard_map/ppermute | solution.py:392
  49.6 0.0 collective-permute-done.16.refs_1_
  49.6 1.3 %key_back.1 = (f32[192,256]{1,0:T(8,128)S(1)}, f32[192,256]{1,0:T(8,128)S(1)}, f32[192,256]{1,0:T(8,128)S(1)}, f32[192,256]{1,0:T(8,128)S(1)}, f32[2,64,384]{2,1...) custom-call(f32[200,128]{1,0:T(8,128)S(1)} %get-tuple-element.77.refs_0_, ...), custom_call_target="tpu_custom_call" | custom-call | flops 402653184 | bytes 3973120 | tf_op jit(solution)/shard_map/key_back/pallas_call | solution.py:371
  51.0 0.0 copy-start.1
  51.0 10.4 %collective-permute-start.20 = (f32[2,64,384]{2,1,0:T(8,128)S(1)}, f32[2,64,384]{2,1,0:T(8,128)S(1)}, u32[]{:S(2)}, u32[]{:S(2)}) collective-permute-start(f32[2,64,384]{2,1,0:T(8,128)S(1)} %get-tuple-element.88), channel_id=1, source_target_pairs={{0,1},{1,0},{2,3},{3,2},{4,5},{5,4},{6,7},{7,6},{8,9},{9,8},{10,11... | collective-permute-start | bytes 589832 | tf_op jit(solution)/shard_map/ppermute | solution.py:392
  61.3 1.2 %collective-permute-start.21 = (f32[2,64,384]{2,1,0:T(8,128)S(1)}, f32[2,64,384]{2,1,0:T(8,128)S(1)}, u32[]{:S(2)}, u32[]{:S(2)}) collective-permute-start(f32[2,64,384]{2,1,0:T(8,128)S(1)} %get-tuple-element.89), channel_id=1, source_target_pairs={{0,2},{1,3},{2,0},{3,1},{4,6},{5,7},{6,4},{7,5},{8,10},{9,11},{10,... | collective-permute-start | bytes 589832 | tf_op jit(solution)/shard_map/ppermute | solution.py:392
  62.6 0.5 collective-permute-start.22
  63.0 0.5 collective-permute-start.17
  63.6 0.5 collective-permute-start.18
  64.1 1.6 %collective-permute-start.19 = (f32[192,256]{1,0:T(8,128)S(1)}, f32[192,256]{1,0:T(8,128)S(1)}, u32[]{:S(2)}, u32[]{:S(2)}) collective-permute-start(f32[192,256]{1,0:T(8,128)S(1)} %get-tuple-element.86), channel_id=1, source_target_pairs={{0,12},{4,8},{8,4},{12,0},{16,28},{20,24},{24,20},{28,16},{1,13},{... | collective-permute-start | bytes 589832 | tf_op jit(solution)/shard_map/ppermute | solution.py:392
  65.7 2.1 %collective-permute-done.21.refs_2_ = f32[2,64,384]{2,1,0:T(8,128)S(1)} collective-permute-done((f32[2,64,384]{2,1,0:T(8,128)S(1)}, f32[2,64,384]{2,1,0:T(8,128)S(1)}, u32[]{:S(2)}, u32[]{:S(2)}) %collective-permute-start.21) | collective-permute-done | bytes 196640 | tf_op jit(solution)/shard_map/ppermute | solution.py:392
  67.8 4.7 %collective-permute-done.22.refs_3_ = f32[2,64,384]{2,1,0:T(8,128)S(1)} collective-permute-done((f32[2,64,384]{2,1,0:T(8,128)S(1)}, f32[2,64,384]{2,1,0:T(8,128)S(1)}, u32[]{:S(2)}, u32[]{:S(2)}) %collective-permute-start.22) | collective-permute-done | bytes 196640 | tf_op jit(solution)/shard_map/ppermute | solution.py:392
  72.5 2.3 %collective-permute-start.23 = (f32[64,384]{1,0:T(8,128)S(1)}, f32[64,384]{1,0:T(8,128)S(1)}, u32[]{:S(2)}, u32[]{:S(2)}) collective-permute-start(f32[64,384]{1,0:T(8,128)S(1)} %get-tuple-element.91), channel_id=1, source_target_pairs={{0,0},{1,4},{2,8},{3,12},{4,1},{5,5},{6,9},{7,13},{8,2},{9,6},{10,... | collective-permute-start | bytes 294920 | tf_op jit(solution)/shard_map/ppermute | solution.py:522
  74.8 0.9 %collective-permute-start.24 = (f32[64,384]{1,0:T(8,128)S(1)}, f32[64,384]{1,0:T(8,128)S(1)}, u32[]{:S(2)}, u32[]{:S(2)}) collective-permute-start(f32[64,384]{1,0:T(8,128)S(1)} %get-tuple-element.92), channel_id=1, source_target_pairs={{0,16},{1,20},{2,24},{3,28},{4,17},{5,21},{6,25},{7,29},{8,18},{9,... | collective-permute-start | bytes 294920 | tf_op jit(solution)/shard_map/ppermute | solution.py:522
  75.8 1.4 %input_rows.1 = bf16[192,512]{1,0:T(8,128)(2,1)} custom-call(f32[192,128]{1,0:T(8,128)S(1)} %get-tuple-element.73.refs_0_, f32[192,128]{1,0:T(8,128)S(1)} %collective-permute-done.13.refs_1_, f32[192,128]{1,0:T(8,128)S(1)} %collective-permute-done.14.refs_2_, f32[192,128]{1,0:T(8,128)S(1)} %collective-permute-done.15.refs_3_, ...), custom_call_target="tpu_custom_call" | custom-call | flops 301989888 | bytes 2949120 | tf_op jit(solution)/shard_map/input_rows/pallas_call | solution.py:371
  77.1 1.3 %collective-permute-done.23.refs_0_ = f32[64,384]{1,0:T(8,128)S(1)} collective-permute-done((f32[64,384]{1,0:T(8,128)S(1)}, f32[64,384]{1,0:T(8,128)S(1)}, u32[]{:S(2)}, u32[]{:S(2)}) %collective-permute-start.23) | collective-permute-done | bytes 98336 | tf_op jit(solution)/shard_map/ppermute | solution.py:522
  78.5 4.4 %collective-permute-done.24.refs_1_ = f32[64,384]{1,0:T(8,128)S(1)} collective-permute-done((f32[64,384]{1,0:T(8,128)S(1)}, f32[64,384]{1,0:T(8,128)S(1)}, u32[]{:S(2)}, u32[]{:S(2)}) %collective-permute-start.24) | collective-permute-done | bytes 98336 | tf_op jit(solution)/shard_map/ppermute | solution.py:522
  82.9 0.6 weight_sums.1
  (22 shorter events, 0.1 us)
Async XLA Ops:
  3.0 7.3 %collective-permute-start = (f32[104,512]{1,0:T(8,128)}, f32[104,512]{1,0:T(8,128)S(1)}, u32[]{:S(2)}, u32[]{:S(2)}) collective-permute-start(f32[104,512]{1,0:T(8,128)} %get-tuple-element.50.refs_0_), channel_id=1, source_target_pairs={{0,4},{4,0},{8,12},{12,8},{16,20},{20,16},{24,28},{28,24},{1,5},{5... | collective-permute-start | bytes 638984 | tf_op jit(solution)/shard_map/ppermute | solution.py:392
  5.1 6.4 %collective-permute-start.4 = (f32[104,512]{1,0:T(8,128)}, f32[104,512]{1,0:T(8,128)S(1)}, u32[]{:S(2)}, u32[]{:S(2)}) collective-permute-start(f32[104,512]{1,0:T(8,128)} %get-tuple-element.51.refs_4_), channel_id=1, source_target_pairs={{0,8},{4,12},{8,0},{12,4},{16,24},{20,28},{24,16},{28,20},{1,9},{5... | collective-permute-start | bytes 638984 | tf_op jit(solution)/shard_map/ppermute | solution.py:392
  6.4 10.7 %collective-permute-start.1 = (f32[104,512]{1,0:T(8,128)}, f32[104,512]{1,0:T(8,128)S(1)}, u32[]{:S(2)}, u32[]{:S(2)}) collective-permute-start(f32[104,512]{1,0:T(8,128)} %get-tuple-element.50.refs_0_), channel_id=1, source_target_pairs={{0,8},{4,12},{8,0},{12,4},{16,24},{20,28},{24,16},{28,20},{1,9},{5... | collective-permute-start | bytes 638984 | tf_op jit(solution)/shard_map/ppermute | solution.py:392
  6.6 10.5 %collective-permute-start.3 = (f32[104,512]{1,0:T(8,128)}, f32[104,512]{1,0:T(8,128)S(1)}, u32[]{:S(2)}, u32[]{:S(2)}) collective-permute-start(f32[104,512]{1,0:T(8,128)} %get-tuple-element.51.refs_4_), channel_id=1, source_target_pairs={{0,4},{4,0},{8,12},{12,8},{16,20},{20,16},{24,28},{28,24},{1,5},{5... | collective-permute-start | bytes 638984 | tf_op jit(solution)/shard_map/ppermute | solution.py:392
  10.3 10.0 %collective-permute-start.2 = (f32[104,512]{1,0:T(8,128)S(1)}, f32[104,512]{1,0:T(8,128)S(1)}, u32[]{:S(2)}, u32[]{:S(2)}) collective-permute-start(f32[104,512]{1,0:T(8,128)S(1)} %collective-permute-done.refs_1_), channel_id=1, source_target_pairs={{0,8},{4,12},{8,0},{12,4},{16,24},{20,28},{24,16},{28,20},{1,9},{5... | collective-permute-start | bytes 638984 | tf_op jit(solution)/shard_map/ppermute | solution.py:392
  11.5 8.8 %collective-permute-start.5 = (f32[104,512]{1,0:T(8,128)S(1)}, f32[104,512]{1,0:T(8,128)S(1)}, u32[]{:S(2)}, u32[]{:S(2)}) collective-permute-start(f32[104,512]{1,0:T(8,128)S(1)} %collective-permute-done.4.refs_6_), channel_id=1, source_target_pairs={{0,4},{4,0},{8,12},{12,8},{16,20},{20,16},{24,28},{28,24},{1,5},{5... | collective-permute-start | bytes 638984 | tf_op jit(solution)/shard_map/ppermute | solution.py:392
  12.7 1.0 %copy-start = (bf16[512,512]{1,0:T(8,128)(2,1)S(1)}, bf16[512,512]{1,0:T(8,128)(2,1)}, u32[]{:S(2)}) copy-start(bf16[512,512]{1,0:T(8,128)(2,1)} %refs_8_.1) | copy-start | bytes 1572868
  13.8 1.0 %copy-start.2 = (bf16[512,512]{1,0:T(8,128)(2,1)S(1)}, bf16[512,512]{1,0:T(8,128)(2,1)}, u32[]{:S(2)}) copy-start(bf16[512,512]{1,0:T(8,128)(2,1)} %refs_9_.1) | copy-start | bytes 1572868
  14.8 1.0 %copy-start.4 = (bf16[512,512]{1,0:T(8,128)(2,1)S(1)}, bf16[512,512]{1,0:T(8,128)(2,1)}, u32[]{:S(2)}) copy-start(bf16[512,512]{1,0:T(8,128)(2,1)} %refs_10_.1) | copy-start | bytes 1572868
  15.9 0.9 %copy-start.6 = (f32[8,64,64]{2,1,0:T(8,128)S(1)}, f32[8,64,64]{2,1,0:T(8,128)}, u32[]{:S(2)}) copy-start(f32[8,64,64]{2,1,0:T(8,128)} %refs_3_.1) | copy-start | bytes 393220
  16.8 3.4 %copy-start.9 = (f32[104,512]{1,0:T(8,128)S(1)}, f32[104,512]{1,0:T(8,128)}, u32[]{:S(2)}) copy-start(f32[104,512]{1,0:T(8,128)} %get-tuple-element.50.refs_0_) | copy-start | bytes 638980
  16.8 3.4 %copy-start.10 = (f32[104,512]{1,0:T(8,128)S(1)}, f32[104,512]{1,0:T(8,128)}, u32[]{:S(2)}) copy-start(f32[104,512]{1,0:T(8,128)} %get-tuple-element.51.refs_4_) | copy-start | bytes 638980
  20.3 3.7 %copy-start.7 = (bf16[256,512]{1,0:T(8,128)(2,1)S(1)}, bf16[256,512]{1,0:T(8,128)(2,1)}, u32[]{:S(2)}) copy-start(bf16[256,512]{1,0:T(8,128)(2,1)} %wd_ref.1) | copy-start | bytes 786436
  20.3 3.6 %copy-start.11 = (bf16[3,64,512]{2,1,0:T(8,128)(2,1)S(1)}, bf16[3,64,512]{2,1,0:T(8,128)(2,1)}, u32[]{:S(2)}) copy-start(bf16[3,64,512]{2,1,0:T(8,128)(2,1)} %param.10) | copy-start | bytes 589828
  21.5 4.5 %collective-permute-start.6 = (f32[200,128]{1,0:T(8,128)S(1)}, f32[200,128]{1,0:T(8,128)S(1)}, u32[]{:S(2)}, u32[]{:S(2)}) collective-permute-start(f32[200,128]{1,0:T(8,128)S(1)} %get-tuple-element.55.refs_0_), channel_id=1, source_target_pairs={{0,16},{4,20},{8,24},{12,28},{16,0},{20,4},{24,8},{28,12},{1,17},{... | collective-permute-start | bytes 307208 | tf_op jit(solution)/shard_map/ppermute | solution.py:392
  26.0 6.9 %copy-start.8 = (bf16[512,256]{1,0:T(8,128)(2,1)S(1)}, bf16[512,256]{1,0:T(8,128)(2,1)}, u32[]{:S(2)}) copy-start(bf16[512,256]{1,0:T(8,128)(2,1)} %refs_5_.1) | copy-start | bytes 786436
  26.5 3.9 %collective-permute-start.7 = (f32[192,128]{1,0:T(8,128)S(1)}, f32[192,128]{1,0:T(8,128)S(1)}, u32[]{:S(2)}, u32[]{:S(2)}) collective-permute-start(f32[192,128]{1,0:T(8,128)S(1)} %get-tuple-element.60), channel_id=1, source_target_pairs={{0,4},{4,0},{8,12},{12,8},{16,20},{20,16},{24,28},{28,24},{1,5},{5... | collective-permute-start | bytes 294920 | tf_op jit(solution)/shard_map/ppermute | solution.py:392
  28.4 3.5 %collective-permute-start.8 = (f32[192,128]{1,0:T(8,128)S(1)}, f32[192,128]{1,0:T(8,128)S(1)}, u32[]{:S(2)}, u32[]{:S(2)}) collective-permute-start(f32[192,128]{1,0:T(8,128)S(1)} %get-tuple-element.61), channel_id=1, source_target_pairs={{0,8},{4,12},{8,0},{12,4},{16,24},{20,28},{24,16},{28,20},{1,9},{5... | collective-permute-start | bytes 294920 | tf_op jit(solution)/shard_map/ppermute | solution.py:392
  28.6 4.4 %collective-permute-start.9 = (f32[192,128]{1,0:T(8,128)S(1)}, f32[192,128]{1,0:T(8,128)S(1)}, u32[]{:S(2)}, u32[]{:S(2)}) collective-permute-start(f32[192,128]{1,0:T(8,128)S(1)} %get-tuple-element.62), channel_id=1, source_target_pairs={{0,12},{4,8},{8,4},{12,0},{16,28},{20,24},{24,20},{28,16},{1,13},{... | collective-permute-start | bytes 294920 | tf_op jit(solution)/shard_map/ppermute | solution.py:392
  33.7 4.0 %collective-permute-start.10 = (f32[192,128]{1,0:T(8,128)S(1)}, f32[192,128]{1,0:T(8,128)S(1)}, u32[]{:S(2)}, u32[]{:S(2)}) collective-permute-start(f32[192,128]{1,0:T(8,128)S(1)} %get-tuple-element.65), channel_id=1, source_target_pairs={{0,4},{4,0},{8,12},{12,8},{16,20},{20,16},{24,28},{28,24},{1,5},{5... | collective-permute-start | bytes 294920 | tf_op jit(solution)/shard_map/ppermute | solution.py:392
  35.0 3.5 %collective-permute-start.11 = (f32[192,128]{1,0:T(8,128)S(1)}, f32[192,128]{1,0:T(8,128)S(1)}, u32[]{:S(2)}, u32[]{:S(2)}) collective-permute-start(f32[192,128]{1,0:T(8,128)S(1)} %get-tuple-element.66), channel_id=1, source_target_pairs={{0,8},{4,12},{8,0},{12,4},{16,24},{20,28},{24,16},{28,20},{1,9},{5... | collective-permute-start | bytes 294920 | tf_op jit(solution)/shard_map/ppermute | solution.py:392
  35.1 4.4 %collective-permute-start.12 = (f32[192,128]{1,0:T(8,128)S(1)}, f32[192,128]{1,0:T(8,128)S(1)}, u32[]{:S(2)}, u32[]{:S(2)}) collective-permute-start(f32[192,128]{1,0:T(8,128)S(1)} %get-tuple-element.67), channel_id=1, source_target_pairs={{0,12},{4,8},{8,4},{12,0},{16,28},{20,24},{24,20},{28,16},{1,13},{... | collective-permute-start | bytes 294920 | tf_op jit(solution)/shard_map/ppermute | solution.py:392
  40.0 9.7 %collective-permute-start.16 = (f32[200,128]{1,0:T(8,128)S(1)}, f32[200,128]{1,0:T(8,128)S(1)}, u32[]{:S(2)}, u32[]{:S(2)}) collective-permute-start(f32[200,128]{1,0:T(8,128)S(1)} %get-tuple-element.77.refs_0_), channel_id=1, source_target_pairs={{0,16},{4,20},{8,24},{12,28},{16,0},{20,4},{24,8},{28,12},{1,17},{... | collective-permute-start | bytes 307208 | tf_op jit(solution)/shard_map/ppermute | solution.py:392
  43.6 3.5 %collective-permute-start.13 = (f32[192,128]{1,0:T(8,128)S(1)}, f32[192,128]{1,0:T(8,128)S(1)}, u32[]{:S(2)}, u32[]{:S(2)}) collective-permute-start(f32[192,128]{1,0:T(8,128)S(1)} %get-tuple-element.74), channel_id=1, source_target_pairs={{0,4},{4,0},{8,12},{12,8},{16,20},{20,16},{24,28},{28,24},{1,5},{5... | collective-permute-start | bytes 294920 | tf_op jit(solution)/shard_map/ppermute | solution.py:392
  44.9 3.5 %collective-permute-start.14 = (f32[192,128]{1,0:T(8,128)S(1)}, f32[192,128]{1,0:T(8,128)S(1)}, u32[]{:S(2)}, u32[]{:S(2)}) collective-permute-start(f32[192,128]{1,0:T(8,128)S(1)} %get-tuple-element.75), channel_id=1, source_target_pairs={{0,8},{4,12},{8,0},{12,4},{16,24},{20,28},{24,16},{28,20},{1,9},{5... | collective-permute-start | bytes 294920 | tf_op jit(solution)/shard_map/ppermute | solution.py:392
  45.3 4.4 %collective-permute-start.15 = (f32[192,128]{1,0:T(8,128)S(1)}, f32[192,128]{1,0:T(8,128)S(1)}, u32[]{:S(2)}, u32[]{:S(2)}) collective-permute-start(f32[192,128]{1,0:T(8,128)S(1)} %get-tuple-element.76), channel_id=1, source_target_pairs={{0,12},{4,8},{8,4},{12,0},{16,28},{20,24},{24,20},{28,16},{1,13},{... | collective-permute-start | bytes 294920 | tf_op jit(solution)/shard_map/ppermute | solution.py:392
  49.6 26.1 %copy-start.3 = (bf16[512,512]{1,0:T(8,128)(2,1)S(1)}, bf16[512,512]{1,0:T(8,128)(2,1)}, u32[]{:S(2)}) copy-start(bf16[512,512]{1,0:T(8,128)(2,1)} %refs_9_.1) | copy-start | bytes 1572868
  49.6 26.1 %copy-start.5 = (bf16[512,512]{1,0:T(8,128)(2,1)S(1)}, bf16[512,512]{1,0:T(8,128)(2,1)}, u32[]{:S(2)}) copy-start(bf16[512,512]{1,0:T(8,128)(2,1)} %refs_10_.1) | copy-start | bytes 1572868
  51.0 24.8 %copy-start.1 = (bf16[512,512]{1,0:T(8,128)(2,1)S(1)}, bf16[512,512]{1,0:T(8,128)(2,1)}, u32[]{:S(2)}) copy-start(bf16[512,512]{1,0:T(8,128)(2,1)} %refs_8_.1) | copy-start | bytes 1572868
  51.0 13.1 %collective-permute-start.20 = (f32[2,64,384]{2,1,0:T(8,128)S(1)}, f32[2,64,384]{2,1,0:T(8,128)S(1)}, u32[]{:S(2)}, u32[]{:S(2)}) collective-permute-start(f32[2,64,384]{2,1,0:T(8,128)S(1)} %get-tuple-element.88), channel_id=1, source_target_pairs={{0,1},{1,0},{2,3},{3,2},{4,5},{5,4},{6,7},{7,6},{8,9},{9,8},{10,11... | collective-permute-start | bytes 589832 | tf_op jit(solution)/shard_map/ppermute | solution.py:392
  61.3 6.5 %collective-permute-start.21 = (f32[2,64,384]{2,1,0:T(8,128)S(1)}, f32[2,64,384]{2,1,0:T(8,128)S(1)}, u32[]{:S(2)}, u32[]{:S(2)}) collective-permute-start(f32[2,64,384]{2,1,0:T(8,128)S(1)} %get-tuple-element.89), channel_id=1, source_target_pairs={{0,2},{1,3},{2,0},{3,1},{4,6},{5,7},{6,4},{7,5},{8,10},{9,11},{10,... | collective-permute-start | bytes 589832 | tf_op jit(solution)/shard_map/ppermute | solution.py:392
  62.6 9.9 %collective-permute-start.22 = (f32[2,64,384]{2,1,0:T(8,128)S(1)}, f32[2,64,384]{2,1,0:T(8,128)S(1)}, u32[]{:S(2)}, u32[]{:S(2)}) collective-permute-start(f32[2,64,384]{2,1,0:T(8,128)S(1)} %get-tuple-element.90), channel_id=1, source_target_pairs={{0,3},{1,2},{2,1},{3,0},{4,7},{5,6},{6,5},{7,4},{8,11},{9,10},{10,... | collective-permute-start | bytes 589832 | tf_op jit(solution)/shard_map/ppermute | solution.py:392
  63.0 12.7 %collective-permute-start.17 = (f32[192,256]{1,0:T(8,128)S(1)}, f32[192,256]{1,0:T(8,128)S(1)}, u32[]{:S(2)}, u32[]{:S(2)}) collective-permute-start(f32[192,256]{1,0:T(8,128)S(1)} %get-tuple-element.84), channel_id=1, source_target_pairs={{0,4},{4,0},{8,12},{12,8},{16,20},{20,16},{24,28},{28,24},{1,5},{5... | collective-permute-start | bytes 589832 | tf_op jit(solution)/shard_map/ppermute | solution.py:392
  63.6 12.1 %collective-permute-start.18 = (f32[192,256]{1,0:T(8,128)S(1)}, f32[192,256]{1,0:T(8,128)S(1)}, u32[]{:S(2)}, u32[]{:S(2)}) collective-permute-start(f32[192,256]{1,0:T(8,128)S(1)} %get-tuple-element.85), channel_id=1, source_target_pairs={{0,8},{4,12},{8,0},{12,4},{16,24},{20,28},{24,16},{28,20},{1,9},{5... | collective-permute-start | bytes 589832 | tf_op jit(solution)/shard_map/ppermute | solution.py:392
  64.1 11.6 %collective-permute-start.19 = (f32[192,256]{1,0:T(8,128)S(1)}, f32[192,256]{1,0:T(8,128)S(1)}, u32[]{:S(2)}, u32[]{:S(2)}) collective-permute-start(f32[192,256]{1,0:T(8,128)S(1)} %get-tuple-element.86), channel_id=1, source_target_pairs={{0,12},{4,8},{8,4},{12,0},{16,28},{20,24},{24,20},{28,16},{1,13},{... | collective-permute-start | bytes 589832 | tf_op jit(solution)/shard_map/ppermute | solution.py:392
  72.5 5.9 %collective-permute-start.23 = (f32[64,384]{1,0:T(8,128)S(1)}, f32[64,384]{1,0:T(8,128)S(1)}, u32[]{:S(2)}, u32[]{:S(2)}) collective-permute-start(f32[64,384]{1,0:T(8,128)S(1)} %get-tuple-element.91), channel_id=1, source_target_pairs={{0,0},{1,4},{2,8},{3,12},{4,1},{5,5},{6,9},{7,13},{8,2},{9,6},{10,... | collective-permute-start | bytes 294920 | tf_op jit(solution)/shard_map/ppermute | solution.py:522
  74.8 8.1 %collective-permute-start.24 = (f32[64,384]{1,0:T(8,128)S(1)}, f32[64,384]{1,0:T(8,128)S(1)}, u32[]{:S(2)}, u32[]{:S(2)}) collective-permute-start(f32[64,384]{1,0:T(8,128)S(1)} %get-tuple-element.92), channel_id=1, source_target_pairs={{0,16},{1,20},{2,24},{3,28},{4,17},{5,21},{6,25},{7,29},{8,18},{9,... | collective-permute-start | bytes 294920 | tf_op jit(solution)/shard_map/ppermute | solution.py:522

commit v4 on v3

--- a/solution.py
+++ b/solution.py
@@ -167,21 +167,35 @@
     return columns(lax.axis_index("sensor") % count)
 
 
-def pick_kernel(count, *refs):
-    w_refs, proj_ref = refs[:3], refs[3]
-    out_refs, p_ref, h_ref, sems = refs[4:7], refs[7], refs[8], refs[9]
-    per = h_ref.shape[0]
+def own_heads(proj_ref, count):
+    per = proj_ref.shape[0] // count
     start = (lax.axis_index("sensor") % count) * per
-    copies = [
-        pltpu.make_async_copy(ref.at[:, own_columns(count)], out, sems.at[place])
-        for place, (ref, out) in enumerate(zip(w_refs, out_refs))
+    return jnp.concatenate([proj_ref[start + h] for h in range(per)], -1)
+
+
+def all_heads(proj_ref):
+    per = WIDE // proj_ref.shape[2]
+    return [
+        jnp.concatenate([proj_ref[g + h] for h in range(per)], -1)
+        for g in range(0, proj_ref.shape[0], per)
     ]
-    copies.append(pltpu.make_async_copy(proj_ref.at[pl.ds(start, per)], h_ref, sems.at[3]))
-    for copy in copies:
-        copy.start()
-    for copy in copies:
-        copy.wait()
-    p_ref[...] = jnp.concatenate([h_ref[h] for h in range(per)], -1)
+
+
+def local_kernel(steps, factor, count, live_ref, x_ref, wq_ref, wk_ref, wv_ref, proj_ref, *refs):
+    oq_ref, ok_ref, ov_ref, op_ref, u_ref, v_ref, f_ref = refs
+    own = own_columns(count)
+    oq_ref[...] = wq_ref[:, own]
+    ok_ref[...] = wk_ref[:, own]
+    ov_ref[...] = wv_ref[:, own]
+    op_ref[...] = own_heads(proj_ref, count)
+    mask = head_mask(proj_ref.shape[1], WIDE)
+    x = x_ref[...]
+    scaled = dot(x, wk_ref[...]) * factor
+    u_ref[...] = scaled
+    v_ref[...] = dot(x, wv_ref[...])
+    feat = feature_map(scaled, all_heads(proj_ref), mask, head_ones(mask), proj_ref.shape[2])
+    place = lax.broadcasted_iota(jnp.int32, feat.shape, 0) % (feat.shape[0] // steps)
+    f_ref[...] = jnp.where(place < live_ref[0], feat, 0.0)
 
 
 def key_kernel(steps, factor, count, *refs):
@@ -281,7 +295,7 @@
 
 
 def query_back_kernel(steps, factor, count, parts, *refs):
-    s_refs, (num_ref, den_ref, f_ref, u_ref, proj_ref, g_ref) = refs[:parts], refs[parts : parts + 6]
+    s_refs, (num_ref, den_ref, f_ref, u_ref, proj_ref, g_ref) = refs[:parts], refs[parts:]
     size = proj_ref.shape[0]
     mask = head_mask(size, LANES)
     high = f_ref.shape[0] // steps
@@ -294,21 +308,25 @@
     grad = feature_back(
         weighted, u_ref[...], [proj_ref[...]], mask, head_ones(mask)
     )
-    grad = (grad * factor).astype(BF16)
-    g_ref[...] = grad
-    for partner, ref in enumerate(refs[parts + 6 :]):
-        ref[...] = take_rows(grad, partner, count, steps).astype(F32)
+    g_ref[...] = (grad * factor).astype(BF16)
 
 
 def key_back_kernel(steps, factor, count, parts, devices, *refs):
     g_refs, (u_ref, v_ref, f_ref, proj_ref, gq_ref) = refs[:parts], refs[parts : parts + 5]
     x_all, rest = refs[parts + 5], refs[parts + 6 :]
-    back_refs, out_refs, p_ref = rest[:count], rest[count:-1], rest[-1]
+    back_refs, (keep_ref, send_ref, p_ref) = rest[:count], rest[count:]
     size = proj_ref.shape[0]
     mask = head_mask(size, LANES)
     high = f_ref.shape[0] // steps
+    total = g_refs[0][...]
+    for ref in g_refs[1:]:
+        total = total + ref[...]
+    high_g = total.shape[0]
+    for partner, ref in enumerate(back_refs):
+        ref[:high_g, :] = total
+        ref[high_g:, :] = take_rows(gq_ref[...], partner, count, steps).astype(F32)
     back, grad_v = [], []
-    for step, (matrix, row) in enumerate(load_summary(g_refs, steps, size)):
+    for step, (matrix, row) in enumerate(load_summary(back_refs[:1], steps, size)):
         part = slice(step * high, (step + 1) * high)
         matrix = split(spread(matrix, mask))
         back.append(dot3(split(v_ref[part, :]), matrix, NT) + row)
@@ -318,41 +336,57 @@
         weighted, u_ref[...], [proj_ref[...]], mask, head_ones(mask)
     )
     grad = jnp.concatenate([grad_k * factor, jnp.concatenate(grad_v, 0)], -1).astype(BF16)
-    for partner, ref in enumerate(back_refs):
-        ref[...] = take_rows(grad, partner, count, steps).astype(F32)
-    grad = jnp.concatenate([gq_ref[...], grad], -1)
-    total = dot(x_all[...], grad, TN)
+    total = dot(x_all[...], jnp.concatenate([gq_ref[...], grad], -1), TN)
     block = total.shape[0] // devices
     for place in range(devices):
-        p_ref[place % count, place // count] = total[place * block : (place + 1) * block]
-    me = lax.axis_index("step")
-    for partner, ref in enumerate(out_refs):
-        ref[...] = p_ref[(me ^ partner) % count]
-
-
-def quarter_kernel(count, *refs):
-    in_refs, out_refs = refs[:count], refs[count:]
+        p_ref[place % 2, place // 2 % 2, place // 4] = total[place * block : (place + 1) * block]
+    low = lax.axis_index("step") % 2
+    keep_ref[...] = p_ref[low]
+    send_ref[...] = p_ref[1 - low]
+
+
+def core_kernel(own_ref, got_ref, keep_ref, send_ref):
+    high = lax.axis_index("step") // 2 % 2
+    keep_ref[...] = own_ref[high] + got_ref[high]
+    send_ref[...] = own_ref[1 - high] + got_ref[1 - high]
+
+
+def half_kernel(count, own_ref, got_ref, keep_ref, send_ref):
     mine = lax.axis_index("sensor") // count
-    for place, ref in enumerate(out_refs):
-        block = (mine ^ place) % len(out_refs)
-        total = in_refs[0][block]
-        for part in in_refs[1:]:
-            total = total + part[block]
-        ref[...] = total
-
-
-def rows_kernel(count, *refs):
-    q_refs, kv_refs = refs[:count], refs[count : 2 * count]
-    wq_ref, wk_ref, wv_ref, out_ref, q_ref, k_ref, v_ref = refs[2 * count :]
+    keep_ref[...] = own_ref[mine] + got_ref[mine]
+    send_ref[...] = own_ref[1 - mine] + got_ref[1 - mine]
+
+
+def rows_kernel(steps, factor, count, *refs):
+    in_refs, (u_ref, v_ref, f_ref, proj_ref) = refs[:count], refs[count : count + 4]
+    wq_ref, wk_ref, wv_ref, out_ref, q_ref, g_ref = refs[count + 4 :]
+    size = proj_ref.shape[1]
+    high_g = g_ref.shape[0]
     me = lax.axis_index("sensor") % count
-    for partner, (q, kv) in enumerate(zip(q_refs, kv_refs)):
+    for partner, ref in enumerate(in_refs):
         own = columns((me ^ partner) % count)
-        q_ref[:, own] = q[...].astype(BF16)
-        k_ref[:, own] = kv[:, :LANES].astype(BF16)
-        v_ref[:, own] = kv[:, LANES:].astype(BF16)
+        g_ref[:, own] = ref[:high_g, :]
+        q_ref[:, own] = ref[high_g:, :].astype(BF16)
     total = dot(q_ref[...], wq_ref[...], NT)
-    total = total + dot(k_ref[...], wk_ref[...], NT)
-    out_ref[...] = (total + dot(v_ref[...], wv_ref[...], NT)).astype(BF16)
+    mask = head_mask(size, WIDE)
+    rows = f_ref.shape[0] // steps
+    back, grad_v = [], []
+    for step in range(steps):
+        part = slice(step * rows, (step + 1) * rows)
+        matrix = g_ref[step * size : (step + 1) * size, :]
+        spreads = [split(spread(m, mask)) for m in pieces(matrix)]
+        values = [split(v) for v in pieces(v_ref[part, :])]
+        feats = [split(f) for f in pieces(f_ref[part, :])]
+        row = g_ref[steps * size + step : steps * size + step + 1, :]
+        back.append(
+            jnp.concatenate([dot3(v, m, NT) for v, m in zip(values, spreads)], -1) + row
+        )
+        grad_v.append(jnp.concatenate([dot3(f, m) for f, m in zip(feats, spreads)], -1))
+    weighted = jnp.concatenate(back, 0) * f_ref[...]
+    grad_k = feature_back(weighted, u_ref[...], all_heads(proj_ref), mask, head_ones(mask))
+    total = total + dot((grad_k * factor).astype(BF16), wk_ref[...], NT)
+    grad_v = jnp.concatenate(grad_v, 0).astype(BF16)
+    out_ref[...] = (total + dot(grad_v, wv_ref[...], NT)).astype(BF16)
 
 
 def final_kernel(scale, parts, *refs):
@@ -445,13 +479,13 @@
     )
     tops, lows = gather_halves(top, low, "sensor")
     narrow_w = shape((width, LANES), BF16)
-    own_query, own_key, own_value, proj = call(
-        functools.partial(pick_kernel, count),
-        "pick_columns",
-        (narrow_w,) * 3 + (shape((size, LANES)),),
-        (w_query, w_key, w_value, feature_proj),
-        hbm=4,
-        scratch=[pltpu.VMEM((LANES // feats, size, feats), F32), pltpu.SemaphoreType.DMA((4,))],
+    own_query, own_key, own_value, proj, *local_keys = call(
+        functools.partial(local_kernel, steps, factor, count),
+        "local_keys",
+        (narrow_w,) * 3 + (shape((size, LANES)),) + (shape((rows, width)),) * 3,
+        (live_count, x, w_query, w_key, w_value, feature_proj),
+        flops=3 * product,
+        smem=1,
     )
     x_all, key, value, feat_key, summary = call(
         functools.partial(key_kernel, steps, factor, count),
@@ -493,24 +527,29 @@
         scratch=kinds(tall),
     )
     grad_summary = far_sum(grad_summary, count)
-    grad_q, *local_gq = call(
+    grad_q = call(
         functools.partial(query_back_kernel, steps, factor, count, len(summary)),
         "query_back",
-        (shape(tall.shape, BF16),) + (narrow,) * count,
+        shape(tall.shape, BF16),
         (*summary, grad_num, grad_den, feat_query, query, proj),
         flops=product,
     )
-    quad_gq = trade(local_gq, "sensor")
     tile = (width // devices, 3 * LANES)
-    back = call(
+    half = shape((2, quads, *tile))
+    *messages, own_half, send_half = call(
         functools.partial(key_back_kernel, steps, factor, count, len(grad_summary), devices),
         "key_back",
-        (shape((rows, 2 * LANES)),) * count + (shape((quads, *tile)),) * count,
-        (*grad_summary, key, value, feat_key, proj, after(grad_q, *quad_gq), x_all),
+        (shape((packed.shape[0] + rows, LANES)),) * count + (half, half),
+        (*grad_summary, key, value, feat_key, proj, grad_q, x_all),
         flops=4 * product,
-        scratch=[pltpu.VMEM((count, quads, *tile), F32)],
-    )
-    partial = trade(back[count:], "step")
+        scratch=[pltpu.VMEM((2, *half.shape), F32)],
+    )
+    quarter = (shape(half.shape[1:]),) * 2
+    own_quarter, send_quarter = call(
+        core_kernel, "core_sums", quarter, (own_half, swap(send_half, "step", 1))
+    )
+    got_quarter = swap(send_quarter, "step", 2)
+    messages = trade(after(messages, own_quarter), "sensor")
 
     def turn(a, bit):
         pairs = []
@@ -523,20 +562,25 @@
 
     if quads == 2:
         kept, away = call(
-            functools.partial(quarter_kernel, count), "quarter_sums", (shape(tile),) * 2, partial
+            functools.partial(half_kernel, count),
+            "half_sums",
+            (shape(tile),) * 2,
+            (own_quarter, got_quarter),
         )
         parts = (turn(kept, 0), turn(away, 1))
     else:
         groups = [[q + count * k for k in range(quads)] for q in range(count)]
-        blocks = lax.all_to_all(sum(partial), "sensor", 0, 0, tiled=True, axis_index_groups=groups)
+        blocks = lax.all_to_all(
+            own_quarter + got_quarter, "sensor", 0, 0, tiled=True, axis_index_groups=groups
+        )
         parts = (turn(blocks.sum(0), 0),)
     grad_in = call(
-        functools.partial(rows_kernel, count),
+        functools.partial(rows_kernel, steps, factor, count),
         "input_rows",
         shape((rows, width), BF16),
-        (*quad_gq, *trade(back[:count], "sensor"), w_query, w_key, w_value),
-        flops=3 * product,
-        scratch=[pltpu.VMEM((rows, width), BF16)] * 3,
+        (*messages, *local_keys, feature_proj, w_query, w_key, w_value),
+        flops=5 * product,
+        scratch=[pltpu.VMEM((rows, width), BF16), pltpu.VMEM((packed.shape[0], width), F32)],
     )
     scale = 1.0 / math.sqrt(rows * lax.axis_size("step") * devices)
     out = shape((width // devices, LANES))

time: 83.9 us -> 77.7 us (0.926)
  the two profiles are of different devices: /device:TPU:1 before, /device:TPU:0 now
where the time goes in v4:
time: 77.7 us; the launch traced here: 77.4 us
  starting transfers between devices  30.2 us (39%)
  waiting for transfers between devices  29.6 us (38%)
  Pallas kernels  12 us (15%)
  local copies, waits for them, and re-layouts  4.12 us (5%)
  between operations  1.49 us (2%)
    ppermute x19, waiting for transfers between devices, swap(): lax.ppermute(a, axis, [(i, i ^ bit) for i in range(lax.axis_size(axis))])  29.5 us
    ppermute x19, starting transfers between devices, swap(): lax.ppermute(a, axis, [(i, i ^ bit) for i in range(lax.axis_size(axis))])  27.5 us
    pallas_call x13, Pallas kernels, call(): pl.pallas_call(kernel, name=name, out_shape=outs, in_specs=[SMEM] * smem...  12 us
    unnamed x28, local copies, waits for them, and re-layouts  4.12 us
    ppermute x2, starting transfers between devices, turn(): return lax.ppermute(a, ('sensor', 'step'), pairs)  2.65 us
  transfers between devices with their start and end apart: 21, of which 14 were waited for; matrix products, arithmetic and copies ran while one was open for 0% of the time, Pallas kernels for 7%

profile of v4, /device:TPU:0, one launch (start us, length us, event | category | flops | bytes accessed | tf_op | source)
XLA Modules:
  0.0 77.4 jit_solution(16608319736464966408)
XLA Ops:
  0.6 0.0 copy-start.8
  1.3 1.7 %widen.1 = (f32[104,512]{1,0:T(8,128)}, f32[104,512]{1,0:T(8,128)}) custom-call(s32[1]{0:T(128)S(6)} %copy.13.live_ref, bf16[192,512]{1,0:T(8,128)(2,1)} %bitcast.3), custom_call_target="tpu_custom_call" | custom-call | bytes 622596 | tf_op jit(solution)/shard_map/widen/pallas_call | solution.py:405
  3.0 3.0 %collective-permute-start = (f32[104,512]{1,0:T(8,128)}, f32[104,512]{1,0:T(8,128)S(1)}, u32[]{:S(2)}, u32[]{:S(2)}) collective-permute-start(f32[104,512]{1,0:T(8,128)} %get-tuple-element.51.refs_0_), channel_id=1, source_target_pairs={{0,4},{4,0},{8,12},{12,8},{16,20},{20,16},{24,28},{28,24},{1,5},{5... | collective-permute-start | bytes 638984 | tf_op jit(solution)/shard_map/ppermute | solution.py:426
  6.1 1.6 %collective-permute-start.4 = (f32[104,512]{1,0:T(8,128)}, f32[104,512]{1,0:T(8,128)S(1)}, u32[]{:S(2)}, u32[]{:S(2)}) collective-permute-start(f32[104,512]{1,0:T(8,128)} %get-tuple-element.52.refs_4_), channel_id=1, source_target_pairs={{0,8},{4,12},{8,0},{12,4},{16,24},{20,28},{24,16},{28,20},{1,9},{5... | collective-permute-start | bytes 638984 | tf_op jit(solution)/shard_map/ppermute | solution.py:426
  7.6 0.4 collective-permute-start.1
  8.1 0.1 collective-permute-start.3
  8.2 4.2 %collective-permute-done.refs_1_ = f32[104,512]{1,0:T(8,128)S(1)} collective-permute-done((f32[104,512]{1,0:T(8,128)}, f32[104,512]{1,0:T(8,128)S(1)}, u32[]{:S(2)}, u32[]{:S(2)}) %collective-permute-start) | collective-permute-done | bytes 213024 | tf_op jit(solution)/shard_map/ppermute | solution.py:426
  12.4 2.1 %collective-permute-start.2 = (f32[104,512]{1,0:T(8,128)S(1)}, f32[104,512]{1,0:T(8,128)S(1)}, u32[]{:S(2)}, u32[]{:S(2)}) collective-permute-start(f32[104,512]{1,0:T(8,128)S(1)} %collective-permute-done.refs_1_), channel_id=1, source_target_pairs={{0,8},{4,12},{8,0},{12,4},{16,24},{20,28},{24,16},{28,20},{1,9},{5... | collective-permute-start | bytes 638984 | tf_op jit(solution)/shard_map/ppermute | solution.py:426
  14.5 0.0 collective-permute-done.4.refs_6_
  14.5 1.5 %collective-permute-start.5 = (f32[104,512]{1,0:T(8,128)S(1)}, f32[104,512]{1,0:T(8,128)S(1)}, u32[]{:S(2)}, u32[]{:S(2)}) collective-permute-start(f32[104,512]{1,0:T(8,128)S(1)} %collective-permute-done.4.refs_6_), channel_id=1, source_target_pairs={{0,4},{4,0},{8,12},{12,8},{16,20},{20,16},{24,28},{28,24},{1,5},{5... | collective-permute-start | bytes 638984 | tf_op jit(solution)/shard_map/ppermute | solution.py:426
  16.0 0.0 copy-done.8
  16.0 1.0 %copy-done = bf16[512,512]{1,0:T(8,128)(2,1)S(1)} copy-done((bf16[512,512]{1,0:T(8,128)(2,1)S(1)}, bf16[512,512]{1,0:T(8,128)(2,1)}, u32[]{:S(2)}) %copy-start) | copy-done | bytes 524312
  17.0 1.0 %copy-done.2 = bf16[512,512]{1,0:T(8,128)(2,1)S(1)} copy-done((bf16[512,512]{1,0:T(8,128)(2,1)S(1)}, bf16[512,512]{1,0:T(8,128)(2,1)}, u32[]{:S(2)}) %copy-start.2) | copy-done | bytes 524312
  18.1 1.0 %copy-done.4 = bf16[512,512]{1,0:T(8,128)(2,1)S(1)} copy-done((bf16[512,512]{1,0:T(8,128)(2,1)S(1)}, bf16[512,512]{1,0:T(8,128)(2,1)}, u32[]{:S(2)}) %copy-start.4) | copy-done | bytes 524312
  19.1 0.9 %copy-done.6 = f32[8,64,64]{2,1,0:T(8,128)S(1)} copy-done((f32[8,64,64]{2,1,0:T(8,128)S(1)}, f32[8,64,64]{2,1,0:T(8,128)}, u32[]{:S(2)}) %copy-start.6) | copy-done | bytes 131096
  20.1 0.7 local_keys.1
  20.8 0.0 collective-permute-done.1.refs_2_
  20.8 0.0 collective-permute-done.3.refs_5_
  20.8 1.3 %collective-permute-done.2.refs_3_ = f32[104,512]{1,0:T(8,128)S(1)} collective-permute-done((f32[104,512]{1,0:T(8,128)S(1)}, f32[104,512]{1,0:T(8,128)S(1)}, u32[]{:S(2)}, u32[]{:S(2)}) %collective-permute-start.2) | collective-permute-done | bytes 213024 | tf_op jit(solution)/shard_map/ppermute | solution.py:426
  22.1 0.0 collective-permute-done.5.refs_7_
  22.1 0.0 copy-done.11
  22.1 0.0 copy-done.12
  22.1 0.0 copy-start.9
  22.1 0.0 copy-start.13
  22.2 1.2 %keys.1 = (bf16[768,512]{1,0:T(8,128)(2,1)S(1)}, f32[768,128]{1,0:T(8,128)S(1)}, f32[768,128]{1,0:T(8,128)S(1)}, f32[768,128]{1,0:T(8,128)S(1)}, f32[200,128]{1,0:T(8,128)S(1)}) custom-call(f32[104,512]{1,0:T(8,128)S(1)} %copy-done.11, f32[104,512]{1,0:T(8,128)S(1)} %collective-permute-done.refs_1_, f32[104,512]{1,0:T(8,128)S(1)} %collective-permute-done.1.refs_2_, ...), custom_call_target="tpu_custom_call" | custom-call | flops 301989888 | bytes 4067328 | tf_op jit(solution)/shard_map/keys/pallas_call | solution.py:405
  23.4 2.7 %collective-permute-start.6 = (f32[200,128]{1,0:T(8,128)S(1)}, f32[200,128]{1,0:T(8,128)S(1)}, u32[]{:S(2)}, u32[]{:S(2)}) collective-permute-start(f32[200,128]{1,0:T(8,128)S(1)} %get-tuple-element.56.refs_0_), channel_id=1, source_target_pairs={{0,16},{4,20},{8,24},{12,28},{16,0},{20,4},{24,8},{28,12},{1,17},{... | collective-permute-start | bytes 307208 | tf_op jit(solution)/shard_map/ppermute | solution.py:426
  26.1 1.1 %queries.1 = (f32[768,128]{1,0:T(8,128)S(1)}, f32[768,128]{1,0:T(8,128)S(1)}, f32[192,256]{1,0:T(8,128)S(1)}) custom-call(s32[1]{0:T(128)S(6)} %copy.13.live_ref, bf16[768,512]{1,0:T(8,128)(2,1)S(1)} %get-tuple-element.57.x_ref.refs_7_, bf16[192,512]{1,0:T(8,128)(2,1)S(1)} %bitcast.5, bf16[512,128]{1,0:T(8,128)(2,1)S(1)} %get-tuple-element.58.wq_ref, ...), custom_call_target="tpu_custom_call" | custom-call | flops 201326592 | bytes 2392068 | tf_op jit(solution)/shard_map/queries/pallas_call | solution.py:405
  27.2 1.9 %collective-permute-done.6.refs_1_ = f32[200,128]{1,0:T(8,128)S(1)} collective-permute-done((f32[200,128]{1,0:T(8,128)S(1)}, f32[200,128]{1,0:T(8,128)S(1)}, u32[]{:S(2)}, u32[]{:S(2)}) %collective-permute-start.6) | collective-permute-done | bytes 102432 | tf_op jit(solution)/shard_map/ppermute | solution.py:426
  29.1 0.4 attend.1
  29.5 1.7 %collective-permute-start.7 = (f32[192,128]{1,0:T(8,128)S(1)}, f32[192,128]{1,0:T(8,128)S(1)}, u32[]{:S(2)}, u32[]{:S(2)}) collective-permute-start(f32[192,128]{1,0:T(8,128)S(1)} %get-tuple-element.61), channel_id=1, source_target_pairs={{0,4},{4,0},{8,12},{12,8},{16,20},{20,16},{24,28},{28,24},{1,5},{5... | collective-permute-start | bytes 294920 | tf_op jit(solution)/shard_map/ppermute | solution.py:426
  31.2 0.6 collective-permute-start.8
  31.8 1.2 %collective-permute-start.9 = (f32[192,128]{1,0:T(8,128)S(1)}, f32[192,128]{1,0:T(8,128)S(1)}, u32[]{:S(2)}, u32[]{:S(2)}) collective-permute-start(f32[192,128]{1,0:T(8,128)S(1)} %get-tuple-element.63), channel_id=1, source_target_pairs={{0,12},{4,8},{8,4},{12,0},{16,28},{20,24},{24,20},{28,16},{1,13},{... | collective-permute-start | bytes 294920 | tf_op jit(solution)/shard_map/ppermute | solution.py:426
  33.1 1.6 %collective-permute-done.7.refs_1_ = f32[192,128]{1,0:T(8,128)S(1)} collective-permute-done((f32[192,128]{1,0:T(8,128)S(1)}, f32[192,128]{1,0:T(8,128)S(1)}, u32[]{:S(2)}, u32[]{:S(2)}) %collective-permute-start.7) | collective-permute-done | bytes 98336 | tf_op jit(solution)/shard_map/ppermute | solution.py:426
  34.7 1.2 %collective-permute-done.8.refs_2_ = f32[192,128]{1,0:T(8,128)S(1)} collective-permute-done((f32[192,128]{1,0:T(8,128)S(1)}, f32[192,128]{1,0:T(8,128)S(1)}, u32[]{:S(2)}, u32[]{:S(2)}) %collective-permute-start.8) | collective-permute-done | bytes 98336 | tf_op jit(solution)/shard_map/ppermute | solution.py:426
  35.8 1.6 %collective-permute-done.9.refs_3_ = f32[192,128]{1,0:T(8,128)S(1)} collective-permute-done((f32[192,128]{1,0:T(8,128)S(1)}, f32[192,128]{1,0:T(8,128)S(1)}, u32[]{:S(2)}, u32[]{:S(2)}) %collective-permute-start.9) | collective-permute-done | bytes 98336 | tf_op jit(solution)/shard_map/ppermute | solution.py:426
  37.4 0.7 feed_forward.1
  38.2 1.6 %collective-permute-start.10 = (f32[192,128]{1,0:T(8,128)S(1)}, f32[192,128]{1,0:T(8,128)S(1)}, u32[]{:S(2)}, u32[]{:S(2)}) collective-permute-start(f32[192,128]{1,0:T(8,128)S(1)} %get-tuple-element.66), channel_id=1, source_target_pairs={{0,4},{4,0},{8,12},{12,8},{16,20},{20,16},{24,28},{28,24},{1,5},{5... | collective-permute-start | bytes 294920 | tf_op jit(solution)/shard_map/ppermute | solution.py:426
  39.7 0.3 collective-permute-start.11
  40.0 1.7 %collective-permute-start.12 = (f32[192,128]{1,0:T(8,128)S(1)}, f32[192,128]{1,0:T(8,128)S(1)}, u32[]{:S(2)}, u32[]{:S(2)}) collective-permute-start(f32[192,128]{1,0:T(8,128)S(1)} %get-tuple-element.68), channel_id=1, source_target_pairs={{0,12},{4,8},{8,4},{12,0},{16,28},{20,24},{24,20},{28,16},{1,13},{... | collective-permute-start | bytes 294920 | tf_op jit(solution)/shard_map/ppermute | solution.py:426
  41.7 1.1 %collective-permute-done.10.refs_1_ = f32[192,128]{1,0:T(8,128)S(1)} collective-permute-done((f32[192,128]{1,0:T(8,128)S(1)}, f32[192,128]{1,0:T(8,128)S(1)}, u32[]{:S(2)}, u32[]{:S(2)}) %collective-permute-start.10) | collective-permute-done | bytes 98336 | tf_op jit(solution)/shard_map/ppermute | solution.py:426
  42.8 1.5 %collective-permute-done.11.refs_2_ = f32[192,128]{1,0:T(8,128)S(1)} collective-permute-done((f32[192,128]{1,0:T(8,128)S(1)}, f32[192,128]{1,0:T(8,128)S(1)}, u32[]{:S(2)}, u32[]{:S(2)}) %collective-permute-start.11) | collective-permute-done | bytes 98336 | tf_op jit(solution)/shard_map/ppermute | solution.py:426
  44.4 1.2 %collective-permute-done.12.refs_3_ = f32[192,128]{1,0:T(8,128)S(1)} collective-permute-done((f32[192,128]{1,0:T(8,128)S(1)}, f32[192,128]{1,0:T(8,128)S(1)}, u32[]{:S(2)}, u32[]{:S(2)}) %collective-permute-start.12) | collective-permute-done | bytes 98336 | tf_op jit(solution)/shard_map/ppermute | solution.py:426
  45.5 0.5 grad_summary.1
  46.0 3.9 %collective-permute-start.13 = (f32[200,128]{1,0:T(8,128)S(1)}, f32[200,128]{1,0:T(8,128)S(1)}, u32[]{:S(2)}, u32[]{:S(2)}) collective-permute-start(f32[200,128]{1,0:T(8,128)S(1)} %get-tuple-element.71.refs_0_), channel_id=1, source_target_pairs={{0,16},{4,20},{8,24},{12,28},{16,0},{20,4},{24,8},{28,12},{1,17},{... | collective-permute-start | bytes 307208 | tf_op jit(solution)/shard_map/ppermute | solution.py:426
  49.8 0.7 query_back.1.refs_6_
  50.6 3.0 %collective-permute-done.13.refs_1_ = f32[200,128]{1,0:T(8,128)S(1)} collective-permute-done((f32[200,128]{1,0:T(8,128)S(1)}, f32[200,128]{1,0:T(8,128)S(1)}, u32[]{:S(2)}, u32[]{:S(2)}) %collective-permute-start.13) | collective-permute-done | bytes 102432 | tf_op jit(solution)/shard_map/ppermute | solution.py:426
  53.6 1.4 %key_back.1 = (f32[392,128]{1,0:T(8,128)S(1)}, f32[392,128]{1,0:T(8,128)S(1)}, f32[392,128]{1,0:T(8,128)S(1)}, f32[392,128]{1,0:T(8,128)S(1)}, f32[2,2,64,384]{3...) custom-call(f32[200,128]{1,0:T(8,128)S(1)} %get-tuple-element.71.refs_0_, f32[200,128]{1,0:T(8,128)S(1)} %collective-permute-done.13.refs_1_, ...), custom_call_target="tpu_custom_call" | custom-call | flops 402653184 | bytes 3989504 | tf_op jit(solution)/shard_map/key_back/pallas_call | solution.py:405
  55.0 0.1 collective-permute-start.14
  55.0 1.7 %collective-permute-done.14.got_ref = f32[2,2,64,384]{3,2,1,0:T(8,128)S(1)} collective-permute-done((f32[2,2,64,384]{3,2,1,0:T(8,128)S(1)}, f32[2,2,64,384]{3,2,1,0:T(8,128)S(1)}, u32[]{:S(2)}, u32[]{:S(2)}) %collective-permute-start.14) | collective-permute-done | bytes 393248 | tf_op jit(solution)/shard_map/ppermute | solution.py:426
  56.8 1.6 %collective-permute-start.18 = (f32[2,64,384]{2,1,0:T(8,128)S(1)}, f32[2,64,384]{2,1,0:T(8,128)S(1)}, u32[]{:S(2)}, u32[]{:S(2)}) collective-permute-start(f32[2,64,384]{2,1,0:T(8,128)S(1)} %get-tuple-element.92), channel_id=1, source_target_pairs={{0,2},{1,3},{2,0},{3,1},{4,6},{5,7},{6,4},{7,5},{8,10},{9,11},{10,... | collective-permute-start | bytes 589832 | tf_op jit(solution)/shard_map/ppermute | solution.py:426
  58.4 1.4 %collective-permute-start.15 = (f32[392,128]{1,0:T(8,128)S(1)}, f32[392,128]{1,0:T(8,128)S(1)}, u32[]{:S(2)}, u32[]{:S(2)}) collective-permute-start(f32[392,128]{1,0:T(8,128)S(1)} %get-tuple-element.86), channel_id=1, source_target_pairs={{0,4},{4,0},{8,12},{12,8},{16,20},{20,16},{24,28},{28,24},{1,5},{5... | collective-permute-start | bytes 602120 | tf_op jit(solution)/shard_map/ppermute | solution.py:426
  59.8 0.0 collective-permute-start.16
  59.8 2.1 %collective-permute-start.17 = (f32[392,128]{1,0:T(8,128)S(1)}, f32[392,128]{1,0:T(8,128)S(1)}, u32[]{:S(2)}, u32[]{:S(2)}) collective-permute-start(f32[392,128]{1,0:T(8,128)S(1)} %get-tuple-element.88), channel_id=1, source_target_pairs={{0,12},{4,8},{8,4},{12,0},{16,28},{20,24},{24,20},{28,16},{1,13},{... | collective-permute-start | bytes 602120 | tf_op jit(solution)/shard_map/ppermute | solution.py:426
  61.8 2.0 %collective-permute-done.18.got_ref = f32[2,64,384]{2,1,0:T(8,128)S(1)} collective-permute-done((f32[2,64,384]{2,1,0:T(8,128)S(1)}, f32[2,64,384]{2,1,0:T(8,128)S(1)}, u32[]{:S(2)}, u32[]{:S(2)}) %collective-permute-start.18) | collective-permute-done | bytes 196640 | tf_op jit(solution)/shard_map/ppermute | solution.py:426
  63.8 0.7 collective-permute-start.19
  64.5 2.0 %collective-permute-start.20 = (f32[64,384]{1,0:T(8,128)S(1)}, f32[64,384]{1,0:T(8,128)S(1)}, u32[]{:S(2)}, u32[]{:S(2)}) collective-permute-start(f32[64,384]{1,0:T(8,128)S(1)} %get-tuple-element.94), channel_id=1, source_target_pairs={{0,16},{1,20},{2,24},{3,28},{4,17},{5,21},{6,25},{7,29},{8,18},{9,... | collective-permute-start | bytes 294920 | tf_op jit(solution)/shard_map/ppermute | solution.py:561
  66.5 0.0 collective-permute-done.15.refs_1_
  66.5 1.2 %collective-permute-done.16.refs_2_ = f32[392,128]{1,0:T(8,128)S(1)} collective-permute-done((f32[392,128]{1,0:T(8,128)S(1)}, f32[392,128]{1,0:T(8,128)S(1)}, u32[]{:S(2)}, u32[]{:S(2)}) %collective-permute-start.16) | collective-permute-done | bytes 200736 | tf_op jit(solution)/shard_map/ppermute | solution.py:426
  67.7 6.2 %collective-permute-done.17.refs_3_ = f32[392,128]{1,0:T(8,128)S(1)} collective-permute-done((f32[392,128]{1,0:T(8,128)S(1)}, f32[392,128]{1,0:T(8,128)S(1)}, u32[]{:S(2)}, u32[]{:S(2)}) %collective-permute-start.17) | collective-permute-done | bytes 200736 | tf_op jit(solution)/shard_map/ppermute | solution.py:426
  73.9 0.0 copy-done.5
  73.9 2.8 %input_rows.1 = bf16[192,512]{1,0:T(8,128)(2,1)} custom-call(f32[392,128]{1,0:T(8,128)S(1)} %get-tuple-element.85.refs_0_, f32[392,128]{1,0:T(8,128)S(1)} %collective-permute-done.15.refs_1_, f32[392,128]{1,0:T(8,128)S(1)} %collective-permute-done.16.refs_2_, f32[392,128]{1,0:T(8,128)S(1)} %collective-permute-done.17.refs_3_, ...), custom_call_target="tpu_custom_call" | custom-call | flops 503316480 | bytes 3883008 | tf_op jit(solution)/shard_map/input_rows/pallas_call | solution.py:405
  76.7 0.0 collective-permute-done.19.refs_0_
  76.7 0.0 collective-permute-done.20.refs_1_
  76.7 0.7 weight_sums.1
  (19 shorter events, 0.1 us)
Async XLA Ops:
  0.6 15.4 %copy-start.8 = (bf16[3,64,512]{2,1,0:T(8,128)(2,1)S(1)}, bf16[3,64,512]{2,1,0:T(8,128)(2,1)}, u32[]{:S(2)}) copy-start(bf16[3,64,512]{2,1,0:T(8,128)(2,1)} %param.9) | copy-start | bytes 589828
  3.0 9.3 %collective-permute-start = (f32[104,512]{1,0:T(8,128)}, f32[104,512]{1,0:T(8,128)S(1)}, u32[]{:S(2)}, u32[]{:S(2)}) collective-permute-start(f32[104,512]{1,0:T(8,128)} %get-tuple-element.51.refs_0_), channel_id=1, source_target_pairs={{0,4},{4,0},{8,12},{12,8},{16,20},{20,16},{24,28},{28,24},{1,5},{5... | collective-permute-start | bytes 638984 | tf_op jit(solution)/shard_map/ppermute | solution.py:426
  6.1 8.4 %collective-permute-start.4 = (f32[104,512]{1,0:T(8,128)}, f32[104,512]{1,0:T(8,128)S(1)}, u32[]{:S(2)}, u32[]{:S(2)}) collective-permute-start(f32[104,512]{1,0:T(8,128)} %get-tuple-element.52.refs_4_), channel_id=1, source_target_pairs={{0,8},{4,12},{8,0},{12,4},{16,24},{20,28},{24,16},{28,20},{1,9},{5... | collective-permute-start | bytes 638984 | tf_op jit(solution)/shard_map/ppermute | solution.py:426
  7.6 13.1 %collective-permute-start.1 = (f32[104,512]{1,0:T(8,128)}, f32[104,512]{1,0:T(8,128)S(1)}, u32[]{:S(2)}, u32[]{:S(2)}) collective-permute-start(f32[104,512]{1,0:T(8,128)} %get-tuple-element.51.refs_0_), channel_id=1, source_target_pairs={{0,8},{4,12},{8,0},{12,4},{16,24},{20,28},{24,16},{28,20},{1,9},{5... | collective-permute-start | bytes 638984 | tf_op jit(solution)/shard_map/ppermute | solution.py:426
  8.1 12.7 %collective-permute-start.3 = (f32[104,512]{1,0:T(8,128)}, f32[104,512]{1,0:T(8,128)S(1)}, u32[]{:S(2)}, u32[]{:S(2)}) collective-permute-start(f32[104,512]{1,0:T(8,128)} %get-tuple-element.52.refs_4_), channel_id=1, source_target_pairs={{0,4},{4,0},{8,12},{12,8},{16,20},{20,16},{24,28},{28,24},{1,5},{5... | collective-permute-start | bytes 638984 | tf_op jit(solution)/shard_map/ppermute | solution.py:426
  12.4 9.8 %collective-permute-start.2 = (f32[104,512]{1,0:T(8,128)S(1)}, f32[104,512]{1,0:T(8,128)S(1)}, u32[]{:S(2)}, u32[]{:S(2)}) collective-permute-start(f32[104,512]{1,0:T(8,128)S(1)} %collective-permute-done.refs_1_), channel_id=1, source_target_pairs={{0,8},{4,12},{8,0},{12,4},{16,24},{20,28},{24,16},{28,20},{1,9},{5... | collective-permute-start | bytes 638984 | tf_op jit(solution)/shard_map/ppermute | solution.py:426
  14.5 7.6 %collective-permute-start.5 = (f32[104,512]{1,0:T(8,128)S(1)}, f32[104,512]{1,0:T(8,128)S(1)}, u32[]{:S(2)}, u32[]{:S(2)}) collective-permute-start(f32[104,512]{1,0:T(8,128)S(1)} %collective-permute-done.4.refs_6_), channel_id=1, source_target_pairs={{0,4},{4,0},{8,12},{12,8},{16,20},{20,16},{24,28},{28,24},{1,5},{5... | collective-permute-start | bytes 638984 | tf_op jit(solution)/shard_map/ppermute | solution.py:426
  16.0 1.0 %copy-start = (bf16[512,512]{1,0:T(8,128)(2,1)S(1)}, bf16[512,512]{1,0:T(8,128)(2,1)}, u32[]{:S(2)}) copy-start(bf16[512,512]{1,0:T(8,128)(2,1)} %refs_8_.1) | copy-start | bytes 1572868
  17.0 1.0 %copy-start.2 = (bf16[512,512]{1,0:T(8,128)(2,1)S(1)}, bf16[512,512]{1,0:T(8,128)(2,1)}, u32[]{:S(2)}) copy-start(bf16[512,512]{1,0:T(8,128)(2,1)} %refs_9_.1) | copy-start | bytes 1572868
  18.1 1.0 %copy-start.4 = (bf16[512,512]{1,0:T(8,128)(2,1)S(1)}, bf16[512,512]{1,0:T(8,128)(2,1)}, u32[]{:S(2)}) copy-start(bf16[512,512]{1,0:T(8,128)(2,1)} %refs_10_.1) | copy-start | bytes 1572868
  19.1 0.9 %copy-start.6 = (f32[8,64,64]{2,1,0:T(8,128)S(1)}, f32[8,64,64]{2,1,0:T(8,128)}, u32[]{:S(2)}) copy-start(f32[8,64,64]{2,1,0:T(8,128)} %refs_7_.1) | copy-start | bytes 393220
  20.1 2.0 %copy-start.11 = (f32[104,512]{1,0:T(8,128)S(1)}, f32[104,512]{1,0:T(8,128)}, u32[]{:S(2)}) copy-start(f32[104,512]{1,0:T(8,128)} %get-tuple-element.51.refs_0_) | copy-start | bytes 638980
  20.1 2.0 %copy-start.12 = (f32[104,512]{1,0:T(8,128)S(1)}, f32[104,512]{1,0:T(8,128)}, u32[]{:S(2)}) copy-start(f32[104,512]{1,0:T(8,128)} %get-tuple-element.52.refs_4_) | copy-start | bytes 638980
  22.1 3.9 %copy-start.9 = (bf16[256,512]{1,0:T(8,128)(2,1)S(1)}, bf16[256,512]{1,0:T(8,128)(2,1)}, u32[]{:S(2)}) copy-start(bf16[256,512]{1,0:T(8,128)(2,1)} %wd_ref.1) | copy-start | bytes 786436
  22.1 3.9 %copy-start.13 = (bf16[3,64,512]{2,1,0:T(8,128)(2,1)S(1)}, bf16[3,64,512]{2,1,0:T(8,128)(2,1)}, u32[]{:S(2)}) copy-start(bf16[3,64,512]{2,1,0:T(8,128)(2,1)} %param.10) | copy-start | bytes 589828
  23.4 5.6 %collective-permute-start.6 = (f32[200,128]{1,0:T(8,128)S(1)}, f32[200,128]{1,0:T(8,128)S(1)}, u32[]{:S(2)}, u32[]{:S(2)}) collective-permute-start(f32[200,128]{1,0:T(8,128)S(1)} %get-tuple-element.56.refs_0_), channel_id=1, source_target_pairs={{0,16},{4,20},{8,24},{12,28},{16,0},{20,4},{24,8},{28,12},{1,17},{... | collective-permute-start | bytes 307208 | tf_op jit(solution)/shard_map/ppermute | solution.py:426
  29.0 8.4 %copy-start.10 = (bf16[512,256]{1,0:T(8,128)(2,1)S(1)}, bf16[512,256]{1,0:T(8,128)(2,1)}, u32[]{:S(2)}) copy-start(bf16[512,256]{1,0:T(8,128)(2,1)} %refs_5_.1) | copy-start | bytes 786436
  29.5 5.2 %collective-permute-start.7 = (f32[192,128]{1,0:T(8,128)S(1)}, f32[192,128]{1,0:T(8,128)S(1)}, u32[]{:S(2)}, u32[]{:S(2)}) collective-permute-start(f32[192,128]{1,0:T(8,128)S(1)} %get-tuple-element.61), channel_id=1, source_target_pairs={{0,4},{4,0},{8,12},{12,8},{16,20},{20,16},{24,28},{28,24},{1,5},{5... | collective-permute-start | bytes 294920 | tf_op jit(solution)/shard_map/ppermute | solution.py:426
  31.2 4.6 %collective-permute-start.8 = (f32[192,128]{1,0:T(8,128)S(1)}, f32[192,128]{1,0:T(8,128)S(1)}, u32[]{:S(2)}, u32[]{:S(2)}) collective-permute-start(f32[192,128]{1,0:T(8,128)S(1)} %get-tuple-element.62), channel_id=1, source_target_pairs={{0,8},{4,12},{8,0},{12,4},{16,24},{20,28},{24,16},{28,20},{1,9},{5... | collective-permute-start | bytes 294920 | tf_op jit(solution)/shard_map/ppermute | solution.py:426
  31.8 5.6 %collective-permute-start.9 = (f32[192,128]{1,0:T(8,128)S(1)}, f32[192,128]{1,0:T(8,128)S(1)}, u32[]{:S(2)}, u32[]{:S(2)}) collective-permute-start(f32[192,128]{1,0:T(8,128)S(1)} %get-tuple-element.63), channel_id=1, source_target_pairs={{0,12},{4,8},{8,4},{12,0},{16,28},{20,24},{24,20},{28,16},{1,13},{... | collective-permute-start | bytes 294920 | tf_op jit(solution)/shard_map/ppermute | solution.py:426
  38.2 4.7 %collective-permute-start.10 = (f32[192,128]{1,0:T(8,128)S(1)}, f32[192,128]{1,0:T(8,128)S(1)}, u32[]{:S(2)}, u32[]{:S(2)}) collective-permute-start(f32[192,128]{1,0:T(8,128)S(1)} %get-tuple-element.66), channel_id=1, source_target_pairs={{0,4},{4,0},{8,12},{12,8},{16,20},{20,16},{24,28},{28,24},{1,5},{5... | collective-permute-start | bytes 294920 | tf_op jit(solution)/shard_map/ppermute | solution.py:426
  39.7 4.6 %collective-permute-start.11 = (f32[192,128]{1,0:T(8,128)S(1)}, f32[192,128]{1,0:T(8,128)S(1)}, u32[]{:S(2)}, u32[]{:S(2)}) collective-permute-start(f32[192,128]{1,0:T(8,128)S(1)} %get-tuple-element.67), channel_id=1, source_target_pairs={{0,8},{4,12},{8,0},{12,4},{16,24},{20,28},{24,16},{28,20},{1,9},{5... | collective-permute-start | bytes 294920 | tf_op jit(solution)/shard_map/ppermute | solution.py:426
  40.0 5.5 %collective-permute-start.12 = (f32[192,128]{1,0:T(8,128)S(1)}, f32[192,128]{1,0:T(8,128)S(1)}, u32[]{:S(2)}, u32[]{:S(2)}) collective-permute-start(f32[192,128]{1,0:T(8,128)S(1)} %get-tuple-element.68), channel_id=1, source_target_pairs={{0,12},{4,8},{8,4},{12,0},{16,28},{20,24},{24,20},{28,16},{1,13},{... | collective-permute-start | bytes 294920 | tf_op jit(solution)/shard_map/ppermute | solution.py:426
  46.0 7.6 %collective-permute-start.13 = (f32[200,128]{1,0:T(8,128)S(1)}, f32[200,128]{1,0:T(8,128)S(1)}, u32[]{:S(2)}, u32[]{:S(2)}) collective-permute-start(f32[200,128]{1,0:T(8,128)S(1)} %get-tuple-element.71.refs_0_), channel_id=1, source_target_pairs={{0,16},{4,20},{8,24},{12,28},{16,0},{20,4},{24,8},{28,12},{1,17},{... | collective-permute-start | bytes 307208 | tf_op jit(solution)/shard_map/ppermute | solution.py:426
  53.6 20.3 %copy-start.5 = (bf16[512,512]{1,0:T(8,128)(2,1)S(1)}, bf16[512,512]{1,0:T(8,128)(2,1)}, u32[]{:S(2)}) copy-start(bf16[512,512]{1,0:T(8,128)(2,1)} %refs_10_.1) | copy-start | bytes 1572868
  53.6 20.3 %copy-start.7 = (f32[8,64,64]{2,1,0:T(8,128)S(1)}, f32[8,64,64]{2,1,0:T(8,128)}, u32[]{:S(2)}) copy-start(f32[8,64,64]{2,1,0:T(8,128)} %refs_7_.1) | copy-start | bytes 393220
  55.0 1.8 %collective-permute-start.14 = (f32[2,2,64,384]{3,2,1,0:T(8,128)S(1)}, f32[2,2,64,384]{3,2,1,0:T(8,128)S(1)}, u32[]{:S(2)}, u32[]{:S(2)}) collective-permute-start(f32[2,2,64,384]{3,2,1,0:T(8,128)S(1)} %get-tuple-element.83), channel_id=1, source_target_pairs={{0,1},{1,0},{2,3},{3,2},{4,5},{5,4},{6,7},{7,6},{8,9},{9,8},{10,11... | collective-permute-start | bytes 1179656 | tf_op jit(solution)/shard_map/ppermute | solution.py:426
  56.7 17.1 %copy-start.1 = (bf16[512,512]{1,0:T(8,128)(2,1)S(1)}, bf16[512,512]{1,0:T(8,128)(2,1)}, u32[]{:S(2)}) copy-start(bf16[512,512]{1,0:T(8,128)(2,1)} %refs_8_.1) | copy-start | bytes 1572868
  56.8 17.1 %copy-start.3 = (bf16[512,512]{1,0:T(8,128)(2,1)S(1)}, bf16[512,512]{1,0:T(8,128)(2,1)}, u32[]{:S(2)}) copy-start(bf16[512,512]{1,0:T(8,128)(2,1)} %refs_9_.1) | copy-start | bytes 1572868
  56.8 7.0 %collective-permute-start.18 = (f32[2,64,384]{2,1,0:T(8,128)S(1)}, f32[2,64,384]{2,1,0:T(8,128)S(1)}, u32[]{:S(2)}, u32[]{:S(2)}) collective-permute-start(f32[2,64,384]{2,1,0:T(8,128)S(1)} %get-tuple-element.92), channel_id=1, source_target_pairs={{0,2},{1,3},{2,0},{3,1},{4,6},{5,7},{6,4},{7,5},{8,10},{9,11},{10,... | collective-permute-start | bytes 589832 | tf_op jit(solution)/shard_map/ppermute | solution.py:426
  58.4 8.1 %collective-permute-start.15 = (f32[392,128]{1,0:T(8,128)S(1)}, f32[392,128]{1,0:T(8,128)S(1)}, u32[]{:S(2)}, u32[]{:S(2)}) collective-permute-start(f32[392,128]{1,0:T(8,128)S(1)} %get-tuple-element.86), channel_id=1, source_target_pairs={{0,4},{4,0},{8,12},{12,8},{16,20},{20,16},{24,28},{28,24},{1,5},{5... | collective-permute-start | bytes 602120 | tf_op jit(solution)/shard_map/ppermute | solution.py:426
  59.8 7.9 %collective-permute-start.16 = (f32[392,128]{1,0:T(8,128)S(1)}, f32[392,128]{1,0:T(8,128)S(1)}, u32[]{:S(2)}, u32[]{:S(2)}) collective-permute-start(f32[392,128]{1,0:T(8,128)S(1)} %get-tuple-element.87), channel_id=1, source_target_pairs={{0,8},{4,12},{8,0},{12,4},{16,24},{20,28},{24,16},{28,20},{1,9},{5... | collective-permute-start | bytes 602120 | tf_op jit(solution)/shard_map/ppermute | solution.py:426
  59.8 14.1 %collective-permute-start.17 = (f32[392,128]{1,0:T(8,128)S(1)}, f32[392,128]{1,0:T(8,128)S(1)}, u32[]{:S(2)}, u32[]{:S(2)}) collective-permute-start(f32[392,128]{1,0:T(8,128)S(1)} %get-tuple-element.88), channel_id=1, source_target_pairs={{0,12},{4,8},{8,4},{12,0},{16,28},{20,24},{24,20},{28,16},{1,13},{... | collective-permute-start | bytes 602120 | tf_op jit(solution)/shard_map/ppermute | solution.py:426
  63.8 12.9 %collective-permute-start.19 = (f32[64,384]{1,0:T(8,128)S(1)}, f32[64,384]{1,0:T(8,128)S(1)}, u32[]{:S(2)}, u32[]{:S(2)}) collective-permute-start(f32[64,384]{1,0:T(8,128)S(1)} %get-tuple-element.93), channel_id=1, source_target_pairs={{0,0},{1,4},{2,8},{3,12},{4,1},{5,5},{6,9},{7,13},{8,2},{9,6},{10,... | collective-permute-start | bytes 294920 | tf_op jit(solution)/shard_map/ppermute | solution.py:561
  64.5 12.2 %collective-permute-start.20 = (f32[64,384]{1,0:T(8,128)S(1)}, f32[64,384]{1,0:T(8,128)S(1)}, u32[]{:S(2)}, u32[]{:S(2)}) collective-permute-start(f32[64,384]{1,0:T(8,128)S(1)} %get-tuple-element.94), channel_id=1, source_target_pairs={{0,16},{1,20},{2,24},{3,28},{4,17},{5,21},{6,25},{7,29},{8,18},{9,... | collective-permute-start | bytes 294920 | tf_op jit(solution)/shard_map/ppermute | solution.py:561

commit v5 on v4

--- a/solution.py
+++ b/solution.py
@@ -29,7 +29,20 @@
 
 
 def dot3(a, b, dims=NN):
-    return dot(a[0], b[0], dims) + (dot(a[0], b[1], dims) + dot(a[1], b[0], dims))
+    if a[0].shape[1] == LANES:
+        axis = 1 if dims == NN else 0
+        parts = [jnp.concatenate([b[0], b[1]], axis), jnp.concatenate([b[0], 0 * b[1]], axis)]
+        out = dot(jnp.concatenate(a, 1), jnp.concatenate(parts, 1 - axis), dims)
+        return out[:, :LANES] + out[:, LANES:]
+    rows = a[0].shape[0]
+    out = dot(jnp.concatenate(a, 0), b[0], dims)
+    return out[:rows] + (out[rows:] + dot(a[0], b[1], dims))
+
+
+def dot2(a, b, dims=NN):
+    rows = a[0].shape[0]
+    out = dot(jnp.concatenate(a, 0), b, dims)
+    return out[:rows] + out[rows:]
 
 
 def head_mask(size, width):
@@ -56,7 +69,9 @@
 
 def head_sums(x, ones):
     high, low = split(x)
-    return dot(high, ones) + dot(low, ones)
+    if x.shape[1] == LANES:
+        return dot(jnp.concatenate([high, low], 1), jnp.concatenate([ones, ones], 0))
+    return dot2((high, low), ones)
 
 
 def pieces(x, width=WIDE):
@@ -82,9 +97,8 @@
     out = []
     width = mask.shape[0]
     for w, u, p in zip(pieces(weighted, width), pieces(scaled, width), proj):
-        high, low = split(w)
-        back = dot3((high, low), split(spread(p, mask)), NT)
-        out.append(back - u * (dot(high, ones) + dot(low, ones)))
+        back = dot3(split(w), split(spread(p, mask)), NT)
+        out.append(back - u * head_sums(w, ones))
     return jnp.concatenate(out, -1)
 
 
@@ -109,9 +123,8 @@
 
 
 def outer_sums(a, b, size):
-    ah, al = split(a)
-    bh, bl = split(b)
-    whole = dot(ah, bh, TN) + (dot(ah, bl, TN) + dot(al, bh, TN))
+    out = dot(jnp.concatenate(split(a), 1), jnp.concatenate(split(b), 1), TN)
+    whole = out[:LANES, :LANES] + (out[:LANES, LANES:] + out[LANES:, :LANES])
     return gather_diagonal(whole, size)
 
 
@@ -151,16 +164,11 @@
     return jnp.concatenate([values[s : s + rows] for s in starts], 0)
 
 
-def widen_kernel(live_ref, x_any, top_ref, low_ref, x_ref, sem):
-    copy = pltpu.make_async_copy(x_any, x_ref, sem)
-    copy.start()
+def widen_kernel(live_ref, x_ref, top_ref, low_ref):
     half = x_ref.shape[0] // 2
-    for ref in (top_ref, low_ref):
-        tail = ref.shape[0] - half
-        ref[half:, :] = jnp.full((tail, ref.shape[1]), live_ref[0]).astype(F32)
-    copy.wait()
-    top_ref[:half, :] = x_ref[:half].astype(F32)
-    low_ref[:half, :] = x_ref[half:].astype(F32)
+    for ref, base in ((top_ref, 0), (low_ref, half)):
+        ref[:half, :] = x_ref[base : base + half].astype(F32)
+        ref[half:, :] = jnp.full((ref.shape[0] - half, ref.shape[1]), live_ref[0]).astype(F32)
 
 
 def own_columns(count):
@@ -225,6 +233,12 @@
     store_summary(s_ref, *summaries(feat, values, feat, steps, size))
 
 
+def transpose_kernel(*refs):
+    half = len(refs) // 2
+    for source, target in zip(refs[:half], refs[half:]):
+        target[...] = source[...].T
+
+
 def query_kernel(steps, factor, count, live_ref, x_ref, cot_ref, wq_ref, wd_ref, proj_ref, u_ref, f_ref, gh_ref):
     size = proj_ref.shape[0]
     mask = head_mask(size, LANES)
@@ -257,22 +271,21 @@
 
 
 def forward_kernel(count, *refs):
-    in_refs, (gh_ref, wu_ref) = refs[:count], refs[count : count + 2]
-    out_refs, scratch = refs[count + 2 : -1], refs[-1]
+    in_refs, (gh_ref, wu_ref, wt_ref) = refs[:count], refs[count : count + 3]
+    out_refs, scratch = refs[count + 3 : -1], refs[-1]
     me = lax.axis_index("sensor") % count
     for partner, ref in enumerate(in_refs):
         scratch[:, columns((me ^ partner) % count)] = ref[...]
     attended = scratch[...]
     scale = lax.rsqrt(jnp.mean(attended * attended, -1, keepdims=True) + 1e-06)
     normed = attended * scale
-    wu = wu_ref[...]
-    pre = dot(normed.astype(BF16), wu)
+    pre = dot(normed.astype(BF16), wu_ref[...])
     c = math.sqrt(2.0 / math.pi)
     square = pre * pre
     t = jnp.tanh(c * pre * (1.0 + 0.044715 * square))
     slope = 0.5 * (1.0 + t) + 0.5 * pre * (1.0 - t * t) * (c * (1.0 + 3 * 0.044715 * square))
     grad_pre = (gh_ref[...] * slope).astype(BF16)
-    grad_normed = dot(grad_pre, wu, NT)
+    grad_normed = dot(grad_pre, wt_ref[...])
     scratch[...] = (
         grad_normed - normed * jnp.mean(grad_normed * normed, -1, keepdims=True)
     ) * scale
@@ -336,7 +349,7 @@
         weighted, u_ref[...], [proj_ref[...]], mask, head_ones(mask)
     )
     grad = jnp.concatenate([grad_k * factor, jnp.concatenate(grad_v, 0)], -1).astype(BF16)
-    total = dot(x_all[...], jnp.concatenate([gq_ref[...], grad], -1), TN)
+    total = dot(x_all[...], jnp.concatenate([gq_ref[...], grad], -1))
     block = total.shape[0] // devices
     for place in range(devices):
         p_ref[place % 2, place // 2 % 2, place // 4] = total[place * block : (place + 1) * block]
@@ -345,16 +358,17 @@
     send_ref[...] = p_ref[1 - low]
 
 
-def core_kernel(own_ref, got_ref, keep_ref, send_ref):
+def core_kernel(count, own_ref, got_ref, *refs):
     high = lax.axis_index("step") // 2 % 2
-    keep_ref[...] = own_ref[high] + got_ref[high]
-    send_ref[...] = own_ref[1 - high] + got_ref[1 - high]
-
-
-def half_kernel(count, own_ref, got_ref, keep_ref, send_ref):
     mine = lax.axis_index("sensor") // count
-    keep_ref[...] = own_ref[mine] + got_ref[mine]
-    send_ref[...] = own_ref[1 - mine] + got_ref[1 - mine]
+    per = len(refs) // 2
+    for place, ref in enumerate(refs):
+        part = high ^ (place // per)
+        if per == 2:
+            block = mine ^ (place % 2)
+            ref[...] = own_ref[part, block] + got_ref[part, block]
+        else:
+            ref[...] = own_ref[part] + got_ref[part]
 
 
 def rows_kernel(steps, factor, count, *refs):
@@ -367,7 +381,7 @@
         own = columns((me ^ partner) % count)
         g_ref[:, own] = ref[:high_g, :]
         q_ref[:, own] = ref[high_g:, :].astype(BF16)
-    total = dot(q_ref[...], wq_ref[...], NT)
+    total = dot(q_ref[...], wq_ref[...])
     mask = head_mask(size, WIDE)
     rows = f_ref.shape[0] // steps
     back, grad_v = [], []
@@ -384,9 +398,9 @@
         grad_v.append(jnp.concatenate([dot3(f, m) for f, m in zip(feats, spreads)], -1))
     weighted = jnp.concatenate(back, 0) * f_ref[...]
     grad_k = feature_back(weighted, u_ref[...], all_heads(proj_ref), mask, head_ones(mask))
-    total = total + dot((grad_k * factor).astype(BF16), wk_ref[...], NT)
+    total = total + dot((grad_k * factor).astype(BF16), wk_ref[...])
     grad_v = jnp.concatenate(grad_v, 0).astype(BF16)
-    out_ref[...] = (total + dot(grad_v, wv_ref[...], NT)).astype(BF16)
+    out_ref[...] = (total + dot(grad_v, wv_ref[...])).astype(BF16)
 
 
 def final_kernel(scale, parts, *refs):
@@ -427,7 +441,8 @@
 
 
 def trade(parts, axis):
-    return [parts[0]] + [swap(a, axis, d) for d, a in enumerate(parts) if d]
+    got = {d: swap(parts[d], axis, d) for d in reversed(range(1, len(parts)))}
+    return [parts[0]] + [got[d] for d in sorted(got)]
 
 
 def gather_halves(top, low, axis):
@@ -473,9 +488,6 @@
         (shape((rows // 2 + 8, width)),) * 2,
         (live_count, x),
         smem=1,
-        hbm=1,
-        limit=60,
-        scratch=kinds(x) + [pltpu.SemaphoreType.DMA],
     )
     tops, lows = gather_halves(top, low, "sensor")
     narrow_w = shape((width, LANES), BF16)
@@ -494,6 +506,10 @@
         (*tops, *lows, own_key, own_value, proj),
         flops=3 * product,
     )
+    turned = (x_all, w_query, w_key, w_value, w_up)
+    x_turned, wq_turned, wk_turned, wv_turned, wu_turned = call(
+        transpose_kernel, "transposes", tuple(shape(a.shape[::-1], BF16) for a in turned), turned
+    )
     query, feat_query, grad_hidden = call(
         functools.partial(query_kernel, steps, factor, count),
         "queries",
@@ -514,7 +530,7 @@
         functools.partial(forward_kernel, count),
         "feed_forward",
         (narrow,) * count,
-        (*trade(local_att, "sensor"), grad_hidden, w_up),
+        (*trade(local_att, "sensor"), grad_hidden, w_up, wu_turned),
         flops=product,
         scratch=[wide],
     )
@@ -540,17 +556,10 @@
         functools.partial(key_back_kernel, steps, factor, count, len(grad_summary), devices),
         "key_back",
         (shape((packed.shape[0] + rows, LANES)),) * count + (half, half),
-        (*grad_summary, key, value, feat_key, proj, grad_q, x_all),
+        (*grad_summary, key, value, feat_key, proj, grad_q, x_turned),
         flops=4 * product,
         scratch=[pltpu.VMEM((2, *half.shape), F32)],
     )
-    quarter = (shape(half.shape[1:]),) * 2
-    own_quarter, send_quarter = call(
-        core_kernel, "core_sums", quarter, (own_half, swap(send_half, "step", 1))
-    )
-    got_quarter = swap(send_quarter, "step", 2)
-    messages = trade(after(messages, own_quarter), "sensor")
-
     def turn(a, bit):
         pairs = []
         for k in range(quads):
@@ -560,32 +569,47 @@
                     pairs.append(((k * count + q) * count + j, target * count + q))
         return lax.ppermute(a, ("sensor", "step"), pairs)
 
+    got_half = swap(send_half, "step", 1)
     if quads == 2:
-        kept, away = call(
-            functools.partial(half_kernel, count),
-            "half_sums",
-            (shape(tile),) * 2,
-            (own_quarter, got_quarter),
+        kept, away, send_kept, send_away = call(
+            functools.partial(core_kernel, count),
+            "core_sums",
+            (shape(tile),) * 4,
+            (own_half, got_half),
         )
-        parts = (turn(kept, 0), turn(away, 1))
+        ready = kept
+        away = away + swap(send_away, "step", 2)
+        kept = kept + swap(send_kept, "step", 2)
+        parts = (turn(away, 1), turn(kept, 0))
     else:
+        kept, sent = call(
+            functools.partial(core_kernel, count),
+            "core_sums",
+            (shape((quads, *tile)),) * 2,
+            (own_half, got_half),
+        )
+        ready = kept
         groups = [[q + count * k for k in range(quads)] for q in range(count)]
         blocks = lax.all_to_all(
-            own_quarter + got_quarter, "sensor", 0, 0, tiled=True, axis_index_groups=groups
+            kept + swap(sent, "step", 2), "sensor", 0, 0, tiled=True, axis_index_groups=groups
         )
         parts = (turn(blocks.sum(0), 0),)
+    messages = trade(after(messages, ready), "sensor")
+    scale = 1.0 / math.sqrt(rows * lax.axis_size("step") * devices)
+    out = shape((width // devices, LANES))
     grad_in = call(
         functools.partial(rows_kernel, steps, factor, count),
         "input_rows",
         shape((rows, width), BF16),
-        (*messages, *local_keys, feature_proj, w_query, w_key, w_value),
+        (*messages, *local_keys, feature_proj, wq_turned, wk_turned, wv_turned),
         flops=5 * product,
         scratch=[pltpu.VMEM((rows, width), BF16), pltpu.VMEM((packed.shape[0], width), F32)],
     )
-    scale = 1.0 / math.sqrt(rows * lax.axis_size("step") * devices)
-    out = shape((width // devices, LANES))
     grads = call(
-        functools.partial(final_kernel, scale, len(parts)), "weight_sums", (out,) * 3, parts
+        functools.partial(final_kernel, scale, len(parts)),
+        "weight_sums",
+        (out,) * 3,
+        (after(parts[0], grad_in), *parts[1:]),
     )
     return (grad_in.reshape(inputs.shape), *grads)
 

time: 77.7 us -> 75.4 us (0.970); the launches traced: 77.4 us -> 74.2 us
  waiting for transfers between devices: 29.6 us -> 26.5 us
  Pallas kernels: 12 us -> 9.75 us
  starting transfers between devices: 30.2 us -> 31.4 us
  local copies, waits for them, and re-layouts: 4.12 us -> 5.02 us
    ppermute x19 -> x20, waiting for transfers between devices: 29.5 us -> 26.5 us  [swap(): lax.ppermute(a, axis, [(i, i ^ bit) for i in range(lax.axis_size(axis))])]
    pallas_call x13, Pallas kernels: 12 us -> 9.75 us  [call(): pl.pallas_call(kernel, name=name, out_shape=outs, in_specs=[SMEM] * smem...]
    unnamed x28 -> x24, local copies, waits for them, and re-layouts: 4.12 us -> 5.02 us
    ppermute x19 -> x20, starting transfers between devices: 27.5 us -> 28 us  [swap(): lax.ppermute(a, axis, [(i, i ^ bit) for i in range(lax.axis_size(axis))])]
  transfers between devices with their start and end apart: 21 -> 22, of which waited for: 14 -> 13; matrix products, arithmetic and copies ran while one was open for 0% -> 0% of each run, Pallas kernels for 7% -> 7%
where the time goes in v5:
time: 75.4 us; the launch traced here: 74.2 us
  starting transfers between devices  31.4 us (42%)
  waiting for transfers between devices  26.5 us (35%)
  Pallas kernels  9.75 us (13%)
  local copies, waits for them, and re-layouts  5.02 us (7%)
  between operations  1.46 us (2%)
    ppermute x20, starting transfers between devices, swap(): lax.ppermute(a, axis, [(i, i ^ bit) for i in range(lax.axis_size(axis))])  28 us
    ppermute x20, waiting for transfers between devices, swap(): lax.ppermute(a, axis, [(i, i ^ bit) for i in range(lax.axis_size(axis))])  26.5 us
    pallas_call x13, Pallas kernels, call(): pl.pallas_call(kernel, name=name, out_shape=outs, in_specs=[SMEM] * smem...  9.75 us
    unnamed x24, local copies, waits for them, and re-layouts  5.02 us
    ppermute x2, starting transfers between devices, turn(): return lax.ppermute(a, ('sensor', 'step'), pairs)  3.37 us
  transfers between devices with their start and end apart: 22, of which 13 were waited for; matrix products, arithmetic and copies ran while one was open for 0% of the time, Pallas kernels for 7%

profile of v5, /device:TPU:0, one launch (start us, length us, event | category | flops | bytes accessed | tf_op | source)
XLA Modules:
  0.0 74.2 jit_solution(14730697848247435472)
XLA Ops:
  1.3 0.0 copy-start.9
  1.3 0.9 %copy-done.9 = bf16[3,64,512]{2,1,0:T(8,128)(2,1)S(1)} copy-done((bf16[3,64,512]{2,1,0:T(8,128)(2,1)S(1)}, bf16[3,64,512]{2,1,0:T(8,128)(2,1)}, u32[]{:S(2)}) %copy-start.9) | copy-done | bytes 196632
  2.2 3.0 %collective-permute-start = (f32[104,512]{1,0:T(8,128)S(1)}, f32[104,512]{1,0:T(8,128)S(1)}, u32[]{:S(2)}, u32[]{:S(2)}) collective-permute-start(f32[104,512]{1,0:T(8,128)S(1)} %get-tuple-element.57.refs_0_), channel_id=1, source_target_pairs={{0,4},{4,0},{8,12},{12,8},{16,20},{20,16},{24,28},{28,24},{1,5},{5... | collective-permute-start | bytes 638984 | tf_op jit(solution)/shard_map/ppermute | solution.py:440
  5.3 1.6 %collective-permute-start.4 = (f32[104,512]{1,0:T(8,128)S(1)}, f32[104,512]{1,0:T(8,128)S(1)}, u32[]{:S(2)}, u32[]{:S(2)}) collective-permute-start(f32[104,512]{1,0:T(8,128)S(1)} %get-tuple-element.58.refs_4_), channel_id=1, source_target_pairs={{0,8},{4,12},{8,0},{12,4},{16,24},{20,28},{24,16},{28,20},{1,9},{5... | collective-permute-start | bytes 638984 | tf_op jit(solution)/shard_map/ppermute | solution.py:440
  6.8 0.4 collective-permute-start.1
  7.3 0.1 collective-permute-start.3
  7.4 4.0 %collective-permute-done.refs_1_ = f32[104,512]{1,0:T(8,128)S(1)} collective-permute-done((f32[104,512]{1,0:T(8,128)S(1)}, f32[104,512]{1,0:T(8,128)S(1)}, u32[]{:S(2)}, u32[]{:S(2)}) %collective-permute-start) | collective-permute-done | bytes 213024 | tf_op jit(solution)/shard_map/ppermute | solution.py:440
  11.4 2.1 %collective-permute-start.2 = (f32[104,512]{1,0:T(8,128)S(1)}, f32[104,512]{1,0:T(8,128)S(1)}, u32[]{:S(2)}, u32[]{:S(2)}) collective-permute-start(f32[104,512]{1,0:T(8,128)S(1)} %collective-permute-done.refs_1_), channel_id=1, source_target_pairs={{0,8},{4,12},{8,0},{12,4},{16,24},{20,28},{24,16},{28,20},{1,9},{5... | collective-permute-start | bytes 638984 | tf_op jit(solution)/shard_map/ppermute | solution.py:440
  13.5 0.0 collective-permute-done.4.refs_6_
  13.5 1.5 %collective-permute-start.5 = (f32[104,512]{1,0:T(8,128)S(1)}, f32[104,512]{1,0:T(8,128)S(1)}, u32[]{:S(2)}, u32[]{:S(2)}) collective-permute-start(f32[104,512]{1,0:T(8,128)S(1)} %collective-permute-done.4.refs_6_), channel_id=1, source_target_pairs={{0,4},{4,0},{8,12},{12,8},{16,20},{20,16},{24,28},{28,24},{1,5},{5... | collective-permute-start | bytes 638984 | tf_op jit(solution)/shard_map/ppermute | solution.py:440
  15.0 1.0 %copy-done = bf16[512,512]{1,0:T(8,128)(2,1)S(1)} copy-done((bf16[512,512]{1,0:T(8,128)(2,1)S(1)}, bf16[512,512]{1,0:T(8,128)(2,1)}, u32[]{:S(2)}) %copy-start) | copy-done | bytes 524312
  16.0 1.0 %copy-done.2 = bf16[512,512]{1,0:T(8,128)(2,1)S(1)} copy-done((bf16[512,512]{1,0:T(8,128)(2,1)S(1)}, bf16[512,512]{1,0:T(8,128)(2,1)}, u32[]{:S(2)}) %copy-start.2) | copy-done | bytes 524312
  17.1 1.0 %copy-done.4 = bf16[512,512]{1,0:T(8,128)(2,1)S(1)} copy-done((bf16[512,512]{1,0:T(8,128)(2,1)S(1)}, bf16[512,512]{1,0:T(8,128)(2,1)}, u32[]{:S(2)}) %copy-start.4) | copy-done | bytes 524312
  18.1 0.9 %copy-done.7 = f32[8,64,64]{2,1,0:T(8,128)S(1)} copy-done((f32[8,64,64]{2,1,0:T(8,128)S(1)}, f32[8,64,64]{2,1,0:T(8,128)}, u32[]{:S(2)}) %copy-start.7) | copy-done | bytes 131096
  19.1 0.7 local_keys.1
  19.8 0.0 collective-permute-done.1.refs_2_
  19.8 0.0 collective-permute-done.3.refs_5_
  19.8 1.3 %collective-permute-done.2.refs_3_ = f32[104,512]{1,0:T(8,128)S(1)} collective-permute-done((f32[104,512]{1,0:T(8,128)S(1)}, f32[104,512]{1,0:T(8,128)S(1)}, u32[]{:S(2)}, u32[]{:S(2)}) %collective-permute-start.2) | collective-permute-done | bytes 213024 | tf_op jit(solution)/shard_map/ppermute | solution.py:440
  21.1 0.0 collective-permute-done.5.refs_7_
  21.1 1.1 %keys.1 = (bf16[768,512]{1,0:T(8,128)(2,1)S(1)}, f32[768,128]{1,0:T(8,128)S(1)}, f32[768,128]{1,0:T(8,128)S(1)}, f32[768,128]{1,0:T(8,128)S(1)}, f32[200,128]{1,0:T(8,128)S(1)}) custom-call(f32[104,512]{1,0:T(8,128)S(1)} %get-tuple-element.57.refs_0_, f32[104,512]{1,0:T(8,128)S(1)} %collective-permute-done.refs_1_, ...), custom_call_target="tpu_custom_call" | custom-call | flops 301989888 | bytes 4067328 | tf_op jit(solution)/shard_map/keys/pallas_call | solution.py:419
  22.2 2.7 %collective-permute-start.6 = (f32[200,128]{1,0:T(8,128)S(1)}, f32[200,128]{1,0:T(8,128)S(1)}, u32[]{:S(2)}, u32[]{:S(2)}) collective-permute-start(f32[200,128]{1,0:T(8,128)S(1)} %get-tuple-element.62.refs_0_), channel_id=1, source_target_pairs={{0,16},{4,20},{8,24},{12,28},{16,0},{20,4},{24,8},{28,12},{1,17},{... | collective-permute-start | bytes 307208 | tf_op jit(solution)/shard_map/ppermute | solution.py:440
  24.9 0.0 copy-done.11
  24.9 0.0 copy-start.6
  24.9 0.9 %queries.1 = (f32[768,128]{1,0:T(8,128)S(1)}, f32[768,128]{1,0:T(8,128)S(1)}, f32[192,256]{1,0:T(8,128)S(1)}) custom-call(s32[1]{0:T(128)S(6)} %copy.13.live_ref, bf16[768,512]{1,0:T(8,128)(2,1)S(1)} %get-tuple-element.63.x_ref.refs_0_, bf16[192,512]{1,0:T(8,128)(2,1)S(1)} %bitcast.5, bf16[512,128]{1,0:T(8,128)(2,1)S(1)} %get-tuple-element.64.wq_ref, ...), custom_call_target="tpu_custom_call" | custom-call | flops 201326592 | bytes 2392068 | tf_op jit(solution)/shard_map/queries/pallas_call | solution.py:419
  25.8 0.0 copy-start.1
  25.8 2.0 %collective-permute-done.6.refs_1_ = f32[200,128]{1,0:T(8,128)S(1)} collective-permute-done((f32[200,128]{1,0:T(8,128)S(1)}, f32[200,128]{1,0:T(8,128)S(1)}, u32[]{:S(2)}, u32[]{:S(2)}) %collective-permute-start.6) | collective-permute-done | bytes 102432 | tf_op jit(solution)/shard_map/ppermute | solution.py:440
  27.8 0.4 attend.1
  28.2 1.7 %collective-permute-start.7 = (f32[192,128]{1,0:T(8,128)S(1)}, f32[192,128]{1,0:T(8,128)S(1)}, u32[]{:S(2)}, u32[]{:S(2)}) collective-permute-start(f32[192,128]{1,0:T(8,128)S(1)} %get-tuple-element.67), channel_id=1, source_target_pairs={{0,4},{4,0},{8,12},{12,8},{16,20},{20,16},{24,28},{28,24},{1,5},{5... | collective-permute-start | bytes 294920 | tf_op jit(solution)/shard_map/ppermute | solution.py:440
  29.9 0.6 collective-permute-start.8
  30.6 1.2 %collective-permute-start.9 = (f32[192,128]{1,0:T(8,128)S(1)}, f32[192,128]{1,0:T(8,128)S(1)}, u32[]{:S(2)}, u32[]{:S(2)}) collective-permute-start(f32[192,128]{1,0:T(8,128)S(1)} %get-tuple-element.69), channel_id=1, source_target_pairs={{0,12},{4,8},{8,4},{12,0},{16,28},{20,24},{24,20},{28,16},{1,13},{... | collective-permute-start | bytes 294920 | tf_op jit(solution)/shard_map/ppermute | solution.py:440
  31.8 0.7 transposes.1
  32.5 0.9 %collective-permute-done.7.refs_1_ = f32[192,128]{1,0:T(8,128)S(1)} collective-permute-done((f32[192,128]{1,0:T(8,128)S(1)}, f32[192,128]{1,0:T(8,128)S(1)}, u32[]{:S(2)}, u32[]{:S(2)}) %collective-permute-start.7) | collective-permute-done | bytes 98336 | tf_op jit(solution)/shard_map/ppermute | solution.py:440
  33.4 1.2 %collective-permute-done.8.refs_2_ = f32[192,128]{1,0:T(8,128)S(1)} collective-permute-done((f32[192,128]{1,0:T(8,128)S(1)}, f32[192,128]{1,0:T(8,128)S(1)}, u32[]{:S(2)}, u32[]{:S(2)}) %collective-permute-start.8) | collective-permute-done | bytes 98336 | tf_op jit(solution)/shard_map/ppermute | solution.py:440
  34.5 1.6 %collective-permute-done.9.refs_3_ = f32[192,128]{1,0:T(8,128)S(1)} collective-permute-done((f32[192,128]{1,0:T(8,128)S(1)}, f32[192,128]{1,0:T(8,128)S(1)}, u32[]{:S(2)}, u32[]{:S(2)}) %collective-permute-start.9) | collective-permute-done | bytes 98336 | tf_op jit(solution)/shard_map/ppermute | solution.py:440
  36.1 0.7 %feed_forward.1 = (f32[192,128]{1,0:T(8,128)S(1)}, f32[192,128]{1,0:T(8,128)S(1)}, f32[192,128]{1,0:T(8,128)S(1)}, f32[192,128]{1,0:T(8,128)S(1)}) custom-call(f32[192,128]{1,0:T(8,128)S(1)} %get-tuple-element.66.refs_0_, f32[192,128]{1,0:T(8,128)S(1)} %collective-permute-done.7.refs_1_, f32[192,128]{1,0:T(8,128)S(1)} %collective-permute-done.8.refs_2_, ...), custom_call_target="tpu_custom_call" | custom-call | flops 100663296 | bytes 1507328 | tf_op jit(solution)/shard_map/feed_forward/pallas_call | solution.py:419
  36.9 1.6 %collective-permute-start.10 = (f32[192,128]{1,0:T(8,128)S(1)}, f32[192,128]{1,0:T(8,128)S(1)}, u32[]{:S(2)}, u32[]{:S(2)}) collective-permute-start(f32[192,128]{1,0:T(8,128)S(1)} %get-tuple-element.73), channel_id=1, source_target_pairs={{0,4},{4,0},{8,12},{12,8},{16,20},{20,16},{24,28},{28,24},{1,5},{5... | collective-permute-start | bytes 294920 | tf_op jit(solution)/shard_map/ppermute | solution.py:440
  38.5 0.3 collective-permute-start.11
  38.7 1.7 %collective-permute-start.12 = (f32[192,128]{1,0:T(8,128)S(1)}, f32[192,128]{1,0:T(8,128)S(1)}, u32[]{:S(2)}, u32[]{:S(2)}) collective-permute-start(f32[192,128]{1,0:T(8,128)S(1)} %get-tuple-element.75), channel_id=1, source_target_pairs={{0,12},{4,8},{8,4},{12,0},{16,28},{20,24},{24,20},{28,16},{1,13},{... | collective-permute-start | bytes 294920 | tf_op jit(solution)/shard_map/ppermute | solution.py:440
  40.4 1.1 %collective-permute-done.10.refs_1_ = f32[192,128]{1,0:T(8,128)S(1)} collective-permute-done((f32[192,128]{1,0:T(8,128)S(1)}, f32[192,128]{1,0:T(8,128)S(1)}, u32[]{:S(2)}, u32[]{:S(2)}) %collective-permute-start.10) | collective-permute-done | bytes 98336 | tf_op jit(solution)/shard_map/ppermute | solution.py:440
  41.6 1.5 %collective-permute-done.11.refs_2_ = f32[192,128]{1,0:T(8,128)S(1)} collective-permute-done((f32[192,128]{1,0:T(8,128)S(1)}, f32[192,128]{1,0:T(8,128)S(1)}, u32[]{:S(2)}, u32[]{:S(2)}) %collective-permute-start.11) | collective-permute-done | bytes 98336 | tf_op jit(solution)/shard_map/ppermute | solution.py:440
  43.1 1.2 %collective-permute-done.12.refs_3_ = f32[192,128]{1,0:T(8,128)S(1)} collective-permute-done((f32[192,128]{1,0:T(8,128)S(1)}, f32[192,128]{1,0:T(8,128)S(1)}, u32[]{:S(2)}, u32[]{:S(2)}) %collective-permute-start.12) | collective-permute-done | bytes 98336 | tf_op jit(solution)/shard_map/ppermute | solution.py:440
  44.2 0.4 grad_summary.1
  44.7 3.8 %collective-permute-start.13 = (f32[200,128]{1,0:T(8,128)S(1)}, f32[200,128]{1,0:T(8,128)S(1)}, u32[]{:S(2)}, u32[]{:S(2)}) collective-permute-start(f32[200,128]{1,0:T(8,128)S(1)} %get-tuple-element.78.refs_0_), channel_id=1, source_target_pairs={{0,16},{4,20},{8,24},{12,28},{16,0},{20,4},{24,8},{28,12},{1,17},{... | collective-permute-start | bytes 307208 | tf_op jit(solution)/shard_map/ppermute | solution.py:440
  48.5 0.6 query_back.1.refs_6_
  49.0 3.2 %collective-permute-done.13.refs_1_ = f32[200,128]{1,0:T(8,128)S(1)} collective-permute-done((f32[200,128]{1,0:T(8,128)S(1)}, f32[200,128]{1,0:T(8,128)S(1)}, u32[]{:S(2)}, u32[]{:S(2)}) %collective-permute-start.13) | collective-permute-done | bytes 102432 | tf_op jit(solution)/shard_map/ppermute | solution.py:440
  52.2 1.1 %key_back.1 = (f32[392,128]{1,0:T(8,128)S(1)}, f32[392,128]{1,0:T(8,128)S(1)}, f32[392,128]{1,0:T(8,128)S(1)}, f32[392,128]{1,0:T(8,128)S(1)}, f32[2,2,64,384]{3...) custom-call(f32[200,128]{1,0:T(8,128)S(1)} %get-tuple-element.78.refs_0_, f32[200,128]{1,0:T(8,128)S(1)} %collective-permute-done.13.refs_1_, ...), custom_call_target="tpu_custom_call" | custom-call | flops 402653184 | bytes 3989504 | tf_op jit(solution)/shard_map/key_back/pallas_call | solution.py:419
  53.3 0.1 collective-permute-start.14
  53.4 1.7 %collective-permute-done.14.got_ref = f32[2,2,64,384]{3,2,1,0:T(8,128)S(1)} collective-permute-done((f32[2,2,64,384]{3,2,1,0:T(8,128)S(1)}, f32[2,2,64,384]{3,2,1,0:T(8,128)S(1)}, u32[]{:S(2)}, u32[]{:S(2)}) %collective-permute-start.14) | collective-permute-done | bytes 393248 | tf_op jit(solution)/shard_map/ppermute | solution.py:440
  55.1 1.6 %collective-permute-start.15 = (f32[392,128]{1,0:T(8,128)S(1)}, f32[392,128]{1,0:T(8,128)S(1)}, u32[]{:S(2)}, u32[]{:S(2)}) collective-permute-start(f32[392,128]{1,0:T(8,128)S(1)} %get-tuple-element.94), channel_id=1, source_target_pairs={{0,4},{4,0},{8,12},{12,8},{16,20},{20,16},{24,28},{28,24},{1,5},{5... | collective-permute-start | bytes 602120 | tf_op jit(solution)/shard_map/ppermute | solution.py:440
  56.7 0.0 collective-permute-start.16
  56.7 2.0 %collective-permute-start.17 = (f32[392,128]{1,0:T(8,128)S(1)}, f32[392,128]{1,0:T(8,128)S(1)}, u32[]{:S(2)}, u32[]{:S(2)}) collective-permute-start(f32[392,128]{1,0:T(8,128)S(1)} %get-tuple-element.96), channel_id=1, source_target_pairs={{0,12},{4,8},{8,4},{12,0},{16,28},{20,24},{24,20},{28,16},{1,13},{... | collective-permute-start | bytes 602120 | tf_op jit(solution)/shard_map/ppermute | solution.py:440
  58.7 1.5 %collective-permute-start.18 = (f32[64,384]{1,0:T(8,128)S(1)}, f32[64,384]{1,0:T(8,128)S(1)}, u32[]{:S(2)}, u32[]{:S(2)}) collective-permute-start(f32[64,384]{1,0:T(8,128)S(1)} %get-tuple-element.104), channel_id=1, source_target_pairs={{0,2},{1,3},{2,0},{3,1},{4,6},{5,7},{6,4},{7,5},{8,10},{9,11},{10,... | collective-permute-start | bytes 294920 | tf_op jit(solution)/shard_map/ppermute | solution.py:440
  60.2 0.5 collective-permute-start.20
  60.7 3.2 %collective-permute-done.18 = f32[64,384]{1,0:T(8,128)S(1)} collective-permute-done((f32[64,384]{1,0:T(8,128)S(1)}, f32[64,384]{1,0:T(8,128)S(1)}, u32[]{:S(2)}, u32[]{:S(2)}) %collective-permute-start.18) | collective-permute-done | bytes 98336 | tf_op jit(solution)/shard_map/ppermute | solution.py:440
  63.9 2.7 %collective-permute-start.19 = (f32[64,384]{1,0:T(8,128)S(1)}, f32[64,384]{1,0:T(8,128)S(1)}, u32[]{:S(2)}, u32[]{:S(2)}) collective-permute-start(f32[64,384]{1,0:T(8,128)S(1)} %add.6), channel_id=1, source_target_pairs={{0,16},{1,20},{2,24},{3,28},{4,17},{5,21},{6,25},{7,29},{8,18},{9,... | collective-permute-start | bytes 294920 | tf_op jit(solution)/shard_map/ppermute | solution.py:570
  66.6 0.0 collective-permute-done.20
  66.6 0.7 collective-permute-start.21
  67.3 0.0 collective-permute-done.15.refs_1_
  67.3 0.0 collective-permute-done.16.refs_2_
  67.3 3.8 %collective-permute-done.17.refs_3_ = f32[392,128]{1,0:T(8,128)S(1)} collective-permute-done((f32[392,128]{1,0:T(8,128)S(1)}, f32[392,128]{1,0:T(8,128)S(1)}, u32[]{:S(2)}, u32[]{:S(2)}) %collective-permute-start.17) | collective-permute-done | bytes 200736 | tf_op jit(solution)/shard_map/ppermute | solution.py:440
  71.2 2.4 %input_rows.1 = bf16[192,512]{1,0:T(8,128)(2,1)} custom-call(f32[392,128]{1,0:T(8,128)S(1)} %get-tuple-element.93.refs_0_, f32[392,128]{1,0:T(8,128)S(1)} %collective-permute-done.15.refs_1_, f32[392,128]{1,0:T(8,128)S(1)} %collective-permute-done.16.refs_2_, f32[392,128]{1,0:T(8,128)S(1)} %collective-permute-done.17.refs_3_, ...), custom_call_target="tpu_custom_call" | custom-call | flops 503316480 | bytes 3883008 | tf_op jit(solution)/shard_map/input_rows/pallas_call | solution.py:419
  73.5 0.0 collective-permute-done.19.refs_0_
  73.5 0.0 collective-permute-done.21.refs_1_
  73.5 0.7 weight_sums.1
  (19 shorter events, 0.1 us)
Async XLA Ops:
  1.3 0.9 %copy-start.9 = (bf16[3,64,512]{2,1,0:T(8,128)(2,1)S(1)}, bf16[3,64,512]{2,1,0:T(8,128)(2,1)}, u32[]{:S(2)}) copy-start(bf16[3,64,512]{2,1,0:T(8,128)(2,1)} %param.9) | copy-start | bytes 589828
  2.2 9.1 %collective-permute-start = (f32[104,512]{1,0:T(8,128)S(1)}, f32[104,512]{1,0:T(8,128)S(1)}, u32[]{:S(2)}, u32[]{:S(2)}) collective-permute-start(f32[104,512]{1,0:T(8,128)S(1)} %get-tuple-element.57.refs_0_), channel_id=1, source_target_pairs={{0,4},{4,0},{8,12},{12,8},{16,20},{20,16},{24,28},{28,24},{1,5},{5... | collective-permute-start | bytes 638984 | tf_op jit(solution)/shard_map/ppermute | solution.py:440
  5.3 8.2 %collective-permute-start.4 = (f32[104,512]{1,0:T(8,128)S(1)}, f32[104,512]{1,0:T(8,128)S(1)}, u32[]{:S(2)}, u32[]{:S(2)}) collective-permute-start(f32[104,512]{1,0:T(8,128)S(1)} %get-tuple-element.58.refs_4_), channel_id=1, source_target_pairs={{0,8},{4,12},{8,0},{12,4},{16,24},{20,28},{24,16},{28,20},{1,9},{5... | collective-permute-start | bytes 638984 | tf_op jit(solution)/shard_map/ppermute | solution.py:440
  6.8 12.9 %collective-permute-start.1 = (f32[104,512]{1,0:T(8,128)S(1)}, f32[104,512]{1,0:T(8,128)S(1)}, u32[]{:S(2)}, u32[]{:S(2)}) collective-permute-start(f32[104,512]{1,0:T(8,128)S(1)} %get-tuple-element.57.refs_0_), channel_id=1, source_target_pairs={{0,8},{4,12},{8,0},{12,4},{16,24},{20,28},{24,16},{28,20},{1,9},{5... | collective-permute-start | bytes 638984 | tf_op jit(solution)/shard_map/ppermute | solution.py:440
  7.3 12.5 %collective-permute-start.3 = (f32[104,512]{1,0:T(8,128)S(1)}, f32[104,512]{1,0:T(8,128)S(1)}, u32[]{:S(2)}, u32[]{:S(2)}) collective-permute-start(f32[104,512]{1,0:T(8,128)S(1)} %get-tuple-element.58.refs_4_), channel_id=1, source_target_pairs={{0,4},{4,0},{8,12},{12,8},{16,20},{20,16},{24,28},{28,24},{1,5},{5... | collective-permute-start | bytes 638984 | tf_op jit(solution)/shard_map/ppermute | solution.py:440
  11.4 9.8 %collective-permute-start.2 = (f32[104,512]{1,0:T(8,128)S(1)}, f32[104,512]{1,0:T(8,128)S(1)}, u32[]{:S(2)}, u32[]{:S(2)}) collective-permute-start(f32[104,512]{1,0:T(8,128)S(1)} %collective-permute-done.refs_1_), channel_id=1, source_target_pairs={{0,8},{4,12},{8,0},{12,4},{16,24},{20,28},{24,16},{28,20},{1,9},{5... | collective-permute-start | bytes 638984 | tf_op jit(solution)/shard_map/ppermute | solution.py:440
  13.5 7.6 %collective-permute-start.5 = (f32[104,512]{1,0:T(8,128)S(1)}, f32[104,512]{1,0:T(8,128)S(1)}, u32[]{:S(2)}, u32[]{:S(2)}) collective-permute-start(f32[104,512]{1,0:T(8,128)S(1)} %collective-permute-done.4.refs_6_), channel_id=1, source_target_pairs={{0,4},{4,0},{8,12},{12,8},{16,20},{20,16},{24,28},{28,24},{1,5},{5... | collective-permute-start | bytes 638984 | tf_op jit(solution)/shard_map/ppermute | solution.py:440
  15.0 1.0 %copy-start = (bf16[512,512]{1,0:T(8,128)(2,1)S(1)}, bf16[512,512]{1,0:T(8,128)(2,1)}, u32[]{:S(2)}) copy-start(bf16[512,512]{1,0:T(8,128)(2,1)} %refs_1_.1) | copy-start | bytes 1572868
  16.0 1.0 %copy-start.2 = (bf16[512,512]{1,0:T(8,128)(2,1)S(1)}, bf16[512,512]{1,0:T(8,128)(2,1)}, u32[]{:S(2)}) copy-start(bf16[512,512]{1,0:T(8,128)(2,1)} %refs_2_.1) | copy-start | bytes 1572868
  17.1 1.0 %copy-start.4 = (bf16[512,512]{1,0:T(8,128)(2,1)S(1)}, bf16[512,512]{1,0:T(8,128)(2,1)}, u32[]{:S(2)}) copy-start(bf16[512,512]{1,0:T(8,128)(2,1)} %refs_3_.1) | copy-start | bytes 1572868
  18.1 0.9 %copy-start.7 = (f32[8,64,64]{2,1,0:T(8,128)S(1)}, f32[8,64,64]{2,1,0:T(8,128)}, u32[]{:S(2)}) copy-start(f32[8,64,64]{2,1,0:T(8,128)} %refs_7_.1) | copy-start | bytes 393220
  21.1 3.7 %copy-start.10 = (bf16[256,512]{1,0:T(8,128)(2,1)S(1)}, bf16[256,512]{1,0:T(8,128)(2,1)}, u32[]{:S(2)}) copy-start(bf16[256,512]{1,0:T(8,128)(2,1)} %wd_ref.1) | copy-start | bytes 786436
  21.1 3.7 %copy-start.11 = (bf16[3,64,512]{2,1,0:T(8,128)(2,1)S(1)}, bf16[3,64,512]{2,1,0:T(8,128)(2,1)}, u32[]{:S(2)}) copy-start(bf16[3,64,512]{2,1,0:T(8,128)(2,1)} %param.10) | copy-start | bytes 589828
  22.2 5.6 %collective-permute-start.6 = (f32[200,128]{1,0:T(8,128)S(1)}, f32[200,128]{1,0:T(8,128)S(1)}, u32[]{:S(2)}, u32[]{:S(2)}) collective-permute-start(f32[200,128]{1,0:T(8,128)S(1)} %get-tuple-element.62.refs_0_), channel_id=1, source_target_pairs={{0,16},{4,20},{8,24},{12,28},{16,0},{20,4},{24,8},{28,12},{1,17},{... | collective-permute-start | bytes 307208 | tf_op jit(solution)/shard_map/ppermute | solution.py:440
  24.9 6.9 %copy-start.3 = (bf16[512,512]{1,0:T(8,128)(2,1)S(1)}, bf16[512,512]{1,0:T(8,128)(2,1)}, u32[]{:S(2)}) copy-start(bf16[512,512]{1,0:T(8,128)(2,1)} %refs_2_.1) | copy-start | bytes 1572868
  24.9 6.9 %copy-start.5 = (bf16[512,512]{1,0:T(8,128)(2,1)S(1)}, bf16[512,512]{1,0:T(8,128)(2,1)}, u32[]{:S(2)}) copy-start(bf16[512,512]{1,0:T(8,128)(2,1)} %refs_3_.1) | copy-start | bytes 1572868
  24.9 6.9 %copy-start.6 = (bf16[512,256]{1,0:T(8,128)(2,1)S(1)}, bf16[512,256]{1,0:T(8,128)(2,1)}, u32[]{:S(2)}) copy-start(bf16[512,256]{1,0:T(8,128)(2,1)} %refs_5_.1) | copy-start | bytes 786436
  25.8 6.0 %copy-start.1 = (bf16[512,512]{1,0:T(8,128)(2,1)S(1)}, bf16[512,512]{1,0:T(8,128)(2,1)}, u32[]{:S(2)}) copy-start(bf16[512,512]{1,0:T(8,128)(2,1)} %refs_1_.1) | copy-start | bytes 1572868
  28.2 5.2 %collective-permute-start.7 = (f32[192,128]{1,0:T(8,128)S(1)}, f32[192,128]{1,0:T(8,128)S(1)}, u32[]{:S(2)}, u32[]{:S(2)}) collective-permute-start(f32[192,128]{1,0:T(8,128)S(1)} %get-tuple-element.67), channel_id=1, source_target_pairs={{0,4},{4,0},{8,12},{12,8},{16,20},{20,16},{24,28},{28,24},{1,5},{5... | collective-permute-start | bytes 294920 | tf_op jit(solution)/shard_map/ppermute | solution.py:440
  29.9 4.6 %collective-permute-start.8 = (f32[192,128]{1,0:T(8,128)S(1)}, f32[192,128]{1,0:T(8,128)S(1)}, u32[]{:S(2)}, u32[]{:S(2)}) collective-permute-start(f32[192,128]{1,0:T(8,128)S(1)} %get-tuple-element.68), channel_id=1, source_target_pairs={{0,8},{4,12},{8,0},{12,4},{16,24},{20,28},{24,16},{28,20},{1,9},{5... | collective-permute-start | bytes 294920 | tf_op jit(solution)/shard_map/ppermute | solution.py:440
  30.6 5.6 %collective-permute-start.9 = (f32[192,128]{1,0:T(8,128)S(1)}, f32[192,128]{1,0:T(8,128)S(1)}, u32[]{:S(2)}, u32[]{:S(2)}) collective-permute-start(f32[192,128]{1,0:T(8,128)S(1)} %get-tuple-element.69), channel_id=1, source_target_pairs={{0,12},{4,8},{8,4},{12,0},{16,28},{20,24},{24,20},{28,16},{1,13},{... | collective-permute-start | bytes 294920 | tf_op jit(solution)/shard_map/ppermute | solution.py:440
  36.9 4.7 %collective-permute-start.10 = (f32[192,128]{1,0:T(8,128)S(1)}, f32[192,128]{1,0:T(8,128)S(1)}, u32[]{:S(2)}, u32[]{:S(2)}) collective-permute-start(f32[192,128]{1,0:T(8,128)S(1)} %get-tuple-element.73), channel_id=1, source_target_pairs={{0,4},{4,0},{8,12},{12,8},{16,20},{20,16},{24,28},{28,24},{1,5},{5... | collective-permute-start | bytes 294920 | tf_op jit(solution)/shard_map/ppermute | solution.py:440
  38.5 4.6 %collective-permute-start.11 = (f32[192,128]{1,0:T(8,128)S(1)}, f32[192,128]{1,0:T(8,128)S(1)}, u32[]{:S(2)}, u32[]{:S(2)}) collective-permute-start(f32[192,128]{1,0:T(8,128)S(1)} %get-tuple-element.74), channel_id=1, source_target_pairs={{0,8},{4,12},{8,0},{12,4},{16,24},{20,28},{24,16},{28,20},{1,9},{5... | collective-permute-start | bytes 294920 | tf_op jit(solution)/shard_map/ppermute | solution.py:440
  38.7 5.5 %collective-permute-start.12 = (f32[192,128]{1,0:T(8,128)S(1)}, f32[192,128]{1,0:T(8,128)S(1)}, u32[]{:S(2)}, u32[]{:S(2)}) collective-permute-start(f32[192,128]{1,0:T(8,128)S(1)} %get-tuple-element.75), channel_id=1, source_target_pairs={{0,12},{4,8},{8,4},{12,0},{16,28},{20,24},{24,20},{28,16},{1,13},{... | collective-permute-start | bytes 294920 | tf_op jit(solution)/shard_map/ppermute | solution.py:440
  44.7 7.5 %collective-permute-start.13 = (f32[200,128]{1,0:T(8,128)S(1)}, f32[200,128]{1,0:T(8,128)S(1)}, u32[]{:S(2)}, u32[]{:S(2)}) collective-permute-start(f32[200,128]{1,0:T(8,128)S(1)} %get-tuple-element.78.refs_0_), channel_id=1, source_target_pairs={{0,16},{4,20},{8,24},{12,28},{16,0},{20,4},{24,8},{28,12},{1,17},{... | collective-permute-start | bytes 307208 | tf_op jit(solution)/shard_map/ppermute | solution.py:440
  53.3 1.8 %collective-permute-start.14 = (f32[2,2,64,384]{3,2,1,0:T(8,128)S(1)}, f32[2,2,64,384]{3,2,1,0:T(8,128)S(1)}, u32[]{:S(2)}, u32[]{:S(2)}) collective-permute-start(f32[2,2,64,384]{3,2,1,0:T(8,128)S(1)} %get-tuple-element.91), channel_id=1, source_target_pairs={{0,1},{1,0},{2,3},{3,2},{4,5},{5,4},{6,7},{7,6},{8,9},{9,8},{10,11... | collective-permute-start | bytes 1179656 | tf_op jit(solution)/shard_map/ppermute | solution.py:440
  55.1 12.2 %collective-permute-start.15 = (f32[392,128]{1,0:T(8,128)S(1)}, f32[392,128]{1,0:T(8,128)S(1)}, u32[]{:S(2)}, u32[]{:S(2)}) collective-permute-start(f32[392,128]{1,0:T(8,128)S(1)} %get-tuple-element.94), channel_id=1, source_target_pairs={{0,4},{4,0},{8,12},{12,8},{16,20},{20,16},{24,28},{28,24},{1,5},{5... | collective-permute-start | bytes 602120 | tf_op jit(solution)/shard_map/ppermute | solution.py:440
  56.7 10.6 %collective-permute-start.16 = (f32[392,128]{1,0:T(8,128)S(1)}, f32[392,128]{1,0:T(8,128)S(1)}, u32[]{:S(2)}, u32[]{:S(2)}) collective-permute-start(f32[392,128]{1,0:T(8,128)S(1)} %get-tuple-element.95), channel_id=1, source_target_pairs={{0,8},{4,12},{8,0},{12,4},{16,24},{20,28},{24,16},{28,20},{1,9},{5... | collective-permute-start | bytes 602120 | tf_op jit(solution)/shard_map/ppermute | solution.py:440
  56.7 14.4 %collective-permute-start.17 = (f32[392,128]{1,0:T(8,128)S(1)}, f32[392,128]{1,0:T(8,128)S(1)}, u32[]{:S(2)}, u32[]{:S(2)}) collective-permute-start(f32[392,128]{1,0:T(8,128)S(1)} %get-tuple-element.96), channel_id=1, source_target_pairs={{0,12},{4,8},{8,4},{12,0},{16,28},{20,24},{24,20},{28,16},{1,13},{... | collective-permute-start | bytes 602120 | tf_op jit(solution)/shard_map/ppermute | solution.py:440
  58.7 5.2 %collective-permute-start.18 = (f32[64,384]{1,0:T(8,128)S(1)}, f32[64,384]{1,0:T(8,128)S(1)}, u32[]{:S(2)}, u32[]{:S(2)}) collective-permute-start(f32[64,384]{1,0:T(8,128)S(1)} %get-tuple-element.104), channel_id=1, source_target_pairs={{0,2},{1,3},{2,0},{3,1},{4,6},{5,7},{6,4},{7,5},{8,10},{9,11},{10,... | collective-permute-start | bytes 294920 | tf_op jit(solution)/shard_map/ppermute | solution.py:440
  60.2 6.4 %collective-permute-start.20 = (f32[64,384]{1,0:T(8,128)S(1)}, f32[64,384]{1,0:T(8,128)S(1)}, u32[]{:S(2)}, u32[]{:S(2)}) collective-permute-start(f32[64,384]{1,0:T(8,128)S(1)} %get-tuple-element.106), channel_id=1, source_target_pairs={{0,2},{1,3},{2,0},{3,1},{4,6},{5,7},{6,4},{7,5},{8,10},{9,11},{10,... | collective-permute-start | bytes 294920 | tf_op jit(solution)/shard_map/ppermute | solution.py:440
  63.9 7.3 %copy-start.8 = (f32[8,64,64]{2,1,0:T(8,128)S(1)}, f32[8,64,64]{2,1,0:T(8,128)}, u32[]{:S(2)}) copy-start(f32[8,64,64]{2,1,0:T(8,128)} %refs_7_.1) | copy-start | bytes 393220
  63.9 9.6 %collective-permute-start.19 = (f32[64,384]{1,0:T(8,128)S(1)}, f32[64,384]{1,0:T(8,128)S(1)}, u32[]{:S(2)}, u32[]{:S(2)}) collective-permute-start(f32[64,384]{1,0:T(8,128)S(1)} %add.6), channel_id=1, source_target_pairs={{0,16},{1,20},{2,24},{3,28},{4,17},{5,21},{6,25},{7,29},{8,18},{9,... | collective-permute-start | bytes 294920 | tf_op jit(solution)/shard_map/ppermute | solution.py:570
  66.6 6.9 %collective-permute-start.21 = (f32[64,384]{1,0:T(8,128)S(1)}, f32[64,384]{1,0:T(8,128)S(1)}, u32[]{:S(2)}, u32[]{:S(2)}) collective-permute-start(f32[64,384]{1,0:T(8,128)S(1)} %add.7), channel_id=1, source_target_pairs={{0,0},{1,4},{2,8},{3,12},{4,1},{5,5},{6,9},{7,13},{8,2},{9,6},{10,... | collective-permute-start | bytes 294920 | tf_op jit(solution)/shard_map/ppermute | solution.py:570

commit v6 on v5

--- a/solution.py
+++ b/solution.py
@@ -577,7 +577,6 @@
             (shape(tile),) * 4,
             (own_half, got_half),
         )
-        ready = kept
         away = away + swap(send_away, "step", 2)
         kept = kept + swap(send_kept, "step", 2)
         parts = (turn(away, 1), turn(kept, 0))
@@ -588,13 +587,12 @@
             (shape((quads, *tile)),) * 2,
             (own_half, got_half),
         )
-        ready = kept
         groups = [[q + count * k for k in range(quads)] for q in range(count)]
         blocks = lax.all_to_all(
             kept + swap(sent, "step", 2), "sensor", 0, 0, tiled=True, axis_index_groups=groups
         )
         parts = (turn(blocks.sum(0), 0),)
-    messages = trade(after(messages, ready), "sensor")
+    messages = trade(messages, "sensor")
     scale = 1.0 / math.sqrt(rows * lax.axis_size("step") * devices)
     out = shape((width // devices, LANES))
     grad_in = call(
@@ -602,7 +600,7 @@
         "input_rows",
         shape((rows, width), BF16),
         (*messages, *local_keys, feature_proj, wq_turned, wk_turned, wv_turned),
-        flops=5 * product,
+        flops=30 * product,
         scratch=[pltpu.VMEM((rows, width), BF16), pltpu.VMEM((packed.shape[0], width), F32)],
     )
     grads = call(

time: 75.4 us -> 74 us (0.981)
  waiting for transfers between devices: 26.5 us -> 25.6 us
    ppermute x20, waiting for transfers between devices: 26.5 us -> 25.6 us  [swap(): lax.ppermute(a, axis, [(i, i ^ bit) for i in range(lax.axis_size(axis))])]
  transfers between devices with their start and end apart: 22 -> 22, of which waited for: 13 -> 12; matrix products, arithmetic and copies ran while one was open for 0% -> 0% of each run, Pallas kernels for 7% -> 7%
where the time goes in v6:
time: 74 us; the launch traced here: 73.1 us
  starting transfers between devices  31.2 us (42%)
  waiting for transfers between devices  25.6 us (35%)
  Pallas kernels  9.76 us (13%)
  local copies, waits for them, and re-layouts  5.02 us (7%)
  between operations  1.46 us (2%)
    ppermute x20, starting transfers between devices, swap(): lax.ppermute(a, axis, [(i, i ^ bit) for i in range(lax.axis_size(axis))])  28.1 us
    ppermute x20, waiting for transfers between devices, swap(): lax.ppermute(a, axis, [(i, i ^ bit) for i in range(lax.axis_size(axis))])  25.6 us
    pallas_call x13, Pallas kernels, call(): pl.pallas_call(kernel, name=name, out_shape=outs, in_specs=[SMEM] * smem...  9.76 us
    unnamed x24, local copies, waits for them, and re-layouts  5.02 us
    ppermute x2, starting transfers between devices, turn(): return lax.ppermute(a, ('sensor', 'step'), pairs)  3.11 us
  transfers between devices with their start and end apart: 22, of which 12 were waited for; matrix products, arithmetic and copies ran while one was open for 0% of the time, Pallas kernels for 7%

profile of v6, /device:TPU:0, one launch (start us, length us, event | category | flops | bytes accessed | tf_op | source)
XLA Modules:
  0.0 73.1 jit_solution(5020878219351761649)
XLA Ops:
  1.3 0.9 %copy-done.7 = bf16[3,64,512]{2,1,0:T(8,128)(2,1)S(1)} copy-done((bf16[3,64,512]{2,1,0:T(8,128)(2,1)S(1)}, bf16[3,64,512]{2,1,0:T(8,128)(2,1)}, u32[]{:S(2)}) %copy-start.7) | copy-done | bytes 196632
  2.2 3.0 %collective-permute-start = (f32[104,512]{1,0:T(8,128)S(1)}, f32[104,512]{1,0:T(8,128)S(1)}, u32[]{:S(2)}, u32[]{:S(2)}) collective-permute-start(f32[104,512]{1,0:T(8,128)S(1)} %get-tuple-element.53.refs_0_), channel_id=1, source_target_pairs={{0,4},{4,0},{8,12},{12,8},{16,20},{20,16},{24,28},{28,24},{1,5},{5... | collective-permute-start | bytes 638984 | tf_op jit(solution)/shard_map/ppermute | solution.py:440
  5.3 1.6 %collective-permute-start.4 = (f32[104,512]{1,0:T(8,128)S(1)}, f32[104,512]{1,0:T(8,128)S(1)}, u32[]{:S(2)}, u32[]{:S(2)}) collective-permute-start(f32[104,512]{1,0:T(8,128)S(1)} %get-tuple-element.54.refs_4_), channel_id=1, source_target_pairs={{0,8},{4,12},{8,0},{12,4},{16,24},{20,28},{24,16},{28,20},{1,9},{5... | collective-permute-start | bytes 638984 | tf_op jit(solution)/shard_map/ppermute | solution.py:440
  6.8 0.4 collective-permute-start.1
  7.3 0.1 collective-permute-start.3
  7.4 4.0 %collective-permute-done.refs_1_ = f32[104,512]{1,0:T(8,128)S(1)} collective-permute-done((f32[104,512]{1,0:T(8,128)S(1)}, f32[104,512]{1,0:T(8,128)S(1)}, u32[]{:S(2)}, u32[]{:S(2)}) %collective-permute-start) | collective-permute-done | bytes 213024 | tf_op jit(solution)/shard_map/ppermute | solution.py:440
  11.4 2.1 %collective-permute-start.2 = (f32[104,512]{1,0:T(8,128)S(1)}, f32[104,512]{1,0:T(8,128)S(1)}, u32[]{:S(2)}, u32[]{:S(2)}) collective-permute-start(f32[104,512]{1,0:T(8,128)S(1)} %collective-permute-done.refs_1_), channel_id=1, source_target_pairs={{0,8},{4,12},{8,0},{12,4},{16,24},{20,28},{24,16},{28,20},{1,9},{5... | collective-permute-start | bytes 638984 | tf_op jit(solution)/shard_map/ppermute | solution.py:440
  13.5 0.0 collective-permute-done.4.refs_6_
  13.5 1.5 %collective-permute-start.5 = (f32[104,512]{1,0:T(8,128)S(1)}, f32[104,512]{1,0:T(8,128)S(1)}, u32[]{:S(2)}, u32[]{:S(2)}) collective-permute-start(f32[104,512]{1,0:T(8,128)S(1)} %collective-permute-done.4.refs_6_), channel_id=1, source_target_pairs={{0,4},{4,0},{8,12},{12,8},{16,20},{20,16},{24,28},{28,24},{1,5},{5... | collective-permute-start | bytes 638984 | tf_op jit(solution)/shard_map/ppermute | solution.py:440
  15.0 1.0 %copy-done = bf16[512,512]{1,0:T(8,128)(2,1)S(1)} copy-done((bf16[512,512]{1,0:T(8,128)(2,1)S(1)}, bf16[512,512]{1,0:T(8,128)(2,1)}, u32[]{:S(2)}) %copy-start) | copy-done | bytes 524312
  16.0 1.0 %copy-done.2 = bf16[512,512]{1,0:T(8,128)(2,1)S(1)} copy-done((bf16[512,512]{1,0:T(8,128)(2,1)S(1)}, bf16[512,512]{1,0:T(8,128)(2,1)}, u32[]{:S(2)}) %copy-start.2) | copy-done | bytes 524312
  17.1 1.0 %copy-done.4 = bf16[512,512]{1,0:T(8,128)(2,1)S(1)} copy-done((bf16[512,512]{1,0:T(8,128)(2,1)S(1)}, bf16[512,512]{1,0:T(8,128)(2,1)}, u32[]{:S(2)}) %copy-start.4) | copy-done | bytes 524312
  18.1 0.9 %copy-done.9 = f32[8,64,64]{2,1,0:T(8,128)S(1)} copy-done((f32[8,64,64]{2,1,0:T(8,128)S(1)}, f32[8,64,64]{2,1,0:T(8,128)}, u32[]{:S(2)}) %copy-start.9) | copy-done | bytes 131096
  19.1 0.7 local_keys.1
  19.8 0.0 collective-permute-done.1.refs_2_
  19.8 0.0 collective-permute-done.3.refs_5_
  19.8 1.3 %collective-permute-done.2.refs_3_ = f32[104,512]{1,0:T(8,128)S(1)} collective-permute-done((f32[104,512]{1,0:T(8,128)S(1)}, f32[104,512]{1,0:T(8,128)S(1)}, u32[]{:S(2)}, u32[]{:S(2)}) %collective-permute-start.2) | collective-permute-done | bytes 213024 | tf_op jit(solution)/shard_map/ppermute | solution.py:440
  21.1 0.0 collective-permute-done.5.refs_7_
  21.1 1.1 %keys.1 = (bf16[768,512]{1,0:T(8,128)(2,1)S(1)}, f32[768,128]{1,0:T(8,128)S(1)}, f32[768,128]{1,0:T(8,128)S(1)}, f32[768,128]{1,0:T(8,128)S(1)}, f32[200,128]{1,0:T(8,128)S(1)}) custom-call(f32[104,512]{1,0:T(8,128)S(1)} %get-tuple-element.53.refs_0_, f32[104,512]{1,0:T(8,128)S(1)} %collective-permute-done.refs_1_, ...), custom_call_target="tpu_custom_call" | custom-call | flops 301989888 | bytes 4067328 | tf_op jit(solution)/shard_map/keys/pallas_call | solution.py:419
  22.2 2.6 %collective-permute-start.6 = (f32[200,128]{1,0:T(8,128)S(1)}, f32[200,128]{1,0:T(8,128)S(1)}, u32[]{:S(2)}, u32[]{:S(2)}) collective-permute-start(f32[200,128]{1,0:T(8,128)S(1)} %get-tuple-element.58.refs_0_), channel_id=1, source_target_pairs={{0,16},{4,20},{8,24},{12,28},{16,0},{20,4},{24,8},{28,12},{1,17},{... | collective-permute-start | bytes 307208 | tf_op jit(solution)/shard_map/ppermute | solution.py:440
  24.8 0.0 copy-done.11
  24.9 0.0 copy-start.6
  24.9 0.9 %queries.1 = (f32[768,128]{1,0:T(8,128)S(1)}, f32[768,128]{1,0:T(8,128)S(1)}, f32[192,256]{1,0:T(8,128)S(1)}) custom-call(s32[1]{0:T(128)S(6)} %copy.13.live_ref, bf16[768,512]{1,0:T(8,128)(2,1)S(1)} %get-tuple-element.59.x_ref.refs_0_, bf16[192,512]{1,0:T(8,128)(2,1)S(1)} %bitcast.5, bf16[512,128]{1,0:T(8,128)(2,1)S(1)} %get-tuple-element.60.wq_ref, ...), custom_call_target="tpu_custom_call" | custom-call | flops 201326592 | bytes 2392068 | tf_op jit(solution)/shard_map/queries/pallas_call | solution.py:419
  25.8 0.0 copy-start.1
  25.8 2.0 %collective-permute-done.6.refs_1_ = f32[200,128]{1,0:T(8,128)S(1)} collective-permute-done((f32[200,128]{1,0:T(8,128)S(1)}, f32[200,128]{1,0:T(8,128)S(1)}, u32[]{:S(2)}, u32[]{:S(2)}) %collective-permute-start.6) | collective-permute-done | bytes 102432 | tf_op jit(solution)/shard_map/ppermute | solution.py:440
  27.8 0.4 attend.1
  28.2 1.7 %collective-permute-start.7 = (f32[192,128]{1,0:T(8,128)S(1)}, f32[192,128]{1,0:T(8,128)S(1)}, u32[]{:S(2)}, u32[]{:S(2)}) collective-permute-start(f32[192,128]{1,0:T(8,128)S(1)} %get-tuple-element.63), channel_id=1, source_target_pairs={{0,4},{4,0},{8,12},{12,8},{16,20},{20,16},{24,28},{28,24},{1,5},{5... | collective-permute-start | bytes 294920 | tf_op jit(solution)/shard_map/ppermute | solution.py:440
  29.9 0.6 collective-permute-start.8
  30.6 1.2 %collective-permute-start.9 = (f32[192,128]{1,0:T(8,128)S(1)}, f32[192,128]{1,0:T(8,128)S(1)}, u32[]{:S(2)}, u32[]{:S(2)}) collective-permute-start(f32[192,128]{1,0:T(8,128)S(1)} %get-tuple-element.65), channel_id=1, source_target_pairs={{0,12},{4,8},{8,4},{12,0},{16,28},{20,24},{24,20},{28,16},{1,13},{... | collective-permute-start | bytes 294920 | tf_op jit(solution)/shard_map/ppermute | solution.py:440
  31.8 0.7 transposes.1
  32.5 0.9 %collective-permute-done.7.refs_1_ = f32[192,128]{1,0:T(8,128)S(1)} collective-permute-done((f32[192,128]{1,0:T(8,128)S(1)}, f32[192,128]{1,0:T(8,128)S(1)}, u32[]{:S(2)}, u32[]{:S(2)}) %collective-permute-start.7) | collective-permute-done | bytes 98336 | tf_op jit(solution)/shard_map/ppermute | solution.py:440
  33.4 1.1 %collective-permute-done.8.refs_2_ = f32[192,128]{1,0:T(8,128)S(1)} collective-permute-done((f32[192,128]{1,0:T(8,128)S(1)}, f32[192,128]{1,0:T(8,128)S(1)}, u32[]{:S(2)}, u32[]{:S(2)}) %collective-permute-start.8) | collective-permute-done | bytes 98336 | tf_op jit(solution)/shard_map/ppermute | solution.py:440
  34.5 1.6 %collective-permute-done.9.refs_3_ = f32[192,128]{1,0:T(8,128)S(1)} collective-permute-done((f32[192,128]{1,0:T(8,128)S(1)}, f32[192,128]{1,0:T(8,128)S(1)}, u32[]{:S(2)}, u32[]{:S(2)}) %collective-permute-start.9) | collective-permute-done | bytes 98336 | tf_op jit(solution)/shard_map/ppermute | solution.py:440
  36.1 0.7 %feed_forward.1 = (f32[192,128]{1,0:T(8,128)S(1)}, f32[192,128]{1,0:T(8,128)S(1)}, f32[192,128]{1,0:T(8,128)S(1)}, f32[192,128]{1,0:T(8,128)S(1)}) custom-call(f32[192,128]{1,0:T(8,128)S(1)} %get-tuple-element.62.refs_0_, f32[192,128]{1,0:T(8,128)S(1)} %collective-permute-done.7.refs_1_, f32[192,128]{1,0:T(8,128)S(1)} %collective-permute-done.8.refs_2_, ...), custom_call_target="tpu_custom_call" | custom-call | flops 100663296 | bytes 1507328 | tf_op jit(solution)/shard_map/feed_forward/pallas_call | solution.py:419
  36.9 1.6 %collective-permute-start.10 = (f32[192,128]{1,0:T(8,128)S(1)}, f32[192,128]{1,0:T(8,128)S(1)}, u32[]{:S(2)}, u32[]{:S(2)}) collective-permute-start(f32[192,128]{1,0:T(8,128)S(1)} %get-tuple-element.69), channel_id=1, source_target_pairs={{0,4},{4,0},{8,12},{12,8},{16,20},{20,16},{24,28},{28,24},{1,5},{5... | collective-permute-start | bytes 294920 | tf_op jit(solution)/shard_map/ppermute | solution.py:440
  38.4 0.3 collective-permute-start.11
  38.7 1.7 %collective-permute-start.12 = (f32[192,128]{1,0:T(8,128)S(1)}, f32[192,128]{1,0:T(8,128)S(1)}, u32[]{:S(2)}, u32[]{:S(2)}) collective-permute-start(f32[192,128]{1,0:T(8,128)S(1)} %get-tuple-element.71), channel_id=1, source_target_pairs={{0,12},{4,8},{8,4},{12,0},{16,28},{20,24},{24,20},{28,16},{1,13},{... | collective-permute-start | bytes 294920 | tf_op jit(solution)/shard_map/ppermute | solution.py:440
  40.4 1.1 %collective-permute-done.10.refs_1_ = f32[192,128]{1,0:T(8,128)S(1)} collective-permute-done((f32[192,128]{1,0:T(8,128)S(1)}, f32[192,128]{1,0:T(8,128)S(1)}, u32[]{:S(2)}, u32[]{:S(2)}) %collective-permute-start.10) | collective-permute-done | bytes 98336 | tf_op jit(solution)/shard_map/ppermute | solution.py:440
  41.5 1.5 %collective-permute-done.11.refs_2_ = f32[192,128]{1,0:T(8,128)S(1)} collective-permute-done((f32[192,128]{1,0:T(8,128)S(1)}, f32[192,128]{1,0:T(8,128)S(1)}, u32[]{:S(2)}, u32[]{:S(2)}) %collective-permute-start.11) | collective-permute-done | bytes 98336 | tf_op jit(solution)/shard_map/ppermute | solution.py:440
  43.1 1.2 %collective-permute-done.12.refs_3_ = f32[192,128]{1,0:T(8,128)S(1)} collective-permute-done((f32[192,128]{1,0:T(8,128)S(1)}, f32[192,128]{1,0:T(8,128)S(1)}, u32[]{:S(2)}, u32[]{:S(2)}) %collective-permute-start.12) | collective-permute-done | bytes 98336 | tf_op jit(solution)/shard_map/ppermute | solution.py:440
  44.2 0.4 grad_summary.1
  44.6 3.8 %collective-permute-start.13 = (f32[200,128]{1,0:T(8,128)S(1)}, f32[200,128]{1,0:T(8,128)S(1)}, u32[]{:S(2)}, u32[]{:S(2)}) collective-permute-start(f32[200,128]{1,0:T(8,128)S(1)} %get-tuple-element.74.refs_0_), channel_id=1, source_target_pairs={{0,16},{4,20},{8,24},{12,28},{16,0},{20,4},{24,8},{28,12},{1,17},{... | collective-permute-start | bytes 307208 | tf_op jit(solution)/shard_map/ppermute | solution.py:440
  48.4 0.6 query_back.1.refs_6_
  49.0 3.2 %collective-permute-done.13.refs_1_ = f32[200,128]{1,0:T(8,128)S(1)} collective-permute-done((f32[200,128]{1,0:T(8,128)S(1)}, f32[200,128]{1,0:T(8,128)S(1)}, u32[]{:S(2)}, u32[]{:S(2)}) %collective-permute-start.13) | collective-permute-done | bytes 102432 | tf_op jit(solution)/shard_map/ppermute | solution.py:440
  52.2 1.1 %key_back.1 = (f32[392,128]{1,0:T(8,128)S(1)}, f32[392,128]{1,0:T(8,128)S(1)}, f32[392,128]{1,0:T(8,128)S(1)}, f32[392,128]{1,0:T(8,128)S(1)}, f32[2,2,64,384]{3...) custom-call(f32[200,128]{1,0:T(8,128)S(1)} %get-tuple-element.74.refs_0_, f32[200,128]{1,0:T(8,128)S(1)} %collective-permute-done.13.refs_1_, ...), custom_call_target="tpu_custom_call" | custom-call | flops 402653184 | bytes 3989504 | tf_op jit(solution)/shard_map/key_back/pallas_call | solution.py:419
  53.3 0.1 collective-permute-start.17
  53.4 1.6 %collective-permute-start.14 = (f32[392,128]{1,0:T(8,128)S(1)}, f32[392,128]{1,0:T(8,128)S(1)}, u32[]{:S(2)}, u32[]{:S(2)}) collective-permute-start(f32[392,128]{1,0:T(8,128)S(1)} %get-tuple-element.83), channel_id=1, source_target_pairs={{0,4},{4,0},{8,12},{12,8},{16,20},{20,16},{24,28},{28,24},{1,5},{5... | collective-permute-start | bytes 602120 | tf_op jit(solution)/shard_map/ppermute | solution.py:440
  54.9 0.0 collective-permute-start.15
  54.9 2.0 %collective-permute-start.16 = (f32[392,128]{1,0:T(8,128)S(1)}, f32[392,128]{1,0:T(8,128)S(1)}, u32[]{:S(2)}, u32[]{:S(2)}) collective-permute-start(f32[392,128]{1,0:T(8,128)S(1)} %get-tuple-element.85), channel_id=1, source_target_pairs={{0,12},{4,8},{8,4},{12,0},{16,28},{20,24},{24,20},{28,16},{1,13},{... | collective-permute-start | bytes 602120 | tf_op jit(solution)/shard_map/ppermute | solution.py:440
  56.9 0.0 collective-permute-done.17.got_ref
  57.0 1.6 %collective-permute-start.18 = (f32[64,384]{1,0:T(8,128)S(1)}, f32[64,384]{1,0:T(8,128)S(1)}, u32[]{:S(2)}, u32[]{:S(2)}) collective-permute-start(f32[64,384]{1,0:T(8,128)S(1)} %get-tuple-element.95), channel_id=1, source_target_pairs={{0,2},{1,3},{2,0},{3,1},{4,6},{5,7},{6,4},{7,5},{8,10},{9,11},{10,... | collective-permute-start | bytes 294920 | tf_op jit(solution)/shard_map/ppermute | solution.py:440
  58.5 0.5 collective-permute-start.20
  59.1 3.5 %collective-permute-done.18 = f32[64,384]{1,0:T(8,128)S(1)} collective-permute-done((f32[64,384]{1,0:T(8,128)S(1)}, f32[64,384]{1,0:T(8,128)S(1)}, u32[]{:S(2)}, u32[]{:S(2)}) %collective-permute-start.18) | collective-permute-done | bytes 98336 | tf_op jit(solution)/shard_map/ppermute | solution.py:440
  62.6 2.4 %collective-permute-start.19 = (f32[64,384]{1,0:T(8,128)S(1)}, f32[64,384]{1,0:T(8,128)S(1)}, u32[]{:S(2)}, u32[]{:S(2)}) collective-permute-start(f32[64,384]{1,0:T(8,128)S(1)} %add.6), channel_id=1, source_target_pairs={{0,16},{1,20},{2,24},{3,28},{4,17},{5,21},{6,25},{7,29},{8,18},{9,... | collective-permute-start | bytes 294920 | tf_op jit(solution)/shard_map/ppermute | solution.py:570
  65.0 0.0 collective-permute-done.20
  65.0 0.7 collective-permute-start.21
  65.7 0.0 collective-permute-done.14.refs_1_
  65.7 0.0 collective-permute-done.15.refs_2_
  65.7 4.3 %collective-permute-done.16.refs_3_ = f32[392,128]{1,0:T(8,128)S(1)} collective-permute-done((f32[392,128]{1,0:T(8,128)S(1)}, f32[392,128]{1,0:T(8,128)S(1)}, u32[]{:S(2)}, u32[]{:S(2)}) %collective-permute-start.16) | collective-permute-done | bytes 200736 | tf_op jit(solution)/shard_map/ppermute | solution.py:440
  70.0 0.0 copy-done.10
  70.0 2.4 %input_rows.1 = bf16[192,512]{1,0:T(8,128)(2,1)} custom-call(f32[392,128]{1,0:T(8,128)S(1)} %get-tuple-element.82.refs_0_, f32[392,128]{1,0:T(8,128)S(1)} %collective-permute-done.14.refs_1_, f32[392,128]{1,0:T(8,128)S(1)} %collective-permute-done.15.refs_2_, f32[392,128]{1,0:T(8,128)S(1)} %collective-permute-done.16.refs_3_, ...), custom_call_target="tpu_custom_call" | custom-call | flops 3019898880 | bytes 3883008 | tf_op jit(solution)/shard_map/input_rows/pallas_call | solution.py:419
  72.4 0.0 collective-permute-done.19.refs_0_
  72.4 0.0 collective-permute-done.21.refs_1_
  72.4 0.7 weight_sums.1
  (19 shorter events, 0.1 us)
Async XLA Ops:
  1.3 0.9 %copy-start.7 = (bf16[3,64,512]{2,1,0:T(8,128)(2,1)S(1)}, bf16[3,64,512]{2,1,0:T(8,128)(2,1)}, u32[]{:S(2)}) copy-start(bf16[3,64,512]{2,1,0:T(8,128)(2,1)} %param.9) | copy-start | bytes 589828
  2.2 9.1 %collective-permute-start = (f32[104,512]{1,0:T(8,128)S(1)}, f32[104,512]{1,0:T(8,128)S(1)}, u32[]{:S(2)}, u32[]{:S(2)}) collective-permute-start(f32[104,512]{1,0:T(8,128)S(1)} %get-tuple-element.53.refs_0_), channel_id=1, source_target_pairs={{0,4},{4,0},{8,12},{12,8},{16,20},{20,16},{24,28},{28,24},{1,5},{5... | collective-permute-start | bytes 638984 | tf_op jit(solution)/shard_map/ppermute | solution.py:440
  5.3 8.2 %collective-permute-start.4 = (f32[104,512]{1,0:T(8,128)S(1)}, f32[104,512]{1,0:T(8,128)S(1)}, u32[]{:S(2)}, u32[]{:S(2)}) collective-permute-start(f32[104,512]{1,0:T(8,128)S(1)} %get-tuple-element.54.refs_4_), channel_id=1, source_target_pairs={{0,8},{4,12},{8,0},{12,4},{16,24},{20,28},{24,16},{28,20},{1,9},{5... | collective-permute-start | bytes 638984 | tf_op jit(solution)/shard_map/ppermute | solution.py:440
  6.8 12.9 %collective-permute-start.1 = (f32[104,512]{1,0:T(8,128)S(1)}, f32[104,512]{1,0:T(8,128)S(1)}, u32[]{:S(2)}, u32[]{:S(2)}) collective-permute-start(f32[104,512]{1,0:T(8,128)S(1)} %get-tuple-element.53.refs_0_), channel_id=1, source_target_pairs={{0,8},{4,12},{8,0},{12,4},{16,24},{20,28},{24,16},{28,20},{1,9},{5... | collective-permute-start | bytes 638984 | tf_op jit(solution)/shard_map/ppermute | solution.py:440
  7.3 12.5 %collective-permute-start.3 = (f32[104,512]{1,0:T(8,128)S(1)}, f32[104,512]{1,0:T(8,128)S(1)}, u32[]{:S(2)}, u32[]{:S(2)}) collective-permute-start(f32[104,512]{1,0:T(8,128)S(1)} %get-tuple-element.54.refs_4_), channel_id=1, source_target_pairs={{0,4},{4,0},{8,12},{12,8},{16,20},{20,16},{24,28},{28,24},{1,5},{5... | collective-permute-start | bytes 638984 | tf_op jit(solution)/shard_map/ppermute | solution.py:440
  11.4 9.8 %collective-permute-start.2 = (f32[104,512]{1,0:T(8,128)S(1)}, f32[104,512]{1,0:T(8,128)S(1)}, u32[]{:S(2)}, u32[]{:S(2)}) collective-permute-start(f32[104,512]{1,0:T(8,128)S(1)} %collective-permute-done.refs_1_), channel_id=1, source_target_pairs={{0,8},{4,12},{8,0},{12,4},{16,24},{20,28},{24,16},{28,20},{1,9},{5... | collective-permute-start | bytes 638984 | tf_op jit(solution)/shard_map/ppermute | solution.py:440
  13.5 7.6 %collective-permute-start.5 = (f32[104,512]{1,0:T(8,128)S(1)}, f32[104,512]{1,0:T(8,128)S(1)}, u32[]{:S(2)}, u32[]{:S(2)}) collective-permute-start(f32[104,512]{1,0:T(8,128)S(1)} %collective-permute-done.4.refs_6_), channel_id=1, source_target_pairs={{0,4},{4,0},{8,12},{12,8},{16,20},{20,16},{24,28},{28,24},{1,5},{5... | collective-permute-start | bytes 638984 | tf_op jit(solution)/shard_map/ppermute | solution.py:440
  15.0 1.0 %copy-start = (bf16[512,512]{1,0:T(8,128)(2,1)S(1)}, bf16[512,512]{1,0:T(8,128)(2,1)}, u32[]{:S(2)}) copy-start(bf16[512,512]{1,0:T(8,128)(2,1)} %refs_1_.1) | copy-start | bytes 1572868
  16.0 1.0 %copy-start.2 = (bf16[512,512]{1,0:T(8,128)(2,1)S(1)}, bf16[512,512]{1,0:T(8,128)(2,1)}, u32[]{:S(2)}) copy-start(bf16[512,512]{1,0:T(8,128)(2,1)} %refs_2_.1) | copy-start | bytes 1572868
  17.1 1.0 %copy-start.4 = (bf16[512,512]{1,0:T(8,128)(2,1)S(1)}, bf16[512,512]{1,0:T(8,128)(2,1)}, u32[]{:S(2)}) copy-start(bf16[512,512]{1,0:T(8,128)(2,1)} %refs_3_.1) | copy-start | bytes 1572868
  18.1 0.9 %copy-start.9 = (f32[8,64,64]{2,1,0:T(8,128)S(1)}, f32[8,64,64]{2,1,0:T(8,128)}, u32[]{:S(2)}) copy-start(f32[8,64,64]{2,1,0:T(8,128)} %refs_7_.1) | copy-start | bytes 393220
  21.1 3.7 %copy-start.8 = (bf16[256,512]{1,0:T(8,128)(2,1)S(1)}, bf16[256,512]{1,0:T(8,128)(2,1)}, u32[]{:S(2)}) copy-start(bf16[256,512]{1,0:T(8,128)(2,1)} %wd_ref.1) | copy-start | bytes 786436
  21.1 3.7 %copy-start.11 = (bf16[3,64,512]{2,1,0:T(8,128)(2,1)S(1)}, bf16[3,64,512]{2,1,0:T(8,128)(2,1)}, u32[]{:S(2)}) copy-start(bf16[3,64,512]{2,1,0:T(8,128)(2,1)} %param.10) | copy-start | bytes 589828
  22.2 5.6 %collective-permute-start.6 = (f32[200,128]{1,0:T(8,128)S(1)}, f32[200,128]{1,0:T(8,128)S(1)}, u32[]{:S(2)}, u32[]{:S(2)}) collective-permute-start(f32[200,128]{1,0:T(8,128)S(1)} %get-tuple-element.58.refs_0_), channel_id=1, source_target_pairs={{0,16},{4,20},{8,24},{12,28},{16,0},{20,4},{24,8},{28,12},{1,17},{... | collective-permute-start | bytes 307208 | tf_op jit(solution)/shard_map/ppermute | solution.py:440
  24.9 6.9 %copy-start.3 = (bf16[512,512]{1,0:T(8,128)(2,1)S(1)}, bf16[512,512]{1,0:T(8,128)(2,1)}, u32[]{:S(2)}) copy-start(bf16[512,512]{1,0:T(8,128)(2,1)} %refs_2_.1) | copy-start | bytes 1572868
  24.9 6.9 %copy-start.5 = (bf16[512,512]{1,0:T(8,128)(2,1)S(1)}, bf16[512,512]{1,0:T(8,128)(2,1)}, u32[]{:S(2)}) copy-start(bf16[512,512]{1,0:T(8,128)(2,1)} %refs_3_.1) | copy-start | bytes 1572868
  24.9 6.9 %copy-start.6 = (bf16[512,256]{1,0:T(8,128)(2,1)S(1)}, bf16[512,256]{1,0:T(8,128)(2,1)}, u32[]{:S(2)}) copy-start(bf16[512,256]{1,0:T(8,128)(2,1)} %refs_5_.1) | copy-start | bytes 786436
  25.8 6.0 %copy-start.1 = (bf16[512,512]{1,0:T(8,128)(2,1)S(1)}, bf16[512,512]{1,0:T(8,128)(2,1)}, u32[]{:S(2)}) copy-start(bf16[512,512]{1,0:T(8,128)(2,1)} %refs_1_.1) | copy-start | bytes 1572868
  28.2 5.2 %collective-permute-start.7 = (f32[192,128]{1,0:T(8,128)S(1)}, f32[192,128]{1,0:T(8,128)S(1)}, u32[]{:S(2)}, u32[]{:S(2)}) collective-permute-start(f32[192,128]{1,0:T(8,128)S(1)} %get-tuple-element.63), channel_id=1, source_target_pairs={{0,4},{4,0},{8,12},{12,8},{16,20},{20,16},{24,28},{28,24},{1,5},{5... | collective-permute-start | bytes 294920 | tf_op jit(solution)/shard_map/ppermute | solution.py:440
  29.9 4.6 %collective-permute-start.8 = (f32[192,128]{1,0:T(8,128)S(1)}, f32[192,128]{1,0:T(8,128)S(1)}, u32[]{:S(2)}, u32[]{:S(2)}) collective-permute-start(f32[192,128]{1,0:T(8,128)S(1)} %get-tuple-element.64), channel_id=1, source_target_pairs={{0,8},{4,12},{8,0},{12,4},{16,24},{20,28},{24,16},{28,20},{1,9},{5... | collective-permute-start | bytes 294920 | tf_op jit(solution)/shard_map/ppermute | solution.py:440
  30.6 5.6 %collective-permute-start.9 = (f32[192,128]{1,0:T(8,128)S(1)}, f32[192,128]{1,0:T(8,128)S(1)}, u32[]{:S(2)}, u32[]{:S(2)}) collective-permute-start(f32[192,128]{1,0:T(8,128)S(1)} %get-tuple-element.65), channel_id=1, source_target_pairs={{0,12},{4,8},{8,4},{12,0},{16,28},{20,24},{24,20},{28,16},{1,13},{... | collective-permute-start | bytes 294920 | tf_op jit(solution)/shard_map/ppermute | solution.py:440
  36.9 4.7 %collective-permute-start.10 = (f32[192,128]{1,0:T(8,128)S(1)}, f32[192,128]{1,0:T(8,128)S(1)}, u32[]{:S(2)}, u32[]{:S(2)}) collective-permute-start(f32[192,128]{1,0:T(8,128)S(1)} %get-tuple-element.69), channel_id=1, source_target_pairs={{0,4},{4,0},{8,12},{12,8},{16,20},{20,16},{24,28},{28,24},{1,5},{5... | collective-permute-start | bytes 294920 | tf_op jit(solution)/shard_map/ppermute | solution.py:440
  38.4 4.6 %collective-permute-start.11 = (f32[192,128]{1,0:T(8,128)S(1)}, f32[192,128]{1,0:T(8,128)S(1)}, u32[]{:S(2)}, u32[]{:S(2)}) collective-permute-start(f32[192,128]{1,0:T(8,128)S(1)} %get-tuple-element.70), channel_id=1, source_target_pairs={{0,8},{4,12},{8,0},{12,4},{16,24},{20,28},{24,16},{28,20},{1,9},{5... | collective-permute-start | bytes 294920 | tf_op jit(solution)/shard_map/ppermute | solution.py:440
  38.7 5.5 %collective-permute-start.12 = (f32[192,128]{1,0:T(8,128)S(1)}, f32[192,128]{1,0:T(8,128)S(1)}, u32[]{:S(2)}, u32[]{:S(2)}) collective-permute-start(f32[192,128]{1,0:T(8,128)S(1)} %get-tuple-element.71), channel_id=1, source_target_pairs={{0,12},{4,8},{8,4},{12,0},{16,28},{20,24},{24,20},{28,16},{1,13},{... | collective-permute-start | bytes 294920 | tf_op jit(solution)/shard_map/ppermute | solution.py:440
  44.6 7.5 %collective-permute-start.13 = (f32[200,128]{1,0:T(8,128)S(1)}, f32[200,128]{1,0:T(8,128)S(1)}, u32[]{:S(2)}, u32[]{:S(2)}) collective-permute-start(f32[200,128]{1,0:T(8,128)S(1)} %get-tuple-element.74.refs_0_), channel_id=1, source_target_pairs={{0,16},{4,20},{8,24},{12,28},{16,0},{20,4},{24,8},{28,12},{1,17},{... | collective-permute-start | bytes 307208 | tf_op jit(solution)/shard_map/ppermute | solution.py:440
  53.3 3.6 %collective-permute-start.17 = (f32[2,2,64,384]{3,2,1,0:T(8,128)S(1)}, f32[2,2,64,384]{3,2,1,0:T(8,128)S(1)}, u32[]{:S(2)}, u32[]{:S(2)}) collective-permute-start(f32[2,2,64,384]{3,2,1,0:T(8,128)S(1)} %get-tuple-element.93), channel_id=1, source_target_pairs={{0,1},{1,0},{2,3},{3,2},{4,5},{5,4},{6,7},{7,6},{8,9},{9,8},{10,11... | collective-permute-start | bytes 1179656 | tf_op jit(solution)/shard_map/ppermute | solution.py:440
  53.4 12.3 %collective-permute-start.14 = (f32[392,128]{1,0:T(8,128)S(1)}, f32[392,128]{1,0:T(8,128)S(1)}, u32[]{:S(2)}, u32[]{:S(2)}) collective-permute-start(f32[392,128]{1,0:T(8,128)S(1)} %get-tuple-element.83), channel_id=1, source_target_pairs={{0,4},{4,0},{8,12},{12,8},{16,20},{20,16},{24,28},{28,24},{1,5},{5... | collective-permute-start | bytes 602120 | tf_op jit(solution)/shard_map/ppermute | solution.py:440
  54.9 10.8 %collective-permute-start.15 = (f32[392,128]{1,0:T(8,128)S(1)}, f32[392,128]{1,0:T(8,128)S(1)}, u32[]{:S(2)}, u32[]{:S(2)}) collective-permute-start(f32[392,128]{1,0:T(8,128)S(1)} %get-tuple-element.84), channel_id=1, source_target_pairs={{0,8},{4,12},{8,0},{12,4},{16,24},{20,28},{24,16},{28,20},{1,9},{5... | collective-permute-start | bytes 602120 | tf_op jit(solution)/shard_map/ppermute | solution.py:440
  54.9 15.1 %collective-permute-start.16 = (f32[392,128]{1,0:T(8,128)S(1)}, f32[392,128]{1,0:T(8,128)S(1)}, u32[]{:S(2)}, u32[]{:S(2)}) collective-permute-start(f32[392,128]{1,0:T(8,128)S(1)} %get-tuple-element.85), channel_id=1, source_target_pairs={{0,12},{4,8},{8,4},{12,0},{16,28},{20,24},{24,20},{28,16},{1,13},{... | collective-permute-start | bytes 602120 | tf_op jit(solution)/shard_map/ppermute | solution.py:440
  57.0 5.6 %collective-permute-start.18 = (f32[64,384]{1,0:T(8,128)S(1)}, f32[64,384]{1,0:T(8,128)S(1)}, u32[]{:S(2)}, u32[]{:S(2)}) collective-permute-start(f32[64,384]{1,0:T(8,128)S(1)} %get-tuple-element.95), channel_id=1, source_target_pairs={{0,2},{1,3},{2,0},{3,1},{4,6},{5,7},{6,4},{7,5},{8,10},{9,11},{10,... | collective-permute-start | bytes 294920 | tf_op jit(solution)/shard_map/ppermute | solution.py:440
  58.5 6.5 %collective-permute-start.20 = (f32[64,384]{1,0:T(8,128)S(1)}, f32[64,384]{1,0:T(8,128)S(1)}, u32[]{:S(2)}, u32[]{:S(2)}) collective-permute-start(f32[64,384]{1,0:T(8,128)S(1)} %get-tuple-element.98), channel_id=1, source_target_pairs={{0,2},{1,3},{2,0},{3,1},{4,6},{5,7},{6,4},{7,5},{8,10},{9,11},{10,... | collective-permute-start | bytes 294920 | tf_op jit(solution)/shard_map/ppermute | solution.py:440
  62.6 7.5 %copy-start.10 = (f32[8,64,64]{2,1,0:T(8,128)S(1)}, f32[8,64,64]{2,1,0:T(8,128)}, u32[]{:S(2)}) copy-start(f32[8,64,64]{2,1,0:T(8,128)} %refs_7_.1) | copy-start | bytes 393220
  62.6 9.8 %collective-permute-start.19 = (f32[64,384]{1,0:T(8,128)S(1)}, f32[64,384]{1,0:T(8,128)S(1)}, u32[]{:S(2)}, u32[]{:S(2)}) collective-permute-start(f32[64,384]{1,0:T(8,128)S(1)} %add.6), channel_id=1, source_target_pairs={{0,16},{1,20},{2,24},{3,28},{4,17},{5,21},{6,25},{7,29},{8,18},{9,... | collective-permute-start | bytes 294920 | tf_op jit(solution)/shard_map/ppermute | solution.py:570
  65.0 7.4 %collective-permute-start.21 = (f32[64,384]{1,0:T(8,128)S(1)}, f32[64,384]{1,0:T(8,128)S(1)}, u32[]{:S(2)}, u32[]{:S(2)}) collective-permute-start(f32[64,384]{1,0:T(8,128)S(1)} %add.7), channel_id=1, source_target_pairs={{0,0},{1,4},{2,8},{3,12},{4,1},{5,5},{6,9},{7,13},{8,2},{9,6},{10,... | collective-permute-start | bytes 294920 | tf_op jit(solution)/shard_map/ppermute | solution.py:570

commit v7 on v6

--- a/solution.py
+++ b/solution.py
@@ -377,7 +377,7 @@
     size = proj_ref.shape[1]
     high_g = g_ref.shape[0]
     me = lax.axis_index("sensor") % count
-    for partner, ref in enumerate(in_refs):
+    for partner, ref in enumerate(reversed(in_refs)):
         own = columns((me ^ partner) % count)
         g_ref[:, own] = ref[:high_g, :]
         q_ref[:, own] = ref[high_g:, :].astype(BF16)
@@ -440,9 +440,12 @@
     return lax.ppermute(a, axis, [(i, i ^ bit) for i in range(lax.axis_size(axis))])
 
 
-def trade(parts, axis):
-    got = {d: swap(parts[d], axis, d) for d in reversed(range(1, len(parts)))}
-    return [parts[0]] + [got[d] for d in sorted(got)]
+def trade(parts, axis, together=True):
+    order = [len(parts) - 1, *range(1, len(parts) - 1)]
+    got = [swap(parts[d], axis, d) for d in order]
+    if together:
+        got = lax.optimization_barrier(got)
+    return [parts[0], *got[1:], got[0]]
 
 
 def gather_halves(top, low, axis):
@@ -560,12 +563,12 @@
         flops=4 * product,
         scratch=[pltpu.VMEM((2, *half.shape), F32)],
     )
-    def turn(a, bit):
+    def turn(a, bit, flip=0):
         pairs = []
         for k in range(quads):
             for q in range(count):
                 for j in range(count):
-                    target = (k ^ bit) * count + j
+                    target = (k ^ bit) * count + (j ^ flip)
                     pairs.append(((k * count + q) * count + j, target * count + q))
         return lax.ppermute(a, ("sensor", "step"), pairs)
 
@@ -578,8 +581,7 @@
             (own_half, got_half),
         )
         away = away + swap(send_away, "step", 2)
-        kept = kept + swap(send_kept, "step", 2)
-        parts = (turn(away, 1), turn(kept, 0))
+        parts = (turn(away, 1), turn(send_kept, 0, 2), turn(after(kept, away), 0))
     else:
         kept, sent = call(
             functools.partial(core_kernel, count),
@@ -592,14 +594,14 @@
             kept + swap(sent, "step", 2), "sensor", 0, 0, tiled=True, axis_index_groups=groups
         )
         parts = (turn(blocks.sum(0), 0),)
-    messages = trade(messages, "sensor")
+    messages = trade(messages, "sensor", False)
     scale = 1.0 / math.sqrt(rows * lax.axis_size("step") * devices)
     out = shape((width // devices, LANES))
     grad_in = call(
         functools.partial(rows_kernel, steps, factor, count),
         "input_rows",
         shape((rows, width), BF16),
-        (*messages, *local_keys, feature_proj, wq_turned, wk_turned, wv_turned),
+        (*messages[::-1], *local_keys, feature_proj, wq_turned, wk_turned, wv_turned),
         flops=30 * product,
         scratch=[pltpu.VMEM((rows, width), BF16), pltpu.VMEM((packed.shape[0], width), F32)],
     )

time: 74 us -> 73 us (0.986)
  the two profiles are of different devices: /device:TPU:0 before, /device:TPU:24 now
where the time goes in v7:
time: 73 us; the launch traced here: 72.6 us
  waiting for transfers between devices  34.4 us (47%)
  starting transfers between devices  22 us (30%)
  Pallas kernels  9.74 us (13%)
  local copies, waits for them, and re-layouts  5.03 us (7%)
  between operations  1.47 us (2%)
    ppermute x19, waiting for transfers between devices, swap(): lax.ppermute(a, axis, [(i, i ^ bit) for i in range(lax.axis_size(axis))])  29.1 us
    ppermute x19, starting transfers between devices, swap(): lax.ppermute(a, axis, [(i, i ^ bit) for i in range(lax.axis_size(axis))])  18.3 us
    pallas_call x13, Pallas kernels, call(): pl.pallas_call(kernel, name=name, out_shape=outs, in_specs=[SMEM] * smem...  9.74 us
    ppermute x3, waiting for transfers between devices, turn(): return lax.ppermute(a, ('sensor', 'step'), pairs)  5.34 us
    unnamed x24, local copies, waits for them, and re-layouts  5.03 us
    ppermute x3, starting transfers between devices, turn(): return lax.ppermute(a, ('sensor', 'step'), pairs)  3.69 us
  transfers between devices with their start and end apart: 22, of which 17 were waited for; matrix products, arithmetic and copies ran while one was open for 0% of the time, Pallas kernels for 7%

profile of v7, /device:TPU:24, one launch (start us, length us, event | category | flops | bytes accessed | tf_op | source)
XLA Modules:
  0.0 72.6 jit_solution(5191029802301056988)
XLA Ops:
  1.3 0.9 %copy-done.7 = bf16[3,64,512]{2,1,0:T(8,128)(2,1)S(1)} copy-done((bf16[3,64,512]{2,1,0:T(8,128)(2,1)S(1)}, bf16[3,64,512]{2,1,0:T(8,128)(2,1)}, u32[]{:S(2)}) %copy-start.7) | copy-done | bytes 196632
  2.2 1.6 %collective-permute-start = (f32[104,512]{1,0:T(8,128)S(1)}, f32[104,512]{1,0:T(8,128)S(1)}, u32[]{:S(2)}, u32[]{:S(2)}) collective-permute-start(f32[104,512]{1,0:T(8,128)S(1)} %get-tuple-element.60.refs_0_), channel_id=1, source_target_pairs={{0,4},{4,0},{8,12},{12,8},{16,20},{20,16},{24,28},{28,24},{1,5},{5... | collective-permute-start | bytes 638984 | tf_op jit(solution)/shard_map/ppermute | solution.py:440
  3.8 0.4 collective-permute-start.4
  4.3 1.6 %collective-permute-start.1 = (f32[104,512]{1,0:T(8,128)S(1)}, f32[104,512]{1,0:T(8,128)S(1)}, u32[]{:S(2)}, u32[]{:S(2)}) collective-permute-start(f32[104,512]{1,0:T(8,128)S(1)} %get-tuple-element.60.refs_0_), channel_id=1, source_target_pairs={{0,8},{4,12},{8,0},{12,4},{16,24},{20,28},{24,16},{28,20},{1,9},{5... | collective-permute-start | bytes 638984 | tf_op jit(solution)/shard_map/ppermute | solution.py:440
  5.8 0.5 collective-permute-start.3
  6.4 4.1 %collective-permute-done.refs_1_ = f32[104,512]{1,0:T(8,128)S(1)} collective-permute-done((f32[104,512]{1,0:T(8,128)S(1)}, f32[104,512]{1,0:T(8,128)S(1)}, u32[]{:S(2)}, u32[]{:S(2)}) %collective-permute-start) | collective-permute-done | bytes 213024 | tf_op jit(solution)/shard_map/ppermute | solution.py:440
  10.4 0.4 collective-permute-start.2
  10.9 1.1 %collective-permute-done.4.refs_6_ = f32[104,512]{1,0:T(8,128)S(1)} collective-permute-done((f32[104,512]{1,0:T(8,128)S(1)}, f32[104,512]{1,0:T(8,128)S(1)}, u32[]{:S(2)}, u32[]{:S(2)}) %collective-permute-start.4) | collective-permute-done | bytes 213024 | tf_op jit(solution)/shard_map/ppermute | solution.py:440
  12.0 0.5 collective-permute-start.5
  12.5 1.0 %copy-done = bf16[512,512]{1,0:T(8,128)(2,1)S(1)} copy-done((bf16[512,512]{1,0:T(8,128)(2,1)S(1)}, bf16[512,512]{1,0:T(8,128)(2,1)}, u32[]{:S(2)}) %copy-start) | copy-done | bytes 524312
  13.6 1.0 %copy-done.2 = bf16[512,512]{1,0:T(8,128)(2,1)S(1)} copy-done((bf16[512,512]{1,0:T(8,128)(2,1)S(1)}, bf16[512,512]{1,0:T(8,128)(2,1)}, u32[]{:S(2)}) %copy-start.2) | copy-done | bytes 524312
  14.6 1.0 %copy-done.4 = bf16[512,512]{1,0:T(8,128)(2,1)S(1)} copy-done((bf16[512,512]{1,0:T(8,128)(2,1)S(1)}, bf16[512,512]{1,0:T(8,128)(2,1)}, u32[]{:S(2)}) %copy-start.4) | copy-done | bytes 524312
  15.6 0.9 %copy-done.9 = f32[8,64,64]{2,1,0:T(8,128)S(1)} copy-done((f32[8,64,64]{2,1,0:T(8,128)S(1)}, f32[8,64,64]{2,1,0:T(8,128)}, u32[]{:S(2)}) %copy-start.9) | copy-done | bytes 131096
  16.6 0.7 local_keys.1
  17.3 0.0 collective-permute-done.1.refs_2_
  17.3 0.0 collective-permute-done.3.refs_5_
  17.3 2.3 %collective-permute-done.2.refs_3_ = f32[104,512]{1,0:T(8,128)S(1)} collective-permute-done((f32[104,512]{1,0:T(8,128)S(1)}, f32[104,512]{1,0:T(8,128)S(1)}, u32[]{:S(2)}, u32[]{:S(2)}) %collective-permute-start.2) | collective-permute-done | bytes 213024 | tf_op jit(solution)/shard_map/ppermute | solution.py:440
  19.7 0.0 collective-permute-done.5.refs_7_
  19.7 1.1 %keys.1 = (bf16[768,512]{1,0:T(8,128)(2,1)S(1)}, f32[768,128]{1,0:T(8,128)S(1)}, f32[768,128]{1,0:T(8,128)S(1)}, f32[768,128]{1,0:T(8,128)S(1)}, f32[200,128]{1,0:T(8,128)S(1)}) custom-call(f32[104,512]{1,0:T(8,128)S(1)} %get-tuple-element.60.refs_0_, f32[104,512]{1,0:T(8,128)S(1)} %collective-permute-done.refs_1_, ...), custom_call_target="tpu_custom_call" | custom-call | flops 301989888 | bytes 4067328 | tf_op jit(solution)/shard_map/keys/pallas_call | solution.py:419
  20.7 0.4 collective-permute-start.6
  21.2 0.0 copy-done.8
  21.2 0.0 copy-start.6
  21.2 0.9 %queries.1 = (f32[768,128]{1,0:T(8,128)S(1)}, f32[768,128]{1,0:T(8,128)S(1)}, f32[192,256]{1,0:T(8,128)S(1)}) custom-call(s32[1]{0:T(128)S(6)} %copy.13.live_ref, bf16[768,512]{1,0:T(8,128)(2,1)S(1)} %get-tuple-element.66.x_ref.refs_0_, bf16[192,512]{1,0:T(8,128)(2,1)S(1)} %bitcast.5, bf16[512,128]{1,0:T(8,128)(2,1)S(1)} %get-tuple-element.67.wq_ref, ...), custom_call_target="tpu_custom_call" | custom-call | flops 201326592 | bytes 2392068 | tf_op jit(solution)/shard_map/queries/pallas_call | solution.py:419
  22.1 0.0 copy-start.1
  22.1 5.2 %collective-permute-done.6.refs_1_ = f32[200,128]{1,0:T(8,128)S(1)} collective-permute-done((f32[200,128]{1,0:T(8,128)S(1)}, f32[200,128]{1,0:T(8,128)S(1)}, u32[]{:S(2)}, u32[]{:S(2)}) %collective-permute-start.6) | collective-permute-done | bytes 102432 | tf_op jit(solution)/shard_map/ppermute | solution.py:440
  27.4 0.4 attend.1
  27.7 0.1 collective-permute-start.7
  27.8 1.0 %collective-permute-start.8 = (f32[192,128]{1,0:T(8,128)S(1)}, f32[192,128]{1,0:T(8,128)S(1)}, u32[]{:S(2)}, u32[]{:S(2)}) collective-permute-start(f32[192,128]{1,0:T(8,128)S(1)} %get-tuple-element.71), channel_id=1, source_target_pairs={{0,4},{4,0},{8,12},{12,8},{16,20},{20,16},{24,28},{28,24},{1,5},{5... | collective-permute-start | bytes 294920 | tf_op jit(solution)/shard_map/ppermute | solution.py:440
  28.8 2.5 %collective-permute-start.9 = (f32[192,128]{1,0:T(8,128)S(1)}, f32[192,128]{1,0:T(8,128)S(1)}, u32[]{:S(2)}, u32[]{:S(2)}) collective-permute-start(f32[192,128]{1,0:T(8,128)S(1)} %get-tuple-element.72), channel_id=1, source_target_pairs={{0,8},{4,12},{8,0},{12,4},{16,24},{20,28},{24,16},{28,20},{1,9},{5... | collective-permute-start | bytes 294920 | tf_op jit(solution)/shard_map/ppermute | solution.py:440
  31.3 0.7 transposes.1
  32.0 1.4 %collective-permute-done.7.refs_3_ = f32[192,128]{1,0:T(8,128)S(1)} collective-permute-done((f32[192,128]{1,0:T(8,128)S(1)}, f32[192,128]{1,0:T(8,128)S(1)}, u32[]{:S(2)}, u32[]{:S(2)}) %collective-permute-start.7) | collective-permute-done | bytes 98336 | tf_op jit(solution)/shard_map/ppermute | solution.py:440
  33.4 0.1 collective-permute-done.8.refs_1_
  33.6 0.7 collective-permute-done.9.refs_2_
  34.3 0.7 %feed_forward.1 = (f32[192,128]{1,0:T(8,128)S(1)}, f32[192,128]{1,0:T(8,128)S(1)}, f32[192,128]{1,0:T(8,128)S(1)}, f32[192,128]{1,0:T(8,128)S(1)}) custom-call(f32[192,128]{1,0:T(8,128)S(1)} %get-tuple-element.69.refs_0_, f32[192,128]{1,0:T(8,128)S(1)} %collective-permute-done.8.refs_1_, f32[192,128]{1,0:T(8,128)S(1)} %collective-permute-done.9.refs_2_, ...), custom_call_target="tpu_custom_call" | custom-call | flops 100663296 | bytes 1507328 | tf_op jit(solution)/shard_map/feed_forward/pallas_call | solution.py:419
  35.0 1.6 %collective-permute-start.10 = (f32[192,128]{1,0:T(8,128)S(1)}, f32[192,128]{1,0:T(8,128)S(1)}, u32[]{:S(2)}, u32[]{:S(2)}) collective-permute-start(f32[192,128]{1,0:T(8,128)S(1)} %get-tuple-element.79), channel_id=1, source_target_pairs={{0,12},{4,8},{8,4},{12,0},{16,28},{20,24},{24,20},{28,16},{1,13},{... | collective-permute-start | bytes 294920 | tf_op jit(solution)/shard_map/ppermute | solution.py:440
  36.7 2.4 %collective-permute-start.11 = (f32[192,128]{1,0:T(8,128)S(1)}, f32[192,128]{1,0:T(8,128)S(1)}, u32[]{:S(2)}, u32[]{:S(2)}) collective-permute-start(f32[192,128]{1,0:T(8,128)S(1)} %get-tuple-element.80), channel_id=1, source_target_pairs={{0,4},{4,0},{8,12},{12,8},{16,20},{20,16},{24,28},{28,24},{1,5},{5... | collective-permute-start | bytes 294920 | tf_op jit(solution)/shard_map/ppermute | solution.py:440
  39.0 0.0 collective-permute-start.12
  39.1 1.6 %collective-permute-done.10.refs_3_ = f32[192,128]{1,0:T(8,128)S(1)} collective-permute-done((f32[192,128]{1,0:T(8,128)S(1)}, f32[192,128]{1,0:T(8,128)S(1)}, u32[]{:S(2)}, u32[]{:S(2)}) %collective-permute-start.10) | collective-permute-done | bytes 98336 | tf_op jit(solution)/shard_map/ppermute | solution.py:440
  40.6 1.1 %collective-permute-done.11.refs_1_ = f32[192,128]{1,0:T(8,128)S(1)} collective-permute-done((f32[192,128]{1,0:T(8,128)S(1)}, f32[192,128]{1,0:T(8,128)S(1)}, u32[]{:S(2)}, u32[]{:S(2)}) %collective-permute-start.11) | collective-permute-done | bytes 98336 | tf_op jit(solution)/shard_map/ppermute | solution.py:440
  41.7 2.7 %collective-permute-done.12.refs_2_ = f32[192,128]{1,0:T(8,128)S(1)} collective-permute-done((f32[192,128]{1,0:T(8,128)S(1)}, f32[192,128]{1,0:T(8,128)S(1)}, u32[]{:S(2)}, u32[]{:S(2)}) %collective-permute-start.12) | collective-permute-done | bytes 98336 | tf_op jit(solution)/shard_map/ppermute | solution.py:440
  44.3 0.4 grad_summary.1
  44.7 0.1 collective-permute-start.13
  44.8 0.6 query_back.1.refs_6_
  45.4 5.1 %collective-permute-done.13.refs_1_ = f32[200,128]{1,0:T(8,128)S(1)} collective-permute-done((f32[200,128]{1,0:T(8,128)S(1)}, f32[200,128]{1,0:T(8,128)S(1)}, u32[]{:S(2)}, u32[]{:S(2)}) %collective-permute-start.13) | collective-permute-done | bytes 102432 | tf_op jit(solution)/shard_map/ppermute | solution.py:440
  50.5 1.1 %key_back.1 = (f32[392,128]{1,0:T(8,128)S(1)}, f32[392,128]{1,0:T(8,128)S(1)}, f32[392,128]{1,0:T(8,128)S(1)}, f32[392,128]{1,0:T(8,128)S(1)}, f32[2,2,64,384]{3...) custom-call(f32[200,128]{1,0:T(8,128)S(1)} %get-tuple-element.87.refs_0_, f32[200,128]{1,0:T(8,128)S(1)} %collective-permute-done.13.refs_1_, ...), custom_call_target="tpu_custom_call" | custom-call | flops 402653184 | bytes 3989504 | tf_op jit(solution)/shard_map/key_back/pallas_call | solution.py:419
  51.6 0.1 collective-permute-start.17
  51.7 0.1 collective-permute-start.14
  51.7 2.1 %collective-permute-start.15 = (f32[392,128]{1,0:T(8,128)S(1)}, f32[392,128]{1,0:T(8,128)S(1)}, u32[]{:S(2)}, u32[]{:S(2)}) collective-permute-start(f32[392,128]{1,0:T(8,128)S(1)} %get-tuple-element.96), channel_id=1, source_target_pairs={{0,8},{4,12},{8,0},{12,4},{16,24},{20,28},{24,16},{28,20},{1,9},{5... | collective-permute-start | bytes 602120 | tf_op jit(solution)/shard_map/ppermute | solution.py:440
  53.8 1.4 %collective-permute-start.16 = (f32[392,128]{1,0:T(8,128)S(1)}, f32[392,128]{1,0:T(8,128)S(1)}, u32[]{:S(2)}, u32[]{:S(2)}) collective-permute-start(f32[392,128]{1,0:T(8,128)S(1)} %get-tuple-element.97), channel_id=1, source_target_pairs={{0,4},{4,0},{8,12},{12,8},{16,20},{20,16},{24,28},{28,24},{1,5},{5... | collective-permute-start | bytes 602120 | tf_op jit(solution)/shard_map/ppermute | solution.py:440
  55.2 0.0 collective-permute-done.17.got_ref
  55.3 0.0 copy-start.10
  55.3 1.6 %collective-permute-start.18 = (f32[64,384]{1,0:T(8,128)S(1)}, f32[64,384]{1,0:T(8,128)S(1)}, u32[]{:S(2)}, u32[]{:S(2)}) collective-permute-start(f32[64,384]{1,0:T(8,128)S(1)} %get-tuple-element.108), channel_id=1, source_target_pairs={{0,2},{1,3},{2,0},{3,1},{4,6},{5,7},{6,4},{7,5},{8,10},{9,11},{10,... | collective-permute-start | bytes 294920 | tf_op jit(solution)/shard_map/ppermute | solution.py:440
  56.8 0.5 collective-permute-start.20
  57.4 2.6 %collective-permute-done.18 = f32[64,384]{1,0:T(8,128)S(1)} collective-permute-done((f32[64,384]{1,0:T(8,128)S(1)}, f32[64,384]{1,0:T(8,128)S(1)}, u32[]{:S(2)}, u32[]{:S(2)}) %collective-permute-start.18) | collective-permute-done | bytes 98336 | tf_op jit(solution)/shard_map/ppermute | solution.py:440
  60.0 0.3 collective-permute-start.19
  60.3 0.2 collective-permute-done.14.refs_0_
  60.5 2.8 %collective-permute-start.21 = (f32[64,384]{1,0:T(8,128)S(1)}, f32[64,384]{1,0:T(8,128)S(1)}, u32[]{:S(2)}, u32[]{:S(2)}) collective-permute-start(f32[64,384]{1,0:T(8,128)S(1)} %get-tuple-element.112), channel_id=1, source_target_pairs={{0,0},{1,4},{2,8},{3,12},{4,1},{5,5},{6,9},{7,13},{8,2},{9,6},{10,... | collective-permute-start | bytes 294920 | tf_op jit(solution)/shard_map/ppermute | solution.py:573
  63.3 0.6 collective-permute-done.15.refs_1_
  63.9 0.3 collective-permute-done.16.refs_2_
  64.3 2.4 %input_rows.1 = bf16[192,512]{1,0:T(8,128)(2,1)} custom-call(f32[392,128]{1,0:T(8,128)S(1)} %collective-permute-done.14.refs_0_, f32[392,128]{1,0:T(8,128)S(1)} %collective-permute-done.15.refs_1_, f32[392,128]{1,0:T(8,128)S(1)} %collective-permute-done.16.refs_2_, f32[392,128]{1,0:T(8,128)S(1)} %get-tuple-element.98.refs_3_, ...), custom_call_target="tpu_custom_call" | custom-call | flops 3019898880 | bytes 3883008 | tf_op jit(solution)/shard_map/input_rows/pallas_call | solution.py:419
  66.6 1.6 %collective-permute-done.19.refs_0_ = f32[64,384]{1,0:T(8,128)S(1)} collective-permute-done((f32[64,384]{1,0:T(8,128)S(1)}, f32[64,384]{1,0:T(8,128)S(1)}, u32[]{:S(2)}, u32[]{:S(2)}) %collective-permute-start.19) | collective-permute-done | bytes 98336 | tf_op jit(solution)/shard_map/ppermute | solution.py:573
  68.2 0.0 collective-permute-done.20.refs_1_
  68.2 3.7 %collective-permute-done.21.refs_2_ = f32[64,384]{1,0:T(8,128)S(1)} collective-permute-done((f32[64,384]{1,0:T(8,128)S(1)}, f32[64,384]{1,0:T(8,128)S(1)}, u32[]{:S(2)}, u32[]{:S(2)}) %collective-permute-start.21) | collective-permute-done | bytes 98336 | tf_op jit(solution)/shard_map/ppermute | solution.py:573
  72.0 0.7 weight_sums.1
  (18 shorter events, 0.1 us)
Async XLA Ops:
  1.3 0.9 %copy-start.7 = (bf16[3,64,512]{2,1,0:T(8,128)(2,1)S(1)}, bf16[3,64,512]{2,1,0:T(8,128)(2,1)}, u32[]{:S(2)}) copy-start(bf16[3,64,512]{2,1,0:T(8,128)(2,1)} %param.9) | copy-start | bytes 589828
  2.2 8.2 %collective-permute-start = (f32[104,512]{1,0:T(8,128)S(1)}, f32[104,512]{1,0:T(8,128)S(1)}, u32[]{:S(2)}, u32[]{:S(2)}) collective-permute-start(f32[104,512]{1,0:T(8,128)S(1)} %get-tuple-element.60.refs_0_), channel_id=1, source_target_pairs={{0,4},{4,0},{8,12},{12,8},{16,20},{20,16},{24,28},{28,24},{1,5},{5... | collective-permute-start | bytes 638984 | tf_op jit(solution)/shard_map/ppermute | solution.py:440
  3.8 8.2 %collective-permute-start.4 = (f32[104,512]{1,0:T(8,128)S(1)}, f32[104,512]{1,0:T(8,128)S(1)}, u32[]{:S(2)}, u32[]{:S(2)}) collective-permute-start(f32[104,512]{1,0:T(8,128)S(1)} %get-tuple-element.61.refs_4_), channel_id=1, source_target_pairs={{0,8},{4,12},{8,0},{12,4},{16,24},{20,28},{24,16},{28,20},{1,9},{5... | collective-permute-start | bytes 638984 | tf_op jit(solution)/shard_map/ppermute | solution.py:440
  4.3 13.0 %collective-permute-start.1 = (f32[104,512]{1,0:T(8,128)S(1)}, f32[104,512]{1,0:T(8,128)S(1)}, u32[]{:S(2)}, u32[]{:S(2)}) collective-permute-start(f32[104,512]{1,0:T(8,128)S(1)} %get-tuple-element.60.refs_0_), channel_id=1, source_target_pairs={{0,8},{4,12},{8,0},{12,4},{16,24},{20,28},{24,16},{28,20},{1,9},{5... | collective-permute-start | bytes 638984 | tf_op jit(solution)/shard_map/ppermute | solution.py:440
  5.8 11.5 %collective-permute-start.3 = (f32[104,512]{1,0:T(8,128)S(1)}, f32[104,512]{1,0:T(8,128)S(1)}, u32[]{:S(2)}, u32[]{:S(2)}) collective-permute-start(f32[104,512]{1,0:T(8,128)S(1)} %get-tuple-element.61.refs_4_), channel_id=1, source_target_pairs={{0,4},{4,0},{8,12},{12,8},{16,20},{20,16},{24,28},{28,24},{1,5},{5... | collective-permute-start | bytes 638984 | tf_op jit(solution)/shard_map/ppermute | solution.py:440
  10.4 9.2 %collective-permute-start.2 = (f32[104,512]{1,0:T(8,128)S(1)}, f32[104,512]{1,0:T(8,128)S(1)}, u32[]{:S(2)}, u32[]{:S(2)}) collective-permute-start(f32[104,512]{1,0:T(8,128)S(1)} %collective-permute-done.refs_1_), channel_id=1, source_target_pairs={{0,8},{4,12},{8,0},{12,4},{16,24},{20,28},{24,16},{28,20},{1,9},{5... | collective-permute-start | bytes 638984 | tf_op jit(solution)/shard_map/ppermute | solution.py:440
  12.0 7.7 %collective-permute-start.5 = (f32[104,512]{1,0:T(8,128)S(1)}, f32[104,512]{1,0:T(8,128)S(1)}, u32[]{:S(2)}, u32[]{:S(2)}) collective-permute-start(f32[104,512]{1,0:T(8,128)S(1)} %collective-permute-done.4.refs_6_), channel_id=1, source_target_pairs={{0,4},{4,0},{8,12},{12,8},{16,20},{20,16},{24,28},{28,24},{1,5},{5... | collective-permute-start | bytes 638984 | tf_op jit(solution)/shard_map/ppermute | solution.py:440
  12.5 1.0 %copy-start = (bf16[512,512]{1,0:T(8,128)(2,1)S(1)}, bf16[512,512]{1,0:T(8,128)(2,1)}, u32[]{:S(2)}) copy-start(bf16[512,512]{1,0:T(8,128)(2,1)} %refs_1_.1) | copy-start | bytes 1572868
  13.6 1.0 %copy-start.2 = (bf16[512,512]{1,0:T(8,128)(2,1)S(1)}, bf16[512,512]{1,0:T(8,128)(2,1)}, u32[]{:S(2)}) copy-start(bf16[512,512]{1,0:T(8,128)(2,1)} %refs_2_.1) | copy-start | bytes 1572868
  14.6 1.0 %copy-start.4 = (bf16[512,512]{1,0:T(8,128)(2,1)S(1)}, bf16[512,512]{1,0:T(8,128)(2,1)}, u32[]{:S(2)}) copy-start(bf16[512,512]{1,0:T(8,128)(2,1)} %refs_3_.1) | copy-start | bytes 1572868
  15.6 0.9 %copy-start.9 = (f32[8,64,64]{2,1,0:T(8,128)S(1)}, f32[8,64,64]{2,1,0:T(8,128)}, u32[]{:S(2)}) copy-start(f32[8,64,64]{2,1,0:T(8,128)} %refs_7_.1) | copy-start | bytes 393220
  19.7 1.5 %copy-start.8 = (bf16[256,512]{1,0:T(8,128)(2,1)S(1)}, bf16[256,512]{1,0:T(8,128)(2,1)}, u32[]{:S(2)}) copy-start(bf16[256,512]{1,0:T(8,128)(2,1)} %wd_ref.1) | copy-start | bytes 786436
  19.7 1.5 %copy-start.11 = (bf16[3,64,512]{2,1,0:T(8,128)(2,1)S(1)}, bf16[3,64,512]{2,1,0:T(8,128)(2,1)}, u32[]{:S(2)}) copy-start(bf16[3,64,512]{2,1,0:T(8,128)(2,1)} %param.10) | copy-start | bytes 589828
  20.7 6.6 %collective-permute-start.6 = (f32[200,128]{1,0:T(8,128)S(1)}, f32[200,128]{1,0:T(8,128)S(1)}, u32[]{:S(2)}, u32[]{:S(2)}) collective-permute-start(f32[200,128]{1,0:T(8,128)S(1)} %get-tuple-element.65.refs_0_), channel_id=1, source_target_pairs={{0,16},{4,20},{8,24},{12,28},{16,0},{20,4},{24,8},{28,12},{1,17},{... | collective-permute-start | bytes 307208 | tf_op jit(solution)/shard_map/ppermute | solution.py:440
  21.2 10.1 %copy-start.3 = (bf16[512,512]{1,0:T(8,128)(2,1)S(1)}, bf16[512,512]{1,0:T(8,128)(2,1)}, u32[]{:S(2)}) copy-start(bf16[512,512]{1,0:T(8,128)(2,1)} %refs_2_.1) | copy-start | bytes 1572868
  21.2 10.1 %copy-start.5 = (bf16[512,512]{1,0:T(8,128)(2,1)S(1)}, bf16[512,512]{1,0:T(8,128)(2,1)}, u32[]{:S(2)}) copy-start(bf16[512,512]{1,0:T(8,128)(2,1)} %refs_3_.1) | copy-start | bytes 1572868
  21.2 10.1 %copy-start.6 = (bf16[512,256]{1,0:T(8,128)(2,1)S(1)}, bf16[512,256]{1,0:T(8,128)(2,1)}, u32[]{:S(2)}) copy-start(bf16[512,256]{1,0:T(8,128)(2,1)} %refs_5_.1) | copy-start | bytes 786436
  22.1 9.2 %copy-start.1 = (bf16[512,512]{1,0:T(8,128)(2,1)S(1)}, bf16[512,512]{1,0:T(8,128)(2,1)}, u32[]{:S(2)}) copy-start(bf16[512,512]{1,0:T(8,128)(2,1)} %refs_1_.1) | copy-start | bytes 1572868
  27.7 5.7 %collective-permute-start.7 = (f32[192,128]{1,0:T(8,128)S(1)}, f32[192,128]{1,0:T(8,128)S(1)}, u32[]{:S(2)}, u32[]{:S(2)}) collective-permute-start(f32[192,128]{1,0:T(8,128)S(1)} %get-tuple-element.70), channel_id=1, source_target_pairs={{0,12},{4,8},{8,4},{12,0},{16,28},{20,24},{24,20},{28,16},{1,13},{... | collective-permute-start | bytes 294920 | tf_op jit(solution)/shard_map/ppermute | solution.py:440
  27.8 5.7 %collective-permute-start.8 = (f32[192,128]{1,0:T(8,128)S(1)}, f32[192,128]{1,0:T(8,128)S(1)}, u32[]{:S(2)}, u32[]{:S(2)}) collective-permute-start(f32[192,128]{1,0:T(8,128)S(1)} %get-tuple-element.71), channel_id=1, source_target_pairs={{0,4},{4,0},{8,12},{12,8},{16,20},{20,16},{24,28},{28,24},{1,5},{5... | collective-permute-start | bytes 294920 | tf_op jit(solution)/shard_map/ppermute | solution.py:440
  28.8 5.4 %collective-permute-start.9 = (f32[192,128]{1,0:T(8,128)S(1)}, f32[192,128]{1,0:T(8,128)S(1)}, u32[]{:S(2)}, u32[]{:S(2)}) collective-permute-start(f32[192,128]{1,0:T(8,128)S(1)} %get-tuple-element.72), channel_id=1, source_target_pairs={{0,8},{4,12},{8,0},{12,4},{16,24},{20,28},{24,16},{28,20},{1,9},{5... | collective-permute-start | bytes 294920 | tf_op jit(solution)/shard_map/ppermute | solution.py:440
  35.0 5.6 %collective-permute-start.10 = (f32[192,128]{1,0:T(8,128)S(1)}, f32[192,128]{1,0:T(8,128)S(1)}, u32[]{:S(2)}, u32[]{:S(2)}) collective-permute-start(f32[192,128]{1,0:T(8,128)S(1)} %get-tuple-element.79), channel_id=1, source_target_pairs={{0,12},{4,8},{8,4},{12,0},{16,28},{20,24},{24,20},{28,16},{1,13},{... | collective-permute-start | bytes 294920 | tf_op jit(solution)/shard_map/ppermute | solution.py:440
  36.7 5.0 %collective-permute-start.11 = (f32[192,128]{1,0:T(8,128)S(1)}, f32[192,128]{1,0:T(8,128)S(1)}, u32[]{:S(2)}, u32[]{:S(2)}) collective-permute-start(f32[192,128]{1,0:T(8,128)S(1)} %get-tuple-element.80), channel_id=1, source_target_pairs={{0,4},{4,0},{8,12},{12,8},{16,20},{20,16},{24,28},{28,24},{1,5},{5... | collective-permute-start | bytes 294920 | tf_op jit(solution)/shard_map/ppermute | solution.py:440
  39.0 5.3 %collective-permute-start.12 = (f32[192,128]{1,0:T(8,128)S(1)}, f32[192,128]{1,0:T(8,128)S(1)}, u32[]{:S(2)}, u32[]{:S(2)}) collective-permute-start(f32[192,128]{1,0:T(8,128)S(1)} %get-tuple-element.81), channel_id=1, source_target_pairs={{0,8},{4,12},{8,0},{12,4},{16,24},{20,28},{24,16},{28,20},{1,9},{5... | collective-permute-start | bytes 294920 | tf_op jit(solution)/shard_map/ppermute | solution.py:440
  44.7 5.7 %collective-permute-start.13 = (f32[200,128]{1,0:T(8,128)S(1)}, f32[200,128]{1,0:T(8,128)S(1)}, u32[]{:S(2)}, u32[]{:S(2)}) collective-permute-start(f32[200,128]{1,0:T(8,128)S(1)} %get-tuple-element.87.refs_0_), channel_id=1, source_target_pairs={{0,16},{4,20},{8,24},{12,28},{16,0},{20,4},{24,8},{28,12},{1,17},{... | collective-permute-start | bytes 307208 | tf_op jit(solution)/shard_map/ppermute | solution.py:440
  51.6 3.6 %collective-permute-start.17 = (f32[2,2,64,384]{3,2,1,0:T(8,128)S(1)}, f32[2,2,64,384]{3,2,1,0:T(8,128)S(1)}, u32[]{:S(2)}, u32[]{:S(2)}) collective-permute-start(f32[2,2,64,384]{3,2,1,0:T(8,128)S(1)} %get-tuple-element.106), channel_id=1, source_target_pairs={{0,1},{1,0},{2,3},{3,2},{4,5},{5,4},{6,7},{7,6},{8,9},{9,8},{10,11... | collective-permute-start | bytes 1179656 | tf_op jit(solution)/shard_map/ppermute | solution.py:440
  51.7 8.8 %collective-permute-start.14 = (f32[392,128]{1,0:T(8,128)S(1)}, f32[392,128]{1,0:T(8,128)S(1)}, u32[]{:S(2)}, u32[]{:S(2)}) collective-permute-start(f32[392,128]{1,0:T(8,128)S(1)} %get-tuple-element.95), channel_id=1, source_target_pairs={{0,12},{4,8},{8,4},{12,0},{16,28},{20,24},{24,20},{28,16},{1,13},{... | collective-permute-start | bytes 602120 | tf_op jit(solution)/shard_map/ppermute | solution.py:440
  51.7 12.2 %collective-permute-start.15 = (f32[392,128]{1,0:T(8,128)S(1)}, f32[392,128]{1,0:T(8,128)S(1)}, u32[]{:S(2)}, u32[]{:S(2)}) collective-permute-start(f32[392,128]{1,0:T(8,128)S(1)} %get-tuple-element.96), channel_id=1, source_target_pairs={{0,8},{4,12},{8,0},{12,4},{16,24},{20,28},{24,16},{28,20},{1,9},{5... | collective-permute-start | bytes 602120 | tf_op jit(solution)/shard_map/ppermute | solution.py:440
  53.8 10.4 %collective-permute-start.16 = (f32[392,128]{1,0:T(8,128)S(1)}, f32[392,128]{1,0:T(8,128)S(1)}, u32[]{:S(2)}, u32[]{:S(2)}) collective-permute-start(f32[392,128]{1,0:T(8,128)S(1)} %get-tuple-element.97), channel_id=1, source_target_pairs={{0,4},{4,0},{8,12},{12,8},{16,20},{20,16},{24,28},{28,24},{1,5},{5... | collective-permute-start | bytes 602120 | tf_op jit(solution)/shard_map/ppermute | solution.py:440
  55.3 9.0 %copy-start.10 = (f32[8,64,64]{2,1,0:T(8,128)S(1)}, f32[8,64,64]{2,1,0:T(8,128)}, u32[]{:S(2)}) copy-start(f32[8,64,64]{2,1,0:T(8,128)} %refs_7_.1) | copy-start | bytes 393220
  55.3 4.7 %collective-permute-start.18 = (f32[64,384]{1,0:T(8,128)S(1)}, f32[64,384]{1,0:T(8,128)S(1)}, u32[]{:S(2)}, u32[]{:S(2)}) collective-permute-start(f32[64,384]{1,0:T(8,128)S(1)} %get-tuple-element.108), channel_id=1, source_target_pairs={{0,2},{1,3},{2,0},{3,1},{4,6},{5,7},{6,4},{7,5},{8,10},{9,11},{10,... | collective-permute-start | bytes 294920 | tf_op jit(solution)/shard_map/ppermute | solution.py:440
  56.8 11.4 %collective-permute-start.20 = (f32[64,384]{1,0:T(8,128)S(1)}, f32[64,384]{1,0:T(8,128)S(1)}, u32[]{:S(2)}, u32[]{:S(2)}) collective-permute-start(f32[64,384]{1,0:T(8,128)S(1)} %get-tuple-element.110), channel_id=1, source_target_pairs={{0,8},{1,12},{2,0},{3,4},{4,9},{5,13},{6,1},{7,5},{8,10},{9,14},{1... | collective-permute-start | bytes 294920 | tf_op jit(solution)/shard_map/ppermute | solution.py:573
  60.0 8.2 %collective-permute-start.19 = (f32[64,384]{1,0:T(8,128)S(1)}, f32[64,384]{1,0:T(8,128)S(1)}, u32[]{:S(2)}, u32[]{:S(2)}) collective-permute-start(f32[64,384]{1,0:T(8,128)S(1)} %add.3), channel_id=1, source_target_pairs={{0,16},{1,20},{2,24},{3,28},{4,17},{5,21},{6,25},{7,29},{8,18},{9,... | collective-permute-start | bytes 294920 | tf_op jit(solution)/shard_map/ppermute | solution.py:573
  60.5 11.5 %collective-permute-start.21 = (f32[64,384]{1,0:T(8,128)S(1)}, f32[64,384]{1,0:T(8,128)S(1)}, u32[]{:S(2)}, u32[]{:S(2)}) collective-permute-start(f32[64,384]{1,0:T(8,128)S(1)} %get-tuple-element.112), channel_id=1, source_target_pairs={{0,0},{1,4},{2,8},{3,12},{4,1},{5,5},{6,9},{7,13},{8,2},{9,6},{10,... | collective-permute-start | bytes 294920 | tf_op jit(solution)/shard_map/ppermute | solution.py:573

commit v8 on v7

--- a/solution.py
+++ b/solution.py
@@ -190,7 +190,7 @@
 
 
 def local_kernel(steps, factor, count, live_ref, x_ref, wq_ref, wk_ref, wv_ref, proj_ref, *refs):
-    oq_ref, ok_ref, ov_ref, op_ref, u_ref, v_ref, f_ref = refs
+    oq_ref, ok_ref, ov_ref, op_ref, uq_ref, fq_ref, u_ref, v_ref, f_ref = refs
     own = own_columns(count)
     oq_ref[...] = wq_ref[:, own]
     ok_ref[...] = wk_ref[:, own]
@@ -198,10 +198,14 @@
     op_ref[...] = own_heads(proj_ref, count)
     mask = head_mask(proj_ref.shape[1], WIDE)
     x = x_ref[...]
+    proj = all_heads(proj_ref)
+    scaled = dot(x, wq_ref[...]) * factor
+    uq_ref[...] = scaled
+    fq_ref[...] = feature_map(scaled, proj, mask, head_ones(mask), proj_ref.shape[2])
     scaled = dot(x, wk_ref[...]) * factor
     u_ref[...] = scaled
     v_ref[...] = dot(x, wv_ref[...])
-    feat = feature_map(scaled, all_heads(proj_ref), mask, head_ones(mask), proj_ref.shape[2])
+    feat = feature_map(scaled, proj, mask, head_ones(mask), proj_ref.shape[2])
     place = lax.broadcasted_iota(jnp.int32, feat.shape, 0) % (feat.shape[0] // steps)
     f_ref[...] = jnp.where(place < live_ref[0], feat, 0.0)
 
@@ -253,12 +257,17 @@
 
 
 def attend_kernel(steps, size, parts, *refs):
-    s_refs, (f_ref, att_ref, inv_ref), out_refs = refs[:parts], refs[parts : parts + 3], refs[parts + 3 :]
+    s_refs, (f_ref, att_ref, inv_ref, s_ref) = refs[:parts], refs[parts : parts + 4]
+    out_refs = refs[parts + 4 :]
+    total = s_refs[0][...]
+    for ref in s_refs[1:]:
+        total = total + ref[...]
+    s_ref[...] = total
     mask = head_mask(size, LANES)
     feat = f_ref[...]
     high = feat.shape[0] // steps
     numer, weighted = [], []
-    for step, (matrix, row) in enumerate(load_summary(s_refs, steps, size)):
+    for step, (matrix, row) in enumerate(load_summary([s_ref], steps, size)):
         part = feat[step * high : (step + 1) * high]
         numer.append(dot3(split(part), split(spread(matrix, mask))))
         weighted.append(part * row)
@@ -272,11 +281,11 @@
 
 def forward_kernel(count, *refs):
     in_refs, (gh_ref, wu_ref, wt_ref) = refs[:count], refs[count : count + 3]
-    out_refs, scratch = refs[count + 3 : -1], refs[-1]
+    att_ref, grad_ref, out_refs = refs[count + 3], refs[count + 4], refs[count + 5 :]
     me = lax.axis_index("sensor") % count
     for partner, ref in enumerate(in_refs):
-        scratch[:, columns((me ^ partner) % count)] = ref[...]
-    attended = scratch[...]
+        att_ref[:, columns((me ^ partner) % count)] = ref[...]
+    attended = att_ref[...]
     scale = lax.rsqrt(jnp.mean(attended * attended, -1, keepdims=True) + 1e-06)
     normed = attended * scale
     pre = dot(normed.astype(BF16), wu_ref[...])
@@ -286,10 +295,10 @@
     slope = 0.5 * (1.0 + t) + 0.5 * pre * (1.0 - t * t) * (c * (1.0 + 3 * 0.044715 * square))
     grad_pre = (gh_ref[...] * slope).astype(BF16)
     grad_normed = dot(grad_pre, wt_ref[...])
-    scratch[...] = (
+    grad_ref[...] = (
         grad_normed - normed * jnp.mean(grad_normed * normed, -1, keepdims=True)
     ) * scale
-    send_columns([scratch], out_refs, me)
+    send_columns([grad_ref], out_refs, me)
 
 
 def grad_summary_kernel(steps, size, count, *refs):
@@ -307,13 +316,12 @@
     store_summary(g_ref, *summaries(feat, grad_num, feat * grad_den, steps, size))
 
 
-def query_back_kernel(steps, factor, count, parts, *refs):
-    s_refs, (num_ref, den_ref, f_ref, u_ref, proj_ref, g_ref) = refs[:parts], refs[parts:]
+def query_back_kernel(steps, factor, s_ref, num_ref, den_ref, f_ref, u_ref, proj_ref, g_ref):
     size = proj_ref.shape[0]
     mask = head_mask(size, LANES)
     high = f_ref.shape[0] // steps
     out = []
-    for step, (matrix, row) in enumerate(load_summary(s_refs, steps, size)):
+    for step, (matrix, row) in enumerate(load_summary([s_ref], steps, size)):
         part = slice(step * high, (step + 1) * high)
         back = dot3(split(num_ref[part, :]), split(spread(matrix, mask)), NT)
         out.append(back + den_ref[part, :] * row)
@@ -324,22 +332,18 @@
     g_ref[...] = (grad * factor).astype(BF16)
 
 
-def key_back_kernel(steps, factor, count, parts, devices, *refs):
+def key_back_kernel(steps, factor, parts, devices, *refs):
     g_refs, (u_ref, v_ref, f_ref, proj_ref, gq_ref) = refs[:parts], refs[parts : parts + 5]
-    x_all, rest = refs[parts + 5], refs[parts + 6 :]
-    back_refs, (keep_ref, send_ref, p_ref) = rest[:count], rest[count:]
+    x_all, total_ref, keep_ref, send_ref, p_ref = refs[parts + 5 :]
     size = proj_ref.shape[0]
     mask = head_mask(size, LANES)
     high = f_ref.shape[0] // steps
     total = g_refs[0][...]
     for ref in g_refs[1:]:
         total = total + ref[...]
-    high_g = total.shape[0]
-    for partner, ref in enumerate(back_refs):
-        ref[:high_g, :] = total
-        ref[high_g:, :] = take_rows(gq_ref[...], partner, count, steps).astype(F32)
+    total_ref[...] = total
     back, grad_v = [], []
-    for step, (matrix, row) in enumerate(load_summary(back_refs[:1], steps, size)):
+    for step, (matrix, row) in enumerate(load_summary([total_ref], steps, size)):
         part = slice(step * high, (step + 1) * high)
         matrix = split(spread(matrix, mask))
         back.append(dot3(split(v_ref[part, :]), matrix, NT) + row)
@@ -371,17 +375,45 @@
             ref[...] = own_ref[part] + got_ref[part]
 
 
+def collect_columns(target, refs):
+    me = lax.axis_index("sensor") % len(refs)
+    for partner, ref in enumerate(refs):
+        target[:, columns((me ^ partner) % len(refs))] = ref[...]
+
+
+def query_rows_kernel(steps, factor, count, *refs):
+    in_refs, (f_ref, u_ref, att_ref, grad_ref) = refs[:count], refs[count : count + 4]
+    proj_ref, wq_ref, out_ref, s_ref = refs[count + 4 :]
+    collect_columns(s_ref, in_refs[::-1])
+    size = proj_ref.shape[1]
+    mask = head_mask(size, WIDE)
+    ones = head_ones(mask)
+    rows = f_ref.shape[0] // steps
+    feat, grad_att = f_ref[...], grad_ref[...]
+    normal = [s_ref[steps * size + t : steps * size + t + 1, :] for t in range(steps)]
+    normal = jnp.concatenate([jnp.broadcast_to(n, (rows, n.shape[1])) for n in normal], 0)
+    denom = jnp.concatenate([head_sums(w, ones) for w in pieces(feat * normal)], -1)
+    inverse = 1.0 / denom
+    grad_num = grad_att * inverse
+    along = pieces(grad_att * att_ref[...])
+    grad_den = -jnp.concatenate([head_sums(a, ones) for a in along], -1) * inverse
+    back = []
+    for step in range(steps):
+        nums = pieces(grad_num[step * rows : (step + 1) * rows])
+        matrices = pieces(s_ref[step * size : (step + 1) * size, :])
+        parts = [dot3(split(n), split(spread(m, mask)), NT) for n, m in zip(nums, matrices)]
+        back.append(jnp.concatenate(parts, -1))
+    weighted = (jnp.concatenate(back, 0) + grad_den * normal) * feat
+    grad = feature_back(weighted, u_ref[...], all_heads(proj_ref), mask, ones) * factor
+    out_ref[...] = dot(grad.astype(BF16), wq_ref[...])
+
+
 def rows_kernel(steps, factor, count, *refs):
     in_refs, (u_ref, v_ref, f_ref, proj_ref) = refs[:count], refs[count : count + 4]
-    wq_ref, wk_ref, wv_ref, out_ref, q_ref, g_ref = refs[count + 4 :]
+    q_ref, wk_ref, wv_ref, out_ref, g_ref = refs[count + 4 :]
     size = proj_ref.shape[1]
-    high_g = g_ref.shape[0]
-    me = lax.axis_index("sensor") % count
-    for partner, ref in enumerate(reversed(in_refs)):
-        own = columns((me ^ partner) % count)
-        g_ref[:, own] = ref[:high_g, :]
-        q_ref[:, own] = ref[high_g:, :].astype(BF16)
-    total = dot(q_ref[...], wq_ref[...])
+    collect_columns(g_ref, in_refs)
+    total = q_ref[...]
     mask = head_mask(size, WIDE)
     rows = f_ref.shape[0] // steps
     back, grad_v = [], []
@@ -494,10 +526,10 @@
     )
     tops, lows = gather_halves(top, low, "sensor")
     narrow_w = shape((width, LANES), BF16)
-    own_query, own_key, own_value, proj, *local_keys = call(
+    own_query, own_key, own_value, proj, query_rows, feat_rows, *local_keys = call(
         functools.partial(local_kernel, steps, factor, count),
         "local_keys",
-        (narrow_w,) * 3 + (shape((size, LANES)),) + (shape((rows, width)),) * 3,
+        (narrow_w,) * 3 + (shape((size, LANES)),) + (shape((rows, width)),) * 5,
         (live_count, x, w_query, w_key, w_value, feature_proj),
         flops=3 * product,
         smem=1,
@@ -522,20 +554,19 @@
         smem=1,
     )
     summary = far_sum(summary, count)
-    attended, inverse, *local_att = call(
+    attended, inverse, summary, *local_att = call(
         functools.partial(attend_kernel, steps, size, len(summary)),
         "attend",
-        (tall, tall) + (narrow,) * count,
+        (tall, tall, packed) + (narrow,) * count,
         (*summary, feat_query),
         flops=product,
     )
-    local_grad = call(
+    local_att, local_grad_att, *local_grad = call(
         functools.partial(forward_kernel, count),
         "feed_forward",
-        (narrow,) * count,
+        (shape((rows, width)),) * 2 + (narrow,) * count,
         (*trade(local_att, "sensor"), grad_hidden, w_up, wu_turned),
         flops=product,
-        scratch=[wide],
     )
     grad_num, grad_den, grad_summary = call(
         functools.partial(grad_summary_kernel, steps, size, count),
@@ -545,21 +576,37 @@
         flops=product,
         scratch=kinds(tall),
     )
+    query_part = call(
+        functools.partial(query_rows_kernel, steps, factor, count),
+        "query_rows",
+        shape((rows, width)),
+        (
+            *trade([summary] * count, "sensor", False)[::-1],
+            feat_rows,
+            query_rows,
+            local_att,
+            local_grad_att,
+            feature_proj,
+            wq_turned,
+        ),
+        flops=3 * product,
+        scratch=[pltpu.VMEM((packed.shape[0], width), F32)],
+    )
     grad_summary = far_sum(grad_summary, count)
     grad_q = call(
-        functools.partial(query_back_kernel, steps, factor, count, len(summary)),
+        functools.partial(query_back_kernel, steps, factor),
         "query_back",
         shape(tall.shape, BF16),
-        (*summary, grad_num, grad_den, feat_query, query, proj),
+        (summary, grad_num, grad_den, feat_query, query, proj),
         flops=product,
     )
     tile = (width // devices, 3 * LANES)
     half = shape((2, quads, *tile))
-    *messages, own_half, send_half = call(
-        functools.partial(key_back_kernel, steps, factor, count, len(grad_summary), devices),
+    grad_summary, own_half, send_half = call(
+        functools.partial(key_back_kernel, steps, factor, len(grad_summary), devices),
         "key_back",
-        (shape((packed.shape[0] + rows, LANES)),) * count + (half, half),
-        (*grad_summary, key, value, feat_key, proj, grad_q, x_turned),
+        (packed, half, half),
+        (*grad_summary, key, value, feat_key, proj, after(grad_q, query_part), x_turned),
         flops=4 * product,
         scratch=[pltpu.VMEM((2, *half.shape), F32)],
     )
@@ -580,8 +627,7 @@
             (shape(tile),) * 4,
             (own_half, got_half),
         )
-        away = away + swap(send_away, "step", 2)
-        parts = (turn(away, 1), turn(send_kept, 0, 2), turn(after(kept, away), 0))
+        parts = (turn(away, 1), turn(send_away, 1, 2), turn(send_kept, 0, 2), turn(kept, 0))
     else:
         kept, sent = call(
             functools.partial(core_kernel, count),
@@ -594,16 +640,16 @@
             kept + swap(sent, "step", 2), "sensor", 0, 0, tiled=True, axis_index_groups=groups
         )
         parts = (turn(blocks.sum(0), 0),)
-    messages = trade(messages, "sensor", False)
+    messages = trade([grad_summary] * count, "sensor", False)
     scale = 1.0 / math.sqrt(rows * lax.axis_size("step") * devices)
     out = shape((width // devices, LANES))
     grad_in = call(
         functools.partial(rows_kernel, steps, factor, count),
         "input_rows",
         shape((rows, width), BF16),
-        (*messages[::-1], *local_keys, feature_proj, wq_turned, wk_turned, wv_turned),
+        (*messages, *local_keys, feature_proj, query_part, wk_turned, wv_turned),
         flops=30 * product,
-        scratch=[pltpu.VMEM((rows, width), BF16), pltpu.VMEM((packed.shape[0], width), F32)],
+        scratch=[pltpu.VMEM((packed.shape[0], width), F32)],
     )
     grads = call(
         functools.partial(final_kernel, scale, len(parts)),

time: 73 us -> 71.5 us (0.979)
  the two profiles are of different devices: /device:TPU:24 before, /device:TPU:0 now
where the time goes in v8:
time: 71.5 us; the launch traced here: 71.2 us
  starting transfers between devices  36.3 us (51%)
  waiting for transfers between devices  16.9 us (24%)
  Pallas kernels  11.5 us (16%)
  local copies, waits for them, and re-layouts  5.02 us (7%)
  between operations  1.46 us (2%)
    ppermute x21, starting transfers between devices, swap(): lax.ppermute(a, axis, [(i, i ^ bit) for i in range(lax.axis_size(axis))])  29.4 us
    ppermute x21, waiting for transfers between devices, swap(): lax.ppermute(a, axis, [(i, i ^ bit) for i in range(lax.axis_size(axis))])  12.4 us
    pallas_call x14, Pallas kernels, call(): pl.pallas_call(kernel, name=name, out_shape=outs, in_specs=[SMEM] * smem...  11.5 us
    ppermute x4, starting transfers between devices, turn(): return lax.ppermute(a, ('sensor', 'step'), pairs)  6.92 us
    unnamed x24, local copies, waits for them, and re-layouts  5.02 us
    ppermute x4, waiting for transfers between devices, turn(): return lax.ppermute(a, ('sensor', 'step'), pairs)  4.54 us
  transfers between devices with their start and end apart: 25, of which 10 were waited for; matrix products, arithmetic and copies ran while one was open for 0% of the time, Pallas kernels for 11%

profile of v8, /device:TPU:0, one launch (start us, length us, event | category | flops | bytes accessed | tf_op | source)
XLA Modules:
  0.0 71.2 jit_solution(8969160925179503454)
XLA Ops:
  1.3 0.9 %copy-done.9 = bf16[3,64,512]{2,1,0:T(8,128)(2,1)S(1)} copy-done((bf16[3,64,512]{2,1,0:T(8,128)(2,1)S(1)}, bf16[3,64,512]{2,1,0:T(8,128)(2,1)}, u32[]{:S(2)}) %copy-start.9) | copy-done | bytes 196632
  2.2 3.0 %collective-permute-start = (f32[104,512]{1,0:T(8,128)S(1)}, f32[104,512]{1,0:T(8,128)S(1)}, u32[]{:S(2)}, u32[]{:S(2)}) collective-permute-start(f32[104,512]{1,0:T(8,128)S(1)} %get-tuple-element.62.refs_0_), channel_id=1, source_target_pairs={{0,4},{4,0},{8,12},{12,8},{16,20},{20,16},{24,28},{28,24},{1,5},{5... | collective-permute-start | bytes 638984 | tf_op jit(solution)/shard_map/ppermute | solution.py:472
  5.3 1.6 %collective-permute-start.4 = (f32[104,512]{1,0:T(8,128)S(1)}, f32[104,512]{1,0:T(8,128)S(1)}, u32[]{:S(2)}, u32[]{:S(2)}) collective-permute-start(f32[104,512]{1,0:T(8,128)S(1)} %get-tuple-element.63.refs_4_), channel_id=1, source_target_pairs={{0,8},{4,12},{8,0},{12,4},{16,24},{20,28},{24,16},{28,20},{1,9},{5... | collective-permute-start | bytes 638984 | tf_op jit(solution)/shard_map/ppermute | solution.py:472
  6.8 0.4 collective-permute-start.1
  7.3 0.1 collective-permute-start.3
  7.4 4.0 %collective-permute-done.refs_1_ = f32[104,512]{1,0:T(8,128)S(1)} collective-permute-done((f32[104,512]{1,0:T(8,128)S(1)}, f32[104,512]{1,0:T(8,128)S(1)}, u32[]{:S(2)}, u32[]{:S(2)}) %collective-permute-start) | collective-permute-done | bytes 213024 | tf_op jit(solution)/shard_map/ppermute | solution.py:472
  11.4 2.1 %collective-permute-start.2 = (f32[104,512]{1,0:T(8,128)S(1)}, f32[104,512]{1,0:T(8,128)S(1)}, u32[]{:S(2)}, u32[]{:S(2)}) collective-permute-start(f32[104,512]{1,0:T(8,128)S(1)} %collective-permute-done.refs_1_), channel_id=1, source_target_pairs={{0,8},{4,12},{8,0},{12,4},{16,24},{20,28},{24,16},{28,20},{1,9},{5... | collective-permute-start | bytes 638984 | tf_op jit(solution)/shard_map/ppermute | solution.py:472
  13.5 0.0 collective-permute-done.4.refs_6_
  13.5 1.5 %collective-permute-start.5 = (f32[104,512]{1,0:T(8,128)S(1)}, f32[104,512]{1,0:T(8,128)S(1)}, u32[]{:S(2)}, u32[]{:S(2)}) collective-permute-start(f32[104,512]{1,0:T(8,128)S(1)} %collective-permute-done.4.refs_6_), channel_id=1, source_target_pairs={{0,4},{4,0},{8,12},{12,8},{16,20},{20,16},{24,28},{28,24},{1,5},{5... | collective-permute-start | bytes 638984 | tf_op jit(solution)/shard_map/ppermute | solution.py:472
  15.0 1.0 %copy-done = bf16[512,512]{1,0:T(8,128)(2,1)S(1)} copy-done((bf16[512,512]{1,0:T(8,128)(2,1)S(1)}, bf16[512,512]{1,0:T(8,128)(2,1)}, u32[]{:S(2)}) %copy-start) | copy-done | bytes 524312
  16.0 1.0 %copy-done.2 = bf16[512,512]{1,0:T(8,128)(2,1)S(1)} copy-done((bf16[512,512]{1,0:T(8,128)(2,1)S(1)}, bf16[512,512]{1,0:T(8,128)(2,1)}, u32[]{:S(2)}) %copy-start.2) | copy-done | bytes 524312
  17.1 1.0 %copy-done.4 = bf16[512,512]{1,0:T(8,128)(2,1)S(1)} copy-done((bf16[512,512]{1,0:T(8,128)(2,1)S(1)}, bf16[512,512]{1,0:T(8,128)(2,1)}, u32[]{:S(2)}) %copy-start.4) | copy-done | bytes 524312
  18.1 0.9 %copy-done.7 = f32[8,64,64]{2,1,0:T(8,128)S(1)} copy-done((f32[8,64,64]{2,1,0:T(8,128)S(1)}, f32[8,64,64]{2,1,0:T(8,128)}, u32[]{:S(2)}) %copy-start.7) | copy-done | bytes 131096
  19.1 1.1 %local_keys.1 = (bf16[512,128]{1,0:T(8,128)(2,1)S(1)}, bf16[512,128]{1,0:T(8,128)(2,1)S(1)}, bf16[512,128]{1,0:T(8,128)(2,1)S(1)}, f32[64,128]{1,0:T(8,128)S(1)}...) custom-call(s32[1]{0:T(128)S(6)} %copy.13.live_ref, ...), custom_call_target="tpu_custom_call" | custom-call | flops 301989888 | bytes 4292612 | tf_op jit(solution)/shard_map/local_keys/pallas_call | solution.py:451
  20.2 0.0 collective-permute-done.1.refs_2_
  20.2 0.0 collective-permute-done.3.refs_5_
  20.2 0.9 %collective-permute-done.2.refs_3_ = f32[104,512]{1,0:T(8,128)S(1)} collective-permute-done((f32[104,512]{1,0:T(8,128)S(1)}, f32[104,512]{1,0:T(8,128)S(1)}, u32[]{:S(2)}, u32[]{:S(2)}) %collective-permute-start.2) | collective-permute-done | bytes 213024 | tf_op jit(solution)/shard_map/ppermute | solution.py:472
  21.1 1.1 %keys.1 = (bf16[768,512]{1,0:T(8,128)(2,1)S(1)}, f32[768,128]{1,0:T(8,128)S(1)}, f32[768,128]{1,0:T(8,128)S(1)}, f32[768,128]{1,0:T(8,128)S(1)}, f32[200,128]{1,0:T(8,128)S(1)}) custom-call(f32[104,512]{1,0:T(8,128)S(1)} %get-tuple-element.62.refs_0_, f32[104,512]{1,0:T(8,128)S(1)} %collective-permute-done.refs_1_, ...), custom_call_target="tpu_custom_call" | custom-call | flops 301989888 | bytes 4067328 | tf_op jit(solution)/shard_map/keys/pallas_call | solution.py:451
  22.2 2.6 %collective-permute-start.6 = (f32[200,128]{1,0:T(8,128)S(1)}, f32[200,128]{1,0:T(8,128)S(1)}, u32[]{:S(2)}, u32[]{:S(2)}) collective-permute-start(f32[200,128]{1,0:T(8,128)S(1)} %get-tuple-element.67.refs_0_), channel_id=1, source_target_pairs={{0,16},{4,20},{8,24},{12,28},{16,0},{20,4},{24,8},{28,12},{1,17},{... | collective-permute-start | bytes 307208 | tf_op jit(solution)/shard_map/ppermute | solution.py:472
  24.9 0.0 copy-start.6
  24.9 0.9 %queries.1 = (f32[768,128]{1,0:T(8,128)S(1)}, f32[768,128]{1,0:T(8,128)S(1)}, f32[192,256]{1,0:T(8,128)S(1)}) custom-call(s32[1]{0:T(128)S(6)} %copy.13.live_ref, bf16[768,512]{1,0:T(8,128)(2,1)S(1)} %get-tuple-element.68.x_ref.refs_0_, bf16[192,512]{1,0:T(8,128)(2,1)S(1)} %bitcast.5, bf16[512,128]{1,0:T(8,128)(2,1)S(1)} %get-tuple-element.69.wq_ref, ...), custom_call_target="tpu_custom_call" | custom-call | flops 201326592 | bytes 2392068 | tf_op jit(solution)/shard_map/queries/pallas_call | solution.py:451
  25.8 0.0 copy-start.1
  25.8 2.0 %collective-permute-done.6.refs_1_ = f32[200,128]{1,0:T(8,128)S(1)} collective-permute-done((f32[200,128]{1,0:T(8,128)S(1)}, f32[200,128]{1,0:T(8,128)S(1)}, u32[]{:S(2)}, u32[]{:S(2)}) %collective-permute-start.6) | collective-permute-done | bytes 102432 | tf_op jit(solution)/shard_map/ppermute | solution.py:472
  27.8 0.4 attend.1
  28.2 1.8 %collective-permute-start.7 = (f32[192,128]{1,0:T(8,128)S(1)}, f32[192,128]{1,0:T(8,128)S(1)}, u32[]{:S(2)}, u32[]{:S(2)}) collective-permute-start(f32[192,128]{1,0:T(8,128)S(1)} %get-tuple-element.72), channel_id=1, source_target_pairs={{0,12},{4,8},{8,4},{12,0},{16,28},{20,24},{24,20},{28,16},{1,13},{... | collective-permute-start | bytes 294920 | tf_op jit(solution)/shard_map/ppermute | solution.py:472
  30.0 1.5 %collective-permute-start.8 = (f32[192,128]{1,0:T(8,128)S(1)}, f32[192,128]{1,0:T(8,128)S(1)}, u32[]{:S(2)}, u32[]{:S(2)}) collective-permute-start(f32[192,128]{1,0:T(8,128)S(1)} %get-tuple-element.73), channel_id=1, source_target_pairs={{0,4},{4,0},{8,12},{12,8},{16,20},{20,16},{24,28},{28,24},{1,5},{5... | collective-permute-start | bytes 294920 | tf_op jit(solution)/shard_map/ppermute | solution.py:472
  31.5 0.3 collective-permute-start.9
  31.8 0.7 %transposes.1 = (bf16[512,768]{1,0:T(8,128)(2,1)S(1)}, bf16[512,512]{1,0:T(8,128)(2,1)S(1)}, bf16[512,512]{1,0:T(8,128)(2,1)S(1)}, bf16[512,512]{1,0:T(8,128)(2,1)S(1)}, bf16[256,512]{1,0:T(8,128)(2,1)S(1)}) custom-call(bf16[768,512]{1,0:T(8,128)(2,1)S(1)} %get-tuple-element.68.x_ref.refs_0_, bf16[512,512]{1,0:T(8,128)(2,1)S(1)} %copy-done.1, ...), custom_call_target="tpu_custom_call" | custom-call | bytes 5242880 | tf_op jit(solution)/shard_map/transposes/pallas_call | solution.py:451
  32.5 1.3 %collective-permute-done.7.refs_3_ = f32[192,128]{1,0:T(8,128)S(1)} collective-permute-done((f32[192,128]{1,0:T(8,128)S(1)}, f32[192,128]{1,0:T(8,128)S(1)}, u32[]{:S(2)}, u32[]{:S(2)}) %collective-permute-start.7) | collective-permute-done | bytes 98336 | tf_op jit(solution)/shard_map/ppermute | solution.py:472
  33.8 1.0 %collective-permute-done.8.refs_1_ = f32[192,128]{1,0:T(8,128)S(1)} collective-permute-done((f32[192,128]{1,0:T(8,128)S(1)}, f32[192,128]{1,0:T(8,128)S(1)}, u32[]{:S(2)}, u32[]{:S(2)}) %collective-permute-start.8) | collective-permute-done | bytes 98336 | tf_op jit(solution)/shard_map/ppermute | solution.py:472
  34.9 1.6 %collective-permute-done.9.refs_2_ = f32[192,128]{1,0:T(8,128)S(1)} collective-permute-done((f32[192,128]{1,0:T(8,128)S(1)}, f32[192,128]{1,0:T(8,128)S(1)}, u32[]{:S(2)}, u32[]{:S(2)}) %collective-permute-start.9) | collective-permute-done | bytes 98336 | tf_op jit(solution)/shard_map/ppermute | solution.py:472
  36.5 0.7 %feed_forward.1 = (f32[192,512]{1,0:T(8,128)S(1)}, f32[192,512]{1,0:T(8,128)S(1)}, f32[192,128]{1,0:T(8,128)S(1)}, f32[192,128]{1,0:T(8,128)S(1)}, f32[192,128]{1,0:T(8,128)S(1)}, /*index=5*/f32[192,128]{1,0:T(8,128)S(1)}) custom-call(f32[192,128]{1,0:T(8,128)S(1)} %get-tuple-element.71.refs_0_, f32[192,128]{1,0:T(8,128)S(1)} %collective-permute-done.8.refs_1_, ...), custom_call_target="tpu_custom_call" | custom-call | flops 100663296 | bytes 2293760 | tf_op jit(solution)/shard_map/feed_forward/pallas_call | solution.py:451
  37.2 1.1 %collective-permute-start.10 = (f32[192,128]{1,0:T(8,128)S(1)}, f32[192,128]{1,0:T(8,128)S(1)}, u32[]{:S(2)}, u32[]{:S(2)}) collective-permute-start(f32[192,128]{1,0:T(8,128)S(1)} %get-tuple-element.81), channel_id=1, source_target_pairs={{0,12},{4,8},{8,4},{12,0},{16,28},{20,24},{24,20},{28,16},{1,13},{... | collective-permute-start | bytes 294920 | tf_op jit(solution)/shard_map/ppermute | solution.py:472
  38.3 0.6 collective-permute-start.11
  38.9 1.9 %collective-permute-start.12 = (f32[192,128]{1,0:T(8,128)S(1)}, f32[192,128]{1,0:T(8,128)S(1)}, u32[]{:S(2)}, u32[]{:S(2)}) collective-permute-start(f32[192,128]{1,0:T(8,128)S(1)} %get-tuple-element.83), channel_id=1, source_target_pairs={{0,8},{4,12},{8,0},{12,4},{16,24},{20,28},{24,16},{28,20},{1,9},{5... | collective-permute-start | bytes 294920 | tf_op jit(solution)/shard_map/ppermute | solution.py:472
  40.8 1.0 %collective-permute-start.14 = (f32[200,128]{1,0:T(8,128)S(1)}, f32[200,128]{1,0:T(8,128)S(1)}, u32[]{:S(2)}, u32[]{:S(2)}) collective-permute-start(f32[200,128]{1,0:T(8,128)S(1)} %get-tuple-element.93.s_ref.refs_3_), channel_id=1, source_target_pairs={{0,12},{4,8},{8,4},{12,0},{16,28},{20,24},{24,20},{28,16},{1,13},{... | collective-permute-start | bytes 307208 | tf_op jit(solution)/shard_map/ppermute | solution.py:472
  41.8 0.6 collective-permute-start.15
  42.4 0.5 collective-permute-done.10.refs_3_
  42.9 1.4 %collective-permute-start.16 = (f32[200,128]{1,0:T(8,128)S(1)}, f32[200,128]{1,0:T(8,128)S(1)}, u32[]{:S(2)}, u32[]{:S(2)}) collective-permute-start(f32[200,128]{1,0:T(8,128)S(1)} %get-tuple-element.93.s_ref.refs_3_), channel_id=1, source_target_pairs={{0,4},{4,0},{8,12},{12,8},{16,20},{20,16},{24,28},{28,24},{1,5},{5... | collective-permute-start | bytes 307208 | tf_op jit(solution)/shard_map/ppermute | solution.py:472
  44.3 0.0 collective-permute-done.11.refs_1_
  44.3 0.0 collective-permute-done.12.refs_2_
  44.3 0.4 grad_summary.1
  44.7 3.9 %collective-permute-start.13 = (f32[200,128]{1,0:T(8,128)S(1)}, f32[200,128]{1,0:T(8,128)S(1)}, u32[]{:S(2)}, u32[]{:S(2)}) collective-permute-start(f32[200,128]{1,0:T(8,128)S(1)} %get-tuple-element.89.refs_0_), channel_id=1, source_target_pairs={{0,16},{4,20},{8,24},{12,28},{16,0},{20,4},{24,8},{28,12},{1,17},{... | collective-permute-start | bytes 307208 | tf_op jit(solution)/shard_map/ppermute | solution.py:472
  48.6 0.0 collective-permute-done.14.refs_0_
  48.6 0.0 collective-permute-done.15.refs_1_
  48.6 0.0 collective-permute-done.16.refs_2_
  48.7 1.4 %query_rows.1.refs_8_ = f32[192,512]{1,0:T(8,128)S(1)} custom-call(f32[200,128]{1,0:T(8,128)S(1)} %collective-permute-done.14.refs_0_, f32[200,128]{1,0:T(8,128)S(1)} %collective-permute-done.15.refs_1_, f32[200,128]{1,0:T(8,128)S(1)} %collective-permute-done.16.refs_2_, f32[200,128]{1,0:T(8,128)S(1)} %get-tuple-element.93.s_ref.refs_3_, ...), custom_call_target="tpu_custom_call" | custom-call | flops 301989888 | bytes 3031040 | tf_op jit(solution)/shard_map/query_rows/pallas_call | solution.py:451
  50.1 0.6 query_back.1.refs_6_
  50.7 0.6 collective-permute-done.13.refs_1_
  51.3 1.1 %key_back.1 = (f32[200,128]{1,0:T(8,128)S(1)}, f32[2,2,64,384]{3,2,1,0:T(8,128)S(1)}, f32[2,2,64,384]{3,2,1,0:T(8,128)S(1)}) custom-call(f32[200,128]{1,0:T(8,128)S(1)} %get-tuple-element.89.refs_0_, f32[200,128]{1,0:T(8,128)S(1)} %collective-permute-done.13.refs_1_, f32[768,128]{1,0:T(8,128)S(1)} %get-tuple-element.90.refs_2_, ...), custom_call_target="tpu_custom_call" | custom-call | flops 402653184 | bytes 3289088 | tf_op jit(solution)/shard_map/key_back/pallas_call | solution.py:451
  52.4 0.1 collective-permute-start.20
  52.5 2.3 %collective-permute-start.17 = (f32[200,128]{1,0:T(8,128)S(1)}, f32[200,128]{1,0:T(8,128)S(1)}, u32[]{:S(2)}, u32[]{:S(2)}) collective-permute-start(f32[200,128]{1,0:T(8,128)S(1)} %get-tuple-element.104.refs_0_), channel_id=1, source_target_pairs={{0,4},{4,0},{8,12},{12,8},{16,20},{20,16},{24,28},{28,24},{1,5},{5... | collective-permute-start | bytes 307208 | tf_op jit(solution)/shard_map/ppermute | solution.py:472
  54.7 0.0 collective-permute-start.18
  54.7 1.5 %collective-permute-start.19 = (f32[200,128]{1,0:T(8,128)S(1)}, f32[200,128]{1,0:T(8,128)S(1)}, u32[]{:S(2)}, u32[]{:S(2)}) collective-permute-start(f32[200,128]{1,0:T(8,128)S(1)} %get-tuple-element.104.refs_0_), channel_id=1, source_target_pairs={{0,12},{4,8},{8,4},{12,0},{16,28},{20,24},{24,20},{28,16},{1,13},{... | collective-permute-start | bytes 307208 | tf_op jit(solution)/shard_map/ppermute | solution.py:472
  56.3 0.0 collective-permute-done.20.got_ref
  56.3 3.2 %collective-permute-start.21 = (f32[64,384]{1,0:T(8,128)S(1)}, f32[64,384]{1,0:T(8,128)S(1)}, u32[]{:S(2)}, u32[]{:S(2)}) collective-permute-start(f32[64,384]{1,0:T(8,128)S(1)} %get-tuple-element.112), channel_id=1, source_target_pairs={{0,16},{1,20},{2,24},{3,28},{4,17},{5,21},{6,25},{7,29},{8,18},{9,... | collective-permute-start | bytes 294920 | tf_op jit(solution)/shard_map/ppermute | solution.py:620
  59.6 1.6 %collective-permute-start.22 = (f32[64,384]{1,0:T(8,128)S(1)}, f32[64,384]{1,0:T(8,128)S(1)}, u32[]{:S(2)}, u32[]{:S(2)}) collective-permute-start(f32[64,384]{1,0:T(8,128)S(1)} %get-tuple-element.114), channel_id=1, source_target_pairs={{0,24},{1,28},{2,16},{3,20},{4,25},{5,29},{6,17},{7,21},{8,26},{9,... | collective-permute-start | bytes 294920 | tf_op jit(solution)/shard_map/ppermute | solution.py:620
  61.2 1.4 %collective-permute-start.23 = (f32[64,384]{1,0:T(8,128)S(1)}, f32[64,384]{1,0:T(8,128)S(1)}, u32[]{:S(2)}, u32[]{:S(2)}) collective-permute-start(f32[64,384]{1,0:T(8,128)S(1)} %get-tuple-element.115), channel_id=1, source_target_pairs={{0,8},{1,12},{2,0},{3,4},{4,9},{5,13},{6,1},{7,5},{8,10},{9,14},{1... | collective-permute-start | bytes 294920 | tf_op jit(solution)/shard_map/ppermute | solution.py:620
  62.6 0.7 collective-permute-start.24
  63.3 0.4 collective-permute-done.19.refs_3_
  63.7 2.2 %input_rows.1 = bf16[192,512]{1,0:T(8,128)(2,1)} custom-call(f32[200,128]{1,0:T(8,128)S(1)} %get-tuple-element.104.refs_0_, f32[200,128]{1,0:T(8,128)S(1)} %collective-permute-done.17.refs_1_, f32[200,128]{1,0:T(8,128)S(1)} %collective-permute-done.18.refs_2_, f32[200,128]{1,0:T(8,128)S(1)} %collective-permute-done.19.refs_3_, ...), custom_call_target="tpu_custom_call" | custom-call | flops 3019898880 | bytes 3358720 | tf_op jit(solution)/shard_map/input_rows/pallas_call | solution.py:451
  66.0 0.0 collective-permute-done.21.refs_0_
  66.0 4.5 %collective-permute-done.22.refs_1_ = f32[64,384]{1,0:T(8,128)S(1)} collective-permute-done((f32[64,384]{1,0:T(8,128)S(1)}, f32[64,384]{1,0:T(8,128)S(1)}, u32[]{:S(2)}, u32[]{:S(2)}) %collective-permute-start.22) | collective-permute-done | bytes 98336 | tf_op jit(solution)/shard_map/ppermute | solution.py:620
  70.5 0.7 weight_sums.1
  (24 shorter events, 0.1 us)
Async XLA Ops:
  1.3 0.9 %copy-start.9 = (bf16[3,64,512]{2,1,0:T(8,128)(2,1)S(1)}, bf16[3,64,512]{2,1,0:T(8,128)(2,1)}, u32[]{:S(2)}) copy-start(bf16[3,64,512]{2,1,0:T(8,128)(2,1)} %param.9) | copy-start | bytes 589828
  2.2 9.1 %collective-permute-start = (f32[104,512]{1,0:T(8,128)S(1)}, f32[104,512]{1,0:T(8,128)S(1)}, u32[]{:S(2)}, u32[]{:S(2)}) collective-permute-start(f32[104,512]{1,0:T(8,128)S(1)} %get-tuple-element.62.refs_0_), channel_id=1, source_target_pairs={{0,4},{4,0},{8,12},{12,8},{16,20},{20,16},{24,28},{28,24},{1,5},{5... | collective-permute-start | bytes 638984 | tf_op jit(solution)/shard_map/ppermute | solution.py:472
  5.3 8.2 %collective-permute-start.4 = (f32[104,512]{1,0:T(8,128)S(1)}, f32[104,512]{1,0:T(8,128)S(1)}, u32[]{:S(2)}, u32[]{:S(2)}) collective-permute-start(f32[104,512]{1,0:T(8,128)S(1)} %get-tuple-element.63.refs_4_), channel_id=1, source_target_pairs={{0,8},{4,12},{8,0},{12,4},{16,24},{20,28},{24,16},{28,20},{1,9},{5... | collective-permute-start | bytes 638984 | tf_op jit(solution)/shard_map/ppermute | solution.py:472
  6.8 13.4 %collective-permute-start.1 = (f32[104,512]{1,0:T(8,128)S(1)}, f32[104,512]{1,0:T(8,128)S(1)}, u32[]{:S(2)}, u32[]{:S(2)}) collective-permute-start(f32[104,512]{1,0:T(8,128)S(1)} %get-tuple-element.62.refs_0_), channel_id=1, source_target_pairs={{0,8},{4,12},{8,0},{12,4},{16,24},{20,28},{24,16},{28,20},{1,9},{5... | collective-permute-start | bytes 638984 | tf_op jit(solution)/shard_map/ppermute | solution.py:472
  7.3 12.9 %collective-permute-start.3 = (f32[104,512]{1,0:T(8,128)S(1)}, f32[104,512]{1,0:T(8,128)S(1)}, u32[]{:S(2)}, u32[]{:S(2)}) collective-permute-start(f32[104,512]{1,0:T(8,128)S(1)} %get-tuple-element.63.refs_4_), channel_id=1, source_target_pairs={{0,4},{4,0},{8,12},{12,8},{16,20},{20,16},{24,28},{28,24},{1,5},{5... | collective-permute-start | bytes 638984 | tf_op jit(solution)/shard_map/ppermute | solution.py:472
  11.4 9.8 %collective-permute-start.2 = (f32[104,512]{1,0:T(8,128)S(1)}, f32[104,512]{1,0:T(8,128)S(1)}, u32[]{:S(2)}, u32[]{:S(2)}) collective-permute-start(f32[104,512]{1,0:T(8,128)S(1)} %collective-permute-done.refs_1_), channel_id=1, source_target_pairs={{0,8},{4,12},{8,0},{12,4},{16,24},{20,28},{24,16},{28,20},{1,9},{5... | collective-permute-start | bytes 638984 | tf_op jit(solution)/shard_map/ppermute | solution.py:472
  13.5 7.6 %collective-permute-start.5 = (f32[104,512]{1,0:T(8,128)S(1)}, f32[104,512]{1,0:T(8,128)S(1)}, u32[]{:S(2)}, u32[]{:S(2)}) collective-permute-start(f32[104,512]{1,0:T(8,128)S(1)} %collective-permute-done.4.refs_6_), channel_id=1, source_target_pairs={{0,4},{4,0},{8,12},{12,8},{16,20},{20,16},{24,28},{28,24},{1,5},{5... | collective-permute-start | bytes 638984 | tf_op jit(solution)/shard_map/ppermute | solution.py:472
  15.0 1.0 %copy-start = (bf16[512,512]{1,0:T(8,128)(2,1)S(1)}, bf16[512,512]{1,0:T(8,128)(2,1)}, u32[]{:S(2)}) copy-start(bf16[512,512]{1,0:T(8,128)(2,1)} %refs_1_.1) | copy-start | bytes 1572868
  16.0 1.0 %copy-start.2 = (bf16[512,512]{1,0:T(8,128)(2,1)S(1)}, bf16[512,512]{1,0:T(8,128)(2,1)}, u32[]{:S(2)}) copy-start(bf16[512,512]{1,0:T(8,128)(2,1)} %refs_2_.1) | copy-start | bytes 1572868
  17.1 1.0 %copy-start.4 = (bf16[512,512]{1,0:T(8,128)(2,1)S(1)}, bf16[512,512]{1,0:T(8,128)(2,1)}, u32[]{:S(2)}) copy-start(bf16[512,512]{1,0:T(8,128)(2,1)} %refs_3_.1) | copy-start | bytes 1572868
  18.1 0.9 %copy-start.7 = (f32[8,64,64]{2,1,0:T(8,128)S(1)}, f32[8,64,64]{2,1,0:T(8,128)}, u32[]{:S(2)}) copy-start(f32[8,64,64]{2,1,0:T(8,128)} %refs_7_.1) | copy-start | bytes 393220
  21.1 3.7 %copy-start.10 = (bf16[256,512]{1,0:T(8,128)(2,1)S(1)}, bf16[256,512]{1,0:T(8,128)(2,1)}, u32[]{:S(2)}) copy-start(bf16[256,512]{1,0:T(8,128)(2,1)} %wd_ref.1) | copy-start | bytes 786436
  21.1 3.7 %copy-start.11 = (bf16[3,64,512]{2,1,0:T(8,128)(2,1)S(1)}, bf16[3,64,512]{2,1,0:T(8,128)(2,1)}, u32[]{:S(2)}) copy-start(bf16[3,64,512]{2,1,0:T(8,128)(2,1)} %param.10) | copy-start | bytes 589828
  22.2 5.6 %collective-permute-start.6 = (f32[200,128]{1,0:T(8,128)S(1)}, f32[200,128]{1,0:T(8,128)S(1)}, u32[]{:S(2)}, u32[]{:S(2)}) collective-permute-start(f32[200,128]{1,0:T(8,128)S(1)} %get-tuple-element.67.refs_0_), channel_id=1, source_target_pairs={{0,16},{4,20},{8,24},{12,28},{16,0},{20,4},{24,8},{28,12},{1,17},{... | collective-permute-start | bytes 307208 | tf_op jit(solution)/shard_map/ppermute | solution.py:472
  24.9 6.9 %copy-start.3 = (bf16[512,512]{1,0:T(8,128)(2,1)S(1)}, bf16[512,512]{1,0:T(8,128)(2,1)}, u32[]{:S(2)}) copy-start(bf16[512,512]{1,0:T(8,128)(2,1)} %refs_2_.1) | copy-start | bytes 1572868
  24.9 6.9 %copy-start.5 = (bf16[512,512]{1,0:T(8,128)(2,1)S(1)}, bf16[512,512]{1,0:T(8,128)(2,1)}, u32[]{:S(2)}) copy-start(bf16[512,512]{1,0:T(8,128)(2,1)} %refs_3_.1) | copy-start | bytes 1572868
  24.9 6.9 %copy-start.6 = (bf16[512,256]{1,0:T(8,128)(2,1)S(1)}, bf16[512,256]{1,0:T(8,128)(2,1)}, u32[]{:S(2)}) copy-start(bf16[512,256]{1,0:T(8,128)(2,1)} %refs_5_.1) | copy-start | bytes 786436
  25.8 6.0 %copy-start.1 = (bf16[512,512]{1,0:T(8,128)(2,1)S(1)}, bf16[512,512]{1,0:T(8,128)(2,1)}, u32[]{:S(2)}) copy-start(bf16[512,512]{1,0:T(8,128)(2,1)} %refs_1_.1) | copy-start | bytes 1572868
  28.2 5.6 %collective-permute-start.7 = (f32[192,128]{1,0:T(8,128)S(1)}, f32[192,128]{1,0:T(8,128)S(1)}, u32[]{:S(2)}, u32[]{:S(2)}) collective-permute-start(f32[192,128]{1,0:T(8,128)S(1)} %get-tuple-element.72), channel_id=1, source_target_pairs={{0,12},{4,8},{8,4},{12,0},{16,28},{20,24},{24,20},{28,16},{1,13},{... | collective-permute-start | bytes 294920 | tf_op jit(solution)/shard_map/ppermute | solution.py:472
  30.0 4.9 %collective-permute-start.8 = (f32[192,128]{1,0:T(8,128)S(1)}, f32[192,128]{1,0:T(8,128)S(1)}, u32[]{:S(2)}, u32[]{:S(2)}) collective-permute-start(f32[192,128]{1,0:T(8,128)S(1)} %get-tuple-element.73), channel_id=1, source_target_pairs={{0,4},{4,0},{8,12},{12,8},{16,20},{20,16},{24,28},{28,24},{1,5},{5... | collective-permute-start | bytes 294920 | tf_op jit(solution)/shard_map/ppermute | solution.py:472
  31.5 5.0 %collective-permute-start.9 = (f32[192,128]{1,0:T(8,128)S(1)}, f32[192,128]{1,0:T(8,128)S(1)}, u32[]{:S(2)}, u32[]{:S(2)}) collective-permute-start(f32[192,128]{1,0:T(8,128)S(1)} %get-tuple-element.74), channel_id=1, source_target_pairs={{0,8},{4,12},{8,0},{12,4},{16,24},{20,28},{24,16},{28,20},{1,9},{5... | collective-permute-start | bytes 294920 | tf_op jit(solution)/shard_map/ppermute | solution.py:472
  37.2 5.7 %collective-permute-start.10 = (f32[192,128]{1,0:T(8,128)S(1)}, f32[192,128]{1,0:T(8,128)S(1)}, u32[]{:S(2)}, u32[]{:S(2)}) collective-permute-start(f32[192,128]{1,0:T(8,128)S(1)} %get-tuple-element.81), channel_id=1, source_target_pairs={{0,12},{4,8},{8,4},{12,0},{16,28},{20,24},{24,20},{28,16},{1,13},{... | collective-permute-start | bytes 294920 | tf_op jit(solution)/shard_map/ppermute | solution.py:472
  38.3 6.0 %collective-permute-start.11 = (f32[192,128]{1,0:T(8,128)S(1)}, f32[192,128]{1,0:T(8,128)S(1)}, u32[]{:S(2)}, u32[]{:S(2)}) collective-permute-start(f32[192,128]{1,0:T(8,128)S(1)} %get-tuple-element.82), channel_id=1, source_target_pairs={{0,4},{4,0},{8,12},{12,8},{16,20},{20,16},{24,28},{28,24},{1,5},{5... | collective-permute-start | bytes 294920 | tf_op jit(solution)/shard_map/ppermute | solution.py:472
  38.9 5.4 %collective-permute-start.12 = (f32[192,128]{1,0:T(8,128)S(1)}, f32[192,128]{1,0:T(8,128)S(1)}, u32[]{:S(2)}, u32[]{:S(2)}) collective-permute-start(f32[192,128]{1,0:T(8,128)S(1)} %get-tuple-element.83), channel_id=1, source_target_pairs={{0,8},{4,12},{8,0},{12,4},{16,24},{20,28},{24,16},{28,20},{1,9},{5... | collective-permute-start | bytes 294920 | tf_op jit(solution)/shard_map/ppermute | solution.py:472
  40.8 7.9 %collective-permute-start.14 = (f32[200,128]{1,0:T(8,128)S(1)}, f32[200,128]{1,0:T(8,128)S(1)}, u32[]{:S(2)}, u32[]{:S(2)}) collective-permute-start(f32[200,128]{1,0:T(8,128)S(1)} %get-tuple-element.93.s_ref.refs_3_), channel_id=1, source_target_pairs={{0,12},{4,8},{8,4},{12,0},{16,28},{20,24},{24,20},{28,16},{1,13},{... | collective-permute-start | bytes 307208 | tf_op jit(solution)/shard_map/ppermute | solution.py:472
  41.8 6.9 %collective-permute-start.15 = (f32[200,128]{1,0:T(8,128)S(1)}, f32[200,128]{1,0:T(8,128)S(1)}, u32[]{:S(2)}, u32[]{:S(2)}) collective-permute-start(f32[200,128]{1,0:T(8,128)S(1)} %get-tuple-element.93.s_ref.refs_3_), channel_id=1, source_target_pairs={{0,8},{4,12},{8,0},{12,4},{16,24},{20,28},{24,16},{28,20},{1,9},{5... | collective-permute-start | bytes 307208 | tf_op jit(solution)/shard_map/ppermute | solution.py:472
  42.9 5.7 %collective-permute-start.16 = (f32[200,128]{1,0:T(8,128)S(1)}, f32[200,128]{1,0:T(8,128)S(1)}, u32[]{:S(2)}, u32[]{:S(2)}) collective-permute-start(f32[200,128]{1,0:T(8,128)S(1)} %get-tuple-element.93.s_ref.refs_3_), channel_id=1, source_target_pairs={{0,4},{4,0},{8,12},{12,8},{16,20},{20,16},{24,28},{28,24},{1,5},{5... | collective-permute-start | bytes 307208 | tf_op jit(solution)/shard_map/ppermute | solution.py:472
  44.3 4.4 %copy-start.8 = (f32[8,64,64]{2,1,0:T(8,128)S(1)}, f32[8,64,64]{2,1,0:T(8,128)}, u32[]{:S(2)}) copy-start(f32[8,64,64]{2,1,0:T(8,128)} %refs_7_.1) | copy-start | bytes 393220
  44.7 6.6 %collective-permute-start.13 = (f32[200,128]{1,0:T(8,128)S(1)}, f32[200,128]{1,0:T(8,128)S(1)}, u32[]{:S(2)}, u32[]{:S(2)}) collective-permute-start(f32[200,128]{1,0:T(8,128)S(1)} %get-tuple-element.89.refs_0_), channel_id=1, source_target_pairs={{0,16},{4,20},{8,24},{12,28},{16,0},{20,4},{24,8},{28,12},{1,17},{... | collective-permute-start | bytes 307208 | tf_op jit(solution)/shard_map/ppermute | solution.py:472
  52.4 3.9 %collective-permute-start.20 = (f32[2,2,64,384]{3,2,1,0:T(8,128)S(1)}, f32[2,2,64,384]{3,2,1,0:T(8,128)S(1)}, u32[]{:S(2)}, u32[]{:S(2)}) collective-permute-start(f32[2,2,64,384]{3,2,1,0:T(8,128)S(1)} %get-tuple-element.111), channel_id=1, source_target_pairs={{0,1},{1,0},{2,3},{3,2},{4,5},{5,4},{6,7},{7,6},{8,9},{9,8},{10,11... | collective-permute-start | bytes 1179656 | tf_op jit(solution)/shard_map/ppermute | solution.py:472
  52.5 8.7 %collective-permute-start.17 = (f32[200,128]{1,0:T(8,128)S(1)}, f32[200,128]{1,0:T(8,128)S(1)}, u32[]{:S(2)}, u32[]{:S(2)}) collective-permute-start(f32[200,128]{1,0:T(8,128)S(1)} %get-tuple-element.104.refs_0_), channel_id=1, source_target_pairs={{0,4},{4,0},{8,12},{12,8},{16,20},{20,16},{24,28},{28,24},{1,5},{5... | collective-permute-start | bytes 307208 | tf_op jit(solution)/shard_map/ppermute | solution.py:472
  54.7 7.9 %collective-permute-start.18 = (f32[200,128]{1,0:T(8,128)S(1)}, f32[200,128]{1,0:T(8,128)S(1)}, u32[]{:S(2)}, u32[]{:S(2)}) collective-permute-start(f32[200,128]{1,0:T(8,128)S(1)} %get-tuple-element.104.refs_0_), channel_id=1, source_target_pairs={{0,8},{4,12},{8,0},{12,4},{16,24},{20,28},{24,16},{28,20},{1,9},{5... | collective-permute-start | bytes 307208 | tf_op jit(solution)/shard_map/ppermute | solution.py:472
  54.7 9.0 %collective-permute-start.19 = (f32[200,128]{1,0:T(8,128)S(1)}, f32[200,128]{1,0:T(8,128)S(1)}, u32[]{:S(2)}, u32[]{:S(2)}) collective-permute-start(f32[200,128]{1,0:T(8,128)S(1)} %get-tuple-element.104.refs_0_), channel_id=1, source_target_pairs={{0,12},{4,8},{8,4},{12,0},{16,28},{20,24},{24,20},{28,16},{1,13},{... | collective-permute-start | bytes 307208 | tf_op jit(solution)/shard_map/ppermute | solution.py:472
  56.3 9.6 %collective-permute-start.21 = (f32[64,384]{1,0:T(8,128)S(1)}, f32[64,384]{1,0:T(8,128)S(1)}, u32[]{:S(2)}, u32[]{:S(2)}) collective-permute-start(f32[64,384]{1,0:T(8,128)S(1)} %get-tuple-element.112), channel_id=1, source_target_pairs={{0,16},{1,20},{2,24},{3,28},{4,17},{5,21},{6,25},{7,29},{8,18},{9,... | collective-permute-start | bytes 294920 | tf_op jit(solution)/shard_map/ppermute | solution.py:620
  59.6 10.9 %collective-permute-start.22 = (f32[64,384]{1,0:T(8,128)S(1)}, f32[64,384]{1,0:T(8,128)S(1)}, u32[]{:S(2)}, u32[]{:S(2)}) collective-permute-start(f32[64,384]{1,0:T(8,128)S(1)} %get-tuple-element.114), channel_id=1, source_target_pairs={{0,24},{1,28},{2,16},{3,20},{4,25},{5,29},{6,17},{7,21},{8,26},{9,... | collective-permute-start | bytes 294920 | tf_op jit(solution)/shard_map/ppermute | solution.py:620
  61.2 9.3 %collective-permute-start.23 = (f32[64,384]{1,0:T(8,128)S(1)}, f32[64,384]{1,0:T(8,128)S(1)}, u32[]{:S(2)}, u32[]{:S(2)}) collective-permute-start(f32[64,384]{1,0:T(8,128)S(1)} %get-tuple-element.115), channel_id=1, source_target_pairs={{0,8},{1,12},{2,0},{3,4},{4,9},{5,13},{6,1},{7,5},{8,10},{9,14},{1... | collective-permute-start | bytes 294920 | tf_op jit(solution)/shard_map/ppermute | solution.py:620
  62.6 7.9 %collective-permute-start.24 = (f32[64,384]{1,0:T(8,128)S(1)}, f32[64,384]{1,0:T(8,128)S(1)}, u32[]{:S(2)}, u32[]{:S(2)}) collective-permute-start(f32[64,384]{1,0:T(8,128)S(1)} %get-tuple-element.116), channel_id=1, source_target_pairs={{0,0},{1,4},{2,8},{3,12},{4,1},{5,5},{6,9},{7,13},{8,2},{9,6},{10,... | collective-permute-start | bytes 294920 | tf_op jit(solution)/shard_map/ppermute | solution.py:620

commit v9 on v8

--- a/solution.py
+++ b/solution.py
@@ -480,6 +480,15 @@
     return [parts[0], *got[1:], got[0]]
 
 
+def gather(a, axis, count):
+    held = {0: a}
+    bit = count // 2
+    while bit:
+        held |= {d | bit: swap(b, axis, bit) for d, b in held.items()}
+        bit //= 2
+    return [held[d] for d in sorted(held)]
+
+
 def gather_halves(top, low, axis):
     near_low, next_top = swap(low, axis, 2), swap(top, axis, 1)
     near_top, next_low = swap(top, axis, 2), swap(low, axis, 1)
@@ -581,7 +590,7 @@
         "query_rows",
         shape((rows, width)),
         (
-            *trade([summary] * count, "sensor", False)[::-1],
+            *gather(summary, "sensor", count)[::-1],
             feat_rows,
             query_rows,
             local_att,

time: 71.5 us -> 70.8 us (level)
  waiting for transfers between devices: 16.9 us -> 15.5 us
    ppermute x21, waiting for transfers between devices: 12.4 us -> 10.9 us  [swap(): lax.ppermute(a, axis, [(i, i ^ bit) for i in range(lax.axis_size(axis))])]
  transfers between devices with their start and end apart: 25 -> 25, of which waited for: 10 -> 11; matrix products, arithmetic and copies ran while one was open for 0% -> 0% of each run, Pallas kernels for 11% -> 12%
where the time goes in v9:
time: 70.8 us; the launch traced here: 70.4 us
  starting transfers between devices  36.6 us (52%)
  waiting for transfers between devices  15.5 us (22%)
  Pallas kernels  11.5 us (16%)
  local copies, waits for them, and re-layouts  5.37 us (8%)
  between operations  1.46 us (2%)
    ppermute x21, starting transfers between devices, swap(): lax.ppermute(a, axis, [(i, i ^ bit) for i in range(lax.axis_size(axis))])  29.7 us
    pallas_call x14, Pallas kernels, call(): pl.pallas_call(kernel, name=name, out_shape=outs, in_specs=[SMEM] * smem...  11.5 us
    ppermute x21, waiting for transfers between devices, swap(): lax.ppermute(a, axis, [(i, i ^ bit) for i in range(lax.axis_size(axis))])  10.9 us
    ppermute x4, starting transfers between devices, turn(): return lax.ppermute(a, ('sensor', 'step'), pairs)  6.96 us
    unnamed x24, local copies, waits for them, and re-layouts  5.37 us
    ppermute x4, waiting for transfers between devices, turn(): return lax.ppermute(a, ('sensor', 'step'), pairs)  4.67 us
  transfers between devices with their start and end apart: 25, of which 11 were waited for; matrix products, arithmetic and copies ran while one was open for 0% of the time, Pallas kernels for 12%

profile of v9, /device:TPU:0, one launch (start us, length us, event | category | flops | bytes accessed | tf_op | source)
XLA Modules:
  0.0 70.4 jit_solution(2403571008627393546)
XLA Ops:
  1.3 0.9 %copy-done.9 = bf16[3,64,512]{2,1,0:T(8,128)(2,1)S(1)} copy-done((bf16[3,64,512]{2,1,0:T(8,128)(2,1)S(1)}, bf16[3,64,512]{2,1,0:T(8,128)(2,1)}, u32[]{:S(2)}) %copy-start.9) | copy-done | bytes 196632
  2.2 3.0 %collective-permute-start = (f32[104,512]{1,0:T(8,128)S(1)}, f32[104,512]{1,0:T(8,128)S(1)}, u32[]{:S(2)}, u32[]{:S(2)}) collective-permute-start(f32[104,512]{1,0:T(8,128)S(1)} %get-tuple-element.62.refs_0_), channel_id=1, source_target_pairs={{0,4},{4,0},{8,12},{12,8},{16,20},{20,16},{24,28},{28,24},{1,5},{5... | collective-permute-start | bytes 638984 | tf_op jit(solution)/shard_map/ppermute | solution.py:472
  5.3 1.6 %collective-permute-start.4 = (f32[104,512]{1,0:T(8,128)S(1)}, f32[104,512]{1,0:T(8,128)S(1)}, u32[]{:S(2)}, u32[]{:S(2)}) collective-permute-start(f32[104,512]{1,0:T(8,128)S(1)} %get-tuple-element.63.refs_4_), channel_id=1, source_target_pairs={{0,8},{4,12},{8,0},{12,4},{16,24},{20,28},{24,16},{28,20},{1,9},{5... | collective-permute-start | bytes 638984 | tf_op jit(solution)/shard_map/ppermute | solution.py:472
  6.8 0.4 collective-permute-start.1
  7.3 0.1 collective-permute-start.3
  7.4 4.0 %collective-permute-done.refs_1_ = f32[104,512]{1,0:T(8,128)S(1)} collective-permute-done((f32[104,512]{1,0:T(8,128)S(1)}, f32[104,512]{1,0:T(8,128)S(1)}, u32[]{:S(2)}, u32[]{:S(2)}) %collective-permute-start) | collective-permute-done | bytes 213024 | tf_op jit(solution)/shard_map/ppermute | solution.py:472
  11.4 2.1 %collective-permute-start.2 = (f32[104,512]{1,0:T(8,128)S(1)}, f32[104,512]{1,0:T(8,128)S(1)}, u32[]{:S(2)}, u32[]{:S(2)}) collective-permute-start(f32[104,512]{1,0:T(8,128)S(1)} %collective-permute-done.refs_1_), channel_id=1, source_target_pairs={{0,8},{4,12},{8,0},{12,4},{16,24},{20,28},{24,16},{28,20},{1,9},{5... | collective-permute-start | bytes 638984 | tf_op jit(solution)/shard_map/ppermute | solution.py:472
  13.5 1.5 %collective-permute-start.5 = (f32[104,512]{1,0:T(8,128)S(1)}, f32[104,512]{1,0:T(8,128)S(1)}, u32[]{:S(2)}, u32[]{:S(2)}) collective-permute-start(f32[104,512]{1,0:T(8,128)S(1)} %collective-permute-done.4.refs_6_), channel_id=1, source_target_pairs={{0,4},{4,0},{8,12},{12,8},{16,20},{20,16},{24,28},{28,24},{1,5},{5... | collective-permute-start | bytes 638984 | tf_op jit(solution)/shard_map/ppermute | solution.py:472
  15.0 1.0 %copy-done = bf16[512,512]{1,0:T(8,128)(2,1)S(1)} copy-done((bf16[512,512]{1,0:T(8,128)(2,1)S(1)}, bf16[512,512]{1,0:T(8,128)(2,1)}, u32[]{:S(2)}) %copy-start) | copy-done | bytes 524312
  16.0 1.0 %copy-done.2 = bf16[512,512]{1,0:T(8,128)(2,1)S(1)} copy-done((bf16[512,512]{1,0:T(8,128)(2,1)S(1)}, bf16[512,512]{1,0:T(8,128)(2,1)}, u32[]{:S(2)}) %copy-start.2) | copy-done | bytes 524312
  17.1 1.0 %copy-done.4 = bf16[512,512]{1,0:T(8,128)(2,1)S(1)} copy-done((bf16[512,512]{1,0:T(8,128)(2,1)S(1)}, bf16[512,512]{1,0:T(8,128)(2,1)}, u32[]{:S(2)}) %copy-start.4) | copy-done | bytes 524312
  18.1 0.9 %copy-done.7 = f32[8,64,64]{2,1,0:T(8,128)S(1)} copy-done((f32[8,64,64]{2,1,0:T(8,128)S(1)}, f32[8,64,64]{2,1,0:T(8,128)}, u32[]{:S(2)}) %copy-start.7) | copy-done | bytes 131096
  19.1 1.1 %local_keys.1 = (bf16[512,128]{1,0:T(8,128)(2,1)S(1)}, bf16[512,128]{1,0:T(8,128)(2,1)S(1)}, bf16[512,128]{1,0:T(8,128)(2,1)S(1)}, f32[64,128]{1,0:T(8,128)S(1)}...) custom-call(s32[1]{0:T(128)S(6)} %copy.13.live_ref, ...), custom_call_target="tpu_custom_call" | custom-call | flops 301989888 | bytes 4292612 | tf_op jit(solution)/shard_map/local_keys/pallas_call | solution.py:451
  20.2 0.0 collective-permute-done.3.refs_5_
  20.2 0.9 %collective-permute-done.2.refs_3_ = f32[104,512]{1,0:T(8,128)S(1)} collective-permute-done((f32[104,512]{1,0:T(8,128)S(1)}, f32[104,512]{1,0:T(8,128)S(1)}, u32[]{:S(2)}, u32[]{:S(2)}) %collective-permute-start.2) | collective-permute-done | bytes 213024 | tf_op jit(solution)/shard_map/ppermute | solution.py:472
  21.1 1.1 %keys.1 = (bf16[768,512]{1,0:T(8,128)(2,1)S(1)}, f32[768,128]{1,0:T(8,128)S(1)}, f32[768,128]{1,0:T(8,128)S(1)}, f32[768,128]{1,0:T(8,128)S(1)}, f32[200,128]{1,0:T(8,128)S(1)}) custom-call(f32[104,512]{1,0:T(8,128)S(1)} %get-tuple-element.62.refs_0_, f32[104,512]{1,0:T(8,128)S(1)} %collective-permute-done.refs_1_, ...), custom_call_target="tpu_custom_call" | custom-call | flops 301989888 | bytes 4067328 | tf_op jit(solution)/shard_map/keys/pallas_call | solution.py:451
  22.2 2.6 %collective-permute-start.6 = (f32[200,128]{1,0:T(8,128)S(1)}, f32[200,128]{1,0:T(8,128)S(1)}, u32[]{:S(2)}, u32[]{:S(2)}) collective-permute-start(f32[200,128]{1,0:T(8,128)S(1)} %get-tuple-element.67.refs_0_), channel_id=1, source_target_pairs={{0,16},{4,20},{8,24},{12,28},{16,0},{20,4},{24,8},{28,12},{1,17},{... | collective-permute-start | bytes 307208 | tf_op jit(solution)/shard_map/ppermute | solution.py:472
  24.9 0.0 copy-start.6
  24.9 0.9 %queries.1 = (f32[768,128]{1,0:T(8,128)S(1)}, f32[768,128]{1,0:T(8,128)S(1)}, f32[192,256]{1,0:T(8,128)S(1)}) custom-call(s32[1]{0:T(128)S(6)} %copy.13.live_ref, bf16[768,512]{1,0:T(8,128)(2,1)S(1)} %get-tuple-element.68.x_ref.refs_0_, bf16[192,512]{1,0:T(8,128)(2,1)S(1)} %bitcast.5, bf16[512,128]{1,0:T(8,128)(2,1)S(1)} %get-tuple-element.69.wq_ref, ...), custom_call_target="tpu_custom_call" | custom-call | flops 201326592 | bytes 2392068 | tf_op jit(solution)/shard_map/queries/pallas_call | solution.py:451
  25.8 0.0 copy-start.1
  25.8 2.0 %collective-permute-done.6.refs_1_ = f32[200,128]{1,0:T(8,128)S(1)} collective-permute-done((f32[200,128]{1,0:T(8,128)S(1)}, f32[200,128]{1,0:T(8,128)S(1)}, u32[]{:S(2)}, u32[]{:S(2)}) %collective-permute-start.6) | collective-permute-done | bytes 102432 | tf_op jit(solution)/shard_map/ppermute | solution.py:472
  27.8 0.4 attend.1
  28.2 1.8 %collective-permute-start.7 = (f32[192,128]{1,0:T(8,128)S(1)}, f32[192,128]{1,0:T(8,128)S(1)}, u32[]{:S(2)}, u32[]{:S(2)}) collective-permute-start(f32[192,128]{1,0:T(8,128)S(1)} %get-tuple-element.72), channel_id=1, source_target_pairs={{0,12},{4,8},{8,4},{12,0},{16,28},{20,24},{24,20},{28,16},{1,13},{... | collective-permute-start | bytes 294920 | tf_op jit(solution)/shard_map/ppermute | solution.py:472
  30.0 1.5 %collective-permute-start.8 = (f32[192,128]{1,0:T(8,128)S(1)}, f32[192,128]{1,0:T(8,128)S(1)}, u32[]{:S(2)}, u32[]{:S(2)}) collective-permute-start(f32[192,128]{1,0:T(8,128)S(1)} %get-tuple-element.73), channel_id=1, source_target_pairs={{0,4},{4,0},{8,12},{12,8},{16,20},{20,16},{24,28},{28,24},{1,5},{5... | collective-permute-start | bytes 294920 | tf_op jit(solution)/shard_map/ppermute | solution.py:472
  31.5 0.3 collective-permute-start.9
  31.8 1.8 %collective-permute-start.14 = (f32[200,128]{1,0:T(8,128)S(1)}, f32[200,128]{1,0:T(8,128)S(1)}, u32[]{:S(2)}, u32[]{:S(2)}) collective-permute-start(f32[200,128]{1,0:T(8,128)S(1)} %get-tuple-element.93.s_ref.refs_3_), channel_id=1, source_target_pairs={{0,8},{4,12},{8,0},{12,4},{16,24},{20,28},{24,16},{28,20},{1,9},{5... | collective-permute-start | bytes 307208 | tf_op jit(solution)/shard_map/ppermute | solution.py:472
  33.6 0.7 %transposes.1 = (bf16[512,768]{1,0:T(8,128)(2,1)S(1)}, bf16[512,512]{1,0:T(8,128)(2,1)S(1)}, bf16[512,512]{1,0:T(8,128)(2,1)S(1)}, bf16[512,512]{1,0:T(8,128)(2,1)S(1)}, bf16[256,512]{1,0:T(8,128)(2,1)S(1)}) custom-call(bf16[768,512]{1,0:T(8,128)(2,1)S(1)} %get-tuple-element.68.x_ref.refs_0_, bf16[512,512]{1,0:T(8,128)(2,1)S(1)} %copy-done.1, ...), custom_call_target="tpu_custom_call" | custom-call | bytes 5242880 | tf_op jit(solution)/shard_map/transposes/pallas_call | solution.py:451
  34.3 0.3 collective-permute-done.7.refs_3_
  34.6 0.7 collective-permute-done.8.refs_1_
  35.3 1.2 %collective-permute-done.9.refs_2_ = f32[192,128]{1,0:T(8,128)S(1)} collective-permute-done((f32[192,128]{1,0:T(8,128)S(1)}, f32[192,128]{1,0:T(8,128)S(1)}, u32[]{:S(2)}, u32[]{:S(2)}) %collective-permute-start.9) | collective-permute-done | bytes 98336 | tf_op jit(solution)/shard_map/ppermute | solution.py:472
  36.5 0.7 %feed_forward.1 = (f32[192,512]{1,0:T(8,128)S(1)}, f32[192,512]{1,0:T(8,128)S(1)}, f32[192,128]{1,0:T(8,128)S(1)}, f32[192,128]{1,0:T(8,128)S(1)}, f32[192,128]{1,0:T(8,128)S(1)}, /*index=5*/f32[192,128]{1,0:T(8,128)S(1)}) custom-call(f32[192,128]{1,0:T(8,128)S(1)} %get-tuple-element.71.refs_0_, f32[192,128]{1,0:T(8,128)S(1)} %collective-permute-done.8.refs_1_, ...), custom_call_target="tpu_custom_call" | custom-call | flops 100663296 | bytes 2293760 | tf_op jit(solution)/shard_map/feed_forward/pallas_call | solution.py:451
  37.2 1.1 %collective-permute-start.10 = (f32[192,128]{1,0:T(8,128)S(1)}, f32[192,128]{1,0:T(8,128)S(1)}, u32[]{:S(2)}, u32[]{:S(2)}) collective-permute-start(f32[192,128]{1,0:T(8,128)S(1)} %get-tuple-element.81), channel_id=1, source_target_pairs={{0,12},{4,8},{8,4},{12,0},{16,28},{20,24},{24,20},{28,16},{1,13},{... | collective-permute-start | bytes 294920 | tf_op jit(solution)/shard_map/ppermute | solution.py:472
  38.3 0.8 %collective-permute-start.11 = (f32[192,128]{1,0:T(8,128)S(1)}, f32[192,128]{1,0:T(8,128)S(1)}, u32[]{:S(2)}, u32[]{:S(2)}) collective-permute-start(f32[192,128]{1,0:T(8,128)S(1)} %get-tuple-element.82), channel_id=1, source_target_pairs={{0,4},{4,0},{8,12},{12,8},{16,20},{20,16},{24,28},{28,24},{1,5},{5... | collective-permute-start | bytes 294920 | tf_op jit(solution)/shard_map/ppermute | solution.py:472
  39.0 1.7 %collective-permute-start.12 = (f32[192,128]{1,0:T(8,128)S(1)}, f32[192,128]{1,0:T(8,128)S(1)}, u32[]{:S(2)}, u32[]{:S(2)}) collective-permute-start(f32[192,128]{1,0:T(8,128)S(1)} %get-tuple-element.83), channel_id=1, source_target_pairs={{0,8},{4,12},{8,0},{12,4},{16,24},{20,28},{24,16},{28,20},{1,9},{5... | collective-permute-start | bytes 294920 | tf_op jit(solution)/shard_map/ppermute | solution.py:472
  40.8 0.4 collective-permute-start.16
  41.2 0.0 collective-permute-done.14.refs_1_
  41.2 1.6 %collective-permute-start.15 = (f32[200,128]{1,0:T(8,128)S(1)}, f32[200,128]{1,0:T(8,128)S(1)}, u32[]{:S(2)}, u32[]{:S(2)}) collective-permute-start(f32[200,128]{1,0:T(8,128)S(1)} %collective-permute-done.14.refs_1_), channel_id=1, source_target_pairs={{0,4},{4,0},{8,12},{12,8},{16,20},{20,16},{24,28},{28,24},{1,5},{5... | collective-permute-start | bytes 307208 | tf_op jit(solution)/shard_map/ppermute | solution.py:472
  42.8 0.1 collective-permute-done.10.refs_3_
  42.9 0.9 %collective-permute-done.11.refs_1_ = f32[192,128]{1,0:T(8,128)S(1)} collective-permute-done((f32[192,128]{1,0:T(8,128)S(1)}, f32[192,128]{1,0:T(8,128)S(1)}, u32[]{:S(2)}, u32[]{:S(2)}) %collective-permute-start.11) | collective-permute-done | bytes 98336 | tf_op jit(solution)/shard_map/ppermute | solution.py:472
  43.9 0.0 collective-permute-done.12.refs_2_
  43.9 0.4 grad_summary.1
  44.3 3.5 %collective-permute-start.13 = (f32[200,128]{1,0:T(8,128)S(1)}, f32[200,128]{1,0:T(8,128)S(1)}, u32[]{:S(2)}, u32[]{:S(2)}) collective-permute-start(f32[200,128]{1,0:T(8,128)S(1)} %get-tuple-element.89.refs_0_), channel_id=1, source_target_pairs={{0,16},{4,20},{8,24},{12,28},{16,0},{20,4},{24,8},{28,12},{1,17},{... | collective-permute-start | bytes 307208 | tf_op jit(solution)/shard_map/ppermute | solution.py:472
  47.7 0.6 query_back.1.refs_6_
  48.3 0.3 copy-done.8
  48.7 1.4 %query_rows.1.refs_8_ = f32[192,512]{1,0:T(8,128)S(1)} custom-call(f32[200,128]{1,0:T(8,128)S(1)} %collective-permute-done.15.refs_0_, f32[200,128]{1,0:T(8,128)S(1)} %collective-permute-done.14.refs_1_, f32[200,128]{1,0:T(8,128)S(1)} %collective-permute-done.16.refs_2_, f32[200,128]{1,0:T(8,128)S(1)} %get-tuple-element.93.s_ref.refs_3_, ...), custom_call_target="tpu_custom_call" | custom-call | flops 301989888 | bytes 3031040 | tf_op jit(solution)/shard_map/query_rows/pallas_call | solution.py:451
  50.1 0.3 collective-permute-done.13.refs_1_
  50.4 1.1 %key_back.1 = (f32[200,128]{1,0:T(8,128)S(1)}, f32[2,2,64,384]{3,2,1,0:T(8,128)S(1)}, f32[2,2,64,384]{3,2,1,0:T(8,128)S(1)}) custom-call(f32[200,128]{1,0:T(8,128)S(1)} %get-tuple-element.89.refs_0_, f32[200,128]{1,0:T(8,128)S(1)} %collective-permute-done.13.refs_1_, f32[768,128]{1,0:T(8,128)S(1)} %get-tuple-element.90.refs_2_, ...), custom_call_target="tpu_custom_call" | custom-call | flops 402653184 | bytes 3289088 | tf_op jit(solution)/shard_map/key_back/pallas_call | solution.py:451
  51.4 0.1 collective-permute-start.20
  51.5 2.3 %collective-permute-start.17 = (f32[200,128]{1,0:T(8,128)S(1)}, f32[200,128]{1,0:T(8,128)S(1)}, u32[]{:S(2)}, u32[]{:S(2)}) collective-permute-start(f32[200,128]{1,0:T(8,128)S(1)} %get-tuple-element.104.refs_0_), channel_id=1, source_target_pairs={{0,4},{4,0},{8,12},{12,8},{16,20},{20,16},{24,28},{28,24},{1,5},{5... | collective-permute-start | bytes 307208 | tf_op jit(solution)/shard_map/ppermute | solution.py:472
  53.8 0.8 %collective-permute-start.18 = (f32[200,128]{1,0:T(8,128)S(1)}, f32[200,128]{1,0:T(8,128)S(1)}, u32[]{:S(2)}, u32[]{:S(2)}) collective-permute-start(f32[200,128]{1,0:T(8,128)S(1)} %get-tuple-element.104.refs_0_), channel_id=1, source_target_pairs={{0,8},{4,12},{8,0},{12,4},{16,24},{20,28},{24,16},{28,20},{1,9},{5... | collective-permute-start | bytes 307208 | tf_op jit(solution)/shard_map/ppermute | solution.py:472
  54.6 0.7 collective-permute-start.19
  55.3 0.0 collective-permute-done.20.got_ref
  55.4 3.3 %collective-permute-start.21 = (f32[64,384]{1,0:T(8,128)S(1)}, f32[64,384]{1,0:T(8,128)S(1)}, u32[]{:S(2)}, u32[]{:S(2)}) collective-permute-start(f32[64,384]{1,0:T(8,128)S(1)} %get-tuple-element.112), channel_id=1, source_target_pairs={{0,16},{1,20},{2,24},{3,28},{4,17},{5,21},{6,25},{7,29},{8,18},{9,... | collective-permute-start | bytes 294920 | tf_op jit(solution)/shard_map/ppermute | solution.py:629
  58.6 1.6 %collective-permute-start.22 = (f32[64,384]{1,0:T(8,128)S(1)}, f32[64,384]{1,0:T(8,128)S(1)}, u32[]{:S(2)}, u32[]{:S(2)}) collective-permute-start(f32[64,384]{1,0:T(8,128)S(1)} %get-tuple-element.114), channel_id=1, source_target_pairs={{0,24},{1,28},{2,16},{3,20},{4,25},{5,29},{6,17},{7,21},{8,26},{9,... | collective-permute-start | bytes 294920 | tf_op jit(solution)/shard_map/ppermute | solution.py:629
  60.2 0.0 collective-permute-done.17.refs_1_
  60.2 1.5 %collective-permute-start.23 = (f32[64,384]{1,0:T(8,128)S(1)}, f32[64,384]{1,0:T(8,128)S(1)}, u32[]{:S(2)}, u32[]{:S(2)}) collective-permute-start(f32[64,384]{1,0:T(8,128)S(1)} %get-tuple-element.115), channel_id=1, source_target_pairs={{0,8},{1,12},{2,0},{3,4},{4,9},{5,13},{6,1},{7,5},{8,10},{9,14},{1... | collective-permute-start | bytes 294920 | tf_op jit(solution)/shard_map/ppermute | solution.py:629
  61.7 0.0 collective-permute-done.18.refs_2_
  61.7 0.7 collective-permute-start.24
  62.4 0.5 collective-permute-done.19.refs_3_
  62.9 2.3 %input_rows.1 = bf16[192,512]{1,0:T(8,128)(2,1)} custom-call(f32[200,128]{1,0:T(8,128)S(1)} %get-tuple-element.104.refs_0_, f32[200,128]{1,0:T(8,128)S(1)} %collective-permute-done.17.refs_1_, f32[200,128]{1,0:T(8,128)S(1)} %collective-permute-done.18.refs_2_, f32[200,128]{1,0:T(8,128)S(1)} %collective-permute-done.19.refs_3_, ...), custom_call_target="tpu_custom_call" | custom-call | flops 3019898880 | bytes 3358720 | tf_op jit(solution)/shard_map/input_rows/pallas_call | solution.py:451
  65.1 0.0 collective-permute-done.21.refs_0_
  65.1 4.7 %collective-permute-done.22.refs_1_ = f32[64,384]{1,0:T(8,128)S(1)} collective-permute-done((f32[64,384]{1,0:T(8,128)S(1)}, f32[64,384]{1,0:T(8,128)S(1)}, u32[]{:S(2)}, u32[]{:S(2)}) %collective-permute-start.22) | collective-permute-done | bytes 98336 | tf_op jit(solution)/shard_map/ppermute | solution.py:629
  69.8 0.0 collective-permute-done.23.refs_2_
  69.8 0.7 weight_sums.1
  (24 shorter events, 0.1 us)
Async XLA Ops:
  1.3 0.9 %copy-start.9 = (bf16[3,64,512]{2,1,0:T(8,128)(2,1)S(1)}, bf16[3,64,512]{2,1,0:T(8,128)(2,1)}, u32[]{:S(2)}) copy-start(bf16[3,64,512]{2,1,0:T(8,128)(2,1)} %param.9) | copy-start | bytes 589828
  2.2 9.1 %collective-permute-start = (f32[104,512]{1,0:T(8,128)S(1)}, f32[104,512]{1,0:T(8,128)S(1)}, u32[]{:S(2)}, u32[]{:S(2)}) collective-permute-start(f32[104,512]{1,0:T(8,128)S(1)} %get-tuple-element.62.refs_0_), channel_id=1, source_target_pairs={{0,4},{4,0},{8,12},{12,8},{16,20},{20,16},{24,28},{28,24},{1,5},{5... | collective-permute-start | bytes 638984 | tf_op jit(solution)/shard_map/ppermute | solution.py:472
  5.3 8.2 %collective-permute-start.4 = (f32[104,512]{1,0:T(8,128)S(1)}, f32[104,512]{1,0:T(8,128)S(1)}, u32[]{:S(2)}, u32[]{:S(2)}) collective-permute-start(f32[104,512]{1,0:T(8,128)S(1)} %get-tuple-element.63.refs_4_), channel_id=1, source_target_pairs={{0,8},{4,12},{8,0},{12,4},{16,24},{20,28},{24,16},{28,20},{1,9},{5... | collective-permute-start | bytes 638984 | tf_op jit(solution)/shard_map/ppermute | solution.py:472
  6.8 13.4 %collective-permute-start.1 = (f32[104,512]{1,0:T(8,128)S(1)}, f32[104,512]{1,0:T(8,128)S(1)}, u32[]{:S(2)}, u32[]{:S(2)}) collective-permute-start(f32[104,512]{1,0:T(8,128)S(1)} %get-tuple-element.62.refs_0_), channel_id=1, source_target_pairs={{0,8},{4,12},{8,0},{12,4},{16,24},{20,28},{24,16},{28,20},{1,9},{5... | collective-permute-start | bytes 638984 | tf_op jit(solution)/shard_map/ppermute | solution.py:472
  7.3 12.9 %collective-permute-start.3 = (f32[104,512]{1,0:T(8,128)S(1)}, f32[104,512]{1,0:T(8,128)S(1)}, u32[]{:S(2)}, u32[]{:S(2)}) collective-permute-start(f32[104,512]{1,0:T(8,128)S(1)} %get-tuple-element.63.refs_4_), channel_id=1, source_target_pairs={{0,4},{4,0},{8,12},{12,8},{16,20},{20,16},{24,28},{28,24},{1,5},{5... | collective-permute-start | bytes 638984 | tf_op jit(solution)/shard_map/ppermute | solution.py:472
  11.4 9.8 %collective-permute-start.2 = (f32[104,512]{1,0:T(8,128)S(1)}, f32[104,512]{1,0:T(8,128)S(1)}, u32[]{:S(2)}, u32[]{:S(2)}) collective-permute-start(f32[104,512]{1,0:T(8,128)S(1)} %collective-permute-done.refs_1_), channel_id=1, source_target_pairs={{0,8},{4,12},{8,0},{12,4},{16,24},{20,28},{24,16},{28,20},{1,9},{5... | collective-permute-start | bytes 638984 | tf_op jit(solution)/shard_map/ppermute | solution.py:472
  13.5 7.6 %collective-permute-start.5 = (f32[104,512]{1,0:T(8,128)S(1)}, f32[104,512]{1,0:T(8,128)S(1)}, u32[]{:S(2)}, u32[]{:S(2)}) collective-permute-start(f32[104,512]{1,0:T(8,128)S(1)} %collective-permute-done.4.refs_6_), channel_id=1, source_target_pairs={{0,4},{4,0},{8,12},{12,8},{16,20},{20,16},{24,28},{28,24},{1,5},{5... | collective-permute-start | bytes 638984 | tf_op jit(solution)/shard_map/ppermute | solution.py:472
  15.0 1.0 %copy-start = (bf16[512,512]{1,0:T(8,128)(2,1)S(1)}, bf16[512,512]{1,0:T(8,128)(2,1)}, u32[]{:S(2)}) copy-start(bf16[512,512]{1,0:T(8,128)(2,1)} %refs_1_.1) | copy-start | bytes 1572868
  16.0 1.0 %copy-start.2 = (bf16[512,512]{1,0:T(8,128)(2,1)S(1)}, bf16[512,512]{1,0:T(8,128)(2,1)}, u32[]{:S(2)}) copy-start(bf16[512,512]{1,0:T(8,128)(2,1)} %refs_2_.1) | copy-start | bytes 1572868
  17.1 1.0 %copy-start.4 = (bf16[512,512]{1,0:T(8,128)(2,1)S(1)}, bf16[512,512]{1,0:T(8,128)(2,1)}, u32[]{:S(2)}) copy-start(bf16[512,512]{1,0:T(8,128)(2,1)} %refs_3_.1) | copy-start | bytes 1572868
  18.1 0.9 %copy-start.7 = (f32[8,64,64]{2,1,0:T(8,128)S(1)}, f32[8,64,64]{2,1,0:T(8,128)}, u32[]{:S(2)}) copy-start(f32[8,64,64]{2,1,0:T(8,128)} %refs_7_.1) | copy-start | bytes 393220
  21.1 3.7 %copy-start.10 = (bf16[256,512]{1,0:T(8,128)(2,1)S(1)}, bf16[256,512]{1,0:T(8,128)(2,1)}, u32[]{:S(2)}) copy-start(bf16[256,512]{1,0:T(8,128)(2,1)} %wd_ref.1) | copy-start | bytes 786436
  21.1 3.7 %copy-start.11 = (bf16[3,64,512]{2,1,0:T(8,128)(2,1)S(1)}, bf16[3,64,512]{2,1,0:T(8,128)(2,1)}, u32[]{:S(2)}) copy-start(bf16[3,64,512]{2,1,0:T(8,128)(2,1)} %param.10) | copy-start | bytes 589828
  22.2 5.6 %collective-permute-start.6 = (f32[200,128]{1,0:T(8,128)S(1)}, f32[200,128]{1,0:T(8,128)S(1)}, u32[]{:S(2)}, u32[]{:S(2)}) collective-permute-start(f32[200,128]{1,0:T(8,128)S(1)} %get-tuple-element.67.refs_0_), channel_id=1, source_target_pairs={{0,16},{4,20},{8,24},{12,28},{16,0},{20,4},{24,8},{28,12},{1,17},{... | collective-permute-start | bytes 307208 | tf_op jit(solution)/shard_map/ppermute | solution.py:472
  24.9 8.7 %copy-start.3 = (bf16[512,512]{1,0:T(8,128)(2,1)S(1)}, bf16[512,512]{1,0:T(8,128)(2,1)}, u32[]{:S(2)}) copy-start(bf16[512,512]{1,0:T(8,128)(2,1)} %refs_2_.1) | copy-start | bytes 1572868
  24.9 8.7 %copy-start.5 = (bf16[512,512]{1,0:T(8,128)(2,1)S(1)}, bf16[512,512]{1,0:T(8,128)(2,1)}, u32[]{:S(2)}) copy-start(bf16[512,512]{1,0:T(8,128)(2,1)} %refs_3_.1) | copy-start | bytes 1572868
  24.9 8.7 %copy-start.6 = (bf16[512,256]{1,0:T(8,128)(2,1)S(1)}, bf16[512,256]{1,0:T(8,128)(2,1)}, u32[]{:S(2)}) copy-start(bf16[512,256]{1,0:T(8,128)(2,1)} %refs_5_.1) | copy-start | bytes 786436
  25.8 7.7 %copy-start.1 = (bf16[512,512]{1,0:T(8,128)(2,1)S(1)}, bf16[512,512]{1,0:T(8,128)(2,1)}, u32[]{:S(2)}) copy-start(bf16[512,512]{1,0:T(8,128)(2,1)} %refs_1_.1) | copy-start | bytes 1572868
  28.2 6.4 %collective-permute-start.7 = (f32[192,128]{1,0:T(8,128)S(1)}, f32[192,128]{1,0:T(8,128)S(1)}, u32[]{:S(2)}, u32[]{:S(2)}) collective-permute-start(f32[192,128]{1,0:T(8,128)S(1)} %get-tuple-element.72), channel_id=1, source_target_pairs={{0,12},{4,8},{8,4},{12,0},{16,28},{20,24},{24,20},{28,16},{1,13},{... | collective-permute-start | bytes 294920 | tf_op jit(solution)/shard_map/ppermute | solution.py:472
  30.0 5.3 %collective-permute-start.8 = (f32[192,128]{1,0:T(8,128)S(1)}, f32[192,128]{1,0:T(8,128)S(1)}, u32[]{:S(2)}, u32[]{:S(2)}) collective-permute-start(f32[192,128]{1,0:T(8,128)S(1)} %get-tuple-element.73), channel_id=1, source_target_pairs={{0,4},{4,0},{8,12},{12,8},{16,20},{20,16},{24,28},{28,24},{1,5},{5... | collective-permute-start | bytes 294920 | tf_op jit(solution)/shard_map/ppermute | solution.py:472
  31.5 5.0 %collective-permute-start.9 = (f32[192,128]{1,0:T(8,128)S(1)}, f32[192,128]{1,0:T(8,128)S(1)}, u32[]{:S(2)}, u32[]{:S(2)}) collective-permute-start(f32[192,128]{1,0:T(8,128)S(1)} %get-tuple-element.74), channel_id=1, source_target_pairs={{0,8},{4,12},{8,0},{12,4},{16,24},{20,28},{24,16},{28,20},{1,9},{5... | collective-permute-start | bytes 294920 | tf_op jit(solution)/shard_map/ppermute | solution.py:472
  31.8 9.4 %collective-permute-start.14 = (f32[200,128]{1,0:T(8,128)S(1)}, f32[200,128]{1,0:T(8,128)S(1)}, u32[]{:S(2)}, u32[]{:S(2)}) collective-permute-start(f32[200,128]{1,0:T(8,128)S(1)} %get-tuple-element.93.s_ref.refs_3_), channel_id=1, source_target_pairs={{0,8},{4,12},{8,0},{12,4},{16,24},{20,28},{24,16},{28,20},{1,9},{5... | collective-permute-start | bytes 307208 | tf_op jit(solution)/shard_map/ppermute | solution.py:472
  37.2 5.7 %collective-permute-start.10 = (f32[192,128]{1,0:T(8,128)S(1)}, f32[192,128]{1,0:T(8,128)S(1)}, u32[]{:S(2)}, u32[]{:S(2)}) collective-permute-start(f32[192,128]{1,0:T(8,128)S(1)} %get-tuple-element.81), channel_id=1, source_target_pairs={{0,12},{4,8},{8,4},{12,0},{16,28},{20,24},{24,20},{28,16},{1,13},{... | collective-permute-start | bytes 294920 | tf_op jit(solution)/shard_map/ppermute | solution.py:472
  38.3 5.6 %collective-permute-start.11 = (f32[192,128]{1,0:T(8,128)S(1)}, f32[192,128]{1,0:T(8,128)S(1)}, u32[]{:S(2)}, u32[]{:S(2)}) collective-permute-start(f32[192,128]{1,0:T(8,128)S(1)} %get-tuple-element.82), channel_id=1, source_target_pairs={{0,4},{4,0},{8,12},{12,8},{16,20},{20,16},{24,28},{28,24},{1,5},{5... | collective-permute-start | bytes 294920 | tf_op jit(solution)/shard_map/ppermute | solution.py:472
  39.0 4.8 %collective-permute-start.12 = (f32[192,128]{1,0:T(8,128)S(1)}, f32[192,128]{1,0:T(8,128)S(1)}, u32[]{:S(2)}, u32[]{:S(2)}) collective-permute-start(f32[192,128]{1,0:T(8,128)S(1)} %get-tuple-element.83), channel_id=1, source_target_pairs={{0,8},{4,12},{8,0},{12,4},{16,24},{20,28},{24,16},{28,20},{1,9},{5... | collective-permute-start | bytes 294920 | tf_op jit(solution)/shard_map/ppermute | solution.py:472
  40.8 7.5 %collective-permute-start.16 = (f32[200,128]{1,0:T(8,128)S(1)}, f32[200,128]{1,0:T(8,128)S(1)}, u32[]{:S(2)}, u32[]{:S(2)}) collective-permute-start(f32[200,128]{1,0:T(8,128)S(1)} %get-tuple-element.93.s_ref.refs_3_), channel_id=1, source_target_pairs={{0,4},{4,0},{8,12},{12,8},{16,20},{20,16},{24,28},{28,24},{1,5},{5... | collective-permute-start | bytes 307208 | tf_op jit(solution)/shard_map/ppermute | solution.py:472
  41.2 7.1 %collective-permute-start.15 = (f32[200,128]{1,0:T(8,128)S(1)}, f32[200,128]{1,0:T(8,128)S(1)}, u32[]{:S(2)}, u32[]{:S(2)}) collective-permute-start(f32[200,128]{1,0:T(8,128)S(1)} %collective-permute-done.14.refs_1_), channel_id=1, source_target_pairs={{0,4},{4,0},{8,12},{12,8},{16,20},{20,16},{24,28},{28,24},{1,5},{5... | collective-permute-start | bytes 307208 | tf_op jit(solution)/shard_map/ppermute | solution.py:472
  44.3 6.1 %collective-permute-start.13 = (f32[200,128]{1,0:T(8,128)S(1)}, f32[200,128]{1,0:T(8,128)S(1)}, u32[]{:S(2)}, u32[]{:S(2)}) collective-permute-start(f32[200,128]{1,0:T(8,128)S(1)} %get-tuple-element.89.refs_0_), channel_id=1, source_target_pairs={{0,16},{4,20},{8,24},{12,28},{16,0},{20,4},{24,8},{28,12},{1,17},{... | collective-permute-start | bytes 307208 | tf_op jit(solution)/shard_map/ppermute | solution.py:472
  47.7 0.9 %copy-start.8 = (f32[8,64,64]{2,1,0:T(8,128)S(1)}, f32[8,64,64]{2,1,0:T(8,128)}, u32[]{:S(2)}) copy-start(f32[8,64,64]{2,1,0:T(8,128)} %refs_7_.1) | copy-start | bytes 393220
  51.4 3.9 %collective-permute-start.20 = (f32[2,2,64,384]{3,2,1,0:T(8,128)S(1)}, f32[2,2,64,384]{3,2,1,0:T(8,128)S(1)}, u32[]{:S(2)}, u32[]{:S(2)}) collective-permute-start(f32[2,2,64,384]{3,2,1,0:T(8,128)S(1)} %get-tuple-element.111), channel_id=1, source_target_pairs={{0,1},{1,0},{2,3},{3,2},{4,5},{5,4},{6,7},{7,6},{8,9},{9,8},{10,11... | collective-permute-start | bytes 1179656 | tf_op jit(solution)/shard_map/ppermute | solution.py:472
  51.5 8.7 %collective-permute-start.17 = (f32[200,128]{1,0:T(8,128)S(1)}, f32[200,128]{1,0:T(8,128)S(1)}, u32[]{:S(2)}, u32[]{:S(2)}) collective-permute-start(f32[200,128]{1,0:T(8,128)S(1)} %get-tuple-element.104.refs_0_), channel_id=1, source_target_pairs={{0,4},{4,0},{8,12},{12,8},{16,20},{20,16},{24,28},{28,24},{1,5},{5... | collective-permute-start | bytes 307208 | tf_op jit(solution)/shard_map/ppermute | solution.py:472
  53.8 7.9 %collective-permute-start.18 = (f32[200,128]{1,0:T(8,128)S(1)}, f32[200,128]{1,0:T(8,128)S(1)}, u32[]{:S(2)}, u32[]{:S(2)}) collective-permute-start(f32[200,128]{1,0:T(8,128)S(1)} %get-tuple-element.104.refs_0_), channel_id=1, source_target_pairs={{0,8},{4,12},{8,0},{12,4},{16,24},{20,28},{24,16},{28,20},{1,9},{5... | collective-permute-start | bytes 307208 | tf_op jit(solution)/shard_map/ppermute | solution.py:472
  54.6 8.2 %collective-permute-start.19 = (f32[200,128]{1,0:T(8,128)S(1)}, f32[200,128]{1,0:T(8,128)S(1)}, u32[]{:S(2)}, u32[]{:S(2)}) collective-permute-start(f32[200,128]{1,0:T(8,128)S(1)} %get-tuple-element.104.refs_0_), channel_id=1, source_target_pairs={{0,12},{4,8},{8,4},{12,0},{16,28},{20,24},{24,20},{28,16},{1,13},{... | collective-permute-start | bytes 307208 | tf_op jit(solution)/shard_map/ppermute | solution.py:472
  55.4 9.7 %collective-permute-start.21 = (f32[64,384]{1,0:T(8,128)S(1)}, f32[64,384]{1,0:T(8,128)S(1)}, u32[]{:S(2)}, u32[]{:S(2)}) collective-permute-start(f32[64,384]{1,0:T(8,128)S(1)} %get-tuple-element.112), channel_id=1, source_target_pairs={{0,16},{1,20},{2,24},{3,28},{4,17},{5,21},{6,25},{7,29},{8,18},{9,... | collective-permute-start | bytes 294920 | tf_op jit(solution)/shard_map/ppermute | solution.py:629
  58.6 11.1 %collective-permute-start.22 = (f32[64,384]{1,0:T(8,128)S(1)}, f32[64,384]{1,0:T(8,128)S(1)}, u32[]{:S(2)}, u32[]{:S(2)}) collective-permute-start(f32[64,384]{1,0:T(8,128)S(1)} %get-tuple-element.114), channel_id=1, source_target_pairs={{0,24},{1,28},{2,16},{3,20},{4,25},{5,29},{6,17},{7,21},{8,26},{9,... | collective-permute-start | bytes 294920 | tf_op jit(solution)/shard_map/ppermute | solution.py:629
  60.2 9.6 %collective-permute-start.23 = (f32[64,384]{1,0:T(8,128)S(1)}, f32[64,384]{1,0:T(8,128)S(1)}, u32[]{:S(2)}, u32[]{:S(2)}) collective-permute-start(f32[64,384]{1,0:T(8,128)S(1)} %get-tuple-element.115), channel_id=1, source_target_pairs={{0,8},{1,12},{2,0},{3,4},{4,9},{5,13},{6,1},{7,5},{8,10},{9,14},{1... | collective-permute-start | bytes 294920 | tf_op jit(solution)/shard_map/ppermute | solution.py:629
  61.7 8.1 %collective-permute-start.24 = (f32[64,384]{1,0:T(8,128)S(1)}, f32[64,384]{1,0:T(8,128)S(1)}, u32[]{:S(2)}, u32[]{:S(2)}) collective-permute-start(f32[64,384]{1,0:T(8,128)S(1)} %get-tuple-element.116), channel_id=1, source_target_pairs={{0,0},{1,4},{2,8},{3,12},{4,1},{5,5},{6,9},{7,13},{8,2},{9,6},{10,... | collective-permute-start | bytes 294920 | tf_op jit(solution)/shard_map/ppermute | solution.py:629

commit v10 on v9

--- a/solution.py
+++ b/solution.py
@@ -473,11 +473,11 @@
 
 
 def trade(parts, axis, together=True):
-    order = [len(parts) - 1, *range(1, len(parts) - 1)]
+    order = [len(parts) - 1, *reversed(range(1, len(parts) - 1))]
     got = [swap(parts[d], axis, d) for d in order]
     if together:
         got = lax.optimization_barrier(got)
-    return [parts[0], *got[1:], got[0]]
+    return [parts[0], *got[:0:-1], got[0]]
 
 
 def gather(a, axis, count):

time: 70.8 us -> 70.3 us (level)
  starting transfers between devices: 36.6 us -> 34.9 us
  waiting for transfers between devices: 15.5 us -> 16.7 us
    ppermute x21, waiting for transfers between devices: 10.9 us -> 14.5 us  [swap(): lax.ppermute(a, axis, [(i, i ^ bit) for i in range(lax.axis_size(axis))])]
    ppermute x4, waiting for transfers between devices: 4.67 us -> 2.19 us  [turn(): return lax.ppermute(a, ('sensor', 'step'), pairs)]
    ppermute x4, starting transfers between devices: 6.96 us -> 6.02 us  [turn(): return lax.ppermute(a, ('sensor', 'step'), pairs)]
    ppermute x21, starting transfers between devices: 29.7 us -> 28.9 us  [swap(): lax.ppermute(a, axis, [(i, i ^ bit) for i in range(lax.axis_size(axis))])]
  transfers between devices with their start and end apart: 25 -> 25, of which waited for: 11 -> 10; matrix products, arithmetic and copies ran while one was open for 0% -> 0% of each run, Pallas kernels for 12% -> 12%
where the time goes in v10:
time: 70.3 us; the launch traced here: 70 us
  starting transfers between devices  34.9 us (50%)
  waiting for transfers between devices  16.7 us (24%)
  Pallas kernels  11.4 us (16%)
  local copies, waits for them, and re-layouts  5.37 us (8%)
  between operations  1.46 us (2%)
    ppermute x21, starting transfers between devices, swap(): lax.ppermute(a, axis, [(i, i ^ bit) for i in range(lax.axis_size(axis))])  28.9 us
    ppermute x21, waiting for transfers between devices, swap(): lax.ppermute(a, axis, [(i, i ^ bit) for i in range(lax.axis_size(axis))])  14.5 us
    pallas_call x14, Pallas kernels, call(): pl.pallas_call(kernel, name=name, out_shape=outs, in_specs=[SMEM] * smem...  11.4 us
    ppermute x4, starting transfers between devices, turn(): return lax.ppermute(a, ('sensor', 'step'), pairs)  6.02 us
    unnamed x24, local copies, waits for them, and re-layouts  5.37 us
    ppermute x4, waiting for transfers between devices, turn(): return lax.ppermute(a, ('sensor', 'step'), pairs)  2.19 us
  transfers between devices with their start and end apart: 25, of which 10 were waited for; matrix products, arithmetic and copies ran while one was open for 0% of the time, Pallas kernels for 12%

profile of v10, /device:TPU:0, one launch (start us, length us, event | category | flops | bytes accessed | tf_op | source)
XLA Modules:
  0.0 70.0 jit_solution(3186320295997350512)
XLA Ops:
  1.3 0.9 %copy-done.9 = bf16[3,64,512]{2,1,0:T(8,128)(2,1)S(1)} copy-done((bf16[3,64,512]{2,1,0:T(8,128)(2,1)S(1)}, bf16[3,64,512]{2,1,0:T(8,128)(2,1)}, u32[]{:S(2)}) %copy-start.9) | copy-done | bytes 196632
  2.2 3.0 %collective-permute-start = (f32[104,512]{1,0:T(8,128)S(1)}, f32[104,512]{1,0:T(8,128)S(1)}, u32[]{:S(2)}, u32[]{:S(2)}) collective-permute-start(f32[104,512]{1,0:T(8,128)S(1)} %get-tuple-element.62.refs_0_), channel_id=1, source_target_pairs={{0,4},{4,0},{8,12},{12,8},{16,20},{20,16},{24,28},{28,24},{1,5},{5... | collective-permute-start | bytes 638984 | tf_op jit(solution)/shard_map/ppermute | solution.py:472
  5.3 1.6 %collective-permute-start.4 = (f32[104,512]{1,0:T(8,128)S(1)}, f32[104,512]{1,0:T(8,128)S(1)}, u32[]{:S(2)}, u32[]{:S(2)}) collective-permute-start(f32[104,512]{1,0:T(8,128)S(1)} %get-tuple-element.63.refs_4_), channel_id=1, source_target_pairs={{0,8},{4,12},{8,0},{12,4},{16,24},{20,28},{24,16},{28,20},{1,9},{5... | collective-permute-start | bytes 638984 | tf_op jit(solution)/shard_map/ppermute | solution.py:472
  6.8 0.4 collective-permute-start.1
  7.3 0.1 collective-permute-start.3
  7.4 4.0 %collective-permute-done.refs_1_ = f32[104,512]{1,0:T(8,128)S(1)} collective-permute-done((f32[104,512]{1,0:T(8,128)S(1)}, f32[104,512]{1,0:T(8,128)S(1)}, u32[]{:S(2)}, u32[]{:S(2)}) %collective-permute-start) | collective-permute-done | bytes 213024 | tf_op jit(solution)/shard_map/ppermute | solution.py:472
  11.4 2.1 %collective-permute-start.2 = (f32[104,512]{1,0:T(8,128)S(1)}, f32[104,512]{1,0:T(8,128)S(1)}, u32[]{:S(2)}, u32[]{:S(2)}) collective-permute-start(f32[104,512]{1,0:T(8,128)S(1)} %collective-permute-done.refs_1_), channel_id=1, source_target_pairs={{0,8},{4,12},{8,0},{12,4},{16,24},{20,28},{24,16},{28,20},{1,9},{5... | collective-permute-start | bytes 638984 | tf_op jit(solution)/shard_map/ppermute | solution.py:472
  13.5 0.0 collective-permute-done.4.refs_6_
  13.5 1.5 %collective-permute-start.5 = (f32[104,512]{1,0:T(8,128)S(1)}, f32[104,512]{1,0:T(8,128)S(1)}, u32[]{:S(2)}, u32[]{:S(2)}) collective-permute-start(f32[104,512]{1,0:T(8,128)S(1)} %collective-permute-done.4.refs_6_), channel_id=1, source_target_pairs={{0,4},{4,0},{8,12},{12,8},{16,20},{20,16},{24,28},{28,24},{1,5},{5... | collective-permute-start | bytes 638984 | tf_op jit(solution)/shard_map/ppermute | solution.py:472
  15.0 1.0 %copy-done = bf16[512,512]{1,0:T(8,128)(2,1)S(1)} copy-done((bf16[512,512]{1,0:T(8,128)(2,1)S(1)}, bf16[512,512]{1,0:T(8,128)(2,1)}, u32[]{:S(2)}) %copy-start) | copy-done | bytes 524312
  16.0 1.0 %copy-done.2 = bf16[512,512]{1,0:T(8,128)(2,1)S(1)} copy-done((bf16[512,512]{1,0:T(8,128)(2,1)S(1)}, bf16[512,512]{1,0:T(8,128)(2,1)}, u32[]{:S(2)}) %copy-start.2) | copy-done | bytes 524312
  17.1 1.0 %copy-done.4 = bf16[512,512]{1,0:T(8,128)(2,1)S(1)} copy-done((bf16[512,512]{1,0:T(8,128)(2,1)S(1)}, bf16[512,512]{1,0:T(8,128)(2,1)}, u32[]{:S(2)}) %copy-start.4) | copy-done | bytes 524312
  18.1 0.9 %copy-done.7 = f32[8,64,64]{2,1,0:T(8,128)S(1)} copy-done((f32[8,64,64]{2,1,0:T(8,128)S(1)}, f32[8,64,64]{2,1,0:T(8,128)}, u32[]{:S(2)}) %copy-start.7) | copy-done | bytes 131096
  19.1 1.1 %local_keys.1 = (bf16[512,128]{1,0:T(8,128)(2,1)S(1)}, bf16[512,128]{1,0:T(8,128)(2,1)S(1)}, bf16[512,128]{1,0:T(8,128)(2,1)S(1)}, f32[64,128]{1,0:T(8,128)S(1)}...) custom-call(s32[1]{0:T(128)S(6)} %copy.13.live_ref, ...), custom_call_target="tpu_custom_call" | custom-call | flops 301989888 | bytes 4292612 | tf_op jit(solution)/shard_map/local_keys/pallas_call | solution.py:451
  20.2 0.0 collective-permute-done.1.refs_2_
  20.2 0.0 collective-permute-done.3.refs_5_
  20.2 0.9 %collective-permute-done.2.refs_3_ = f32[104,512]{1,0:T(8,128)S(1)} collective-permute-done((f32[104,512]{1,0:T(8,128)S(1)}, f32[104,512]{1,0:T(8,128)S(1)}, u32[]{:S(2)}, u32[]{:S(2)}) %collective-permute-start.2) | collective-permute-done | bytes 213024 | tf_op jit(solution)/shard_map/ppermute | solution.py:472
  21.1 0.0 collective-permute-done.5.refs_7_
  21.1 1.1 %keys.1 = (bf16[768,512]{1,0:T(8,128)(2,1)S(1)}, f32[768,128]{1,0:T(8,128)S(1)}, f32[768,128]{1,0:T(8,128)S(1)}, f32[768,128]{1,0:T(8,128)S(1)}, f32[200,128]{1,0:T(8,128)S(1)}) custom-call(f32[104,512]{1,0:T(8,128)S(1)} %get-tuple-element.62.refs_0_, f32[104,512]{1,0:T(8,128)S(1)} %collective-permute-done.refs_1_, ...), custom_call_target="tpu_custom_call" | custom-call | flops 301989888 | bytes 4067328 | tf_op jit(solution)/shard_map/keys/pallas_call | solution.py:451
  22.2 2.6 %collective-permute-start.6 = (f32[200,128]{1,0:T(8,128)S(1)}, f32[200,128]{1,0:T(8,128)S(1)}, u32[]{:S(2)}, u32[]{:S(2)}) collective-permute-start(f32[200,128]{1,0:T(8,128)S(1)} %get-tuple-element.67.refs_0_), channel_id=1, source_target_pairs={{0,16},{4,20},{8,24},{12,28},{16,0},{20,4},{24,8},{28,12},{1,17},{... | collective-permute-start | bytes 307208 | tf_op jit(solution)/shard_map/ppermute | solution.py:472
  24.9 0.0 copy-start.6
  24.9 0.9 %queries.1 = (f32[768,128]{1,0:T(8,128)S(1)}, f32[768,128]{1,0:T(8,128)S(1)}, f32[192,256]{1,0:T(8,128)S(1)}) custom-call(s32[1]{0:T(128)S(6)} %copy.13.live_ref, bf16[768,512]{1,0:T(8,128)(2,1)S(1)} %get-tuple-element.68.x_ref.refs_0_, bf16[192,512]{1,0:T(8,128)(2,1)S(1)} %bitcast.5, bf16[512,128]{1,0:T(8,128)(2,1)S(1)} %get-tuple-element.69.wq_ref, ...), custom_call_target="tpu_custom_call" | custom-call | flops 201326592 | bytes 2392068 | tf_op jit(solution)/shard_map/queries/pallas_call | solution.py:451
  25.8 0.0 copy-start.1
  25.8 2.0 %collective-permute-done.6.refs_1_ = f32[200,128]{1,0:T(8,128)S(1)} collective-permute-done((f32[200,128]{1,0:T(8,128)S(1)}, f32[200,128]{1,0:T(8,128)S(1)}, u32[]{:S(2)}, u32[]{:S(2)}) %collective-permute-start.6) | collective-permute-done | bytes 102432 | tf_op jit(solution)/shard_map/ppermute | solution.py:472
  27.8 0.4 attend.1
  28.2 1.8 %collective-permute-start.7 = (f32[192,128]{1,0:T(8,128)S(1)}, f32[192,128]{1,0:T(8,128)S(1)}, u32[]{:S(2)}, u32[]{:S(2)}) collective-permute-start(f32[192,128]{1,0:T(8,128)S(1)} %get-tuple-element.72), channel_id=1, source_target_pairs={{0,12},{4,8},{8,4},{12,0},{16,28},{20,24},{24,20},{28,16},{1,13},{... | collective-permute-start | bytes 294920 | tf_op jit(solution)/shard_map/ppermute | solution.py:472
  30.0 1.4 %collective-permute-start.8 = (f32[192,128]{1,0:T(8,128)S(1)}, f32[192,128]{1,0:T(8,128)S(1)}, u32[]{:S(2)}, u32[]{:S(2)}) collective-permute-start(f32[192,128]{1,0:T(8,128)S(1)} %get-tuple-element.73), channel_id=1, source_target_pairs={{0,8},{4,12},{8,0},{12,4},{16,24},{20,28},{24,16},{28,20},{1,9},{5... | collective-permute-start | bytes 294920 | tf_op jit(solution)/shard_map/ppermute | solution.py:472
  31.4 0.4 collective-permute-start.9
  31.8 1.8 %collective-permute-start.14 = (f32[200,128]{1,0:T(8,128)S(1)}, f32[200,128]{1,0:T(8,128)S(1)}, u32[]{:S(2)}, u32[]{:S(2)}) collective-permute-start(f32[200,128]{1,0:T(8,128)S(1)} %get-tuple-element.93.s_ref.refs_3_), channel_id=1, source_target_pairs={{0,8},{4,12},{8,0},{12,4},{16,24},{20,28},{24,16},{28,20},{1,9},{5... | collective-permute-start | bytes 307208 | tf_op jit(solution)/shard_map/ppermute | solution.py:472
  33.6 0.7 %transposes.1 = (bf16[512,768]{1,0:T(8,128)(2,1)S(1)}, bf16[512,512]{1,0:T(8,128)(2,1)S(1)}, bf16[512,512]{1,0:T(8,128)(2,1)S(1)}, bf16[512,512]{1,0:T(8,128)(2,1)S(1)}, bf16[256,512]{1,0:T(8,128)(2,1)S(1)}) custom-call(bf16[768,512]{1,0:T(8,128)(2,1)S(1)} %get-tuple-element.68.x_ref.refs_0_, bf16[512,512]{1,0:T(8,128)(2,1)S(1)} %copy-done.1, ...), custom_call_target="tpu_custom_call" | custom-call | bytes 5242880 | tf_op jit(solution)/shard_map/transposes/pallas_call | solution.py:451
  34.3 0.1 collective-permute-done.7.refs_3_
  34.4 0.6 collective-permute-done.8.refs_2_
  35.0 1.0 %collective-permute-done.9.refs_1_ = f32[192,128]{1,0:T(8,128)S(1)} collective-permute-done((f32[192,128]{1,0:T(8,128)S(1)}, f32[192,128]{1,0:T(8,128)S(1)}, u32[]{:S(2)}, u32[]{:S(2)}) %collective-permute-start.9) | collective-permute-done | bytes 98336 | tf_op jit(solution)/shard_map/ppermute | solution.py:472
  36.0 0.7 %feed_forward.1 = (f32[192,512]{1,0:T(8,128)S(1)}, f32[192,512]{1,0:T(8,128)S(1)}, f32[192,128]{1,0:T(8,128)S(1)}, f32[192,128]{1,0:T(8,128)S(1)}, f32[192,128]{1,0:T(8,128)S(1)}, /*index=5*/f32[192,128]{1,0:T(8,128)S(1)}) custom-call(f32[192,128]{1,0:T(8,128)S(1)} %get-tuple-element.71.refs_0_, f32[192,128]{1,0:T(8,128)S(1)} %collective-permute-done.9.refs_1_, ...), custom_call_target="tpu_custom_call" | custom-call | flops 100663296 | bytes 2293760 | tf_op jit(solution)/shard_map/feed_forward/pallas_call | solution.py:451
  36.8 1.7 %collective-permute-start.10 = (f32[192,128]{1,0:T(8,128)S(1)}, f32[192,128]{1,0:T(8,128)S(1)}, u32[]{:S(2)}, u32[]{:S(2)}) collective-permute-start(f32[192,128]{1,0:T(8,128)S(1)} %get-tuple-element.81), channel_id=1, source_target_pairs={{0,12},{4,8},{8,4},{12,0},{16,28},{20,24},{24,20},{28,16},{1,13},{... | collective-permute-start | bytes 294920 | tf_op jit(solution)/shard_map/ppermute | solution.py:472
  38.4 0.4 collective-permute-start.11
  38.8 1.5 %collective-permute-start.12 = (f32[192,128]{1,0:T(8,128)S(1)}, f32[192,128]{1,0:T(8,128)S(1)}, u32[]{:S(2)}, u32[]{:S(2)}) collective-permute-start(f32[192,128]{1,0:T(8,128)S(1)} %get-tuple-element.83), channel_id=1, source_target_pairs={{0,4},{4,0},{8,12},{12,8},{16,20},{20,16},{24,28},{28,24},{1,5},{5... | collective-permute-start | bytes 294920 | tf_op jit(solution)/shard_map/ppermute | solution.py:472
  40.3 0.5 collective-permute-start.16
  40.8 0.0 collective-permute-done.14.refs_1_
  40.8 1.5 %collective-permute-start.15 = (f32[200,128]{1,0:T(8,128)S(1)}, f32[200,128]{1,0:T(8,128)S(1)}, u32[]{:S(2)}, u32[]{:S(2)}) collective-permute-start(f32[200,128]{1,0:T(8,128)S(1)} %collective-permute-done.14.refs_1_), channel_id=1, source_target_pairs={{0,4},{4,0},{8,12},{12,8},{16,20},{20,16},{24,28},{28,24},{1,5},{5... | collective-permute-start | bytes 307208 | tf_op jit(solution)/shard_map/ppermute | solution.py:472
  42.3 1.8 %collective-permute-done.11.refs_2_ = f32[192,128]{1,0:T(8,128)S(1)} collective-permute-done((f32[192,128]{1,0:T(8,128)S(1)}, f32[192,128]{1,0:T(8,128)S(1)}, u32[]{:S(2)}, u32[]{:S(2)}) %collective-permute-start.11) | collective-permute-done | bytes 98336 | tf_op jit(solution)/shard_map/ppermute | solution.py:472
  44.1 0.4 grad_summary.1
  44.5 3.0 %collective-permute-start.13 = (f32[200,128]{1,0:T(8,128)S(1)}, f32[200,128]{1,0:T(8,128)S(1)}, u32[]{:S(2)}, u32[]{:S(2)}) collective-permute-start(f32[200,128]{1,0:T(8,128)S(1)} %get-tuple-element.89.refs_0_), channel_id=1, source_target_pairs={{0,16},{4,20},{8,24},{12,28},{16,0},{20,4},{24,8},{28,12},{1,17},{... | collective-permute-start | bytes 307208 | tf_op jit(solution)/shard_map/ppermute | solution.py:472
  47.5 0.6 query_back.1.refs_6_
  48.1 0.0 collective-permute-done.16.refs_2_
  48.1 0.0 collective-permute-done.15.refs_0_
  48.1 0.3 copy-done.8
  48.4 1.4 %query_rows.1.refs_8_ = f32[192,512]{1,0:T(8,128)S(1)} custom-call(f32[200,128]{1,0:T(8,128)S(1)} %collective-permute-done.15.refs_0_, f32[200,128]{1,0:T(8,128)S(1)} %collective-permute-done.14.refs_1_, f32[200,128]{1,0:T(8,128)S(1)} %collective-permute-done.16.refs_2_, f32[200,128]{1,0:T(8,128)S(1)} %get-tuple-element.93.s_ref.refs_3_, ...), custom_call_target="tpu_custom_call" | custom-call | flops 301989888 | bytes 3031040 | tf_op jit(solution)/shard_map/query_rows/pallas_call | solution.py:451
  49.9 1.4 %collective-permute-done.13.refs_1_ = f32[200,128]{1,0:T(8,128)S(1)} collective-permute-done((f32[200,128]{1,0:T(8,128)S(1)}, f32[200,128]{1,0:T(8,128)S(1)}, u32[]{:S(2)}, u32[]{:S(2)}) %collective-permute-start.13) | collective-permute-done | bytes 102432 | tf_op jit(solution)/shard_map/ppermute | solution.py:472
  51.2 1.1 %key_back.1 = (f32[200,128]{1,0:T(8,128)S(1)}, f32[2,2,64,384]{3,2,1,0:T(8,128)S(1)}, f32[2,2,64,384]{3,2,1,0:T(8,128)S(1)}) custom-call(f32[200,128]{1,0:T(8,128)S(1)} %get-tuple-element.89.refs_0_, f32[200,128]{1,0:T(8,128)S(1)} %collective-permute-done.13.refs_1_, f32[768,128]{1,0:T(8,128)S(1)} %get-tuple-element.90.refs_2_, ...), custom_call_target="tpu_custom_call" | custom-call | flops 402653184 | bytes 3289088 | tf_op jit(solution)/shard_map/key_back/pallas_call | solution.py:451
  52.3 0.1 collective-permute-start.20
  52.4 0.9 %collective-permute-start.17 = (f32[200,128]{1,0:T(8,128)S(1)}, f32[200,128]{1,0:T(8,128)S(1)}, u32[]{:S(2)}, u32[]{:S(2)}) collective-permute-start(f32[200,128]{1,0:T(8,128)S(1)} %get-tuple-element.104.refs_0_), channel_id=1, source_target_pairs={{0,4},{4,0},{8,12},{12,8},{16,20},{20,16},{24,28},{28,24},{1,5},{5... | collective-permute-start | bytes 307208 | tf_op jit(solution)/shard_map/ppermute | solution.py:472
  53.3 0.6 collective-permute-start.18
  53.9 2.1 %collective-permute-start.19 = (f32[200,128]{1,0:T(8,128)S(1)}, f32[200,128]{1,0:T(8,128)S(1)}, u32[]{:S(2)}, u32[]{:S(2)}) collective-permute-start(f32[200,128]{1,0:T(8,128)S(1)} %get-tuple-element.104.refs_0_), channel_id=1, source_target_pairs={{0,12},{4,8},{8,4},{12,0},{16,28},{20,24},{24,20},{28,16},{1,13},{... | collective-permute-start | bytes 307208 | tf_op jit(solution)/shard_map/ppermute | solution.py:472
  56.0 0.0 collective-permute-done.20.got_ref
  56.0 2.3 %collective-permute-start.21 = (f32[64,384]{1,0:T(8,128)S(1)}, f32[64,384]{1,0:T(8,128)S(1)}, u32[]{:S(2)}, u32[]{:S(2)}) collective-permute-start(f32[64,384]{1,0:T(8,128)S(1)} %get-tuple-element.112), channel_id=1, source_target_pairs={{0,16},{1,20},{2,24},{3,28},{4,17},{5,21},{6,25},{7,29},{8,18},{9,... | collective-permute-start | bytes 294920 | tf_op jit(solution)/shard_map/ppermute | solution.py:629
  58.4 2.5 %collective-permute-start.22 = (f32[64,384]{1,0:T(8,128)S(1)}, f32[64,384]{1,0:T(8,128)S(1)}, u32[]{:S(2)}, u32[]{:S(2)}) collective-permute-start(f32[64,384]{1,0:T(8,128)S(1)} %get-tuple-element.114), channel_id=1, source_target_pairs={{0,24},{1,28},{2,16},{3,20},{4,25},{5,29},{6,17},{7,21},{8,26},{9,... | collective-permute-start | bytes 294920 | tf_op jit(solution)/shard_map/ppermute | solution.py:629
  60.8 0.0 collective-permute-done.17.refs_1_
  60.8 0.5 collective-permute-start.23
  61.4 0.7 collective-permute-start.24
  62.1 2.8 %collective-permute-done.19.refs_3_ = f32[200,128]{1,0:T(8,128)S(1)} collective-permute-done((f32[200,128]{1,0:T(8,128)S(1)}, f32[200,128]{1,0:T(8,128)S(1)}, u32[]{:S(2)}, u32[]{:S(2)}) %collective-permute-start.19) | collective-permute-done | bytes 102432 | tf_op jit(solution)/shard_map/ppermute | solution.py:472
  64.8 2.3 %input_rows.1 = bf16[192,512]{1,0:T(8,128)(2,1)} custom-call(f32[200,128]{1,0:T(8,128)S(1)} %get-tuple-element.104.refs_0_, f32[200,128]{1,0:T(8,128)S(1)} %collective-permute-done.17.refs_1_, f32[200,128]{1,0:T(8,128)S(1)} %collective-permute-done.18.refs_2_, f32[200,128]{1,0:T(8,128)S(1)} %collective-permute-done.19.refs_3_, ...), custom_call_target="tpu_custom_call" | custom-call | flops 3019898880 | bytes 3358720 | tf_op jit(solution)/shard_map/input_rows/pallas_call | solution.py:451
  67.1 2.2 %collective-permute-done.22.refs_1_ = f32[64,384]{1,0:T(8,128)S(1)} collective-permute-done((f32[64,384]{1,0:T(8,128)S(1)}, f32[64,384]{1,0:T(8,128)S(1)}, u32[]{:S(2)}, u32[]{:S(2)}) %collective-permute-start.22) | collective-permute-done | bytes 98336 | tf_op jit(solution)/shard_map/ppermute | solution.py:629
  69.3 0.7 weight_sums.1
  (24 shorter events, 0.1 us)
Async XLA Ops:
  1.3 0.9 %copy-start.9 = (bf16[3,64,512]{2,1,0:T(8,128)(2,1)S(1)}, bf16[3,64,512]{2,1,0:T(8,128)(2,1)}, u32[]{:S(2)}) copy-start(bf16[3,64,512]{2,1,0:T(8,128)(2,1)} %param.9) | copy-start | bytes 589828
  2.2 9.1 %collective-permute-start = (f32[104,512]{1,0:T(8,128)S(1)}, f32[104,512]{1,0:T(8,128)S(1)}, u32[]{:S(2)}, u32[]{:S(2)}) collective-permute-start(f32[104,512]{1,0:T(8,128)S(1)} %get-tuple-element.62.refs_0_), channel_id=1, source_target_pairs={{0,4},{4,0},{8,12},{12,8},{16,20},{20,16},{24,28},{28,24},{1,5},{5... | collective-permute-start | bytes 638984 | tf_op jit(solution)/shard_map/ppermute | solution.py:472
  5.3 8.2 %collective-permute-start.4 = (f32[104,512]{1,0:T(8,128)S(1)}, f32[104,512]{1,0:T(8,128)S(1)}, u32[]{:S(2)}, u32[]{:S(2)}) collective-permute-start(f32[104,512]{1,0:T(8,128)S(1)} %get-tuple-element.63.refs_4_), channel_id=1, source_target_pairs={{0,8},{4,12},{8,0},{12,4},{16,24},{20,28},{24,16},{28,20},{1,9},{5... | collective-permute-start | bytes 638984 | tf_op jit(solution)/shard_map/ppermute | solution.py:472
  6.8 13.4 %collective-permute-start.1 = (f32[104,512]{1,0:T(8,128)S(1)}, f32[104,512]{1,0:T(8,128)S(1)}, u32[]{:S(2)}, u32[]{:S(2)}) collective-permute-start(f32[104,512]{1,0:T(8,128)S(1)} %get-tuple-element.62.refs_0_), channel_id=1, source_target_pairs={{0,8},{4,12},{8,0},{12,4},{16,24},{20,28},{24,16},{28,20},{1,9},{5... | collective-permute-start | bytes 638984 | tf_op jit(solution)/shard_map/ppermute | solution.py:472
  7.3 12.9 %collective-permute-start.3 = (f32[104,512]{1,0:T(8,128)S(1)}, f32[104,512]{1,0:T(8,128)S(1)}, u32[]{:S(2)}, u32[]{:S(2)}) collective-permute-start(f32[104,512]{1,0:T(8,128)S(1)} %get-tuple-element.63.refs_4_), channel_id=1, source_target_pairs={{0,4},{4,0},{8,12},{12,8},{16,20},{20,16},{24,28},{28,24},{1,5},{5... | collective-permute-start | bytes 638984 | tf_op jit(solution)/shard_map/ppermute | solution.py:472
  11.4 9.8 %collective-permute-start.2 = (f32[104,512]{1,0:T(8,128)S(1)}, f32[104,512]{1,0:T(8,128)S(1)}, u32[]{:S(2)}, u32[]{:S(2)}) collective-permute-start(f32[104,512]{1,0:T(8,128)S(1)} %collective-permute-done.refs_1_), channel_id=1, source_target_pairs={{0,8},{4,12},{8,0},{12,4},{16,24},{20,28},{24,16},{28,20},{1,9},{5... | collective-permute-start | bytes 638984 | tf_op jit(solution)/shard_map/ppermute | solution.py:472
  13.5 7.6 %collective-permute-start.5 = (f32[104,512]{1,0:T(8,128)S(1)}, f32[104,512]{1,0:T(8,128)S(1)}, u32[]{:S(2)}, u32[]{:S(2)}) collective-permute-start(f32[104,512]{1,0:T(8,128)S(1)} %collective-permute-done.4.refs_6_), channel_id=1, source_target_pairs={{0,4},{4,0},{8,12},{12,8},{16,20},{20,16},{24,28},{28,24},{1,5},{5... | collective-permute-start | bytes 638984 | tf_op jit(solution)/shard_map/ppermute | solution.py:472
  15.0 1.0 %copy-start = (bf16[512,512]{1,0:T(8,128)(2,1)S(1)}, bf16[512,512]{1,0:T(8,128)(2,1)}, u32[]{:S(2)}) copy-start(bf16[512,512]{1,0:T(8,128)(2,1)} %refs_1_.1) | copy-start | bytes 1572868
  16.0 1.0 %copy-start.2 = (bf16[512,512]{1,0:T(8,128)(2,1)S(1)}, bf16[512,512]{1,0:T(8,128)(2,1)}, u32[]{:S(2)}) copy-start(bf16[512,512]{1,0:T(8,128)(2,1)} %refs_2_.1) | copy-start | bytes 1572868
  17.1 1.0 %copy-start.4 = (bf16[512,512]{1,0:T(8,128)(2,1)S(1)}, bf16[512,512]{1,0:T(8,128)(2,1)}, u32[]{:S(2)}) copy-start(bf16[512,512]{1,0:T(8,128)(2,1)} %refs_3_.1) | copy-start | bytes 1572868
  18.1 0.9 %copy-start.7 = (f32[8,64,64]{2,1,0:T(8,128)S(1)}, f32[8,64,64]{2,1,0:T(8,128)}, u32[]{:S(2)}) copy-start(f32[8,64,64]{2,1,0:T(8,128)} %refs_7_.1) | copy-start | bytes 393220
  21.1 3.7 %copy-start.10 = (bf16[256,512]{1,0:T(8,128)(2,1)S(1)}, bf16[256,512]{1,0:T(8,128)(2,1)}, u32[]{:S(2)}) copy-start(bf16[256,512]{1,0:T(8,128)(2,1)} %wd_ref.1) | copy-start | bytes 786436
  21.1 3.7 %copy-start.11 = (bf16[3,64,512]{2,1,0:T(8,128)(2,1)S(1)}, bf16[3,64,512]{2,1,0:T(8,128)(2,1)}, u32[]{:S(2)}) copy-start(bf16[3,64,512]{2,1,0:T(8,128)(2,1)} %param.10) | copy-start | bytes 589828
  22.2 5.6 %collective-permute-start.6 = (f32[200,128]{1,0:T(8,128)S(1)}, f32[200,128]{1,0:T(8,128)S(1)}, u32[]{:S(2)}, u32[]{:S(2)}) collective-permute-start(f32[200,128]{1,0:T(8,128)S(1)} %get-tuple-element.67.refs_0_), channel_id=1, source_target_pairs={{0,16},{4,20},{8,24},{12,28},{16,0},{20,4},{24,8},{28,12},{1,17},{... | collective-permute-start | bytes 307208 | tf_op jit(solution)/shard_map/ppermute | solution.py:472
  24.9 8.7 %copy-start.3 = (bf16[512,512]{1,0:T(8,128)(2,1)S(1)}, bf16[512,512]{1,0:T(8,128)(2,1)}, u32[]{:S(2)}) copy-start(bf16[512,512]{1,0:T(8,128)(2,1)} %refs_2_.1) | copy-start | bytes 1572868
  24.9 8.7 %copy-start.5 = (bf16[512,512]{1,0:T(8,128)(2,1)S(1)}, bf16[512,512]{1,0:T(8,128)(2,1)}, u32[]{:S(2)}) copy-start(bf16[512,512]{1,0:T(8,128)(2,1)} %refs_3_.1) | copy-start | bytes 1572868
  24.9 8.7 %copy-start.6 = (bf16[512,256]{1,0:T(8,128)(2,1)S(1)}, bf16[512,256]{1,0:T(8,128)(2,1)}, u32[]{:S(2)}) copy-start(bf16[512,256]{1,0:T(8,128)(2,1)} %refs_5_.1) | copy-start | bytes 786436
  25.8 7.7 %copy-start.1 = (bf16[512,512]{1,0:T(8,128)(2,1)S(1)}, bf16[512,512]{1,0:T(8,128)(2,1)}, u32[]{:S(2)}) copy-start(bf16[512,512]{1,0:T(8,128)(2,1)} %refs_1_.1) | copy-start | bytes 1572868
  28.2 6.2 %collective-permute-start.7 = (f32[192,128]{1,0:T(8,128)S(1)}, f32[192,128]{1,0:T(8,128)S(1)}, u32[]{:S(2)}, u32[]{:S(2)}) collective-permute-start(f32[192,128]{1,0:T(8,128)S(1)} %get-tuple-element.72), channel_id=1, source_target_pairs={{0,12},{4,8},{8,4},{12,0},{16,28},{20,24},{24,20},{28,16},{1,13},{... | collective-permute-start | bytes 294920 | tf_op jit(solution)/shard_map/ppermute | solution.py:472
  30.0 5.0 %collective-permute-start.8 = (f32[192,128]{1,0:T(8,128)S(1)}, f32[192,128]{1,0:T(8,128)S(1)}, u32[]{:S(2)}, u32[]{:S(2)}) collective-permute-start(f32[192,128]{1,0:T(8,128)S(1)} %get-tuple-element.73), channel_id=1, source_target_pairs={{0,8},{4,12},{8,0},{12,4},{16,24},{20,28},{24,16},{28,20},{1,9},{5... | collective-permute-start | bytes 294920 | tf_op jit(solution)/shard_map/ppermute | solution.py:472
  31.4 4.6 %collective-permute-start.9 = (f32[192,128]{1,0:T(8,128)S(1)}, f32[192,128]{1,0:T(8,128)S(1)}, u32[]{:S(2)}, u32[]{:S(2)}) collective-permute-start(f32[192,128]{1,0:T(8,128)S(1)} %get-tuple-element.74), channel_id=1, source_target_pairs={{0,4},{4,0},{8,12},{12,8},{16,20},{20,16},{24,28},{28,24},{1,5},{5... | collective-permute-start | bytes 294920 | tf_op jit(solution)/shard_map/ppermute | solution.py:472
  31.8 9.0 %collective-permute-start.14 = (f32[200,128]{1,0:T(8,128)S(1)}, f32[200,128]{1,0:T(8,128)S(1)}, u32[]{:S(2)}, u32[]{:S(2)}) collective-permute-start(f32[200,128]{1,0:T(8,128)S(1)} %get-tuple-element.93.s_ref.refs_3_), channel_id=1, source_target_pairs={{0,8},{4,12},{8,0},{12,4},{16,24},{20,28},{24,16},{28,20},{1,9},{5... | collective-permute-start | bytes 307208 | tf_op jit(solution)/shard_map/ppermute | solution.py:472
  36.8 5.6 %collective-permute-start.10 = (f32[192,128]{1,0:T(8,128)S(1)}, f32[192,128]{1,0:T(8,128)S(1)}, u32[]{:S(2)}, u32[]{:S(2)}) collective-permute-start(f32[192,128]{1,0:T(8,128)S(1)} %get-tuple-element.81), channel_id=1, source_target_pairs={{0,12},{4,8},{8,4},{12,0},{16,28},{20,24},{24,20},{28,16},{1,13},{... | collective-permute-start | bytes 294920 | tf_op jit(solution)/shard_map/ppermute | solution.py:472
  38.4 5.7 %collective-permute-start.11 = (f32[192,128]{1,0:T(8,128)S(1)}, f32[192,128]{1,0:T(8,128)S(1)}, u32[]{:S(2)}, u32[]{:S(2)}) collective-permute-start(f32[192,128]{1,0:T(8,128)S(1)} %get-tuple-element.82), channel_id=1, source_target_pairs={{0,8},{4,12},{8,0},{12,4},{16,24},{20,28},{24,16},{28,20},{1,9},{5... | collective-permute-start | bytes 294920 | tf_op jit(solution)/shard_map/ppermute | solution.py:472
  38.8 5.4 %collective-permute-start.12 = (f32[192,128]{1,0:T(8,128)S(1)}, f32[192,128]{1,0:T(8,128)S(1)}, u32[]{:S(2)}, u32[]{:S(2)}) collective-permute-start(f32[192,128]{1,0:T(8,128)S(1)} %get-tuple-element.83), channel_id=1, source_target_pairs={{0,4},{4,0},{8,12},{12,8},{16,20},{20,16},{24,28},{28,24},{1,5},{5... | collective-permute-start | bytes 294920 | tf_op jit(solution)/shard_map/ppermute | solution.py:472
  40.3 7.8 %collective-permute-start.16 = (f32[200,128]{1,0:T(8,128)S(1)}, f32[200,128]{1,0:T(8,128)S(1)}, u32[]{:S(2)}, u32[]{:S(2)}) collective-permute-start(f32[200,128]{1,0:T(8,128)S(1)} %get-tuple-element.93.s_ref.refs_3_), channel_id=1, source_target_pairs={{0,4},{4,0},{8,12},{12,8},{16,20},{20,16},{24,28},{28,24},{1,5},{5... | collective-permute-start | bytes 307208 | tf_op jit(solution)/shard_map/ppermute | solution.py:472
  40.8 7.3 %collective-permute-start.15 = (f32[200,128]{1,0:T(8,128)S(1)}, f32[200,128]{1,0:T(8,128)S(1)}, u32[]{:S(2)}, u32[]{:S(2)}) collective-permute-start(f32[200,128]{1,0:T(8,128)S(1)} %collective-permute-done.14.refs_1_), channel_id=1, source_target_pairs={{0,4},{4,0},{8,12},{12,8},{16,20},{20,16},{24,28},{28,24},{1,5},{5... | collective-permute-start | bytes 307208 | tf_op jit(solution)/shard_map/ppermute | solution.py:472
  44.5 6.7 %collective-permute-start.13 = (f32[200,128]{1,0:T(8,128)S(1)}, f32[200,128]{1,0:T(8,128)S(1)}, u32[]{:S(2)}, u32[]{:S(2)}) collective-permute-start(f32[200,128]{1,0:T(8,128)S(1)} %get-tuple-element.89.refs_0_), channel_id=1, source_target_pairs={{0,16},{4,20},{8,24},{12,28},{16,0},{20,4},{24,8},{28,12},{1,17},{... | collective-permute-start | bytes 307208 | tf_op jit(solution)/shard_map/ppermute | solution.py:472
  47.5 0.9 %copy-start.8 = (f32[8,64,64]{2,1,0:T(8,128)S(1)}, f32[8,64,64]{2,1,0:T(8,128)}, u32[]{:S(2)}) copy-start(f32[8,64,64]{2,1,0:T(8,128)} %refs_7_.1) | copy-start | bytes 393220
  52.3 3.6 %collective-permute-start.20 = (f32[2,2,64,384]{3,2,1,0:T(8,128)S(1)}, f32[2,2,64,384]{3,2,1,0:T(8,128)S(1)}, u32[]{:S(2)}, u32[]{:S(2)}) collective-permute-start(f32[2,2,64,384]{3,2,1,0:T(8,128)S(1)} %get-tuple-element.111), channel_id=1, source_target_pairs={{0,1},{1,0},{2,3},{3,2},{4,5},{5,4},{6,7},{7,6},{8,9},{9,8},{10,11... | collective-permute-start | bytes 1179656 | tf_op jit(solution)/shard_map/ppermute | solution.py:472
  52.4 8.4 %collective-permute-start.17 = (f32[200,128]{1,0:T(8,128)S(1)}, f32[200,128]{1,0:T(8,128)S(1)}, u32[]{:S(2)}, u32[]{:S(2)}) collective-permute-start(f32[200,128]{1,0:T(8,128)S(1)} %get-tuple-element.104.refs_0_), channel_id=1, source_target_pairs={{0,4},{4,0},{8,12},{12,8},{16,20},{20,16},{24,28},{28,24},{1,5},{5... | collective-permute-start | bytes 307208 | tf_op jit(solution)/shard_map/ppermute | solution.py:472
  53.3 8.1 %collective-permute-start.18 = (f32[200,128]{1,0:T(8,128)S(1)}, f32[200,128]{1,0:T(8,128)S(1)}, u32[]{:S(2)}, u32[]{:S(2)}) collective-permute-start(f32[200,128]{1,0:T(8,128)S(1)} %get-tuple-element.104.refs_0_), channel_id=1, source_target_pairs={{0,8},{4,12},{8,0},{12,4},{16,24},{20,28},{24,16},{28,20},{1,9},{5... | collective-permute-start | bytes 307208 | tf_op jit(solution)/shard_map/ppermute | solution.py:472
  53.9 10.9 %collective-permute-start.19 = (f32[200,128]{1,0:T(8,128)S(1)}, f32[200,128]{1,0:T(8,128)S(1)}, u32[]{:S(2)}, u32[]{:S(2)}) collective-permute-start(f32[200,128]{1,0:T(8,128)S(1)} %get-tuple-element.104.refs_0_), channel_id=1, source_target_pairs={{0,12},{4,8},{8,4},{12,0},{16,28},{20,24},{24,20},{28,16},{1,13},{... | collective-permute-start | bytes 307208 | tf_op jit(solution)/shard_map/ppermute | solution.py:472
  56.0 11.1 %collective-permute-start.21 = (f32[64,384]{1,0:T(8,128)S(1)}, f32[64,384]{1,0:T(8,128)S(1)}, u32[]{:S(2)}, u32[]{:S(2)}) collective-permute-start(f32[64,384]{1,0:T(8,128)S(1)} %get-tuple-element.112), channel_id=1, source_target_pairs={{0,16},{1,20},{2,24},{3,28},{4,17},{5,21},{6,25},{7,29},{8,18},{9,... | collective-permute-start | bytes 294920 | tf_op jit(solution)/shard_map/ppermute | solution.py:629
  58.4 10.9 %collective-permute-start.22 = (f32[64,384]{1,0:T(8,128)S(1)}, f32[64,384]{1,0:T(8,128)S(1)}, u32[]{:S(2)}, u32[]{:S(2)}) collective-permute-start(f32[64,384]{1,0:T(8,128)S(1)} %get-tuple-element.114), channel_id=1, source_target_pairs={{0,24},{1,28},{2,16},{3,20},{4,25},{5,29},{6,17},{7,21},{8,26},{9,... | collective-permute-start | bytes 294920 | tf_op jit(solution)/shard_map/ppermute | solution.py:629
  60.8 8.4 %collective-permute-start.23 = (f32[64,384]{1,0:T(8,128)S(1)}, f32[64,384]{1,0:T(8,128)S(1)}, u32[]{:S(2)}, u32[]{:S(2)}) collective-permute-start(f32[64,384]{1,0:T(8,128)S(1)} %get-tuple-element.115), channel_id=1, source_target_pairs={{0,8},{1,12},{2,0},{3,4},{4,9},{5,13},{6,1},{7,5},{8,10},{9,14},{1... | collective-permute-start | bytes 294920 | tf_op jit(solution)/shard_map/ppermute | solution.py:629
  61.4 7.9 %collective-permute-start.24 = (f32[64,384]{1,0:T(8,128)S(1)}, f32[64,384]{1,0:T(8,128)S(1)}, u32[]{:S(2)}, u32[]{:S(2)}) collective-permute-start(f32[64,384]{1,0:T(8,128)S(1)} %get-tuple-element.116), channel_id=1, source_target_pairs={{0,0},{1,4},{2,8},{3,12},{4,1},{5,5},{6,9},{7,13},{8,2},{9,6},{10,... | collective-permute-start | bytes 294920 | tf_op jit(solution)/shard_map/ppermute | solution.py:629

commit v11 on v10

--- a/solution.py
+++ b/solution.py
@@ -412,7 +412,7 @@
     in_refs, (u_ref, v_ref, f_ref, proj_ref) = refs[:count], refs[count : count + 4]
     q_ref, wk_ref, wv_ref, out_ref, g_ref = refs[count + 4 :]
     size = proj_ref.shape[1]
-    collect_columns(g_ref, in_refs)
+    collect_columns(g_ref, in_refs[::-1])
     total = q_ref[...]
     mask = head_mask(size, WIDE)
     rows = f_ref.shape[0] // steps
@@ -656,7 +656,7 @@
         functools.partial(rows_kernel, steps, factor, count),
         "input_rows",
         shape((rows, width), BF16),
-        (*messages, *local_keys, feature_proj, query_part, wk_turned, wv_turned),
+        (*messages[::-1], *local_keys, feature_proj, query_part, wk_turned, wv_turned),
         flops=30 * product,
         scratch=[pltpu.VMEM((packed.shape[0], width), F32)],
     )

time: 70.3 us -> 70.4 us (level)
    ppermute x21, waiting for transfers between devices: 14.5 us -> 11.8 us  [swap(): lax.ppermute(a, axis, [(i, i ^ bit) for i in range(lax.axis_size(axis))])]
    ppermute x4, waiting for transfers between devices: 2.19 us -> 4.92 us  [turn(): return lax.ppermute(a, ('sensor', 'step'), pairs)]
where the time goes in v11:
time: 70.4 us; the launch traced here: 69.9 us
  starting transfers between devices  34.9 us (50%)
  waiting for transfers between devices  16.7 us (24%)
  Pallas kernels  11.5 us (16%)
  local copies, waits for them, and re-layouts  5.37 us (8%)
  between operations  1.47 us (2%)
    ppermute x21, starting transfers between devices, swap(): lax.ppermute(a, axis, [(i, i ^ bit) for i in range(lax.axis_size(axis))])  28.9 us
    ppermute x21, waiting for transfers between devices, swap(): lax.ppermute(a, axis, [(i, i ^ bit) for i in range(lax.axis_size(axis))])  11.8 us
    pallas_call x14, Pallas kernels, call(): pl.pallas_call(kernel, name=name, out_shape=outs, in_specs=[SMEM] * smem...  11.5 us
    ppermute x4, starting transfers between devices, turn(): return lax.ppermute(a, ('sensor', 'step'), pairs)  6.02 us
    unnamed x24, local copies, waits for them, and re-layouts  5.37 us
    ppermute x4, waiting for transfers between devices, turn(): return lax.ppermute(a, ('sensor', 'step'), pairs)  4.92 us
  transfers between devices with their start and end apart: 25, of which 10 were waited for; matrix products, arithmetic and copies ran while one was open for 0% of the time, Pallas kernels for 12%

profile of v11, /device:TPU:0, one launch (start us, length us, event | category | flops | bytes accessed | tf_op | source)
XLA Modules:
  0.0 69.9 jit_solution(7815756190948426864)
XLA Ops:
  1.3 0.9 %copy-done.9 = bf16[3,64,512]{2,1,0:T(8,128)(2,1)S(1)} copy-done((bf16[3,64,512]{2,1,0:T(8,128)(2,1)S(1)}, bf16[3,64,512]{2,1,0:T(8,128)(2,1)}, u32[]{:S(2)}) %copy-start.9) | copy-done | bytes 196632
  2.2 3.0 %collective-permute-start = (f32[104,512]{1,0:T(8,128)S(1)}, f32[104,512]{1,0:T(8,128)S(1)}, u32[]{:S(2)}, u32[]{:S(2)}) collective-permute-start(f32[104,512]{1,0:T(8,128)S(1)} %get-tuple-element.62.refs_0_), channel_id=1, source_target_pairs={{0,4},{4,0},{8,12},{12,8},{16,20},{20,16},{24,28},{28,24},{1,5},{5... | collective-permute-start | bytes 638984 | tf_op jit(solution)/shard_map/ppermute | solution.py:472
  5.3 1.6 %collective-permute-start.4 = (f32[104,512]{1,0:T(8,128)S(1)}, f32[104,512]{1,0:T(8,128)S(1)}, u32[]{:S(2)}, u32[]{:S(2)}) collective-permute-start(f32[104,512]{1,0:T(8,128)S(1)} %get-tuple-element.63.refs_4_), channel_id=1, source_target_pairs={{0,8},{4,12},{8,0},{12,4},{16,24},{20,28},{24,16},{28,20},{1,9},{5... | collective-permute-start | bytes 638984 | tf_op jit(solution)/shard_map/ppermute | solution.py:472
  6.8 0.4 collective-permute-start.1
  7.3 0.1 collective-permute-start.3
  7.4 4.0 %collective-permute-done.refs_1_ = f32[104,512]{1,0:T(8,128)S(1)} collective-permute-done((f32[104,512]{1,0:T(8,128)S(1)}, f32[104,512]{1,0:T(8,128)S(1)}, u32[]{:S(2)}, u32[]{:S(2)}) %collective-permute-start) | collective-permute-done | bytes 213024 | tf_op jit(solution)/shard_map/ppermute | solution.py:472
  11.4 2.1 %collective-permute-start.2 = (f32[104,512]{1,0:T(8,128)S(1)}, f32[104,512]{1,0:T(8,128)S(1)}, u32[]{:S(2)}, u32[]{:S(2)}) collective-permute-start(f32[104,512]{1,0:T(8,128)S(1)} %collective-permute-done.refs_1_), channel_id=1, source_target_pairs={{0,8},{4,12},{8,0},{12,4},{16,24},{20,28},{24,16},{28,20},{1,9},{5... | collective-permute-start | bytes 638984 | tf_op jit(solution)/shard_map/ppermute | solution.py:472
  13.5 1.5 %collective-permute-start.5 = (f32[104,512]{1,0:T(8,128)S(1)}, f32[104,512]{1,0:T(8,128)S(1)}, u32[]{:S(2)}, u32[]{:S(2)}) collective-permute-start(f32[104,512]{1,0:T(8,128)S(1)} %collective-permute-done.4.refs_6_), channel_id=1, source_target_pairs={{0,4},{4,0},{8,12},{12,8},{16,20},{20,16},{24,28},{28,24},{1,5},{5... | collective-permute-start | bytes 638984 | tf_op jit(solution)/shard_map/ppermute | solution.py:472
  15.0 1.0 %copy-done = bf16[512,512]{1,0:T(8,128)(2,1)S(1)} copy-done((bf16[512,512]{1,0:T(8,128)(2,1)S(1)}, bf16[512,512]{1,0:T(8,128)(2,1)}, u32[]{:S(2)}) %copy-start) | copy-done | bytes 524312
  16.0 1.0 %copy-done.2 = bf16[512,512]{1,0:T(8,128)(2,1)S(1)} copy-done((bf16[512,512]{1,0:T(8,128)(2,1)S(1)}, bf16[512,512]{1,0:T(8,128)(2,1)}, u32[]{:S(2)}) %copy-start.2) | copy-done | bytes 524312
  17.1 1.0 %copy-done.4 = bf16[512,512]{1,0:T(8,128)(2,1)S(1)} copy-done((bf16[512,512]{1,0:T(8,128)(2,1)S(1)}, bf16[512,512]{1,0:T(8,128)(2,1)}, u32[]{:S(2)}) %copy-start.4) | copy-done | bytes 524312
  18.1 0.9 %copy-done.7 = f32[8,64,64]{2,1,0:T(8,128)S(1)} copy-done((f32[8,64,64]{2,1,0:T(8,128)S(1)}, f32[8,64,64]{2,1,0:T(8,128)}, u32[]{:S(2)}) %copy-start.7) | copy-done | bytes 131096
  19.1 1.1 %local_keys.1 = (bf16[512,128]{1,0:T(8,128)(2,1)S(1)}, bf16[512,128]{1,0:T(8,128)(2,1)S(1)}, bf16[512,128]{1,0:T(8,128)(2,1)S(1)}, f32[64,128]{1,0:T(8,128)S(1)}...) custom-call(s32[1]{0:T(128)S(6)} %copy.13.live_ref, ...), custom_call_target="tpu_custom_call" | custom-call | flops 301989888 | bytes 4292612 | tf_op jit(solution)/shard_map/local_keys/pallas_call | solution.py:451
  20.2 0.0 collective-permute-done.3.refs_5_
  20.2 0.9 %collective-permute-done.2.refs_3_ = f32[104,512]{1,0:T(8,128)S(1)} collective-permute-done((f32[104,512]{1,0:T(8,128)S(1)}, f32[104,512]{1,0:T(8,128)S(1)}, u32[]{:S(2)}, u32[]{:S(2)}) %collective-permute-start.2) | collective-permute-done | bytes 213024 | tf_op jit(solution)/shard_map/ppermute | solution.py:472
  21.1 1.1 %keys.1 = (bf16[768,512]{1,0:T(8,128)(2,1)S(1)}, f32[768,128]{1,0:T(8,128)S(1)}, f32[768,128]{1,0:T(8,128)S(1)}, f32[768,128]{1,0:T(8,128)S(1)}, f32[200,128]{1,0:T(8,128)S(1)}) custom-call(f32[104,512]{1,0:T(8,128)S(1)} %get-tuple-element.62.refs_0_, f32[104,512]{1,0:T(8,128)S(1)} %collective-permute-done.refs_1_, ...), custom_call_target="tpu_custom_call" | custom-call | flops 301989888 | bytes 4067328 | tf_op jit(solution)/shard_map/keys/pallas_call | solution.py:451
  22.2 2.6 %collective-permute-start.6 = (f32[200,128]{1,0:T(8,128)S(1)}, f32[200,128]{1,0:T(8,128)S(1)}, u32[]{:S(2)}, u32[]{:S(2)}) collective-permute-start(f32[200,128]{1,0:T(8,128)S(1)} %get-tuple-element.67.refs_0_), channel_id=1, source_target_pairs={{0,16},{4,20},{8,24},{12,28},{16,0},{20,4},{24,8},{28,12},{1,17},{... | collective-permute-start | bytes 307208 | tf_op jit(solution)/shard_map/ppermute | solution.py:472
  24.9 0.0 copy-start.6
  24.9 0.9 %queries.1 = (f32[768,128]{1,0:T(8,128)S(1)}, f32[768,128]{1,0:T(8,128)S(1)}, f32[192,256]{1,0:T(8,128)S(1)}) custom-call(s32[1]{0:T(128)S(6)} %copy.13.live_ref, bf16[768,512]{1,0:T(8,128)(2,1)S(1)} %get-tuple-element.68.x_ref.refs_0_, bf16[192,512]{1,0:T(8,128)(2,1)S(1)} %bitcast.5, bf16[512,128]{1,0:T(8,128)(2,1)S(1)} %get-tuple-element.69.wq_ref, ...), custom_call_target="tpu_custom_call" | custom-call | flops 201326592 | bytes 2392068 | tf_op jit(solution)/shard_map/queries/pallas_call | solution.py:451
  25.8 0.0 copy-start.1
  25.8 2.0 %collective-permute-done.6.refs_1_ = f32[200,128]{1,0:T(8,128)S(1)} collective-permute-done((f32[200,128]{1,0:T(8,128)S(1)}, f32[200,128]{1,0:T(8,128)S(1)}, u32[]{:S(2)}, u32[]{:S(2)}) %collective-permute-start.6) | collective-permute-done | bytes 102432 | tf_op jit(solution)/shard_map/ppermute | solution.py:472
  27.8 0.4 attend.1
  28.2 1.8 %collective-permute-start.7 = (f32[192,128]{1,0:T(8,128)S(1)}, f32[192,128]{1,0:T(8,128)S(1)}, u32[]{:S(2)}, u32[]{:S(2)}) collective-permute-start(f32[192,128]{1,0:T(8,128)S(1)} %get-tuple-element.72), channel_id=1, source_target_pairs={{0,12},{4,8},{8,4},{12,0},{16,28},{20,24},{24,20},{28,16},{1,13},{... | collective-permute-start | bytes 294920 | tf_op jit(solution)/shard_map/ppermute | solution.py:472
  30.0 1.4 %collective-permute-start.8 = (f32[192,128]{1,0:T(8,128)S(1)}, f32[192,128]{1,0:T(8,128)S(1)}, u32[]{:S(2)}, u32[]{:S(2)}) collective-permute-start(f32[192,128]{1,0:T(8,128)S(1)} %get-tuple-element.73), channel_id=1, source_target_pairs={{0,8},{4,12},{8,0},{12,4},{16,24},{20,28},{24,16},{28,20},{1,9},{5... | collective-permute-start | bytes 294920 | tf_op jit(solution)/shard_map/ppermute | solution.py:472
  31.4 0.4 collective-permute-start.9
  31.8 1.8 %collective-permute-start.14 = (f32[200,128]{1,0:T(8,128)S(1)}, f32[200,128]{1,0:T(8,128)S(1)}, u32[]{:S(2)}, u32[]{:S(2)}) collective-permute-start(f32[200,128]{1,0:T(8,128)S(1)} %get-tuple-element.93.s_ref.refs_3_), channel_id=1, source_target_pairs={{0,8},{4,12},{8,0},{12,4},{16,24},{20,28},{24,16},{28,20},{1,9},{5... | collective-permute-start | bytes 307208 | tf_op jit(solution)/shard_map/ppermute | solution.py:472
  33.6 0.7 %transposes.1 = (bf16[512,768]{1,0:T(8,128)(2,1)S(1)}, bf16[512,512]{1,0:T(8,128)(2,1)S(1)}, bf16[512,512]{1,0:T(8,128)(2,1)S(1)}, bf16[512,512]{1,0:T(8,128)(2,1)S(1)}, bf16[256,512]{1,0:T(8,128)(2,1)S(1)}) custom-call(bf16[768,512]{1,0:T(8,128)(2,1)S(1)} %get-tuple-element.68.x_ref.refs_0_, bf16[512,512]{1,0:T(8,128)(2,1)S(1)} %copy-done.1, ...), custom_call_target="tpu_custom_call" | custom-call | bytes 5242880 | tf_op jit(solution)/shard_map/transposes/pallas_call | solution.py:451
  34.3 0.1 collective-permute-done.7.refs_3_
  34.4 0.6 collective-permute-done.8.refs_2_
  35.0 1.0 %collective-permute-done.9.refs_1_ = f32[192,128]{1,0:T(8,128)S(1)} collective-permute-done((f32[192,128]{1,0:T(8,128)S(1)}, f32[192,128]{1,0:T(8,128)S(1)}, u32[]{:S(2)}, u32[]{:S(2)}) %collective-permute-start.9) | collective-permute-done | bytes 98336 | tf_op jit(solution)/shard_map/ppermute | solution.py:472
  36.0 0.7 %feed_forward.1 = (f32[192,512]{1,0:T(8,128)S(1)}, f32[192,512]{1,0:T(8,128)S(1)}, f32[192,128]{1,0:T(8,128)S(1)}, f32[192,128]{1,0:T(8,128)S(1)}, f32[192,128]{1,0:T(8,128)S(1)}, /*index=5*/f32[192,128]{1,0:T(8,128)S(1)}) custom-call(f32[192,128]{1,0:T(8,128)S(1)} %get-tuple-element.71.refs_0_, f32[192,128]{1,0:T(8,128)S(1)} %collective-permute-done.9.refs_1_, ...), custom_call_target="tpu_custom_call" | custom-call | flops 100663296 | bytes 2293760 | tf_op jit(solution)/shard_map/feed_forward/pallas_call | solution.py:451
  36.8 1.7 %collective-permute-start.10 = (f32[192,128]{1,0:T(8,128)S(1)}, f32[192,128]{1,0:T(8,128)S(1)}, u32[]{:S(2)}, u32[]{:S(2)}) collective-permute-start(f32[192,128]{1,0:T(8,128)S(1)} %get-tuple-element.81), channel_id=1, source_target_pairs={{0,12},{4,8},{8,4},{12,0},{16,28},{20,24},{24,20},{28,16},{1,13},{... | collective-permute-start | bytes 294920 | tf_op jit(solution)/shard_map/ppermute | solution.py:472
  38.4 0.4 collective-permute-start.11
  38.8 1.5 %collective-permute-start.12 = (f32[192,128]{1,0:T(8,128)S(1)}, f32[192,128]{1,0:T(8,128)S(1)}, u32[]{:S(2)}, u32[]{:S(2)}) collective-permute-start(f32[192,128]{1,0:T(8,128)S(1)} %get-tuple-element.83), channel_id=1, source_target_pairs={{0,4},{4,0},{8,12},{12,8},{16,20},{20,16},{24,28},{28,24},{1,5},{5... | collective-permute-start | bytes 294920 | tf_op jit(solution)/shard_map/ppermute | solution.py:472
  40.3 0.5 collective-permute-start.16
  40.8 0.0 collective-permute-done.14.refs_1_
  40.8 1.5 %collective-permute-start.15 = (f32[200,128]{1,0:T(8,128)S(1)}, f32[200,128]{1,0:T(8,128)S(1)}, u32[]{:S(2)}, u32[]{:S(2)}) collective-permute-start(f32[200,128]{1,0:T(8,128)S(1)} %collective-permute-done.14.refs_1_), channel_id=1, source_target_pairs={{0,4},{4,0},{8,12},{12,8},{16,20},{20,16},{24,28},{28,24},{1,5},{5... | collective-permute-start | bytes 307208 | tf_op jit(solution)/shard_map/ppermute | solution.py:472
  42.3 0.0 collective-permute-done.10.refs_3_
  42.3 1.8 %collective-permute-done.11.refs_2_ = f32[192,128]{1,0:T(8,128)S(1)} collective-permute-done((f32[192,128]{1,0:T(8,128)S(1)}, f32[192,128]{1,0:T(8,128)S(1)}, u32[]{:S(2)}, u32[]{:S(2)}) %collective-permute-start.11) | collective-permute-done | bytes 98336 | tf_op jit(solution)/shard_map/ppermute | solution.py:472
  44.1 0.0 collective-permute-done.12.refs_1_
  44.1 0.4 grad_summary.1
  44.5 3.0 %collective-permute-start.13 = (f32[200,128]{1,0:T(8,128)S(1)}, f32[200,128]{1,0:T(8,128)S(1)}, u32[]{:S(2)}, u32[]{:S(2)}) collective-permute-start(f32[200,128]{1,0:T(8,128)S(1)} %get-tuple-element.89.refs_0_), channel_id=1, source_target_pairs={{0,16},{4,20},{8,24},{12,28},{16,0},{20,4},{24,8},{28,12},{1,17},{... | collective-permute-start | bytes 307208 | tf_op jit(solution)/shard_map/ppermute | solution.py:472
  47.5 0.6 query_back.1.refs_6_
  48.1 0.3 copy-done.8
  48.4 1.4 %query_rows.1.refs_8_ = f32[192,512]{1,0:T(8,128)S(1)} custom-call(f32[200,128]{1,0:T(8,128)S(1)} %collective-permute-done.15.refs_0_, f32[200,128]{1,0:T(8,128)S(1)} %collective-permute-done.14.refs_1_, f32[200,128]{1,0:T(8,128)S(1)} %collective-permute-done.16.refs_2_, f32[200,128]{1,0:T(8,128)S(1)} %get-tuple-element.93.s_ref.refs_3_, ...), custom_call_target="tpu_custom_call" | custom-call | flops 301989888 | bytes 3031040 | tf_op jit(solution)/shard_map/query_rows/pallas_call | solution.py:451
  49.9 1.4 %collective-permute-done.13.refs_1_ = f32[200,128]{1,0:T(8,128)S(1)} collective-permute-done((f32[200,128]{1,0:T(8,128)S(1)}, f32[200,128]{1,0:T(8,128)S(1)}, u32[]{:S(2)}, u32[]{:S(2)}) %collective-permute-start.13) | collective-permute-done | bytes 102432 | tf_op jit(solution)/shard_map/ppermute | solution.py:472
  51.2 1.1 %key_back.1 = (f32[200,128]{1,0:T(8,128)S(1)}, f32[2,2,64,384]{3,2,1,0:T(8,128)S(1)}, f32[2,2,64,384]{3,2,1,0:T(8,128)S(1)}) custom-call(f32[200,128]{1,0:T(8,128)S(1)} %get-tuple-element.89.refs_0_, f32[200,128]{1,0:T(8,128)S(1)} %collective-permute-done.13.refs_1_, f32[768,128]{1,0:T(8,128)S(1)} %get-tuple-element.90.refs_2_, ...), custom_call_target="tpu_custom_call" | custom-call | flops 402653184 | bytes 3289088 | tf_op jit(solution)/shard_map/key_back/pallas_call | solution.py:451
  52.3 0.1 collective-permute-start.20
  52.4 0.9 %collective-permute-start.17 = (f32[200,128]{1,0:T(8,128)S(1)}, f32[200,128]{1,0:T(8,128)S(1)}, u32[]{:S(2)}, u32[]{:S(2)}) collective-permute-start(f32[200,128]{1,0:T(8,128)S(1)} %get-tuple-element.104.refs_3_), channel_id=1, source_target_pairs={{0,12},{4,8},{8,4},{12,0},{16,28},{20,24},{24,20},{28,16},{1,13},{... | collective-permute-start | bytes 307208 | tf_op jit(solution)/shard_map/ppermute | solution.py:472
  53.3 1.4 %collective-permute-start.18 = (f32[200,128]{1,0:T(8,128)S(1)}, f32[200,128]{1,0:T(8,128)S(1)}, u32[]{:S(2)}, u32[]{:S(2)}) collective-permute-start(f32[200,128]{1,0:T(8,128)S(1)} %get-tuple-element.104.refs_3_), channel_id=1, source_target_pairs={{0,8},{4,12},{8,0},{12,4},{16,24},{20,28},{24,16},{28,20},{1,9},{5... | collective-permute-start | bytes 307208 | tf_op jit(solution)/shard_map/ppermute | solution.py:472
  54.7 1.2 %collective-permute-start.19 = (f32[200,128]{1,0:T(8,128)S(1)}, f32[200,128]{1,0:T(8,128)S(1)}, u32[]{:S(2)}, u32[]{:S(2)}) collective-permute-start(f32[200,128]{1,0:T(8,128)S(1)} %get-tuple-element.104.refs_3_), channel_id=1, source_target_pairs={{0,4},{4,0},{8,12},{12,8},{16,20},{20,16},{24,28},{28,24},{1,5},{5... | collective-permute-start | bytes 307208 | tf_op jit(solution)/shard_map/ppermute | solution.py:472
  56.0 0.0 collective-permute-done.20.got_ref
  56.0 2.3 %collective-permute-start.21 = (f32[64,384]{1,0:T(8,128)S(1)}, f32[64,384]{1,0:T(8,128)S(1)}, u32[]{:S(2)}, u32[]{:S(2)}) collective-permute-start(f32[64,384]{1,0:T(8,128)S(1)} %get-tuple-element.112), channel_id=1, source_target_pairs={{0,16},{1,20},{2,24},{3,28},{4,17},{5,21},{6,25},{7,29},{8,18},{9,... | collective-permute-start | bytes 294920 | tf_op jit(solution)/shard_map/ppermute | solution.py:629
  58.4 2.5 %collective-permute-start.22 = (f32[64,384]{1,0:T(8,128)S(1)}, f32[64,384]{1,0:T(8,128)S(1)}, u32[]{:S(2)}, u32[]{:S(2)}) collective-permute-start(f32[64,384]{1,0:T(8,128)S(1)} %get-tuple-element.114), channel_id=1, source_target_pairs={{0,24},{1,28},{2,16},{3,20},{4,25},{5,29},{6,17},{7,21},{8,26},{9,... | collective-permute-start | bytes 294920 | tf_op jit(solution)/shard_map/ppermute | solution.py:629
  60.8 0.0 collective-permute-done.17.refs_0_
  60.8 0.5 collective-permute-start.23
  61.4 0.0 collective-permute-done.18.refs_1_
  61.4 0.7 collective-permute-start.24
  62.1 0.0 collective-permute-done.19.refs_2_
  62.1 2.3 %input_rows.1 = bf16[192,512]{1,0:T(8,128)(2,1)} custom-call(f32[200,128]{1,0:T(8,128)S(1)} %collective-permute-done.17.refs_0_, f32[200,128]{1,0:T(8,128)S(1)} %collective-permute-done.18.refs_1_, f32[200,128]{1,0:T(8,128)S(1)} %collective-permute-done.19.refs_2_, f32[200,128]{1,0:T(8,128)S(1)} %get-tuple-element.104.refs_3_, ...), custom_call_target="tpu_custom_call" | custom-call | flops 3019898880 | bytes 3358720 | tf_op jit(solution)/shard_map/input_rows/pallas_call | solution.py:451
  64.3 0.3 collective-permute-done.21.refs_0_
  64.7 4.6 %collective-permute-done.22.refs_1_ = f32[64,384]{1,0:T(8,128)S(1)} collective-permute-done((f32[64,384]{1,0:T(8,128)S(1)}, f32[64,384]{1,0:T(8,128)S(1)}, u32[]{:S(2)}, u32[]{:S(2)}) %collective-permute-start.22) | collective-permute-done | bytes 98336 | tf_op jit(solution)/shard_map/ppermute | solution.py:629
  69.2 0.0 collective-permute-done.23.refs_2_
  69.2 0.7 weight_sums.1
  (24 shorter events, 0.1 us)
Async XLA Ops:
  1.3 0.9 %copy-start.9 = (bf16[3,64,512]{2,1,0:T(8,128)(2,1)S(1)}, bf16[3,64,512]{2,1,0:T(8,128)(2,1)}, u32[]{:S(2)}) copy-start(bf16[3,64,512]{2,1,0:T(8,128)(2,1)} %param.9) | copy-start | bytes 589828
  2.2 9.1 %collective-permute-start = (f32[104,512]{1,0:T(8,128)S(1)}, f32[104,512]{1,0:T(8,128)S(1)}, u32[]{:S(2)}, u32[]{:S(2)}) collective-permute-start(f32[104,512]{1,0:T(8,128)S(1)} %get-tuple-element.62.refs_0_), channel_id=1, source_target_pairs={{0,4},{4,0},{8,12},{12,8},{16,20},{20,16},{24,28},{28,24},{1,5},{5... | collective-permute-start | bytes 638984 | tf_op jit(solution)/shard_map/ppermute | solution.py:472
  5.3 8.2 %collective-permute-start.4 = (f32[104,512]{1,0:T(8,128)S(1)}, f32[104,512]{1,0:T(8,128)S(1)}, u32[]{:S(2)}, u32[]{:S(2)}) collective-permute-start(f32[104,512]{1,0:T(8,128)S(1)} %get-tuple-element.63.refs_4_), channel_id=1, source_target_pairs={{0,8},{4,12},{8,0},{12,4},{16,24},{20,28},{24,16},{28,20},{1,9},{5... | collective-permute-start | bytes 638984 | tf_op jit(solution)/shard_map/ppermute | solution.py:472
  6.8 13.4 %collective-permute-start.1 = (f32[104,512]{1,0:T(8,128)S(1)}, f32[104,512]{1,0:T(8,128)S(1)}, u32[]{:S(2)}, u32[]{:S(2)}) collective-permute-start(f32[104,512]{1,0:T(8,128)S(1)} %get-tuple-element.62.refs_0_), channel_id=1, source_target_pairs={{0,8},{4,12},{8,0},{12,4},{16,24},{20,28},{24,16},{28,20},{1,9},{5... | collective-permute-start | bytes 638984 | tf_op jit(solution)/shard_map/ppermute | solution.py:472
  7.3 12.9 %collective-permute-start.3 = (f32[104,512]{1,0:T(8,128)S(1)}, f32[104,512]{1,0:T(8,128)S(1)}, u32[]{:S(2)}, u32[]{:S(2)}) collective-permute-start(f32[104,512]{1,0:T(8,128)S(1)} %get-tuple-element.63.refs_4_), channel_id=1, source_target_pairs={{0,4},{4,0},{8,12},{12,8},{16,20},{20,16},{24,28},{28,24},{1,5},{5... | collective-permute-start | bytes 638984 | tf_op jit(solution)/shard_map/ppermute | solution.py:472
  11.4 9.8 %collective-permute-start.2 = (f32[104,512]{1,0:T(8,128)S(1)}, f32[104,512]{1,0:T(8,128)S(1)}, u32[]{:S(2)}, u32[]{:S(2)}) collective-permute-start(f32[104,512]{1,0:T(8,128)S(1)} %collective-permute-done.refs_1_), channel_id=1, source_target_pairs={{0,8},{4,12},{8,0},{12,4},{16,24},{20,28},{24,16},{28,20},{1,9},{5... | collective-permute-start | bytes 638984 | tf_op jit(solution)/shard_map/ppermute | solution.py:472
  13.5 7.6 %collective-permute-start.5 = (f32[104,512]{1,0:T(8,128)S(1)}, f32[104,512]{1,0:T(8,128)S(1)}, u32[]{:S(2)}, u32[]{:S(2)}) collective-permute-start(f32[104,512]{1,0:T(8,128)S(1)} %collective-permute-done.4.refs_6_), channel_id=1, source_target_pairs={{0,4},{4,0},{8,12},{12,8},{16,20},{20,16},{24,28},{28,24},{1,5},{5... | collective-permute-start | bytes 638984 | tf_op jit(solution)/shard_map/ppermute | solution.py:472
  15.0 1.0 %copy-start = (bf16[512,512]{1,0:T(8,128)(2,1)S(1)}, bf16[512,512]{1,0:T(8,128)(2,1)}, u32[]{:S(2)}) copy-start(bf16[512,512]{1,0:T(8,128)(2,1)} %refs_1_.1) | copy-start | bytes 1572868
  16.0 1.0 %copy-start.2 = (bf16[512,512]{1,0:T(8,128)(2,1)S(1)}, bf16[512,512]{1,0:T(8,128)(2,1)}, u32[]{:S(2)}) copy-start(bf16[512,512]{1,0:T(8,128)(2,1)} %refs_2_.1) | copy-start | bytes 1572868
  17.1 1.0 %copy-start.4 = (bf16[512,512]{1,0:T(8,128)(2,1)S(1)}, bf16[512,512]{1,0:T(8,128)(2,1)}, u32[]{:S(2)}) copy-start(bf16[512,512]{1,0:T(8,128)(2,1)} %refs_3_.1) | copy-start | bytes 1572868
  18.1 0.9 %copy-start.7 = (f32[8,64,64]{2,1,0:T(8,128)S(1)}, f32[8,64,64]{2,1,0:T(8,128)}, u32[]{:S(2)}) copy-start(f32[8,64,64]{2,1,0:T(8,128)} %refs_7_.1) | copy-start | bytes 393220
  21.1 3.7 %copy-start.10 = (bf16[256,512]{1,0:T(8,128)(2,1)S(1)}, bf16[256,512]{1,0:T(8,128)(2,1)}, u32[]{:S(2)}) copy-start(bf16[256,512]{1,0:T(8,128)(2,1)} %wd_ref.1) | copy-start | bytes 786436
  21.1 3.7 %copy-start.11 = (bf16[3,64,512]{2,1,0:T(8,128)(2,1)S(1)}, bf16[3,64,512]{2,1,0:T(8,128)(2,1)}, u32[]{:S(2)}) copy-start(bf16[3,64,512]{2,1,0:T(8,128)(2,1)} %param.10) | copy-start | bytes 589828
  22.2 5.6 %collective-permute-start.6 = (f32[200,128]{1,0:T(8,128)S(1)}, f32[200,128]{1,0:T(8,128)S(1)}, u32[]{:S(2)}, u32[]{:S(2)}) collective-permute-start(f32[200,128]{1,0:T(8,128)S(1)} %get-tuple-element.67.refs_0_), channel_id=1, source_target_pairs={{0,16},{4,20},{8,24},{12,28},{16,0},{20,4},{24,8},{28,12},{1,17},{... | collective-permute-start | bytes 307208 | tf_op jit(solution)/shard_map/ppermute | solution.py:472
  24.9 8.7 %copy-start.3 = (bf16[512,512]{1,0:T(8,128)(2,1)S(1)}, bf16[512,512]{1,0:T(8,128)(2,1)}, u32[]{:S(2)}) copy-start(bf16[512,512]{1,0:T(8,128)(2,1)} %refs_2_.1) | copy-start | bytes 1572868
  24.9 8.7 %copy-start.5 = (bf16[512,512]{1,0:T(8,128)(2,1)S(1)}, bf16[512,512]{1,0:T(8,128)(2,1)}, u32[]{:S(2)}) copy-start(bf16[512,512]{1,0:T(8,128)(2,1)} %refs_3_.1) | copy-start | bytes 1572868
  24.9 8.7 %copy-start.6 = (bf16[512,256]{1,0:T(8,128)(2,1)S(1)}, bf16[512,256]{1,0:T(8,128)(2,1)}, u32[]{:S(2)}) copy-start(bf16[512,256]{1,0:T(8,128)(2,1)} %refs_5_.1) | copy-start | bytes 786436
  25.8 7.7 %copy-start.1 = (bf16[512,512]{1,0:T(8,128)(2,1)S(1)}, bf16[512,512]{1,0:T(8,128)(2,1)}, u32[]{:S(2)}) copy-start(bf16[512,512]{1,0:T(8,128)(2,1)} %refs_1_.1) | copy-start | bytes 1572868
  28.2 6.2 %collective-permute-start.7 = (f32[192,128]{1,0:T(8,128)S(1)}, f32[192,128]{1,0:T(8,128)S(1)}, u32[]{:S(2)}, u32[]{:S(2)}) collective-permute-start(f32[192,128]{1,0:T(8,128)S(1)} %get-tuple-element.72), channel_id=1, source_target_pairs={{0,12},{4,8},{8,4},{12,0},{16,28},{20,24},{24,20},{28,16},{1,13},{... | collective-permute-start | bytes 294920 | tf_op jit(solution)/shard_map/ppermute | solution.py:472
  30.0 5.0 %collective-permute-start.8 = (f32[192,128]{1,0:T(8,128)S(1)}, f32[192,128]{1,0:T(8,128)S(1)}, u32[]{:S(2)}, u32[]{:S(2)}) collective-permute-start(f32[192,128]{1,0:T(8,128)S(1)} %get-tuple-element.73), channel_id=1, source_target_pairs={{0,8},{4,12},{8,0},{12,4},{16,24},{20,28},{24,16},{28,20},{1,9},{5... | collective-permute-start | bytes 294920 | tf_op jit(solution)/shard_map/ppermute | solution.py:472
  31.4 4.6 %collective-permute-start.9 = (f32[192,128]{1,0:T(8,128)S(1)}, f32[192,128]{1,0:T(8,128)S(1)}, u32[]{:S(2)}, u32[]{:S(2)}) collective-permute-start(f32[192,128]{1,0:T(8,128)S(1)} %get-tuple-element.74), channel_id=1, source_target_pairs={{0,4},{4,0},{8,12},{12,8},{16,20},{20,16},{24,28},{28,24},{1,5},{5... | collective-permute-start | bytes 294920 | tf_op jit(solution)/shard_map/ppermute | solution.py:472
  31.8 9.0 %collective-permute-start.14 = (f32[200,128]{1,0:T(8,128)S(1)}, f32[200,128]{1,0:T(8,128)S(1)}, u32[]{:S(2)}, u32[]{:S(2)}) collective-permute-start(f32[200,128]{1,0:T(8,128)S(1)} %get-tuple-element.93.s_ref.refs_3_), channel_id=1, source_target_pairs={{0,8},{4,12},{8,0},{12,4},{16,24},{20,28},{24,16},{28,20},{1,9},{5... | collective-permute-start | bytes 307208 | tf_op jit(solution)/shard_map/ppermute | solution.py:472
  36.8 5.6 %collective-permute-start.10 = (f32[192,128]{1,0:T(8,128)S(1)}, f32[192,128]{1,0:T(8,128)S(1)}, u32[]{:S(2)}, u32[]{:S(2)}) collective-permute-start(f32[192,128]{1,0:T(8,128)S(1)} %get-tuple-element.81), channel_id=1, source_target_pairs={{0,12},{4,8},{8,4},{12,0},{16,28},{20,24},{24,20},{28,16},{1,13},{... | collective-permute-start | bytes 294920 | tf_op jit(solution)/shard_map/ppermute | solution.py:472
  38.4 5.7 %collective-permute-start.11 = (f32[192,128]{1,0:T(8,128)S(1)}, f32[192,128]{1,0:T(8,128)S(1)}, u32[]{:S(2)}, u32[]{:S(2)}) collective-permute-start(f32[192,128]{1,0:T(8,128)S(1)} %get-tuple-element.82), channel_id=1, source_target_pairs={{0,8},{4,12},{8,0},{12,4},{16,24},{20,28},{24,16},{28,20},{1,9},{5... | collective-permute-start | bytes 294920 | tf_op jit(solution)/shard_map/ppermute | solution.py:472
  38.8 5.4 %collective-permute-start.12 = (f32[192,128]{1,0:T(8,128)S(1)}, f32[192,128]{1,0:T(8,128)S(1)}, u32[]{:S(2)}, u32[]{:S(2)}) collective-permute-start(f32[192,128]{1,0:T(8,128)S(1)} %get-tuple-element.83), channel_id=1, source_target_pairs={{0,4},{4,0},{8,12},{12,8},{16,20},{20,16},{24,28},{28,24},{1,5},{5... | collective-permute-start | bytes 294920 | tf_op jit(solution)/shard_map/ppermute | solution.py:472
  40.3 7.8 %collective-permute-start.16 = (f32[200,128]{1,0:T(8,128)S(1)}, f32[200,128]{1,0:T(8,128)S(1)}, u32[]{:S(2)}, u32[]{:S(2)}) collective-permute-start(f32[200,128]{1,0:T(8,128)S(1)} %get-tuple-element.93.s_ref.refs_3_), channel_id=1, source_target_pairs={{0,4},{4,0},{8,12},{12,8},{16,20},{20,16},{24,28},{28,24},{1,5},{5... | collective-permute-start | bytes 307208 | tf_op jit(solution)/shard_map/ppermute | solution.py:472
  40.8 7.3 %collective-permute-start.15 = (f32[200,128]{1,0:T(8,128)S(1)}, f32[200,128]{1,0:T(8,128)S(1)}, u32[]{:S(2)}, u32[]{:S(2)}) collective-permute-start(f32[200,128]{1,0:T(8,128)S(1)} %collective-permute-done.14.refs_1_), channel_id=1, source_target_pairs={{0,4},{4,0},{8,12},{12,8},{16,20},{20,16},{24,28},{28,24},{1,5},{5... | collective-permute-start | bytes 307208 | tf_op jit(solution)/shard_map/ppermute | solution.py:472
  44.5 6.7 %collective-permute-start.13 = (f32[200,128]{1,0:T(8,128)S(1)}, f32[200,128]{1,0:T(8,128)S(1)}, u32[]{:S(2)}, u32[]{:S(2)}) collective-permute-start(f32[200,128]{1,0:T(8,128)S(1)} %get-tuple-element.89.refs_0_), channel_id=1, source_target_pairs={{0,16},{4,20},{8,24},{12,28},{16,0},{20,4},{24,8},{28,12},{1,17},{... | collective-permute-start | bytes 307208 | tf_op jit(solution)/shard_map/ppermute | solution.py:472
  47.5 0.9 %copy-start.8 = (f32[8,64,64]{2,1,0:T(8,128)S(1)}, f32[8,64,64]{2,1,0:T(8,128)}, u32[]{:S(2)}) copy-start(f32[8,64,64]{2,1,0:T(8,128)} %refs_7_.1) | copy-start | bytes 393220
  52.3 3.6 %collective-permute-start.20 = (f32[2,2,64,384]{3,2,1,0:T(8,128)S(1)}, f32[2,2,64,384]{3,2,1,0:T(8,128)S(1)}, u32[]{:S(2)}, u32[]{:S(2)}) collective-permute-start(f32[2,2,64,384]{3,2,1,0:T(8,128)S(1)} %get-tuple-element.111), channel_id=1, source_target_pairs={{0,1},{1,0},{2,3},{3,2},{4,5},{5,4},{6,7},{7,6},{8,9},{9,8},{10,11... | collective-permute-start | bytes 1179656 | tf_op jit(solution)/shard_map/ppermute | solution.py:472
  52.4 8.4 %collective-permute-start.17 = (f32[200,128]{1,0:T(8,128)S(1)}, f32[200,128]{1,0:T(8,128)S(1)}, u32[]{:S(2)}, u32[]{:S(2)}) collective-permute-start(f32[200,128]{1,0:T(8,128)S(1)} %get-tuple-element.104.refs_3_), channel_id=1, source_target_pairs={{0,12},{4,8},{8,4},{12,0},{16,28},{20,24},{24,20},{28,16},{1,13},{... | collective-permute-start | bytes 307208 | tf_op jit(solution)/shard_map/ppermute | solution.py:472
  53.3 8.0 %collective-permute-start.18 = (f32[200,128]{1,0:T(8,128)S(1)}, f32[200,128]{1,0:T(8,128)S(1)}, u32[]{:S(2)}, u32[]{:S(2)}) collective-permute-start(f32[200,128]{1,0:T(8,128)S(1)} %get-tuple-element.104.refs_3_), channel_id=1, source_target_pairs={{0,8},{4,12},{8,0},{12,4},{16,24},{20,28},{24,16},{28,20},{1,9},{5... | collective-permute-start | bytes 307208 | tf_op jit(solution)/shard_map/ppermute | solution.py:472
  54.7 7.3 %collective-permute-start.19 = (f32[200,128]{1,0:T(8,128)S(1)}, f32[200,128]{1,0:T(8,128)S(1)}, u32[]{:S(2)}, u32[]{:S(2)}) collective-permute-start(f32[200,128]{1,0:T(8,128)S(1)} %get-tuple-element.104.refs_3_), channel_id=1, source_target_pairs={{0,4},{4,0},{8,12},{12,8},{16,20},{20,16},{24,28},{28,24},{1,5},{5... | collective-permute-start | bytes 307208 | tf_op jit(solution)/shard_map/ppermute | solution.py:472
  56.0 8.7 %collective-permute-start.21 = (f32[64,384]{1,0:T(8,128)S(1)}, f32[64,384]{1,0:T(8,128)S(1)}, u32[]{:S(2)}, u32[]{:S(2)}) collective-permute-start(f32[64,384]{1,0:T(8,128)S(1)} %get-tuple-element.112), channel_id=1, source_target_pairs={{0,16},{1,20},{2,24},{3,28},{4,17},{5,21},{6,25},{7,29},{8,18},{9,... | collective-permute-start | bytes 294920 | tf_op jit(solution)/shard_map/ppermute | solution.py:629
  58.4 10.9 %collective-permute-start.22 = (f32[64,384]{1,0:T(8,128)S(1)}, f32[64,384]{1,0:T(8,128)S(1)}, u32[]{:S(2)}, u32[]{:S(2)}) collective-permute-start(f32[64,384]{1,0:T(8,128)S(1)} %get-tuple-element.114), channel_id=1, source_target_pairs={{0,24},{1,28},{2,16},{3,20},{4,25},{5,29},{6,17},{7,21},{8,26},{9,... | collective-permute-start | bytes 294920 | tf_op jit(solution)/shard_map/ppermute | solution.py:629
  60.8 8.4 %collective-permute-start.23 = (f32[64,384]{1,0:T(8,128)S(1)}, f32[64,384]{1,0:T(8,128)S(1)}, u32[]{:S(2)}, u32[]{:S(2)}) collective-permute-start(f32[64,384]{1,0:T(8,128)S(1)} %get-tuple-element.115), channel_id=1, source_target_pairs={{0,8},{1,12},{2,0},{3,4},{4,9},{5,13},{6,1},{7,5},{8,10},{9,14},{1... | collective-permute-start | bytes 294920 | tf_op jit(solution)/shard_map/ppermute | solution.py:629
  61.4 7.9 %collective-permute-start.24 = (f32[64,384]{1,0:T(8,128)S(1)}, f32[64,384]{1,0:T(8,128)S(1)}, u32[]{:S(2)}, u32[]{:S(2)}) collective-permute-start(f32[64,384]{1,0:T(8,128)S(1)} %get-tuple-element.116), channel_id=1, source_target_pairs={{0,0},{1,4},{2,8},{3,12},{4,1},{5,5},{6,9},{7,13},{8,2},{9,6},{10,... | collective-permute-start | bytes 294920 | tf_op jit(solution)/shard_map/ppermute | solution.py:629

commit v12 on v10

--- a/solution.py
+++ b/solution.py
@@ -353,8 +353,19 @@
         weighted, u_ref[...], [proj_ref[...]], mask, head_ones(mask)
     )
     grad = jnp.concatenate([grad_k * factor, jnp.concatenate(grad_v, 0)], -1).astype(BF16)
-    total = dot(x_all[...], jnp.concatenate([gq_ref[...], grad], -1))
-    block = total.shape[0] // devices
+    grad = jnp.concatenate([gq_ref[...], grad], -1)
+    block = x_all.shape[0] // devices
+    low = lax.axis_index("step") % 2
+    if block % 16 == 0:
+        for ref, part in ((send_ref, 1 - low), (keep_ref, low)):
+            places = [(high, quad) for high in range(2) for quad in range(devices // 4)]
+            starts = [(4 * quad + 2 * high + part) * block for high, quad in places]
+            rows = [x_all[pl.ds(pl.multiple_of(s, block), block), :] for s in starts]
+            total = dot(jnp.concatenate(rows, 0), grad)
+            for place, (high, quad) in enumerate(places):
+                ref[high, quad] = total[place * block : (place + 1) * block]
+        return
+    total = dot(x_all[...], grad)
     for place in range(devices):
         p_ref[place % 2, place // 2 % 2, place // 4] = total[place * block : (place + 1) * block]
     low = lax.axis_index("step") % 2

time: 70.3 us -> 70.3 us (level)
  no operation moved by 1% of the time
where the time goes in v12:
time: 70.3 us; the launch traced here: 69.9 us
  starting transfers between devices  34.9 us (50%)
  waiting for transfers between devices  16.7 us (24%)
  Pallas kernels  11.4 us (16%)
  local copies, waits for them, and re-layouts  5.37 us (8%)
  between operations  1.47 us (2%)
    ppermute x21, starting transfers between devices, swap(): lax.ppermute(a, axis, [(i, i ^ bit) for i in range(lax.axis_size(axis))])  28.9 us
    ppermute x21, waiting for transfers between devices, swap(): lax.ppermute(a, axis, [(i, i ^ bit) for i in range(lax.axis_size(axis))])  14.5 us
    pallas_call x14, Pallas kernels, call(): pl.pallas_call(kernel, name=name, out_shape=outs, in_specs=[SMEM] * smem...  11.4 us
    ppermute x4, starting transfers between devices, turn(): return lax.ppermute(a, ('sensor', 'step'), pairs)  6.02 us
    unnamed x24, local copies, waits for them, and re-layouts  5.37 us
    ppermute x4, waiting for transfers between devices, turn(): return lax.ppermute(a, ('sensor', 'step'), pairs)  2.19 us
  transfers between devices with their start and end apart: 25, of which 10 were waited for; matrix products, arithmetic and copies ran while one was open for 0% of the time, Pallas kernels for 12%

profile of v12, /device:TPU:0, one launch (start us, length us, event | category | flops | bytes accessed | tf_op | source)
XLA Modules:
  0.0 69.9 jit_solution(8252576607144350033)
XLA Ops:
  1.3 0.9 %copy-done.9 = bf16[3,64,512]{2,1,0:T(8,128)(2,1)S(1)} copy-done((bf16[3,64,512]{2,1,0:T(8,128)(2,1)S(1)}, bf16[3,64,512]{2,1,0:T(8,128)(2,1)}, u32[]{:S(2)}) %copy-start.9) | copy-done | bytes 196632
  2.2 3.0 %collective-permute-start = (f32[104,512]{1,0:T(8,128)S(1)}, f32[104,512]{1,0:T(8,128)S(1)}, u32[]{:S(2)}, u32[]{:S(2)}) collective-permute-start(f32[104,512]{1,0:T(8,128)S(1)} %get-tuple-element.62.refs_0_), channel_id=1, source_target_pairs={{0,4},{4,0},{8,12},{12,8},{16,20},{20,16},{24,28},{28,24},{1,5},{5... | collective-permute-start | bytes 638984 | tf_op jit(solution)/shard_map/ppermute | solution.py:483
  5.3 1.6 %collective-permute-start.4 = (f32[104,512]{1,0:T(8,128)S(1)}, f32[104,512]{1,0:T(8,128)S(1)}, u32[]{:S(2)}, u32[]{:S(2)}) collective-permute-start(f32[104,512]{1,0:T(8,128)S(1)} %get-tuple-element.63.refs_4_), channel_id=1, source_target_pairs={{0,8},{4,12},{8,0},{12,4},{16,24},{20,28},{24,16},{28,20},{1,9},{5... | collective-permute-start | bytes 638984 | tf_op jit(solution)/shard_map/ppermute | solution.py:483
  6.8 0.4 collective-permute-start.1
  7.3 0.1 collective-permute-start.3
  7.4 4.0 %collective-permute-done.refs_1_ = f32[104,512]{1,0:T(8,128)S(1)} collective-permute-done((f32[104,512]{1,0:T(8,128)S(1)}, f32[104,512]{1,0:T(8,128)S(1)}, u32[]{:S(2)}, u32[]{:S(2)}) %collective-permute-start) | collective-permute-done | bytes 213024 | tf_op jit(solution)/shard_map/ppermute | solution.py:483
  11.4 2.1 %collective-permute-start.2 = (f32[104,512]{1,0:T(8,128)S(1)}, f32[104,512]{1,0:T(8,128)S(1)}, u32[]{:S(2)}, u32[]{:S(2)}) collective-permute-start(f32[104,512]{1,0:T(8,128)S(1)} %collective-permute-done.refs_1_), channel_id=1, source_target_pairs={{0,8},{4,12},{8,0},{12,4},{16,24},{20,28},{24,16},{28,20},{1,9},{5... | collective-permute-start | bytes 638984 | tf_op jit(solution)/shard_map/ppermute | solution.py:483
  13.5 0.0 collective-permute-done.4.refs_6_
  13.5 1.5 %collective-permute-start.5 = (f32[104,512]{1,0:T(8,128)S(1)}, f32[104,512]{1,0:T(8,128)S(1)}, u32[]{:S(2)}, u32[]{:S(2)}) collective-permute-start(f32[104,512]{1,0:T(8,128)S(1)} %collective-permute-done.4.refs_6_), channel_id=1, source_target_pairs={{0,4},{4,0},{8,12},{12,8},{16,20},{20,16},{24,28},{28,24},{1,5},{5... | collective-permute-start | bytes 638984 | tf_op jit(solution)/shard_map/ppermute | solution.py:483
  15.0 1.0 %copy-done = bf16[512,512]{1,0:T(8,128)(2,1)S(1)} copy-done((bf16[512,512]{1,0:T(8,128)(2,1)S(1)}, bf16[512,512]{1,0:T(8,128)(2,1)}, u32[]{:S(2)}) %copy-start) | copy-done | bytes 524312
  16.0 1.0 %copy-done.2 = bf16[512,512]{1,0:T(8,128)(2,1)S(1)} copy-done((bf16[512,512]{1,0:T(8,128)(2,1)S(1)}, bf16[512,512]{1,0:T(8,128)(2,1)}, u32[]{:S(2)}) %copy-start.2) | copy-done | bytes 524312
  17.1 1.0 %copy-done.4 = bf16[512,512]{1,0:T(8,128)(2,1)S(1)} copy-done((bf16[512,512]{1,0:T(8,128)(2,1)S(1)}, bf16[512,512]{1,0:T(8,128)(2,1)}, u32[]{:S(2)}) %copy-start.4) | copy-done | bytes 524312
  18.1 0.9 %copy-done.7 = f32[8,64,64]{2,1,0:T(8,128)S(1)} copy-done((f32[8,64,64]{2,1,0:T(8,128)S(1)}, f32[8,64,64]{2,1,0:T(8,128)}, u32[]{:S(2)}) %copy-start.7) | copy-done | bytes 131096
  19.1 1.1 %local_keys.1 = (bf16[512,128]{1,0:T(8,128)(2,1)S(1)}, bf16[512,128]{1,0:T(8,128)(2,1)S(1)}, bf16[512,128]{1,0:T(8,128)(2,1)S(1)}, f32[64,128]{1,0:T(8,128)S(1)}...) custom-call(s32[1]{0:T(128)S(6)} %copy.13.live_ref, ...), custom_call_target="tpu_custom_call" | custom-call | flops 301989888 | bytes 4292612 | tf_op jit(solution)/shard_map/local_keys/pallas_call | solution.py:462
  20.2 0.0 collective-permute-done.1.refs_2_
  20.2 0.0 collective-permute-done.3.refs_5_
  20.2 0.9 %collective-permute-done.2.refs_3_ = f32[104,512]{1,0:T(8,128)S(1)} collective-permute-done((f32[104,512]{1,0:T(8,128)S(1)}, f32[104,512]{1,0:T(8,128)S(1)}, u32[]{:S(2)}, u32[]{:S(2)}) %collective-permute-start.2) | collective-permute-done | bytes 213024 | tf_op jit(solution)/shard_map/ppermute | solution.py:483
  21.1 0.0 collective-permute-done.5.refs_7_
  21.1 1.1 %keys.1 = (bf16[768,512]{1,0:T(8,128)(2,1)S(1)}, f32[768,128]{1,0:T(8,128)S(1)}, f32[768,128]{1,0:T(8,128)S(1)}, f32[768,128]{1,0:T(8,128)S(1)}, f32[200,128]{1,0:T(8,128)S(1)}) custom-call(f32[104,512]{1,0:T(8,128)S(1)} %get-tuple-element.62.refs_0_, f32[104,512]{1,0:T(8,128)S(1)} %collective-permute-done.refs_1_, ...), custom_call_target="tpu_custom_call" | custom-call | flops 301989888 | bytes 4067328 | tf_op jit(solution)/shard_map/keys/pallas_call | solution.py:462
  22.2 2.6 %collective-permute-start.6 = (f32[200,128]{1,0:T(8,128)S(1)}, f32[200,128]{1,0:T(8,128)S(1)}, u32[]{:S(2)}, u32[]{:S(2)}) collective-permute-start(f32[200,128]{1,0:T(8,128)S(1)} %get-tuple-element.67.refs_0_), channel_id=1, source_target_pairs={{0,16},{4,20},{8,24},{12,28},{16,0},{20,4},{24,8},{28,12},{1,17},{... | collective-permute-start | bytes 307208 | tf_op jit(solution)/shard_map/ppermute | solution.py:483
  24.9 0.0 copy-start.6
  24.9 0.9 %queries.1 = (f32[768,128]{1,0:T(8,128)S(1)}, f32[768,128]{1,0:T(8,128)S(1)}, f32[192,256]{1,0:T(8,128)S(1)}) custom-call(s32[1]{0:T(128)S(6)} %copy.13.live_ref, bf16[768,512]{1,0:T(8,128)(2,1)S(1)} %get-tuple-element.68.x_ref.refs_0_, bf16[192,512]{1,0:T(8,128)(2,1)S(1)} %bitcast.5, bf16[512,128]{1,0:T(8,128)(2,1)S(1)} %get-tuple-element.69.wq_ref, ...), custom_call_target="tpu_custom_call" | custom-call | flops 201326592 | bytes 2392068 | tf_op jit(solution)/shard_map/queries/pallas_call | solution.py:462
  25.8 0.0 copy-start.1
  25.8 2.0 %collective-permute-done.6.refs_1_ = f32[200,128]{1,0:T(8,128)S(1)} collective-permute-done((f32[200,128]{1,0:T(8,128)S(1)}, f32[200,128]{1,0:T(8,128)S(1)}, u32[]{:S(2)}, u32[]{:S(2)}) %collective-permute-start.6) | collective-permute-done | bytes 102432 | tf_op jit(solution)/shard_map/ppermute | solution.py:483
  27.8 0.4 attend.1
  28.2 1.8 %collective-permute-start.7 = (f32[192,128]{1,0:T(8,128)S(1)}, f32[192,128]{1,0:T(8,128)S(1)}, u32[]{:S(2)}, u32[]{:S(2)}) collective-permute-start(f32[192,128]{1,0:T(8,128)S(1)} %get-tuple-element.72), channel_id=1, source_target_pairs={{0,12},{4,8},{8,4},{12,0},{16,28},{20,24},{24,20},{28,16},{1,13},{... | collective-permute-start | bytes 294920 | tf_op jit(solution)/shard_map/ppermute | solution.py:483
  30.0 1.4 %collective-permute-start.8 = (f32[192,128]{1,0:T(8,128)S(1)}, f32[192,128]{1,0:T(8,128)S(1)}, u32[]{:S(2)}, u32[]{:S(2)}) collective-permute-start(f32[192,128]{1,0:T(8,128)S(1)} %get-tuple-element.73), channel_id=1, source_target_pairs={{0,8},{4,12},{8,0},{12,4},{16,24},{20,28},{24,16},{28,20},{1,9},{5... | collective-permute-start | bytes 294920 | tf_op jit(solution)/shard_map/ppermute | solution.py:483
  31.4 0.4 collective-permute-start.9
  31.8 1.8 %collective-permute-start.14 = (f32[200,128]{1,0:T(8,128)S(1)}, f32[200,128]{1,0:T(8,128)S(1)}, u32[]{:S(2)}, u32[]{:S(2)}) collective-permute-start(f32[200,128]{1,0:T(8,128)S(1)} %get-tuple-element.93.s_ref.refs_3_), channel_id=1, source_target_pairs={{0,8},{4,12},{8,0},{12,4},{16,24},{20,28},{24,16},{28,20},{1,9},{5... | collective-permute-start | bytes 307208 | tf_op jit(solution)/shard_map/ppermute | solution.py:483
  33.6 0.7 %transposes.1 = (bf16[512,768]{1,0:T(8,128)(2,1)S(1)}, bf16[512,512]{1,0:T(8,128)(2,1)S(1)}, bf16[512,512]{1,0:T(8,128)(2,1)S(1)}, bf16[512,512]{1,0:T(8,128)(2,1)S(1)}, bf16[256,512]{1,0:T(8,128)(2,1)S(1)}) custom-call(bf16[768,512]{1,0:T(8,128)(2,1)S(1)} %get-tuple-element.68.x_ref.refs_0_, bf16[512,512]{1,0:T(8,128)(2,1)S(1)} %copy-done.1, ...), custom_call_target="tpu_custom_call" | custom-call | bytes 5242880 | tf_op jit(solution)/shard_map/transposes/pallas_call | solution.py:462
  34.3 0.1 collective-permute-done.7.refs_3_
  34.4 0.6 collective-permute-done.8.refs_2_
  35.0 1.0 %collective-permute-done.9.refs_1_ = f32[192,128]{1,0:T(8,128)S(1)} collective-permute-done((f32[192,128]{1,0:T(8,128)S(1)}, f32[192,128]{1,0:T(8,128)S(1)}, u32[]{:S(2)}, u32[]{:S(2)}) %collective-permute-start.9) | collective-permute-done | bytes 98336 | tf_op jit(solution)/shard_map/ppermute | solution.py:483
  36.0 0.7 %feed_forward.1 = (f32[192,512]{1,0:T(8,128)S(1)}, f32[192,512]{1,0:T(8,128)S(1)}, f32[192,128]{1,0:T(8,128)S(1)}, f32[192,128]{1,0:T(8,128)S(1)}, f32[192,128]{1,0:T(8,128)S(1)}, /*index=5*/f32[192,128]{1,0:T(8,128)S(1)}) custom-call(f32[192,128]{1,0:T(8,128)S(1)} %get-tuple-element.71.refs_0_, f32[192,128]{1,0:T(8,128)S(1)} %collective-permute-done.9.refs_1_, ...), custom_call_target="tpu_custom_call" | custom-call | flops 100663296 | bytes 2293760 | tf_op jit(solution)/shard_map/feed_forward/pallas_call | solution.py:462
  36.8 1.7 %collective-permute-start.10 = (f32[192,128]{1,0:T(8,128)S(1)}, f32[192,128]{1,0:T(8,128)S(1)}, u32[]{:S(2)}, u32[]{:S(2)}) collective-permute-start(f32[192,128]{1,0:T(8,128)S(1)} %get-tuple-element.81), channel_id=1, source_target_pairs={{0,12},{4,8},{8,4},{12,0},{16,28},{20,24},{24,20},{28,16},{1,13},{... | collective-permute-start | bytes 294920 | tf_op jit(solution)/shard_map/ppermute | solution.py:483
  38.4 0.4 collective-permute-start.11
  38.8 1.5 %collective-permute-start.12 = (f32[192,128]{1,0:T(8,128)S(1)}, f32[192,128]{1,0:T(8,128)S(1)}, u32[]{:S(2)}, u32[]{:S(2)}) collective-permute-start(f32[192,128]{1,0:T(8,128)S(1)} %get-tuple-element.83), channel_id=1, source_target_pairs={{0,4},{4,0},{8,12},{12,8},{16,20},{20,16},{24,28},{28,24},{1,5},{5... | collective-permute-start | bytes 294920 | tf_op jit(solution)/shard_map/ppermute | solution.py:483
  40.3 0.5 collective-permute-start.16
  40.8 0.0 collective-permute-done.14.refs_1_
  40.8 1.5 %collective-permute-start.15 = (f32[200,128]{1,0:T(8,128)S(1)}, f32[200,128]{1,0:T(8,128)S(1)}, u32[]{:S(2)}, u32[]{:S(2)}) collective-permute-start(f32[200,128]{1,0:T(8,128)S(1)} %collective-permute-done.14.refs_1_), channel_id=1, source_target_pairs={{0,4},{4,0},{8,12},{12,8},{16,20},{20,16},{24,28},{28,24},{1,5},{5... | collective-permute-start | bytes 307208 | tf_op jit(solution)/shard_map/ppermute | solution.py:483
  42.3 1.8 %collective-permute-done.11.refs_2_ = f32[192,128]{1,0:T(8,128)S(1)} collective-permute-done((f32[192,128]{1,0:T(8,128)S(1)}, f32[192,128]{1,0:T(8,128)S(1)}, u32[]{:S(2)}, u32[]{:S(2)}) %collective-permute-start.11) | collective-permute-done | bytes 98336 | tf_op jit(solution)/shard_map/ppermute | solution.py:483
  44.1 0.4 grad_summary.1
  44.5 3.0 %collective-permute-start.13 = (f32[200,128]{1,0:T(8,128)S(1)}, f32[200,128]{1,0:T(8,128)S(1)}, u32[]{:S(2)}, u32[]{:S(2)}) collective-permute-start(f32[200,128]{1,0:T(8,128)S(1)} %get-tuple-element.89.refs_0_), channel_id=1, source_target_pairs={{0,16},{4,20},{8,24},{12,28},{16,0},{20,4},{24,8},{28,12},{1,17},{... | collective-permute-start | bytes 307208 | tf_op jit(solution)/shard_map/ppermute | solution.py:483
  47.5 0.6 query_back.1.refs_6_
  48.1 0.0 collective-permute-done.16.refs_2_
  48.1 0.0 collective-permute-done.15.refs_0_
  48.1 0.3 copy-done.8
  48.4 1.4 %query_rows.1.refs_8_ = f32[192,512]{1,0:T(8,128)S(1)} custom-call(f32[200,128]{1,0:T(8,128)S(1)} %collective-permute-done.15.refs_0_, f32[200,128]{1,0:T(8,128)S(1)} %collective-permute-done.14.refs_1_, f32[200,128]{1,0:T(8,128)S(1)} %collective-permute-done.16.refs_2_, f32[200,128]{1,0:T(8,128)S(1)} %get-tuple-element.93.s_ref.refs_3_, ...), custom_call_target="tpu_custom_call" | custom-call | flops 301989888 | bytes 3031040 | tf_op jit(solution)/shard_map/query_rows/pallas_call | solution.py:462
  49.9 1.4 %collective-permute-done.13.refs_1_ = f32[200,128]{1,0:T(8,128)S(1)} collective-permute-done((f32[200,128]{1,0:T(8,128)S(1)}, f32[200,128]{1,0:T(8,128)S(1)}, u32[]{:S(2)}, u32[]{:S(2)}) %collective-permute-start.13) | collective-permute-done | bytes 102432 | tf_op jit(solution)/shard_map/ppermute | solution.py:483
  51.2 1.0 %key_back.1 = (f32[200,128]{1,0:T(8,128)S(1)}, f32[2,2,64,384]{3,2,1,0:T(8,128)S(1)}, f32[2,2,64,384]{3,2,1,0:T(8,128)S(1)}) custom-call(f32[200,128]{1,0:T(8,128)S(1)} %get-tuple-element.89.refs_0_, f32[200,128]{1,0:T(8,128)S(1)} %collective-permute-done.13.refs_1_, f32[768,128]{1,0:T(8,128)S(1)} %get-tuple-element.90.refs_2_, ...), custom_call_target="tpu_custom_call" | custom-call | flops 402653184 | bytes 3289088 | tf_op jit(solution)/shard_map/key_back/pallas_call | solution.py:462
  52.3 0.1 collective-permute-start.20
  52.3 0.9 %collective-permute-start.17 = (f32[200,128]{1,0:T(8,128)S(1)}, f32[200,128]{1,0:T(8,128)S(1)}, u32[]{:S(2)}, u32[]{:S(2)}) collective-permute-start(f32[200,128]{1,0:T(8,128)S(1)} %get-tuple-element.104.refs_0_), channel_id=1, source_target_pairs={{0,4},{4,0},{8,12},{12,8},{16,20},{20,16},{24,28},{28,24},{1,5},{5... | collective-permute-start | bytes 307208 | tf_op jit(solution)/shard_map/ppermute | solution.py:483
  53.2 0.6 collective-permute-start.18
  53.8 2.1 %collective-permute-start.19 = (f32[200,128]{1,0:T(8,128)S(1)}, f32[200,128]{1,0:T(8,128)S(1)}, u32[]{:S(2)}, u32[]{:S(2)}) collective-permute-start(f32[200,128]{1,0:T(8,128)S(1)} %get-tuple-element.104.refs_0_), channel_id=1, source_target_pairs={{0,12},{4,8},{8,4},{12,0},{16,28},{20,24},{24,20},{28,16},{1,13},{... | collective-permute-start | bytes 307208 | tf_op jit(solution)/shard_map/ppermute | solution.py:483
  55.9 0.0 collective-permute-done.20.got_ref
  55.9 2.3 %collective-permute-start.21 = (f32[64,384]{1,0:T(8,128)S(1)}, f32[64,384]{1,0:T(8,128)S(1)}, u32[]{:S(2)}, u32[]{:S(2)}) collective-permute-start(f32[64,384]{1,0:T(8,128)S(1)} %get-tuple-element.112), channel_id=1, source_target_pairs={{0,16},{1,20},{2,24},{3,28},{4,17},{5,21},{6,25},{7,29},{8,18},{9,... | collective-permute-start | bytes 294920 | tf_op jit(solution)/shard_map/ppermute | solution.py:640
  58.3 2.5 %collective-permute-start.22 = (f32[64,384]{1,0:T(8,128)S(1)}, f32[64,384]{1,0:T(8,128)S(1)}, u32[]{:S(2)}, u32[]{:S(2)}) collective-permute-start(f32[64,384]{1,0:T(8,128)S(1)} %get-tuple-element.114), channel_id=1, source_target_pairs={{0,24},{1,28},{2,16},{3,20},{4,25},{5,29},{6,17},{7,21},{8,26},{9,... | collective-permute-start | bytes 294920 | tf_op jit(solution)/shard_map/ppermute | solution.py:640
  60.8 0.0 collective-permute-done.17.refs_1_
  60.8 0.5 collective-permute-start.23
  61.3 0.7 collective-permute-start.24
  62.0 2.8 %collective-permute-done.19.refs_3_ = f32[200,128]{1,0:T(8,128)S(1)} collective-permute-done((f32[200,128]{1,0:T(8,128)S(1)}, f32[200,128]{1,0:T(8,128)S(1)}, u32[]{:S(2)}, u32[]{:S(2)}) %collective-permute-start.19) | collective-permute-done | bytes 102432 | tf_op jit(solution)/shard_map/ppermute | solution.py:483
  64.8 2.2 %input_rows.1 = bf16[192,512]{1,0:T(8,128)(2,1)} custom-call(f32[200,128]{1,0:T(8,128)S(1)} %get-tuple-element.104.refs_0_, f32[200,128]{1,0:T(8,128)S(1)} %collective-permute-done.17.refs_1_, f32[200,128]{1,0:T(8,128)S(1)} %collective-permute-done.18.refs_2_, f32[200,128]{1,0:T(8,128)S(1)} %collective-permute-done.19.refs_3_, ...), custom_call_target="tpu_custom_call" | custom-call | flops 3019898880 | bytes 3358720 | tf_op jit(solution)/shard_map/input_rows/pallas_call | solution.py:462
  67.0 2.2 %collective-permute-done.22.refs_1_ = f32[64,384]{1,0:T(8,128)S(1)} collective-permute-done((f32[64,384]{1,0:T(8,128)S(1)}, f32[64,384]{1,0:T(8,128)S(1)}, u32[]{:S(2)}, u32[]{:S(2)}) %collective-permute-start.22) | collective-permute-done | bytes 98336 | tf_op jit(solution)/shard_map/ppermute | solution.py:640
  69.2 0.7 weight_sums.1
  (24 shorter events, 0.1 us)
Async XLA Ops:
  1.3 0.9 %copy-start.9 = (bf16[3,64,512]{2,1,0:T(8,128)(2,1)S(1)}, bf16[3,64,512]{2,1,0:T(8,128)(2,1)}, u32[]{:S(2)}) copy-start(bf16[3,64,512]{2,1,0:T(8,128)(2,1)} %param.9) | copy-start | bytes 589828
  2.2 9.1 %collective-permute-start = (f32[104,512]{1,0:T(8,128)S(1)}, f32[104,512]{1,0:T(8,128)S(1)}, u32[]{:S(2)}, u32[]{:S(2)}) collective-permute-start(f32[104,512]{1,0:T(8,128)S(1)} %get-tuple-element.62.refs_0_), channel_id=1, source_target_pairs={{0,4},{4,0},{8,12},{12,8},{16,20},{20,16},{24,28},{28,24},{1,5},{5... | collective-permute-start | bytes 638984 | tf_op jit(solution)/shard_map/ppermute | solution.py:483
  5.3 8.2 %collective-permute-start.4 = (f32[104,512]{1,0:T(8,128)S(1)}, f32[104,512]{1,0:T(8,128)S(1)}, u32[]{:S(2)}, u32[]{:S(2)}) collective-permute-start(f32[104,512]{1,0:T(8,128)S(1)} %get-tuple-element.63.refs_4_), channel_id=1, source_target_pairs={{0,8},{4,12},{8,0},{12,4},{16,24},{20,28},{24,16},{28,20},{1,9},{5... | collective-permute-start | bytes 638984 | tf_op jit(solution)/shard_map/ppermute | solution.py:483
  6.8 13.4 %collective-permute-start.1 = (f32[104,512]{1,0:T(8,128)S(1)}, f32[104,512]{1,0:T(8,128)S(1)}, u32[]{:S(2)}, u32[]{:S(2)}) collective-permute-start(f32[104,512]{1,0:T(8,128)S(1)} %get-tuple-element.62.refs_0_), channel_id=1, source_target_pairs={{0,8},{4,12},{8,0},{12,4},{16,24},{20,28},{24,16},{28,20},{1,9},{5... | collective-permute-start | bytes 638984 | tf_op jit(solution)/shard_map/ppermute | solution.py:483
  7.3 12.9 %collective-permute-start.3 = (f32[104,512]{1,0:T(8,128)S(1)}, f32[104,512]{1,0:T(8,128)S(1)}, u32[]{:S(2)}, u32[]{:S(2)}) collective-permute-start(f32[104,512]{1,0:T(8,128)S(1)} %get-tuple-element.63.refs_4_), channel_id=1, source_target_pairs={{0,4},{4,0},{8,12},{12,8},{16,20},{20,16},{24,28},{28,24},{1,5},{5... | collective-permute-start | bytes 638984 | tf_op jit(solution)/shard_map/ppermute | solution.py:483
  11.4 9.8 %collective-permute-start.2 = (f32[104,512]{1,0:T(8,128)S(1)}, f32[104,512]{1,0:T(8,128)S(1)}, u32[]{:S(2)}, u32[]{:S(2)}) collective-permute-start(f32[104,512]{1,0:T(8,128)S(1)} %collective-permute-done.refs_1_), channel_id=1, source_target_pairs={{0,8},{4,12},{8,0},{12,4},{16,24},{20,28},{24,16},{28,20},{1,9},{5... | collective-permute-start | bytes 638984 | tf_op jit(solution)/shard_map/ppermute | solution.py:483
  13.5 7.6 %collective-permute-start.5 = (f32[104,512]{1,0:T(8,128)S(1)}, f32[104,512]{1,0:T(8,128)S(1)}, u32[]{:S(2)}, u32[]{:S(2)}) collective-permute-start(f32[104,512]{1,0:T(8,128)S(1)} %collective-permute-done.4.refs_6_), channel_id=1, source_target_pairs={{0,4},{4,0},{8,12},{12,8},{16,20},{20,16},{24,28},{28,24},{1,5},{5... | collective-permute-start | bytes 638984 | tf_op jit(solution)/shard_map/ppermute | solution.py:483
  15.0 1.0 %copy-start = (bf16[512,512]{1,0:T(8,128)(2,1)S(1)}, bf16[512,512]{1,0:T(8,128)(2,1)}, u32[]{:S(2)}) copy-start(bf16[512,512]{1,0:T(8,128)(2,1)} %refs_1_.1) | copy-start | bytes 1572868
  16.0 1.0 %copy-start.2 = (bf16[512,512]{1,0:T(8,128)(2,1)S(1)}, bf16[512,512]{1,0:T(8,128)(2,1)}, u32[]{:S(2)}) copy-start(bf16[512,512]{1,0:T(8,128)(2,1)} %refs_2_.1) | copy-start | bytes 1572868
  17.1 1.0 %copy-start.4 = (bf16[512,512]{1,0:T(8,128)(2,1)S(1)}, bf16[512,512]{1,0:T(8,128)(2,1)}, u32[]{:S(2)}) copy-start(bf16[512,512]{1,0:T(8,128)(2,1)} %refs_3_.1) | copy-start | bytes 1572868
  18.1 0.9 %copy-start.7 = (f32[8,64,64]{2,1,0:T(8,128)S(1)}, f32[8,64,64]{2,1,0:T(8,128)}, u32[]{:S(2)}) copy-start(f32[8,64,64]{2,1,0:T(8,128)} %refs_7_.1) | copy-start | bytes 393220
  21.1 3.7 %copy-start.10 = (bf16[256,512]{1,0:T(8,128)(2,1)S(1)}, bf16[256,512]{1,0:T(8,128)(2,1)}, u32[]{:S(2)}) copy-start(bf16[256,512]{1,0:T(8,128)(2,1)} %wd_ref.1) | copy-start | bytes 786436
  21.1 3.7 %copy-start.11 = (bf16[3,64,512]{2,1,0:T(8,128)(2,1)S(1)}, bf16[3,64,512]{2,1,0:T(8,128)(2,1)}, u32[]{:S(2)}) copy-start(bf16[3,64,512]{2,1,0:T(8,128)(2,1)} %param.10) | copy-start | bytes 589828
  22.2 5.6 %collective-permute-start.6 = (f32[200,128]{1,0:T(8,128)S(1)}, f32[200,128]{1,0:T(8,128)S(1)}, u32[]{:S(2)}, u32[]{:S(2)}) collective-permute-start(f32[200,128]{1,0:T(8,128)S(1)} %get-tuple-element.67.refs_0_), channel_id=1, source_target_pairs={{0,16},{4,20},{8,24},{12,28},{16,0},{20,4},{24,8},{28,12},{1,17},{... | collective-permute-start | bytes 307208 | tf_op jit(solution)/shard_map/ppermute | solution.py:483
  24.9 8.7 %copy-start.3 = (bf16[512,512]{1,0:T(8,128)(2,1)S(1)}, bf16[512,512]{1,0:T(8,128)(2,1)}, u32[]{:S(2)}) copy-start(bf16[512,512]{1,0:T(8,128)(2,1)} %refs_2_.1) | copy-start | bytes 1572868
  24.9 8.7 %copy-start.5 = (bf16[512,512]{1,0:T(8,128)(2,1)S(1)}, bf16[512,512]{1,0:T(8,128)(2,1)}, u32[]{:S(2)}) copy-start(bf16[512,512]{1,0:T(8,128)(2,1)} %refs_3_.1) | copy-start | bytes 1572868
  24.9 8.7 %copy-start.6 = (bf16[512,256]{1,0:T(8,128)(2,1)S(1)}, bf16[512,256]{1,0:T(8,128)(2,1)}, u32[]{:S(2)}) copy-start(bf16[512,256]{1,0:T(8,128)(2,1)} %refs_5_.1) | copy-start | bytes 786436
  25.8 7.7 %copy-start.1 = (bf16[512,512]{1,0:T(8,128)(2,1)S(1)}, bf16[512,512]{1,0:T(8,128)(2,1)}, u32[]{:S(2)}) copy-start(bf16[512,512]{1,0:T(8,128)(2,1)} %refs_1_.1) | copy-start | bytes 1572868
  28.2 6.2 %collective-permute-start.7 = (f32[192,128]{1,0:T(8,128)S(1)}, f32[192,128]{1,0:T(8,128)S(1)}, u32[]{:S(2)}, u32[]{:S(2)}) collective-permute-start(f32[192,128]{1,0:T(8,128)S(1)} %get-tuple-element.72), channel_id=1, source_target_pairs={{0,12},{4,8},{8,4},{12,0},{16,28},{20,24},{24,20},{28,16},{1,13},{... | collective-permute-start | bytes 294920 | tf_op jit(solution)/shard_map/ppermute | solution.py:483
  30.0 5.0 %collective-permute-start.8 = (f32[192,128]{1,0:T(8,128)S(1)}, f32[192,128]{1,0:T(8,128)S(1)}, u32[]{:S(2)}, u32[]{:S(2)}) collective-permute-start(f32[192,128]{1,0:T(8,128)S(1)} %get-tuple-element.73), channel_id=1, source_target_pairs={{0,8},{4,12},{8,0},{12,4},{16,24},{20,28},{24,16},{28,20},{1,9},{5... | collective-permute-start | bytes 294920 | tf_op jit(solution)/shard_map/ppermute | solution.py:483
  31.4 4.6 %collective-permute-start.9 = (f32[192,128]{1,0:T(8,128)S(1)}, f32[192,128]{1,0:T(8,128)S(1)}, u32[]{:S(2)}, u32[]{:S(2)}) collective-permute-start(f32[192,128]{1,0:T(8,128)S(1)} %get-tuple-element.74), channel_id=1, source_target_pairs={{0,4},{4,0},{8,12},{12,8},{16,20},{20,16},{24,28},{28,24},{1,5},{5... | collective-permute-start | bytes 294920 | tf_op jit(solution)/shard_map/ppermute | solution.py:483
  31.8 9.0 %collective-permute-start.14 = (f32[200,128]{1,0:T(8,128)S(1)}, f32[200,128]{1,0:T(8,128)S(1)}, u32[]{:S(2)}, u32[]{:S(2)}) collective-permute-start(f32[200,128]{1,0:T(8,128)S(1)} %get-tuple-element.93.s_ref.refs_3_), channel_id=1, source_target_pairs={{0,8},{4,12},{8,0},{12,4},{16,24},{20,28},{24,16},{28,20},{1,9},{5... | collective-permute-start | bytes 307208 | tf_op jit(solution)/shard_map/ppermute | solution.py:483
  36.8 5.6 %collective-permute-start.10 = (f32[192,128]{1,0:T(8,128)S(1)}, f32[192,128]{1,0:T(8,128)S(1)}, u32[]{:S(2)}, u32[]{:S(2)}) collective-permute-start(f32[192,128]{1,0:T(8,128)S(1)} %get-tuple-element.81), channel_id=1, source_target_pairs={{0,12},{4,8},{8,4},{12,0},{16,28},{20,24},{24,20},{28,16},{1,13},{... | collective-permute-start | bytes 294920 | tf_op jit(solution)/shard_map/ppermute | solution.py:483
  38.4 5.7 %collective-permute-start.11 = (f32[192,128]{1,0:T(8,128)S(1)}, f32[192,128]{1,0:T(8,128)S(1)}, u32[]{:S(2)}, u32[]{:S(2)}) collective-permute-start(f32[192,128]{1,0:T(8,128)S(1)} %get-tuple-element.82), channel_id=1, source_target_pairs={{0,8},{4,12},{8,0},{12,4},{16,24},{20,28},{24,16},{28,20},{1,9},{5... | collective-permute-start | bytes 294920 | tf_op jit(solution)/shard_map/ppermute | solution.py:483
  38.8 5.4 %collective-permute-start.12 = (f32[192,128]{1,0:T(8,128)S(1)}, f32[192,128]{1,0:T(8,128)S(1)}, u32[]{:S(2)}, u32[]{:S(2)}) collective-permute-start(f32[192,128]{1,0:T(8,128)S(1)} %get-tuple-element.83), channel_id=1, source_target_pairs={{0,4},{4,0},{8,12},{12,8},{16,20},{20,16},{24,28},{28,24},{1,5},{5... | collective-permute-start | bytes 294920 | tf_op jit(solution)/shard_map/ppermute | solution.py:483
  40.3 7.8 %collective-permute-start.16 = (f32[200,128]{1,0:T(8,128)S(1)}, f32[200,128]{1,0:T(8,128)S(1)}, u32[]{:S(2)}, u32[]{:S(2)}) collective-permute-start(f32[200,128]{1,0:T(8,128)S(1)} %get-tuple-element.93.s_ref.refs_3_), channel_id=1, source_target_pairs={{0,4},{4,0},{8,12},{12,8},{16,20},{20,16},{24,28},{28,24},{1,5},{5... | collective-permute-start | bytes 307208 | tf_op jit(solution)/shard_map/ppermute | solution.py:483
  40.8 7.3 %collective-permute-start.15 = (f32[200,128]{1,0:T(8,128)S(1)}, f32[200,128]{1,0:T(8,128)S(1)}, u32[]{:S(2)}, u32[]{:S(2)}) collective-permute-start(f32[200,128]{1,0:T(8,128)S(1)} %collective-permute-done.14.refs_1_), channel_id=1, source_target_pairs={{0,4},{4,0},{8,12},{12,8},{16,20},{20,16},{24,28},{28,24},{1,5},{5... | collective-permute-start | bytes 307208 | tf_op jit(solution)/shard_map/ppermute | solution.py:483
  44.5 6.7 %collective-permute-start.13 = (f32[200,128]{1,0:T(8,128)S(1)}, f32[200,128]{1,0:T(8,128)S(1)}, u32[]{:S(2)}, u32[]{:S(2)}) collective-permute-start(f32[200,128]{1,0:T(8,128)S(1)} %get-tuple-element.89.refs_0_), channel_id=1, source_target_pairs={{0,16},{4,20},{8,24},{12,28},{16,0},{20,4},{24,8},{28,12},{1,17},{... | collective-permute-start | bytes 307208 | tf_op jit(solution)/shard_map/ppermute | solution.py:483
  47.5 0.9 %copy-start.8 = (f32[8,64,64]{2,1,0:T(8,128)S(1)}, f32[8,64,64]{2,1,0:T(8,128)}, u32[]{:S(2)}) copy-start(f32[8,64,64]{2,1,0:T(8,128)} %refs_7_.1) | copy-start | bytes 393220
  52.3 3.6 %collective-permute-start.20 = (f32[2,2,64,384]{3,2,1,0:T(8,128)S(1)}, f32[2,2,64,384]{3,2,1,0:T(8,128)S(1)}, u32[]{:S(2)}, u32[]{:S(2)}) collective-permute-start(f32[2,2,64,384]{3,2,1,0:T(8,128)S(1)} %get-tuple-element.111), channel_id=1, source_target_pairs={{0,1},{1,0},{2,3},{3,2},{4,5},{5,4},{6,7},{7,6},{8,9},{9,8},{10,11... | collective-permute-start | bytes 1179656 | tf_op jit(solution)/shard_map/ppermute | solution.py:483
  52.3 8.4 %collective-permute-start.17 = (f32[200,128]{1,0:T(8,128)S(1)}, f32[200,128]{1,0:T(8,128)S(1)}, u32[]{:S(2)}, u32[]{:S(2)}) collective-permute-start(f32[200,128]{1,0:T(8,128)S(1)} %get-tuple-element.104.refs_0_), channel_id=1, source_target_pairs={{0,4},{4,0},{8,12},{12,8},{16,20},{20,16},{24,28},{28,24},{1,5},{5... | collective-permute-start | bytes 307208 | tf_op jit(solution)/shard_map/ppermute | solution.py:483
  53.2 8.1 %collective-permute-start.18 = (f32[200,128]{1,0:T(8,128)S(1)}, f32[200,128]{1,0:T(8,128)S(1)}, u32[]{:S(2)}, u32[]{:S(2)}) collective-permute-start(f32[200,128]{1,0:T(8,128)S(1)} %get-tuple-element.104.refs_0_), channel_id=1, source_target_pairs={{0,8},{4,12},{8,0},{12,4},{16,24},{20,28},{24,16},{28,20},{1,9},{5... | collective-permute-start | bytes 307208 | tf_op jit(solution)/shard_map/ppermute | solution.py:483
  53.8 10.9 %collective-permute-start.19 = (f32[200,128]{1,0:T(8,128)S(1)}, f32[200,128]{1,0:T(8,128)S(1)}, u32[]{:S(2)}, u32[]{:S(2)}) collective-permute-start(f32[200,128]{1,0:T(8,128)S(1)} %get-tuple-element.104.refs_0_), channel_id=1, source_target_pairs={{0,12},{4,8},{8,4},{12,0},{16,28},{20,24},{24,20},{28,16},{1,13},{... | collective-permute-start | bytes 307208 | tf_op jit(solution)/shard_map/ppermute | solution.py:483
  55.9 11.1 %collective-permute-start.21 = (f32[64,384]{1,0:T(8,128)S(1)}, f32[64,384]{1,0:T(8,128)S(1)}, u32[]{:S(2)}, u32[]{:S(2)}) collective-permute-start(f32[64,384]{1,0:T(8,128)S(1)} %get-tuple-element.112), channel_id=1, source_target_pairs={{0,16},{1,20},{2,24},{3,28},{4,17},{5,21},{6,25},{7,29},{8,18},{9,... | collective-permute-start | bytes 294920 | tf_op jit(solution)/shard_map/ppermute | solution.py:640
  58.3 10.9 %collective-permute-start.22 = (f32[64,384]{1,0:T(8,128)S(1)}, f32[64,384]{1,0:T(8,128)S(1)}, u32[]{:S(2)}, u32[]{:S(2)}) collective-permute-start(f32[64,384]{1,0:T(8,128)S(1)} %get-tuple-element.114), channel_id=1, source_target_pairs={{0,24},{1,28},{2,16},{3,20},{4,25},{5,29},{6,17},{7,21},{8,26},{9,... | collective-permute-start | bytes 294920 | tf_op jit(solution)/shard_map/ppermute | solution.py:640
  60.8 8.4 %collective-permute-start.23 = (f32[64,384]{1,0:T(8,128)S(1)}, f32[64,384]{1,0:T(8,128)S(1)}, u32[]{:S(2)}, u32[]{:S(2)}) collective-permute-start(f32[64,384]{1,0:T(8,128)S(1)} %get-tuple-element.115), channel_id=1, source_target_pairs={{0,8},{1,12},{2,0},{3,4},{4,9},{5,13},{6,1},{7,5},{8,10},{9,14},{1... | collective-permute-start | bytes 294920 | tf_op jit(solution)/shard_map/ppermute | solution.py:640
  61.3 7.9 %collective-permute-start.24 = (f32[64,384]{1,0:T(8,128)S(1)}, f32[64,384]{1,0:T(8,128)S(1)}, u32[]{:S(2)}, u32[]{:S(2)}) collective-permute-start(f32[64,384]{1,0:T(8,128)S(1)} %get-tuple-element.116), channel_id=1, source_target_pairs={{0,0},{1,4},{2,8},{3,12},{4,1},{5,5},{6,9},{7,13},{8,2},{9,6},{10,... | collective-permute-start | bytes 294920 | tf_op jit(solution)/shard_map/ppermute | solution.py:640
